TPU v7x, 32 devices: a whole 2x2x4 slice. The times are simulated.
32 devices in a mesh: dp: 4 (over y, x), ctx: 8 (over z, core).
Axes of the slice: x: 2, y: 2, z: 4, core: 2. Of those that a mesh axis runs over, the one named last changes fastest.
Arguments:
- q_nope: bfloat16 [4, 1024, 8192], P('dp', 'ctx'), may hold values from -6 to 6
- q_rope: bfloat16 [4, 1024, 4096], P('dp', 'ctx'), may hold values from -6 to 6
- grad_out: bfloat16 [4, 1024, 8192], P('dp', 'ctx'), may hold values from -6 to 6
- log_total: float32 [4, 64, 1024], P('dp', None, 'ctx'), may hold values from 5 to 6.5
- kv_latent: bfloat16 [4, 1024, 320], P('dp', 'ctx'), may hold values from -6 to 6
- up_weight: bfloat16 [256, 16384], P('ctx'), may hold values from -0.375 to 0.375
- selected: int32 [4, 16, 3], P('dp', 'ctx'), may hold values from -1 to 14, as said below
- offered: int32 [4, 8, 4], P('dp'), may hold values from 0 to 1, as said below
Outputs:
- grad_q_nope: bfloat16 [4, 1024, 8192], P('dp', 'ctx')
- grad_q_rope: bfloat16 [4, 1024, 4096], P('dp', 'ctx')
- grad_latent: float32 [4, 1024, 320], P('dp', 'ctx')
- grad_weight: float32 [256, 16384], P('ctx')
Inputs may be any that keep to these rules, and one draw needn't show every extreme that they name: offered[b, s, m] is a block number within group s's 128/64 blocks; in matching m group s offers it to group s + m + 1. `selected`: each list holds distinct global block ids, then -1 entries; every id is an earlier block of the query block's own group or a block offered to that group in one of the four matchings; a query block that is not the first of its group always lists the block just before it.
All inputs are finite; a program needn't handle non-finite values.
Results may differ from a plain program's by a relative error of at most 0.0028.
The roundings to bfloat16 on the way count: a program that leaves them out, or rounds other values in their place, can miss the bound.
Values may be sent and summed in bfloat16 or wider, within the bound.
No kernel may reach another device: no remote copies, remote signals or barrier semaphores. Data moves between devices by JAX's collectives and lax.ppermute only.
A program may use at most 192 MiB of HBM per device.

v0:
```python
import jax
import jax.numpy as jnp
from jax import lax
from jax.sharding import PartitionSpec as P

LAT = 256
ROPE = 64
NOPE = 128
VDIM = 128
BLOCK = 64


partner_offsets = (1, 2, 3, 4)


def from_behind(value, axis, steps):
    count = lax.axis_size(axis)
    initial, last = (max(0, -steps), min(count, count - steps))
    return lax.ppermute(value, axis, [(source, source + steps) for source in range(initial, last)])


def allowed_mask(selection, key_ids, first_query):
    query_ids = first_query + jnp.arange(selection.shape[0], dtype=jnp.int32)
    same_block = key_ids[None, :] == query_ids[:, None]
    picked = (
        jnp.any(selection[:, :, None] == key_ids[None, None, :], axis=1) & (key_ids >= 0)[None, :]
    )
    inner = jnp.arange(BLOCK, dtype=jnp.int32)
    causal = inner[:, None] >= inner[None, :]
    block_mask = picked[:, None, :, None] | same_block[:, None, :, None] & causal[None, :, None, :]
    return block_mask.reshape(selection.shape[0] * BLOCK, key_ids.shape[0] * BLOCK)


def head_backward(
    queries, rope_queries, out_grads, totals, key_part, value_part, rope_keys, allowed
):
    softmax_scale = 1.0 / jnp.sqrt(jnp.float32(NOPE + ROPE))
    scores = (
        jnp.einsum("qhd,khd->hqk", queries, key_part, preferred_element_type=jnp.float32)
        + jnp.einsum("qhd,kd->hqk", rope_queries, rope_keys, preferred_element_type=jnp.float32)
    ) * softmax_scale
    probabilities = jnp.where(allowed[None], jnp.exp(scores - totals[:, :, None]), jnp.float32(0.0))
    prob_grads = jnp.einsum(
        "qhd,khd->hqk", out_grads, value_part, preferred_element_type=jnp.float32
    )
    row_dot = jnp.sum(probabilities * prob_grads, axis=2, keepdims=True)
    score_grads = (probabilities * (prob_grads - row_dot)).astype(jnp.bfloat16)
    probs_low = probabilities.astype(jnp.bfloat16)
    grad_nope = (
        jnp.einsum("hqk,khd->qhd", score_grads, key_part, preferred_element_type=jnp.float32)
        * softmax_scale
    ).astype(jnp.bfloat16)
    grad_rope = (
        jnp.einsum("hqk,kd->qhd", score_grads, rope_keys, preferred_element_type=jnp.float32)
        * softmax_scale
    ).astype(jnp.bfloat16)
    key_grad = (
        jnp.einsum("hqk,qhd->khd", score_grads, queries, preferred_element_type=jnp.float32)
        * softmax_scale
    )
    value_grad = jnp.einsum(
        "hqk,qhd->khd", probs_low, out_grads, preferred_element_type=jnp.float32
    )
    both_grads = jnp.concatenate([key_grad, value_grad], axis=2).astype(jnp.bfloat16)
    rope_grad = (
        jnp.einsum("hqk,qhd->kd", score_grads, rope_queries, preferred_element_type=jnp.float32)
        * softmax_scale
    )
    return (grad_nope, grad_rope, both_grads, rope_grad)


def group_backward(queries, rope_queries, out_grads, totals, candidates, weight, allowed):
    latent_cols = candidates[:, :LAT]
    rope_keys = candidates[:, LAT:]
    expanded = jnp.dot(latent_cols, weight, preferred_element_type=jnp.float32).astype(jnp.bfloat16)
    query_len = queries.shape[0]
    key_len = candidates.shape[0]
    head_count = totals.shape[0]
    per_group = 8
    groups = head_count // per_group

    def regroup(array, width, length):
        return array.reshape(length, groups, per_group, width).transpose(1, 0, 2, 3)

    both_parts = regroup(expanded, NOPE + VDIM, key_len)
    items = (
        regroup(queries, NOPE, query_len),
        regroup(rope_queries, ROPE, query_len),
        regroup(out_grads, VDIM, query_len),
        totals.reshape(groups, per_group, query_len),
        both_parts[..., :NOPE],
        both_parts[..., NOPE:],
    )

    def one_heads(entry):
        return head_backward(
            entry[0], entry[1], entry[2], entry[3], entry[4], entry[5], rope_keys, allowed
        )

    results = lax.map(one_heads, items)
    grad_nope = results[0].transpose(1, 0, 2, 3).reshape(query_len, head_count * NOPE)
    grad_rope = results[1].transpose(1, 0, 2, 3).reshape(query_len, head_count * ROPE)
    key_grads = results[2].transpose(1, 0, 2, 3).reshape(key_len, head_count * (NOPE + VDIM))
    rope_part = jnp.sum(results[3], axis=0)
    latent_grad = lax.dot_general(
        key_grads, weight, (((1,), (1,)), ((), ())), preferred_element_type=jnp.float32
    )
    cand_grad = jnp.concatenate([latent_grad, rope_part], axis=1)
    return (grad_nope, grad_rope, key_grads, cand_grad)


def shards(q_nope, q_rope, grad_out, log_total, kv_latent, up_weight, selected, offered):
    group_index = lax.axis_index("ctx")
    group_len = kv_latent.shape[1]
    per_block = group_len // BLOCK
    weight = lax.all_gather(up_weight, "ctx", axis=0, tiled=True)
    own_rows = kv_latent[0]
    offer_plan = offered[0]
    pieces = [own_rows]
    piece_ids = [group_index * per_block + jnp.arange(per_block, dtype=jnp.int32)]
    for matching, offset in enumerate(partner_offsets):
        block_index = offer_plan[group_index, matching]
        block_rows = lax.dynamic_slice_in_dim(own_rows, block_index * BLOCK, BLOCK, 0)
        pieces.append(from_behind(block_rows, "ctx", offset))
        source = group_index - offset
        sender = jnp.maximum(source, 0)
        piece_ids.append(
            jnp.where(source >= 0, sender * per_block + offer_plan[sender, matching], -1)[None]
        )
    candidates = jnp.concatenate(pieces, axis=0)
    key_ids = jnp.concatenate(piece_ids, axis=0)
    allowed = allowed_mask(selected[0], key_ids, group_index * per_block)
    grad_nope, grad_rope, key_grads, cand_grad = group_backward(
        q_nope[0], q_rope[0], grad_out[0], log_total[0], candidates, weight, allowed
    )
    grad_rows = cand_grad[:group_len]
    for matching, offset in enumerate(partner_offsets):
        outgoing = cand_grad[group_len + matching * BLOCK : group_len + (matching + 1) * BLOCK]
        returned = from_behind(outgoing, "ctx", -offset)
        first_row = offer_plan[group_index, matching] * BLOCK
        current = lax.dynamic_slice_in_dim(grad_rows, first_row, BLOCK, 0)
        grad_rows = lax.dynamic_update_slice_in_dim(grad_rows, current + returned, first_row, 0)
    latent_cols = candidates[:, :LAT]
    shard_sum = lax.psum_scatter(
        lax.dot_general(
            latent_cols, key_grads, (((0,), (0,)), ((), ())), preferred_element_type=jnp.float32
        ),
        "ctx",
        scatter_dimension=0,
        tiled=True,
    )
    grad_weight = lax.psum(shard_sum, "dp")
    return (grad_nope[None], grad_rope[None], grad_rows[None], grad_weight)


def solution(mesh):
    in_specs = (
        P("dp", "ctx", None),
        P("dp", "ctx", None),
        P("dp", "ctx", None),
        P("dp", None, "ctx"),
        P("dp", "ctx", None),
        P("ctx", None),
        P("dp", "ctx", None),
        P("dp", None, None),
    )
    out_specs = (P("dp", "ctx", None), P("dp", "ctx", None), P("dp", "ctx", None), P("ctx", None))
    return jax.shard_map(shards, mesh=mesh, in_specs=in_specs, out_specs=out_specs, check_vma=False)
```

profile of v0, /device:TPU:0, one launch (start us, length us, event | category | flops | bytes accessed | tf_op | source)
XLA Modules:
  0.0 522.7 jit_solution(15037529249201123977)
XLA Ops:
  8.0 1.7 constant_dynamic-slice_fusion
  12.2 1.9 dynamic-slice_bitcast_fusion.1
  14.1 5.9 %collective-permute-start.3 = (bf16[64,320]{0,1:T(8,128)(2,1)}, bf16[64,320]{0,1:T(8,128)(2,1)S(1)}, u32[]{:S(2)}, u32[]{:S(2)}) collective-permute-start(bf16[64,320]{0,1:T(8,128)(2,1)} %get-tuple-element.189), channel_id=1, source_target_pairs={{0,4},{1,5},{2,6},{3,7},{8,12},{9,13},{10,14},{11,15},{16,20},{17,... | collective-permute-start | bytes 122888 | tf_op jit(solution)/shard_map/ppermute | solution.py:19
  20.0 3.5 collective-permute-start.1
  24.8 2.8 collective-permute-start.2
  32.6 3.2 copy.34
  35.9 4.1 copy.36
  41.1 53.4 %all-gather.2.cloned.1.call-done = bf16[256,16384]{1,0:T(8,128)(2,1)} async-done(((bf16[32,16384]{1,0:T(8,128)(2,1)}), bf16[256,16384]{1,0:T(8,128)(2,1)}) %all-gather.2.cloned.1.call-update) | async-done | bytes 8388624 | tf_op jit(solution)/shard_map/all_gather | solution.py:116
  94.4 11.4 %convolution_convert_fusion.1 = bf16[384,16384]{1,0:T(8,128)(2,1)} fusion(bf16[256,16384]{1,0:T(8,128)(2,1)} %all-gather.2.cloned.1.call-done, bf16[384,320]{0,1:T(8,128)(2,1)S(1)} %concatenate.28), kind=kOutput, calls=%fused_computation.57 | convolution fusion | flops 3227516928 | bytes 21168128 | tf_op jit(solution)/shard_map/dot_general | solution.py:75
  105.8 7.9 %copy.47 = bf16[48,8,64,256]{3,2,1,0:T(8,128)(2,1)S(1)} copy(bf16[48,8,64,256]{3,1,2,0:T(8,128)(2,1)} %bitcast.184) | data formatting | bytes 25165824
  113.8 20.5 %copy.49 = bf16[384,8,8,256]{3,0,2,1:T(8,128)(2,1)S(1)} copy(bf16[384,8,8,256]{3,2,1,0:T(8,128)(2,1)S(1)} %bitcast.183) | data formatting | bytes 25165824 | tf_op jit(solution)/shard_map/reshape | solution.py:83
  134.3 6.0 %fusion.54 = (bf16[8,384,8,128]{3,1,2,0:T(8,128)(2,1)}, bf16[8,384,8,128]{3,1,2,0:T(8,128)(2,1)}) fusion(bf16[8,384,8,256]{3,1,2,0:T(8,128)(2,1)S(1)} %bitcast.182), kind=kLoop, calls=%fused_computation.97 | loop fusion | bytes 25165824 | tf_op jit(solution)/shard_map/slice | solution.py:92
  140.3 111.6 %while.17 = (s32[]{:T(128)}, bf16[8,128,8,128]{1,3,2,0:T(8,128)(2,1)}, bf16[8,128,8,64]{1,3,2,0:T(8,128)(2,1)}, bf16[8,384,8,256]{1,3,2,0:T(8,128)(2,1)}, f32[8,...) while((s32[]{:T(128)}, ...), condition=%wide.region_3.4_spmd.clone, body=%wide.region_1.3_spmd.clone.sunk | while | flops 663084032 | bytes 25718988 | solution.py:100
  141.4 1.7 fusion.99
  144.8 1.7 multiply_reduce_fusion.2
  150.6 2.3 fusion.101
  155.4 1.7 fusion.99
  157.1 1.6 fusion.100
  158.7 1.8 multiply_reduce_fusion.2
  164.6 2.3 fusion.101
  169.3 1.7 fusion.99
  171.0 1.6 fusion.100
  172.6 1.7 multiply_reduce_fusion.2
  178.5 2.3 fusion.101
  183.2 1.7 fusion.99
  186.6 1.7 multiply_reduce_fusion.2
  192.4 2.3 fusion.101
  197.2 1.7 fusion.99
  200.5 1.8 multiply_reduce_fusion.2
  206.4 2.3 fusion.101
  211.1 1.7 fusion.99
  212.8 1.6 fusion.100
  214.5 1.7 multiply_reduce_fusion.2
  220.3 2.3 fusion.101
  225.1 1.7 fusion.99
  226.8 1.6 fusion.100
  228.5 1.7 multiply_reduce_fusion.2
  234.3 2.3 fusion.101
  239.0 1.7 fusion.99
  242.4 1.8 multiply_reduce_fusion.2
  248.3 2.3 fusion.101
  251.9 15.8 %fusion.47 = f32[256,16384]{1,0:T(8,128)} fusion(bf16[384,16384]{0,1:T(8,128)(2,1)} %bitcast.185, bf16[384,320]{0,1:T(8,128)(2,1)S(1)} %copy-done.1), kind=kOutput, calls=%fused_computation.67 | convolution fusion | flops 3221225472 | bytes 29556736 | tf_op jit(solution)/shard_map/dot_general | solution.py:145
  269.3 2.9 copy.44
  272.2 169.7 %reduce-scatter.2.cloned.1.call-done = f32[32,16384]{1,0:T(8,128)} async-done(((f32[256,16384]{1,0:T(8,128)}), f32[32,16384]{1,0:T(8,128)}) %reduce-scatter.2.cloned.1.call-update) | async-done | bytes 2097168 | tf_op jit(solution)/shard_map/reduce_scatter | solution.py:144
  442.0 10.7 %fusion.55 = f32[384,256]{0,1:T(8,128)S(1)} fusion(bf16[256,16384]{1,0:T(8,128)(2,1)} %all-gather.2.cloned.1.call-done, bf16[384,16384]{0,1:T(8,128)(2,1)} %bitcast.186), kind=kOutput, calls=%fused_computation.98 | convolution fusion | flops 3221225472 | bytes 21364736 | tf_op jit(solution)/shard_map/dot_general | solution.py:105
  460.3 6.0 %collective-permute-done.5 = f32[64,320]{0,1:T(8,128)S(1)} collective-permute-done((f32[64,320]{0,1:T(8,128)S(1)}, f32[64,320]{0,1:T(8,128)S(1)}, u32[]{:S(2)}, u32[]{:S(2)}) %collective-permute-start.5) | collective-permute-done | bytes 81952 | tf_op jit(solution)/shard_map/ppermute | solution.py:19
  470.5 42.6 %all-reduce.2.cloned.1.call-done = f32[32,16384]{1,0:T(8,128)} async-done(((f32[32,16384]{1,0:T(8,128)}), f32[32,16384]{1,0:T(8,128)}) %all-reduce.2.cloned.1.call-update) | async-done | bytes 2097168 | tf_op jit(solution)/shard_map/psum | solution.py:152
  513.1 3.0 copy.74
  (134 shorter events, 77.1 us)
Async XLA Ops:
  7.2 24.1 %copy-start.5 = (bf16[1,128,4096]{2,1,0:T(8,128)(2,1)S(1)}, bf16[1,128,4096]{2,1,0:T(8,128)(2,1)}, u32[]{:S(2)}) copy-start(bf16[1,128,4096]{2,1,0:T(8,128)(2,1)} %param.11) | copy-start | bytes 3145732
  7.2 87.3 %all-gather.2.cloned.1.call-start = ((), (), s32[]{:S(2)}) async-start(), calls=%async_computation.1 | async-start | bytes 9437184 | tf_op jit(solution)/shard_map/all_gather | solution.py:116
  7.9 434.0 %reduce-scatter.2.cloned.1.call-start = ((), (), s32[]{:S(2)}) async-start(), calls=%async_computation.2 | async-start | bytes 18874368 | tf_op jit(solution)/shard_map/reduce_scatter | solution.py:144
  14.1 25.9 %collective-permute-start.3 = (bf16[64,320]{0,1:T(8,128)(2,1)}, bf16[64,320]{0,1:T(8,128)(2,1)S(1)}, u32[]{:S(2)}, u32[]{:S(2)}) collective-permute-start(bf16[64,320]{0,1:T(8,128)(2,1)} %get-tuple-element.189), channel_id=1, source_target_pairs={{0,4},{1,5},{2,6},{3,7},{8,12},{9,13},{10,14},{11,15},{16,20},{17,... | collective-permute-start | bytes 122888 | tf_op jit(solution)/shard_map/ppermute | solution.py:19
  20.0 20.0 %collective-permute-start.1 = (bf16[64,320]{0,1:T(8,128)(2,1)S(1)}, bf16[64,320]{0,1:T(8,128)(2,1)S(1)}, u32[]{:S(2)}, u32[]{:S(2)}) collective-permute-start(bf16[64,320]{0,1:T(8,128)(2,1)S(1)} %get-tuple-element.190), channel_id=1, source_target_pairs={{0,2},{1,3},{2,4},{3,5},{4,6},{5,7},{8,10},{9,11},{10,12},{11,13},... | collective-permute-start | bytes 122888 | tf_op jit(solution)/shard_map/ppermute | solution.py:19
  23.5 16.5 %collective-permute-start = (bf16[64,320]{0,1:T(8,128)(2,1)S(1)}, bf16[64,320]{0,1:T(8,128)(2,1)S(1)}, u32[]{:S(2)}, u32[]{:S(2)}) collective-permute-start(bf16[64,320]{0,1:T(8,128)(2,1)S(1)} %get-tuple-element.191), channel_id=1, source_target_pairs={{0,1},{1,2},{2,3},{3,4},{4,5},{5,6},{6,7},{8,9},{9,10},{10,11},{11... | collective-permute-start | bytes 122888 | tf_op jit(solution)/shard_map/ppermute | solution.py:19
  24.8 15.2 %collective-permute-start.2 = (bf16[64,320]{0,1:T(8,128)(2,1)S(1)}, bf16[64,320]{0,1:T(8,128)(2,1)}, u32[]{:S(2)}, u32[]{:S(2)}) collective-permute-start(bf16[64,320]{0,1:T(8,128)(2,1)S(1)} %get-tuple-element.192), channel_id=1, source_target_pairs={{0,3},{1,4},{2,5},{3,6},{4,7},{8,11},{9,12},{10,13},{11,14},{12,15... | collective-permute-start | bytes 122888 | tf_op jit(solution)/shard_map/ppermute | solution.py:19
  35.8 4.2 copy-start.4
  41.1 64.8 %copy-start = (bf16[384,320]{0,1:T(8,128)(2,1)}, bf16[384,320]{0,1:T(8,128)(2,1)S(1)}, u32[]{:S(2)}) copy-start(bf16[384,320]{0,1:T(8,128)(2,1)S(1)} %concatenate.28) | copy-start | bytes 737284
  134.3 6.0 %slice-start = ((bf16[384,320]{0,1:T(8,128)(2,1)}), bf16[384,64]{0,1:T(8,128)(2,1)S(1)}, s32[]{:S(2)}) async-start(bf16[384,320]{0,1:T(8,128)(2,1)} %copy-done), calls=%async_computation.4 | async-start | bytes 98304 | tf_op jit(solution)/shard_map/slice | solution.py:74
  140.3 111.6 %copy-start.1 = (bf16[384,320]{0,1:T(8,128)(2,1)S(1)}, bf16[384,320]{0,1:T(8,128)(2,1)}, u32[]{:S(2)}) copy-start(bf16[384,320]{0,1:T(8,128)(2,1)} %copy-done) | copy-start | bytes 737284
  267.7 1.6 copy-start.3
  267.7 245.3 %all-reduce.2.cloned.1.call-start = ((), (), s32[]{:S(2)}) async-start(), calls=%async_computation.3 | async-start | bytes 4194304 | tf_op jit(solution)/shard_map/psum | solution.py:152
  442.0 16.1 %copy-start.6 = (bf16[8,128,8,64]{1,3,2,0:T(8,128)(2,1)S(1)}, bf16[8,128,8,64]{1,3,2,0:T(8,128)(2,1)}, u32[]{:S(2)}) copy-start(bf16[8,128,8,64]{1,3,2,0:T(8,128)(2,1)} %get-tuple-element.75) | copy-start | bytes 3145732
  452.9 16.5 %collective-permute-start.7 = (f32[64,320]{0,1:T(8,128)S(1)}, f32[64,320]{0,1:T(8,128)S(1)}, u32[]{:S(2)}, u32[]{:S(2)}) collective-permute-start(f32[64,320]{0,1:T(8,128)S(1)} %get-tuple-element.185), channel_id=1, source_target_pairs={{4,0},{5,1},{6,2},{7,3},{12,8},{13,9},{14,10},{15,11},{20,16},{21,... | collective-permute-start | bytes 245768 | tf_op jit(solution)/shard_map/ppermute | solution.py:19
  454.2 5.2 %collective-permute-start.4 = (f32[64,320]{0,1:T(8,128)S(1)}, f32[64,320]{0,1:T(8,128)S(1)}, u32[]{:S(2)}, u32[]{:S(2)}) collective-permute-start(f32[64,320]{0,1:T(8,128)S(1)} %get-tuple-element.186), channel_id=1, source_target_pairs={{1,0},{2,1},{3,2},{4,3},{5,4},{6,5},{7,6},{9,8},{10,9},{11,10},{12... | collective-permute-start | bytes 245768 | tf_op jit(solution)/shard_map/ppermute | solution.py:19
  455.5 10.8 %collective-permute-start.5 = (f32[64,320]{0,1:T(8,128)S(1)}, f32[64,320]{0,1:T(8,128)S(1)}, u32[]{:S(2)}, u32[]{:S(2)}) collective-permute-start(f32[64,320]{0,1:T(8,128)S(1)} %get-tuple-element.187), channel_id=1, source_target_pairs={{2,0},{3,1},{4,2},{5,3},{6,4},{7,5},{10,8},{11,9},{12,10},{13,11},... | collective-permute-start | bytes 245768 | tf_op jit(solution)/shard_map/ppermute | solution.py:19
  456.8 11.4 %collective-permute-start.6 = (f32[64,320]{0,1:T(8,128)S(1)}, f32[64,320]{0,1:T(8,128)S(1)}, u32[]{:S(2)}, u32[]{:S(2)}) collective-permute-start(f32[64,320]{0,1:T(8,128)S(1)} %get-tuple-element.188), channel_id=1, source_target_pairs={{3,0},{4,1},{5,2},{6,3},{7,4},{11,8},{12,9},{13,10},{14,11},{15,12... | collective-permute-start | bytes 245768 | tf_op jit(solution)/shard_map/ppermute | solution.py:19
  470.5 45.6 %copy-start.2 = (f32[1,128,320]{1,2,0:T(8,128)}, f32[1,128,320]{1,2,0:T(8,128)S(1)}, u32[]{:S(2)}) copy-start(f32[1,128,320]{1,2,0:T(8,128)S(1)} %dynamic_update_slice.32) | copy-start | bytes 491524
Sparse Core Ops, SparseCore 0:
  9.6 84.7 all-gather.1
  267.9 174.0 reduce-scatter.1
  445.0 67.9 all-reduce.1
where the time goes:
time: 525 us; the launch traced here: 523 us
  waiting for transfers between devices  273 us (52%)
  matrix products  128 us (24%)
  local copies, waits for them, and re-layouts  67.8 us (13%)
  between operations  19.3 us (4%)
  starting transfers between devices  18.8 us (4%)
  other arithmetic  15.1 us (3%)
    reduce_scatter x1, waiting for transfers between devices, shards(): lax.psum_scatter(lax.dot_general(latent_cols, key_grads, (((0,), (0,)), (...  170 us
    all_gather x1, waiting for transfers between devices, shards(): weight = lax.all_gather(up_weight, 'ctx', axis=0, tiled=True)  53.4 us
    psum x1, waiting for transfers between devices, shards(): grad_weight = lax.psum(shard_sum, 'dp')  42.6 us
    unnamed x20, local copies, waits for them, and re-layouts  22.5 us
    reshape x1, local copies, waits for them, and re-layouts, regroup(): return array.reshape(length, groups, per_group, width).transpose(1, 0, 2, 3)  20.5 us
    ppermute x8, starting transfers between devices, from_behind(): lax.ppermute(value, axis, [(source, source + steps) for source in range(i...  18.7 us
    dot_general x8, matrix products, head_backward(): jnp.einsum('hqk,khd->qhd', score_grads, key_part, preferred_element_type=...  18.6 us
    dot_general x1, matrix products, shards(): lax.dot_general(latent_cols, key_grads, (((0,), (0,)), ((), ())), preferr...  15.8 us
  transfers between devices with their start and end apart: 11, of which 5 were waited for; matrix products, arithmetic and copies ran while one was open for 6% of the time, Pallas kernels for 0%

commit v1 on v0

v1 whole, which is shorter than its diff:
```python
import functools

import jax
import jax.numpy as jnp
from jax import lax
from jax.experimental import pallas as pl
from jax.experimental.pallas import tpu as pltpu
from jax.sharding import PartitionSpec as P

LAT = 256
ROPE = 64
NOPE = 128
VDIM = 128
BLOCK = 64

partner_offsets = (1, 2, 3, 4)
HIDDEN = -1e30
KERNEL_BYTES = 12 * 1024 * 1024
INPUT_BYTES = 56 * 1024 * 1024


def from_behind(value, axis, steps):
    count = lax.axis_size(axis)
    initial, last = (max(0, -steps), min(count, count - steps))
    return lax.ppermute(value, axis, [(source, source + steps) for source in range(initial, last)])


def exchange(value, axis, bits):
    count = lax.axis_size(axis)
    return lax.ppermute(value, axis, [(source, source ^ bits) for source in range(count)])


def after(value, *earlier):
    return lax.optimization_barrier((value, *earlier))[0]


def dot(left, right, left_dim, right_dim):
    return lax.dot_general(
        left,
        right,
        (((left_dim,), (right_dim,)), ((), ())),
        preferred_element_type=jnp.float32,
    )


def heads_kernel(
    place,
    q_own, rope_own, out_own, tot_own,
    q_sib, rope_sib, out_sib, tot_sib,
    weight, cand, cand_t, rope_keys, bias,
    *rest,
    earlier,
):
    gq_own, gr_own, sib_grads, *weight_grads, lat_sum, rope_sum = rest[earlier:]
    scale = 1.0 / jnp.sqrt(jnp.float32(NOPE + ROPE))
    rows = cand.shape[0] // 2
    half = weight_grads[0].shape[0]
    part = pl.program_id(0) * (len(weight_grads) // 2) // pl.num_programs(0)
    sib_q, sib_rope = sib_grads.at[:, : 2 * NOPE], sib_grads.at[:, 2 * NOPE :]
    lane_half = lax.broadcasted_iota(jnp.int32, (rows, 2 * ROPE), 1) // ROPE

    @pl.when(pl.program_id(0) == 0)
    def _():
        lat_sum[...] = jnp.zeros_like(lat_sum)
        rope_sum[...] = jnp.zeros_like(rope_sum)

    groups = (
        (q_own, rope_own, out_own, tot_own, gq_own, gr_own),
        (q_sib, rope_sib, out_sib, tot_sib, sib_q, sib_rope),
    )
    rope_grads = [None, None]
    for head in range(2):
        columns = pl.ds(head * (NOPE + VDIM), NOPE + VDIM)
        head_weight = weight[:, columns]
        expanded = dot(cand[...], head_weight, 1, 0).astype(jnp.bfloat16)
        both_grads = []
        for side, (q_ref, rope_ref, out_ref, tot_ref, gq_ref, gr_ref) in enumerate(groups):
            own_rows = slice(side * rows, (side + 1) * rows)
            here = pl.ds(head * NOPE, NOPE)
            rope_part = jnp.where(
                lane_half == head, rope_keys[own_rows, :], jnp.zeros((), jnp.bfloat16)
            )
            keys = jnp.concatenate([expanded[own_rows, :NOPE], rope_part], axis=1)
            values = expanded[own_rows, NOPE:]
            queries = jnp.concatenate([q_ref[:, here], rope_ref[...]], axis=1)
            out_grads = out_ref[:, here]
            scores = dot(keys, queries, 1, 1) * scale
            probs = jnp.exp(scores - tot_ref[0, head : head + 1, :] + bias[own_rows, :])
            prob_grads = dot(values, out_grads, 1, 1)
            row_dot = jnp.sum(probs * prob_grads, axis=0, keepdims=True)
            score_grads = (probs * (prob_grads - row_dot)).astype(jnp.bfloat16)
            query_grad = dot(score_grads, keys, 0, 0) * scale
            gq_ref[:, here] = query_grad[:, :NOPE].astype(jnp.bfloat16)
            if head == 0:
                rope_grads[side] = query_grad[:, NOPE:]
            else:
                gr_ref[...] = (rope_grads[side] + query_grad[:, NOPE:]).astype(jnp.bfloat16)
            key_grad = dot(score_grads, queries, 1, 0) * scale
            value_grad = dot(probs.astype(jnp.bfloat16), out_grads, 1, 0)
            rope_sum[own_rows, :] += jnp.where(lane_half == head, key_grad[:, NOPE:], 0.0)
            both_grads.append(
                jnp.concatenate([key_grad[:, :NOPE], value_grad], axis=1).astype(jnp.bfloat16)
            )
        key_grads = jnp.concatenate(both_grads, axis=0)
        lat_sum[...] += dot(key_grads, head_weight, 1, 1)
        weight_grad = dot(cand_t[...], key_grads, 1, 0)
        for at in range(len(weight_grads) // 2):

            @pl.when(part == at)
            def _():
                weight_grads[2 * at][:, columns] = weight_grad[:half]
                weight_grads[2 * at + 1][:, columns] = weight_grad[half:]


def chunk_backward(place, own, packed, totals, weight, shared, earlier, sizes, parts):
    q_own, rope_own, out_own = own
    tot_own, tot_sib = totals
    cand, cand_t, rope_keys, bias = shared
    tokens = q_own.shape[0]
    chunks, pairs = sizes
    wide, narrow = 2 * NOPE, 2 * ROPE
    span = pairs * (2 * wide + narrow)
    mine = lambda p, place: (place[0] * 2 + place[1]) * pairs + p
    theirs = lambda p, place: place[0] * pairs + p
    part_pairs = pairs // parts

    def part_block(part):
        return lambda p, place: (0, jnp.clip(p - part * part_pairs, 0, part_pairs - 1))

    whole = lambda array: pl.BlockSpec(array.shape, lambda p, place: (0, 0))
    in_specs = [
        pl.BlockSpec((tokens, wide), lambda p, place: (0, mine(p, place))),
        pl.BlockSpec((tokens, narrow), lambda p, place: (0, mine(p, place))),
        pl.BlockSpec((tokens, wide), lambda p, place: (0, mine(p, place))),
        pl.BlockSpec((1, 2, tokens), lambda p, place: (mine(p, place), 0, 0)),
        pl.BlockSpec((tokens, wide), lambda p, place: (0, place[0] * (span // wide) + p)),
        pl.BlockSpec(
            (tokens, narrow),
            lambda p, place: (0, place[0] * (span // narrow) + pairs * wide // narrow + p),
        ),
        pl.BlockSpec(
            (tokens, wide),
            lambda p, place: (0, place[0] * (span // wide) + pairs * (wide + narrow) // wide + p),
        ),
        pl.BlockSpec((1, 2, tokens), lambda p, place: (theirs(p, place), 0, 0)),
        pl.BlockSpec((LAT, 2 * (NOPE + VDIM)), lambda p, place: (0, p)),
        whole(cand),
        whole(cand_t),
        whole(rope_keys),
        whole(bias),
    ]
    operands = [q_own, rope_own, out_own, tot_own, packed, packed, packed, tot_sib, weight]
    operands += [cand, cand_t, rope_keys, bias]
    aliases = {}
    if earlier is not None:
        for index, array in enumerate(earlier):
            aliases[1 + len(operands)] = index
            in_specs.append(pl.BlockSpec(memory_space=pl.ANY))
            operands.append(array)
    columns = weight.shape[1]
    bf16, f32 = jnp.bfloat16, jnp.float32
    out_shape = [
        jax.ShapeDtypeStruct(q_own.shape, bf16),
        jax.ShapeDtypeStruct(rope_own.shape, bf16),
        jax.ShapeDtypeStruct((tokens, chunks * pairs * (wide + narrow)), bf16),
        *[jax.ShapeDtypeStruct((LAT // 2, columns // parts), f32)] * (2 * parts),
        jax.ShapeDtypeStruct((cand.shape[0], LAT), f32),
        jax.ShapeDtypeStruct((cand.shape[0], narrow), f32),
    ]
    out_specs = [
        pl.BlockSpec((tokens, wide), lambda p, place: (0, mine(p, place))),
        pl.BlockSpec((tokens, narrow), lambda p, place: (0, mine(p, place))),
        pl.BlockSpec((tokens, wide + narrow), lambda p, place: (0, theirs(p, place))),
        *[
            pl.BlockSpec((LAT // 2, 2 * (NOPE + VDIM)), part_block(part // 2))
            for part in range(2 * parts)
        ],
        pl.BlockSpec((cand.shape[0], LAT), lambda p, place: (0, 0)),
        pl.BlockSpec((cand.shape[0], narrow), lambda p, place: (0, 0)),
    ]
    return pl.pallas_call(
        functools.partial(heads_kernel, earlier=len(aliases)),
        grid_spec=pltpu.PrefetchScalarGridSpec(
            num_scalar_prefetch=1, grid=(pairs,), in_specs=in_specs, out_specs=out_specs
        ),
        out_shape=out_shape,
        input_output_aliases=aliases,
        compiler_params=pltpu.CompilerParams(vmem_limit_bytes=KERNEL_BYTES),
        cost_estimate=pl.CostEstimate(
            flops=pairs * 1_000_000_000, bytes_accessed=pairs * 3_000_000, transcendentals=0
        ),
        name="heads_backward",
    )(place, *operands)


def place_kernel(place, received, q_in, rope_in, q_out, rope_out):
    wide, narrow = 2 * NOPE, 2 * ROPE
    for pair in range(q_out.shape[1] // wide):
        start = pair * (wide + narrow)
        q_out[:, pair * wide : (pair + 1) * wide] = received[:, start : start + wide]
        rope_out[:, pair * narrow : (pair + 1) * narrow] = received[
            :, start + wide : start + wide + narrow
        ]


def place_columns(place, received, q_full, rope_full, chunks):
    tokens = q_full.shape[0]
    q_cols, rope_cols = q_full.shape[1] // chunks // 2, rope_full.shape[1] // chunks // 2
    put = lambda c, place: (0, c * 2 + 1 - place[1])
    return pl.pallas_call(
        place_kernel,
        grid_spec=pltpu.PrefetchScalarGridSpec(
            num_scalar_prefetch=1,
            grid=(chunks,),
            in_specs=[
                pl.BlockSpec((tokens, q_cols + rope_cols), lambda c, place: (0, c)),
                pl.BlockSpec(memory_space=pl.ANY),
                pl.BlockSpec(memory_space=pl.ANY),
            ],
            out_specs=[
                pl.BlockSpec((tokens, q_cols), put),
                pl.BlockSpec((tokens, rope_cols), put),
            ],
        ),
        out_shape=[
            jax.ShapeDtypeStruct(q_full.shape, q_full.dtype),
            jax.ShapeDtypeStruct(rope_full.shape, rope_full.dtype),
        ],
        input_output_aliases={2: 0, 3: 1},
        compiler_params=pltpu.CompilerParams(vmem_limit_bytes=KERNEL_BYTES),
        cost_estimate=pl.CostEstimate(flops=0, bytes_accessed=4_000_000, transcendentals=0),
        name="place_columns",
    )(place, received, q_full, rope_full)


def stack_kernel(*refs, arrangement):
    outs = refs[len(refs) - len(arrangement) :]
    for out, sources in zip(outs, arrangement):
        row = 0
        for index, block in sources:
            piece = refs[index]
            columns = slice(block * out.shape[1], (block + 1) * out.shape[1])
            out[row : row + piece.shape[0], :] = piece[:, columns]
            row += piece.shape[0]


def stack(inputs, arrangement, columns):
    whole = lambda shape: pl.BlockSpec(shape, lambda: (0, 0))
    shapes = [(sum(inputs[i].shape[0] for i, _ in sources), columns) for sources in arrangement]
    return pl.pallas_call(
        functools.partial(stack_kernel, arrangement=arrangement),
        in_specs=[whole(array.shape) for array in inputs],
        out_specs=[whole(shape) for shape in shapes],
        out_shape=[jax.ShapeDtypeStruct(shape, inputs[0].dtype) for shape in shapes],
        compiler_params=pltpu.CompilerParams(vmem_limit_bytes=KERNEL_BYTES),
        cost_estimate=pl.CostEstimate(flops=0, bytes_accessed=2_000_000, transcendentals=0),
        name="stack",
    )(*inputs)


def leave_kernel(place, *refs):
    *inputs, leaving, near, distant = refs
    staying, half = (near, distant), len(inputs) // 2
    width = inputs[0].shape[1]
    for at in range(half):
        leaving[:, at * width : (at + 1) * width] = inputs[at][...]
        staying[at][...] = inputs[half + at][...]


def weight_parts(place, up_weight, chunks, far):
    rows = up_weight.shape[0]
    width = up_weight.shape[1] // chunks // 2

    def column_block(t, other):
        def block(i, place):
            return (0, (place[0] ^ t) * 2 + (1 - place[1] if other else place[1]))

        return pl.BlockSpec((rows, width), block)

    return pl.pallas_call(
        leave_kernel,
        grid_spec=pltpu.PrefetchScalarGridSpec(
            num_scalar_prefetch=1,
            grid=(1,),
            in_specs=[column_block(t, other) for other in (True, False) for t in (0, far)],
            out_specs=[pl.BlockSpec((rows, 2 * width), lambda i, place: (0, 0))]
            + [pl.BlockSpec((rows, width), lambda i, place: (0, 0))] * 2,
        ),
        out_shape=[jax.ShapeDtypeStruct((rows, 2 * width), up_weight.dtype)]
        + [jax.ShapeDtypeStruct((rows, width), up_weight.dtype)] * 2,
        compiler_params=pltpu.CompilerParams(vmem_limit_bytes=INPUT_BYTES),
        cost_estimate=pl.CostEstimate(flops=0, bytes_accessed=1_000_000, transcendentals=0),
        name="weight_parts",
    )(place, *[up_weight] * 4)


def lay_kernel(place, *refs):
    *pieces, out = refs
    width = out.shape[1] // 4
    for step in range(len(pieces) // 2):
        early, late = pieces[2 * step], pieces[2 * step + 1]

        @pl.when(pl.program_id(0) == step)
        def _():
            for which in range(2):
                source = slice(which * width, (which + 1) * width)
                out[:, 2 * which * width : (2 * which + 1) * width] = early[:, source]
                out[:, (2 * which + 1) * width : (2 * which + 2) * width] = late[:, source]


def lay_out(place, pieces):
    rows, columns = pieces[0].shape
    count = len(pieces) // 2
    return pl.pallas_call(
        lay_kernel,
        grid_spec=pltpu.PrefetchScalarGridSpec(
            num_scalar_prefetch=1,
            grid=(count,),
            in_specs=[pl.BlockSpec((rows, columns), lambda t, place: (0, 0))] * len(pieces),
            out_specs=pl.BlockSpec((rows, 2 * columns), lambda t, place: (0, place[0] ^ t)),
        ),
        out_shape=jax.ShapeDtypeStruct((rows, count * 2 * columns), pieces[0].dtype),
        compiler_params=pltpu.CompilerParams(vmem_limit_bytes=KERNEL_BYTES),
        cost_estimate=pl.CostEstimate(flops=0, bytes_accessed=4_000_000, transcendentals=0),
        name="lay_out",
    )(place, *pieces)


def pack_kernel(place, q_ref, rope_ref, out_ref, packed):
    q_cols, rope_cols = q_ref.shape[1], rope_ref.shape[1]
    packed[:, :q_cols] = q_ref[...]
    packed[:, q_cols : q_cols + rope_cols] = rope_ref[...]
    packed[:, q_cols + rope_cols :] = out_ref[...]


def pack_columns(place, arrays, chunks):
    tokens = arrays[0].shape[0]
    widths = [array.shape[1] // chunks // 2 for array in arrays]
    theirs = lambda c, place: (0, c * 2 + 1 - place[1])
    return pl.pallas_call(
        pack_kernel,
        grid_spec=pltpu.PrefetchScalarGridSpec(
            num_scalar_prefetch=1,
            grid=(chunks,),
            in_specs=[pl.BlockSpec((tokens, width), theirs) for width in widths],
            out_specs=pl.BlockSpec((tokens, sum(widths)), lambda c, place: (0, c)),
        ),
        out_shape=jax.ShapeDtypeStruct((tokens, chunks * sum(widths)), arrays[0].dtype),
        compiler_params=pltpu.CompilerParams(vmem_limit_bytes=INPUT_BYTES),
        cost_estimate=pl.CostEstimate(flops=0, bytes_accessed=5_000_000, transcendentals=0),
        name="pack_columns",
    )(place, *arrays)


def halving_order(count):
    bits = count.bit_length() - 1
    partners = []
    for place in range(count):
        partner = place & 1
        for bit in range(1, bits):
            partner |= ((place >> (bits - bit)) & 1) << bit
        partners.append(partner)
    return partners


def channel_order(ctx, lat_block):
    channel = lax.broadcasted_iota(jnp.int32, (LAT, LAT), 0)
    place = lax.broadcasted_iota(jnp.int32, (LAT, LAT), 1)
    count = LAT // lat_block
    bits = count.bit_length() - 1
    block = place // lat_block
    partner = block & 1
    for bit in range(1, bits):
        partner |= ((block >> (bits - bit)) & 1) << bit
    return channel == (ctx ^ partner) * lat_block + place % lat_block


def collect_kernel(plan, own, sib, cand, cand_t, rope_keys, bias, *, blocks, lat_block):
    pieces = []
    key_at = lax.broadcasted_iota(jnp.int32, (BLOCK, 2 * BLOCK), 0)
    query = lax.broadcasted_iota(jnp.int32, (BLOCK, 2 * BLOCK), 1)
    per_side = len(blocks) // 2
    for block, other in enumerate(blocks):
        rows_ref = sib if other else own
        start = pl.multiple_of(plan[1 + block], 16)
        rows = rows_ref[pl.ds(start, BLOCK), :]
        usable = plan[1 + len(blocks) + block]
        pieces.append(jnp.where(usable > 0, rows, jnp.zeros_like(rows)))
        side, at = divmod(block, per_side)
        kinds = (sib if side else own)[2 * BLOCK : 2 * BLOCK + 16, :][:1].astype(jnp.float32)
        kind = jnp.where(
            query < BLOCK, kinds[:, 2 * at : 2 * at + 1], kinds[:, 2 * at + 1 : 2 * at + 2]
        )
        allowed = (kind > 1.5) | (kind > 0.5) & (key_at <= query % BLOCK)
        bias[block * BLOCK : (block + 1) * BLOCK, :] = jnp.where(allowed, 0.0, HIDDEN)
    both = jnp.concatenate(pieces, axis=0)
    order = channel_order(plan[0], lat_block).astype(jnp.bfloat16)
    latent = both[:, :LAT]
    cand[...] = dot(latent, order, 1, 0).astype(jnp.bfloat16)
    cand_t[...] = dot(order, latent, 0, 1).astype(jnp.bfloat16)
    twice = lax.broadcasted_iota(jnp.int32, (ROPE, 2 * ROPE), 0)
    twice = twice == lax.broadcasted_iota(jnp.int32, (ROPE, 2 * ROPE), 1) % ROPE
    rope_keys[...] = dot(both[:, LAT:], twice.astype(jnp.bfloat16), 1, 0).astype(jnp.bfloat16)


def collect(plan, own, sib, blocks, lat_block):
    rows = len(blocks) * BLOCK
    bf16 = jnp.bfloat16
    shapes = [((rows, LAT), bf16), ((LAT, rows), bf16), ((rows, 2 * ROPE), bf16)]
    shapes.append(((rows, 2 * BLOCK), jnp.float32))
    whole = lambda shape: pl.BlockSpec(shape, lambda i, plan: (0, 0))
    return pl.pallas_call(
        functools.partial(collect_kernel, blocks=blocks, lat_block=lat_block),
        grid_spec=pltpu.PrefetchScalarGridSpec(
            num_scalar_prefetch=1,
            grid=(1,),
            in_specs=[whole(own.shape), whole(sib.shape)],
            out_specs=[whole(shape) for shape, _ in shapes],
        ),
        out_shape=[jax.ShapeDtypeStruct(shape, dtype) for shape, dtype in shapes],
        compiler_params=pltpu.CompilerParams(vmem_limit_bytes=KERNEL_BYTES),
        cost_estimate=pl.CostEstimate(
            flops=250_000_000, bytes_accessed=3_000_000, transcendentals=0
        ),
        name="collect",
    )(plan, own, sib)


def spread_kernel(plan, *refs, blocks, lat_block):
    *sums, own, sib = refs
    count = len(sums) // 2
    latent, rope = sums[0][...], sums[count][...]
    for index in range(1, count):
        latent, rope = latent + sums[index][...], rope + sums[count + index][...]
    order = channel_order(plan[0], lat_block).astype(jnp.float32)
    latent = lax.dot_general(
        latent,
        order,
        (((1,), (1,)), ((), ())),
        precision=lax.Precision.HIGHEST,
        preferred_element_type=jnp.float32,
    )
    rows = jnp.concatenate([latent, rope[:, :ROPE] + rope[:, ROPE:]], axis=1)
    own[...] = jnp.zeros_like(own)
    sib[...] = jnp.zeros_like(sib)
    for block, other in enumerate(blocks):
        here = pl.ds(pl.multiple_of(plan[1 + block], 16), BLOCK)
        target = sib if other else own
        target[here, :] += rows[block * BLOCK : (block + 1) * BLOCK]


def spread(plan, latents, ropes, rows, blocks, lat_block):
    shape = (rows, LAT + ROPE)
    sums = [*latents, *ropes]
    return pl.pallas_call(
        functools.partial(spread_kernel, blocks=blocks, lat_block=lat_block),
        grid_spec=pltpu.PrefetchScalarGridSpec(
            num_scalar_prefetch=1,
            grid=(1,),
            in_specs=[pl.BlockSpec(array.shape, lambda i, plan: (0, 0)) for array in sums],
            out_specs=[pl.BlockSpec(shape, lambda i, plan: (0, 0))] * 2,
        ),
        out_shape=[jax.ShapeDtypeStruct(shape, jnp.float32)] * 2,
        compiler_params=pltpu.CompilerParams(vmem_limit_bytes=KERNEL_BYTES),
        cost_estimate=pl.CostEstimate(
            flops=700_000_000, bytes_accessed=6_000_000, transcendentals=0
        ),
        name="spread",
    )(plan, *sums)


def halve(value, axis, bit):
    half = value.shape[0] // 2
    return value[:half] + exchange(value[half:], axis, bit)


def shards(q_nope, q_rope, grad_out, log_total, kv_latent, up_weight, selected, offered):
    n_dp, n_ctx = lax.axis_size("dp"), lax.axis_size("ctx")
    dp, ctx = lax.axis_index("dp"), lax.axis_index("ctx")
    core = ctx % 2
    group_len = kv_latent.shape[1]
    per_block = group_len // BLOCK
    heads = log_total.shape[1]
    part_heads = heads // n_dp // 2
    pairs = part_heads // 2
    part_cols = part_heads * (NOPE + VDIM)
    far = n_dp - 1
    lat_block = up_weight.shape[0]

    place = jnp.stack([dp, core]).astype(jnp.int32)

    leaving, *staying = weight_parts(place, up_weight, n_dp, far)
    crossed = exchange(leaving, "ctx", 1)
    crossed, q_nope, q_rope, grad_out, log_total, kv_latent = lax.optimization_barrier(
        (crossed, q_nope, q_rope, grad_out, log_total, kv_latent)
    )
    chip_rows = stack(
        [*staying, crossed], (((0, 0), (2, 0)), ((1, 0), (2, 1))), part_cols
    )
    chip_rows, q_nope, q_rope, grad_out, log_total, kv_latent = lax.optimization_barrier(
        (chip_rows, q_nope, q_rope, grad_out, log_total, kv_latent)
    )
    queries, rope_queries, out_grads = q_nope[0], q_rope[0], grad_out[0]

    packed = exchange(
        pack_columns(place, (queries, rope_queries, out_grads), n_dp), "ctx", 1
    )
    totals = log_total[0].reshape(n_dp, 2, pairs, 2, group_len)
    tot_sib = exchange(lax.dynamic_index_in_dim(totals, 1 - core, 1, keepdims=False), "ctx", 1)
    totals = (
        totals.reshape(n_dp * 2 * pairs, 2, group_len),
        tot_sib.reshape(n_dp * pairs, 2, group_len),
    )

    offer_plan = offered[0]
    span = group_len + 16
    blocks, starts, usables = [], [], []
    for side in range(2):
        group = ctx ^ side
        offsets = [0] * per_block + list(partner_offsets)
        blocks += [(offset + side) % 2 for offset in offsets]
        source = jnp.stack([group - offset for offset in offsets])
        sender = jnp.maximum(source, 0)
        inner = jnp.concatenate(
            [
                jnp.arange(per_block, dtype=jnp.int32),
                offer_plan[sender[per_block:], jnp.arange(len(partner_offsets))],
            ]
        )
        usable = source >= 0
        behind = ctx // 2 - sender // 2
        starts.append(jnp.where(usable, behind * span + inner * BLOCK, 0))
        usables.append(usable)
        if side == 0:
            ids = jnp.where(usable, sender * per_block + inner, -1)
            query_ids = group * per_block + jnp.arange(per_block, dtype=jnp.int32)
            picked = jnp.any(selected[0][None, :, :] == ids[:, None, None], axis=2)
            picked = picked & (ids >= 0)[:, None]
            same = ids[:, None] == query_ids[None, :]
            kinds = jnp.where(picked, 2.0, jnp.where(same, 1.0, 0.0)).reshape(1, -1)
    plan = jnp.concatenate([ctx[None], *starts, *usables]).astype(jnp.int32)
    kinds = jnp.pad(kinds.astype(jnp.bfloat16), ((0, 15), (0, LAT + ROPE - kinds.shape[1])))
    bundle = jnp.concatenate([kv_latent[0], kinds], axis=0)
    bundles = [bundle, from_behind(bundle, "ctx", 2), from_behind(bundle, "ctx", 4)]
    own_bundles = stack(bundles, (((0, 0), (1, 0), (2, 0)),), LAT + ROPE)[0]
    sib_bundles = exchange(own_bundles, "ctx", 1)
    shared = collect(plan, own_bundles, sib_bundles, tuple(blocks), lat_block)

    partners = halving_order(n_ctx)[::2]
    weights = {}
    for order, t in enumerate((0, far)):
        at_step = {0: chip_rows[order]}
        if order:
            at_step[0] = after(at_step[0], packed, tot_sib, sib_bundles)
        for step in range(4, n_ctx, 4):
            at_step[step] = exchange(at_step[0], "ctx", step)
        for step in range(2, n_ctx, 4):
            at_step[step] = exchange(at_step[step - 2], "ctx", 2)
        pieces = [at_step[partner] for partner in partners]
        weights[t] = stack(
            pieces, (tuple((index, 0) for index in range(len(pieces))),), part_cols
        )[0]
    for t in range(1, far):
        weights[t] = exchange(weights[0], "dp", t)

    earlier = None
    weight_grads, latents, ropes = {}, [], []
    for t in [0, far] + list(range(1, far)):
        split = 1 if t in (0, far) else 2
        rest = chunk_backward(
            jnp.stack([dp ^ t, core]).astype(jnp.int32),
            (queries, rope_queries, out_grads),
            packed,
            totals,
            weights[t],
            shared,
            earlier,
            (n_dp, pairs),
            split,
        )
        earlier, rest = rest[:3], rest[3:]
        weight_grads[t] = (rest[0 : 2 * split : 2], rest[1 : 2 * split : 2])
        latents.append(rest[-2])
        ropes.append(rest[-1])

    q_full, rope_full, sib_grads = earlier
    received = exchange(sib_grads, "ctx", 1)
    grad_nope, grad_rope = place_columns(place, received, q_full, rope_full, n_dp)

    own_grads, sib_grads = spread(plan, latents, ropes, 3 * span, tuple(blocks), lat_block)
    grad_rows = own_grads + exchange(sib_grads, "ctx", 1)
    by_chip = [grad_rows[at * span : at * span + group_len] for at in range(3)]
    grad_rows = by_chip[0]
    for chips in (1, 2):
        grad_rows = grad_rows + from_behind(by_chip[chips], "ctx", -2 * chips)

    bits = [1 << b for b in range(n_dp.bit_length() - 1)]
    half_cols = part_cols // 2
    sums = []
    for side, order in enumerate((bits, bits[::-1])):
        parts = {t: list(weight_grads[t][side]) for t in weight_grads}
        for bit in order:
            arrived = {}
            for t in sorted((t for t in parts if t & bit), reverse=True):
                arrived[t ^ bit] = [exchange(part, "dp", bit) for part in parts[t]]
            summed = {}
            for t, more in arrived.items():
                mine = parts[t]
                pieces = []
                for half in range(2):
                    columns = slice(half * half_cols, (half + 1) * half_cols)
                    pieces.append(
                        (mine[half] if len(mine) == 2 else mine[0][:, columns])
                        + (more[half] if len(more) == 2 else more[0][:, columns])
                    )
                summed[t] = pieces
            parts = summed
        sums.append(parts[0])

    ctx_bits = [1 << b for b in range(1, n_ctx.bit_length() - 1)]
    finished = []
    for half in range(2):
        rows = sums[0][half] + exchange(sums[1][half], "ctx", ctx_bits[0])
        for bit in ctx_bits[1:]:
            rows = halve(rows, "ctx", bit)
        kept, crossed = rows[:lat_block], exchange(rows[lat_block:], "ctx", 1)
        piece = jnp.where(
            core == 0,
            jnp.concatenate([kept, crossed], axis=1),
            jnp.concatenate([crossed, kept], axis=1),
        )
        finished.append([piece] + [exchange(piece, "dp", t) for t in range(1, n_dp)])
    grad_weight = lay_out(place, [piece for both in zip(*finished) for piece in both])
    return (grad_nope[None], grad_rope[None], grad_rows[None], grad_weight)


def solution(mesh):
    in_specs = (
        P("dp", "ctx", None),
        P("dp", "ctx", None),
        P("dp", "ctx", None),
        P("dp", None, "ctx"),
        P("dp", "ctx", None),
        P("ctx", None),
        P("dp", "ctx", None),
        P("dp", None, None),
    )
    out_specs = (P("dp", "ctx", None), P("dp", "ctx", None), P("dp", "ctx", None), P("ctx", None))
    return jax.shard_map(shards, mesh=mesh, in_specs=in_specs, out_specs=out_specs, check_vma=False)
```

time: 525 us -> 258 us (0.49)
  waiting for transfers between devices: 273 us -> 87 us
  matrix products: 128 us -> 0 us
  Pallas kernels: 0 us -> 77 us
  local copies, waits for them, and re-layouts: 67.8 us -> 29.9 us
  starting transfers between devices: 18.8 us -> 51.7 us
  between operations: 19.3 us -> 1.06 us
    reduce_scatter x1 -> x0, waiting for transfers between devices: 170 us -> none  [shards(): lax.psum_scatter(lax.dot_general(latent_cols, key_grads, (((0,), (0,)), (...]
    dot_general x67 -> x0, matrix products: 128 us -> none  [the longest x8 18.6 us: head_backward(): jnp.einsum('hqk,khd->qhd', score_grads, key_part, preferred_element_type=...]
    pallas_call x0 -> x14, Pallas kernels: none -> 77 us  [the longest x4 55.6 us: chunk_backward(): pl.pallas_call(functools.partial(heads_kernel, earlier=len(aliases)), gri...]
    ppermute x0 -> x36, waiting for transfers between devices: none -> 71.3 us  [exchange(): lax.ppermute(value, axis, [(source, source ^ bits) for source in range(co...]
    all_gather x1 -> x0, waiting for transfers between devices: 53.4 us -> none  [shards(): weight = lax.all_gather(up_weight, 'ctx', axis=0, tiled=True)]
    psum x1 -> x0, waiting for transfers between devices: 42.6 us -> none  [shards(): grad_weight = lax.psum(shard_sum, 'dp')]
    ppermute x0 -> x36, starting transfers between devices: none -> 40 us  [exchange(): lax.ppermute(value, axis, [(source, source ^ bits) for source in range(co...]
    reshape x1 -> x0, local copies, waits for them, and re-layouts: 20.5 us -> none  [regroup(): return array.reshape(length, groups, per_group, width).transpose(1, 0, 2, 3)]
  transfers between devices with their start and end apart: 11 -> 40, of which waited for: 5 -> 16; matrix products, arithmetic and copies ran while one was open for 6% -> 7% of each run, Pallas kernels for 0% -> 25%
where the time goes in v1:
time: 258 us; the launch traced here: 257 us
  waiting for transfers between devices  87 us (34%)
  Pallas kernels  77 us (30%)
  starting transfers between devices  51.7 us (20%)
  local copies, waits for them, and re-layouts  29.9 us (12%)
  other arithmetic  10.6 us (4%)
    ppermute x36, waiting for transfers between devices, exchange(): lax.ppermute(value, axis, [(source, source ^ bits) for source in range(co...  71.3 us
    pallas_call x4, Pallas kernels, chunk_backward(): pl.pallas_call(functools.partial(heads_kernel, earlier=len(aliases)), gri...  55.6 us
    ppermute x36, starting transfers between devices, exchange(): lax.ppermute(value, axis, [(source, source ^ bits) for source in range(co...  40 us
    unnamed x91, local copies, waits for them, and re-layouts  23.9 us
    ppermute x4, waiting for transfers between devices, from_behind(): lax.ppermute(value, axis, [(source, source + steps) for source in range(i...  15.7 us
    ppermute x4, starting transfers between devices, from_behind(): lax.ppermute(value, axis, [(source, source + steps) for source in range(i...  11.7 us
  transfers between devices with their start and end apart: 40, of which 16 were waited for; matrix products, arithmetic and copies ran while one was open for 7% of the time, Pallas kernels for 25%

profile of v1, /device:TPU:0, one launch (start us, length us, event | category | flops | bytes accessed | tf_op | source)
XLA Modules:
  0.0 257.2 jit_solution(6373071662554418026)
XLA Ops:
  1.3 2.6 weight_parts.1
  8.3 4.8 %pack_columns.1 = bf16[128,10240]{1,0:T(8,128)(2,1)} custom-call(s32[2]{0:T(128)} %pad_add_fusion.place, bf16[128,8192]{1,0:T(8,128)(2,1)} %bitcast.48, bf16[128,4096]{1,0:T(8,128)(2,1)} %bitcast.58, bf16[128,8192]{1,0:T(8,128)(2,1)} %bitcast.53), custom_call_target="tpu_custom_call" | custom-call | bytes 5000000 | tf_op jit(solution)/shard_map/pack_columns/pallas_call | solution.py:340
  15.1 5.6 %collective-permute-start.8 = (bf16[144,320]{1,0:T(8,128)(2,1)S(1)}, bf16[144,320]{1,0:T(8,128)(2,1)S(1)}, u32[]{:S(2)}, u32[]{:S(2)}) collective-permute-start(bf16[144,320]{1,0:T(8,128)(2,1)S(1)} %fusion.3.refs_0_), channel_id=1, source_target_pairs={{0,4},{1,5},{2,6},{3,7},{8,12},{9,13},{10,14},{11,15},{16,20},{17,... | collective-permute-start | bytes 276488 | tf_op jit(solution)/shard_map/ppermute | solution.py:25
  20.7 3.5 %collective-permute-start.7 = (bf16[144,320]{1,0:T(8,128)(2,1)S(1)}, bf16[144,320]{1,0:T(8,128)(2,1)S(1)}, u32[]{:S(2)}, u32[]{:S(2)}) collective-permute-start(bf16[144,320]{1,0:T(8,128)(2,1)S(1)} %fusion.3.refs_0_), channel_id=1, source_target_pairs={{0,2},{1,3},{2,4},{3,5},{4,6},{5,7},{8,10},{9,11},{10,12},{11,13},... | collective-permute-start | bytes 276488 | tf_op jit(solution)/shard_map/ppermute | solution.py:25
  25.0 2.7 %collective-permute-done.7.refs_1_ = bf16[144,320]{1,0:T(8,128)(2,1)S(1)} collective-permute-done((bf16[144,320]{1,0:T(8,128)(2,1)S(1)}, bf16[144,320]{1,0:T(8,128)(2,1)S(1)}, u32[]{:S(2)}, u32[]{:S(2)}) %collective-permute-start.7) | collective-permute-done | bytes 92192 | tf_op jit(solution)/shard_map/ppermute | solution.py:25
  29.1 7.8 %collective-permute-start.4 = (bf16[64,2048]{1,0:T(8,128)(2,1)}, bf16[64,2048]{1,0:T(8,128)(2,1)}, u32[]{:S(2)}, u32[]{:S(2)}) collective-permute-start(bf16[64,2048]{1,0:T(8,128)(2,1)} %get-tuple-element.78.refs_0_), channel_id=1, source_target_pairs={{0,2},{1,3},{2,0},{3,1},{4,6},{5,7},{6,4},{7,5},{8,10},{9,11},{10,... | collective-permute-start | bytes 786440 | tf_op jit(solution)/shard_map/ppermute | solution.py:30
  36.9 2.7 %collective-permute-done.3.refs_1_ = bf16[64,2048]{1,0:T(8,128)(2,1)} collective-permute-done((bf16[64,2048]{1,0:T(8,128)(2,1)}, bf16[64,2048]{1,0:T(8,128)(2,1)}, u32[]{:S(2)}, u32[]{:S(2)}) %collective-permute-start.3) | collective-permute-done | bytes 262176 | tf_op jit(solution)/shard_map/ppermute | solution.py:30
  39.6 1.6 collective-permute-start.5
  41.2 3.5 %collective-permute-start.11 = (bf16[64,2048]{1,0:T(8,128)(2,1)}, bf16[64,2048]{1,0:T(8,128)(2,1)}, u32[]{:S(2)}, u32[]{:S(2)}) collective-permute-start(bf16[64,2048]{1,0:T(8,128)(2,1)} %get-tuple-element.85.refs_0_), channel_id=1, source_target_pairs={{0,4},{1,5},{2,6},{3,7},{4,0},{5,1},{6,2},{7,3},{8,12},{9,13},{10,... | collective-permute-start | bytes 786440 | tf_op jit(solution)/shard_map/ppermute | solution.py:30
  46.0 2.0 collect.1
  48.0 8.3 %collective-permute-done.5.refs_3_ = bf16[64,2048]{1,0:T(8,128)(2,1)} collective-permute-done((bf16[64,2048]{1,0:T(8,128)(2,1)}, bf16[64,2048]{1,0:T(8,128)(2,1)}, u32[]{:S(2)}, u32[]{:S(2)}) %collective-permute-start.5) | collective-permute-done | bytes 262176 | tf_op jit(solution)/shard_map/ppermute | solution.py:30
  56.4 2.2 stack.94.weight
  58.6 1.5 collective-permute-start.10
  60.1 1.5 collective-permute-start.6
  61.6 2.0 collective-permute-start.13
  63.7 1.6 copy-done.3
  66.5 14.1 %heads_backward.4 = (bf16[128,8192]{1,0:T(8,128)(2,1)}, bf16[128,4096]{1,0:T(8,128)(2,1)}, bf16[128,6144]{1,0:T(8,128)(2,1)S(1)}, f32[128,2048]{1,0:T(8,128)S(1)...) custom-call(s32[2]{0:T(128)S(1)} %copy-done.37, bf16[128,8192]{1,0:T(8,128)(2,1)S(1)} %bitcast.49, ...), custom_call_target="tpu_custom_call" | custom-call | flops 4000000000 | bytes 12000000 | tf_op jit(solution)/shard_map/heads_backward/pallas_call | solution.py:181
  85.3 13.4 %heads_backward.5 = (bf16[128,8192]{1,0:T(8,128)(2,1)}, bf16[128,4096]{1,0:T(8,128)(2,1)}, bf16[128,6144]{1,0:T(8,128)(2,1)S(1)}, f32[128,2048]{1,0:T(8,128)S(1)...) custom-call(s32[2]{0:T(128)S(1)} %pad_add_fusion.4.place, ...), custom_call_target="tpu_custom_call", output_to_operand_aliasing={{0}: (14, {}), {1}: (15, {}), {2}: (16, {})} | custom-call | flops 4000000000 | bytes 12000000 | tf_op jit(solution)/shard_map/heads_backward/pallas_call | solution.py:181
  103.8 1.6 copy-done.2
  105.4 1.6 copy-done.5
  111.5 14.2 %heads_backward.6 = (bf16[128,8192]{1,0:T(8,128)(2,1)}, bf16[128,4096]{1,0:T(8,128)(2,1)}, bf16[128,6144]{1,0:T(8,128)(2,1)S(1)}, f32[128,1024]{1,0:T(8,128)S(1)...) custom-call(s32[2]{0:T(128)S(1)} %pad_add_fusion.3.place, ...), custom_call_target="tpu_custom_call", output_to_operand_aliasing={{0}: (14, {}), {1}: (15, {}), {2}: (16, {})} | custom-call | flops 4000000000 | bytes 12000000 | tf_op jit(solution)/shard_map/heads_backward/pallas_call | solution.py:181
  125.7 14.0 %heads_backward.7 = (bf16[128,8192]{1,0:T(8,128)(2,1)}, bf16[128,4096]{1,0:T(8,128)(2,1)}, bf16[128,6144]{1,0:T(8,128)(2,1)S(1)}, f32[128,1024]{1,0:T(8,128)S(1)...) custom-call(s32[2]{0:T(128)S(1)} %pad_add_fusion.1.place, ...), custom_call_target="tpu_custom_call", output_to_operand_aliasing={{0}: (14, {}), {1}: (15, {}), {2}: (16, {})} | custom-call | flops 4000000000 | bytes 12000000 | tf_op jit(solution)/shard_map/heads_backward/pallas_call | solution.py:181
  139.7 1.5 collective-permute-start.21
  143.1 1.6 collective-permute-start.30
  145.1 1.5 collective-permute-start.18
  147.9 6.7 %collective-permute-done.21 = f32[128,1024]{1,0:T(8,128)S(1)} collective-permute-done((f32[128,1024]{1,0:T(8,128)S(1)}, f32[128,1024]{1,0:T(8,128)S(1)}, u32[]{:S(2)}, u32[]{:S(2)}) %collective-permute-start.21) | collective-permute-done | bytes 524320 | tf_op jit(solution)/shard_map/ppermute | solution.py:30
  154.6 1.5 collective-permute-start.27
  156.0 7.1 %collective-permute-done.29 = f32[128,1024]{1,0:T(8,128)S(1)} collective-permute-done((f32[128,1024]{1,0:T(8,128)S(1)}, f32[128,1024]{1,0:T(8,128)S(1)}, u32[]{:S(2)}, u32[]{:S(2)}) %collective-permute-start.29) | collective-permute-done | bytes 524320 | tf_op jit(solution)/shard_map/ppermute | solution.py:30
  163.1 1.5 collective-permute-start.28
  165.2 4.1 %collective-permute-done.23 = f32[128,1024]{1,0:T(8,128)S(1)} collective-permute-done((f32[128,1024]{1,0:T(8,128)S(1)}, f32[128,1024]{1,0:T(8,128)S(1)}, u32[]{:S(2)}, u32[]{:S(2)}) %collective-permute-start.23) | collective-permute-done | bytes 524320 | tf_op jit(solution)/shard_map/ppermute | solution.py:30
  170.6 9.9 %collective-permute-done.18 = f32[128,1024]{1,0:T(8,128)S(1)} collective-permute-done((f32[128,1024]{1,0:T(8,128)S(1)}, f32[128,1024]{1,0:T(8,128)S(1)}, u32[]{:S(2)}, u32[]{:S(2)}) %collective-permute-start.18) | collective-permute-done | bytes 524320 | tf_op jit(solution)/shard_map/ppermute | solution.py:30
  180.5 1.6 spread.1
  184.0 4.6 %collective-permute-done.27 = f32[128,1024]{1,0:T(8,128)} collective-permute-done((f32[128,1024]{1,0:T(8,128)}, f32[128,1024]{1,0:T(8,128)}, u32[]{:S(2)}, u32[]{:S(2)}) %collective-permute-start.27) | collective-permute-done | bytes 524320 | tf_op jit(solution)/shard_map/ppermute | solution.py:30
  188.6 2.7 %collective-permute-done.24 = f32[128,1024]{1,0:T(8,128)} collective-permute-done((f32[128,1024]{1,0:T(8,128)}, f32[128,1024]{1,0:T(8,128)}, u32[]{:S(2)}, u32[]{:S(2)}) %collective-permute-start.24) | collective-permute-done | bytes 524320 | tf_op jit(solution)/shard_map/ppermute | solution.py:30
  191.3 3.1 %add_add_fusion.1 = (f32[128,1024]{1,0:T(8,128)}, f32[128,1024]{1,0:T(8,128)S(1)}) fusion(f32[128,1024]{1,0:T(8,128)} %collective-permute-done.31, f32[128,1024]{1,0:T(8,128)} %collective-permute-done.28, f32[128,1024]{1,0:T(8,128)} %collective-permute-done.27, f32[128,2048]{1,0:T(8,128)S(1)} %copy-done.18, f32[128,1024]{1,0:T(8,128)} %collective-permute-done.24, ...), kind=kLoop, calls=%fused_computation.7 | loop fusion | flops 786432 | bytes 5242880 | tf_op jit(solution)/shard_map/add | solution.py:623
  195.1 3.0 %collective-permute-start.25 = (f32[64,1024]{1,0:T(8,128)}, f32[64,1024]{1,0:T(8,128)S(1)}, u32[]{:S(2)}, u32[]{:S(2)}) collective-permute-start(f32[64,1024]{1,0:T(8,128)} %slice.94), channel_id=1, source_target_pairs={{0,4},{1,5},{2,6},{3,7},{4,0},{5,1},{6,2},{7,3},{8,12},{9,13},{10,... | collective-permute-start | bytes 786440 | tf_op jit(solution)/shard_map/ppermute | solution.py:30
  198.2 2.2 copy.34
  202.0 13.5 %collective-permute-done.25 = f32[64,1024]{1,0:T(8,128)S(1)} collective-permute-done((f32[64,1024]{1,0:T(8,128)}, f32[64,1024]{1,0:T(8,128)S(1)}, u32[]{:S(2)}, u32[]{:S(2)}) %collective-permute-start.25) | collective-permute-done | bytes 262176 | tf_op jit(solution)/shard_map/ppermute | solution.py:30
  215.6 4.2 %collective-permute-done.32 = f32[64,1024]{1,0:T(8,128)S(1)} collective-permute-done((f32[64,1024]{1,0:T(8,128)S(1)}, f32[64,1024]{1,0:T(8,128)S(1)}, u32[]{:S(2)}, u32[]{:S(2)}) %collective-permute-start.32) | collective-permute-done | bytes 262176 | tf_op jit(solution)/shard_map/ppermute | solution.py:30
  220.0 2.5 collective-permute-start.38
  226.4 5.6 %collective-permute-done.16 = f32[128,320]{1,0:T(8,128)S(1)} collective-permute-done((f32[128,320]{1,0:T(8,128)S(1)}, f32[128,320]{1,0:T(8,128)S(1)}, u32[]{:S(2)}, u32[]{:S(2)}) %collective-permute-start.16) | collective-permute-done | bytes 163872 | tf_op jit(solution)/shard_map/ppermute | solution.py:25
  232.5 7.5 %collective-permute-done.17 = f32[128,320]{1,0:T(8,128)S(1)} collective-permute-done((f32[128,320]{1,0:T(8,128)S(1)}, f32[128,320]{1,0:T(8,128)S(1)}, u32[]{:S(2)}, u32[]{:S(2)}) %collective-permute-start.17) | collective-permute-done | bytes 163872 | tf_op jit(solution)/shard_map/ppermute | solution.py:25
  240.5 1.5 collective-permute-start.37
  242.7 1.5 collective-permute-start.35
  245.0 2.4 place_columns.1
  247.4 3.0 %collective-permute-done.39.refs_7_ = f32[32,2048]{1,0:T(8,128)} collective-permute-done((f32[32,2048]{1,0:T(8,128)}, f32[32,2048]{1,0:T(8,128)}, u32[]{:S(2)}, u32[]{:S(2)}) %collective-permute-start.39) | collective-permute-done | bytes 262176 | tf_op jit(solution)/shard_map/ppermute | solution.py:30
  250.5 3.2 %collective-permute-done.37.refs_5_ = f32[32,2048]{1,0:T(8,128)S(1)} collective-permute-done((f32[32,2048]{1,0:T(8,128)}, f32[32,2048]{1,0:T(8,128)S(1)}, u32[]{:S(2)}, u32[]{:S(2)}) %collective-permute-start.37) | collective-permute-done | bytes 262176 | tf_op jit(solution)/shard_map/ppermute | solution.py:30
  253.6 3.6 %lay_out.1 = f32[32,16384]{1,0:T(8,128)} custom-call(s32[2]{0:T(128)S(1)} %copy-done.37, f32[32,2048]{1,0:T(8,128)S(1)} %maximum_select_fusion.refs_0_, f32[32,2048]{1,0:T(8,128)} %maximum_select_fusion.1.refs_1_, f32[32,2048]{1,0:T(8,128)} %collective-permute-done.34.refs_2_, f32[32,2048]{1,0:T(8,128)S(1)} %collective-permute-done.35.refs_3_, ...), custom_call_target="tpu_custom_call" | custom-call | bytes 4000000 | tf_op jit(solution)/shard_map/lay_out/pallas_call | solution.py:314
  (179 shorter events, 42.6 us)
Async XLA Ops:
  3.9 1.8 collective-permute-start
  13.2 15.3 %copy-start.25 = (f32[1,64,128]{2,1,0:T(8,128)S(1)}, f32[1,64,128]{2,1,0:T(8,128)}, u32[]{:S(2)}) copy-start(f32[1,64,128]{2,1,0:T(8,128)} %param.11) | copy-start | bytes 98308
  13.2 28.0 %collective-permute-start.1 = (bf16[128,10240]{1,0:T(8,128)(2,1)}, bf16[128,10240]{1,0:T(8,128)(2,1)S(1)}, u32[]{:S(2)}, u32[]{:S(2)}) collective-permute-start(bf16[128,10240]{1,0:T(8,128)(2,1)} %pack_columns.1), channel_id=1, source_target_pairs={{0,1},{1,0},{2,3},{3,2},{4,5},{5,4},{6,7},{7,6},{8,9},{9,8},{10,11... | collective-permute-start | bytes 7864328 | tf_op jit(solution)/shard_map/ppermute | solution.py:30
  15.1 9.9 %collective-permute-start.8 = (bf16[144,320]{1,0:T(8,128)(2,1)S(1)}, bf16[144,320]{1,0:T(8,128)(2,1)S(1)}, u32[]{:S(2)}, u32[]{:S(2)}) collective-permute-start(bf16[144,320]{1,0:T(8,128)(2,1)S(1)} %fusion.3.refs_0_), channel_id=1, source_target_pairs={{0,4},{1,5},{2,6},{3,7},{8,12},{9,13},{10,14},{11,15},{16,20},{17,... | collective-permute-start | bytes 276488 | tf_op jit(solution)/shard_map/ppermute | solution.py:25
  20.7 6.9 %collective-permute-start.7 = (bf16[144,320]{1,0:T(8,128)(2,1)S(1)}, bf16[144,320]{1,0:T(8,128)(2,1)S(1)}, u32[]{:S(2)}, u32[]{:S(2)}) collective-permute-start(bf16[144,320]{1,0:T(8,128)(2,1)S(1)} %fusion.3.refs_0_), channel_id=1, source_target_pairs={{0,2},{1,3},{2,4},{3,5},{4,6},{5,7},{8,10},{9,11},{10,12},{11,13},... | collective-permute-start | bytes 276488 | tf_op jit(solution)/shard_map/ppermute | solution.py:25
  24.3 39.4 %copy-start.37 = (s32[2]{0:T(128)S(1)}, s32[2]{0:T(128)}, u32[]{:S(2)}) copy-start(s32[2]{0:T(128)} %pad_add_fusion.place) | copy-start | bytes 28
  24.9 14.7 %collective-permute-start.3 = (bf16[64,2048]{1,0:T(8,128)(2,1)}, bf16[64,2048]{1,0:T(8,128)(2,1)}, u32[]{:S(2)}, u32[]{:S(2)}) collective-permute-start(bf16[64,2048]{1,0:T(8,128)(2,1)} %get-tuple-element.78.refs_0_), channel_id=1, source_target_pairs={{0,4},{1,5},{2,6},{3,7},{4,0},{5,1},{6,2},{7,3},{8,12},{9,13},{10,... | collective-permute-start | bytes 786440 | tf_op jit(solution)/shard_map/ppermute | solution.py:30
  27.7 13.5 %collective-permute-start.9 = (bf16[432,320]{1,0:T(8,128)(2,1)S(1)}, bf16[432,320]{1,0:T(8,128)(2,1)}, u32[]{:S(2)}, u32[]{:S(2)}) collective-permute-start(bf16[432,320]{1,0:T(8,128)(2,1)S(1)} %stack.95.own), channel_id=1, source_target_pairs={{0,1},{1,0},{2,3},{3,2},{4,5},{5,4},{6,7},{7,6},{8,9},{9,8},{10,11... | collective-permute-start | bytes 829448 | tf_op jit(solution)/shard_map/ppermute | solution.py:30
  28.5 12.7 %collective-permute-start.2 = (f32[4,4,2,128]{3,2,1,0:T(2,128)S(1)}, f32[4,4,2,128]{3,2,1,0:T(2,128)S(1)}, u32[]{:S(2)}, u32[]{:S(2)}) collective-permute-start(f32[4,4,2,128]{3,2,1,0:T(2,128)S(1)} %dynamic-slice_bitcast_fusion), channel_id=1, source_target_pairs={{0,1},{1,0},{2,3},{3,2},{4,5},{5,4},{6,7},{7,6},{8,9},{9,8},{10,11... | collective-permute-start | bytes 49160 | tf_op jit(solution)/shard_map/ppermute | solution.py:30
  29.1 19.0 %collective-permute-start.4 = (bf16[64,2048]{1,0:T(8,128)(2,1)}, bf16[64,2048]{1,0:T(8,128)(2,1)}, u32[]{:S(2)}, u32[]{:S(2)}) collective-permute-start(bf16[64,2048]{1,0:T(8,128)(2,1)} %get-tuple-element.78.refs_0_), channel_id=1, source_target_pairs={{0,2},{1,3},{2,0},{3,1},{4,6},{5,7},{6,4},{7,5},{8,10},{9,11},{10,... | collective-permute-start | bytes 786440 | tf_op jit(solution)/shard_map/ppermute | solution.py:30
  39.6 16.7 %collective-permute-start.5 = (bf16[64,2048]{1,0:T(8,128)(2,1)}, bf16[64,2048]{1,0:T(8,128)(2,1)}, u32[]{:S(2)}, u32[]{:S(2)}) collective-permute-start(bf16[64,2048]{1,0:T(8,128)(2,1)} %collective-permute-done.3.refs_1_), channel_id=1, source_target_pairs={{0,2},{1,3},{2,0},{3,1},{4,6},{5,7},{6,4},{7,5},{8,10},{9,11},{10,... | collective-permute-start | bytes 786440 | tf_op jit(solution)/shard_map/ppermute | solution.py:30
  41.2 20.4 %collective-permute-start.11 = (bf16[64,2048]{1,0:T(8,128)(2,1)}, bf16[64,2048]{1,0:T(8,128)(2,1)}, u32[]{:S(2)}, u32[]{:S(2)}) collective-permute-start(bf16[64,2048]{1,0:T(8,128)(2,1)} %get-tuple-element.85.refs_0_), channel_id=1, source_target_pairs={{0,4},{1,5},{2,6},{3,7},{4,0},{5,1},{6,2},{7,3},{8,12},{9,13},{10,... | collective-permute-start | bytes 786440 | tf_op jit(solution)/shard_map/ppermute | solution.py:30
  44.8 18.9 %copy-start.1 = (bf16[1,128,8192]{2,1,0:T(8,128)(2,1)S(1)}, bf16[1,128,8192]{2,1,0:T(8,128)(2,1)}, u32[]{:S(2)}) copy-start(bf16[1,128,8192]{2,1,0:T(8,128)(2,1)} %param.8) | copy-start | bytes 6291460
  48.0 36.7 %copy-start.13 = (f32[768,128]{1,0:T(8,128)}, f32[768,128]{1,0:T(8,128)S(1)}, u32[]{:S(2)}) copy-start(f32[768,128]{1,0:T(8,128)S(1)} %get-tuple-element.83.bias) | copy-start | bytes 1179652
  48.0 36.7 %copy-start.15 = (bf16[768,128]{1,0:T(8,128)(2,1)}, bf16[768,128]{1,0:T(8,128)(2,1)S(1)}, u32[]{:S(2)}) copy-start(bf16[768,128]{1,0:T(8,128)(2,1)S(1)} %get-tuple-element.82.rope_keys) | copy-start | bytes 589828
  58.6 45.2 %collective-permute-start.10 = (bf16[256,2048]{1,0:T(8,128)(2,1)}, bf16[256,2048]{1,0:T(8,128)(2,1)}, u32[]{:S(2)}, u32[]{:S(2)}) collective-permute-start(bf16[256,2048]{1,0:T(8,128)(2,1)} %stack.94.weight), channel_id=1, source_target_pairs={{0,8},{8,0},{16,24},{24,16},{1,9},{9,1},{17,25},{25,17},{2,10},{10... | collective-permute-start | bytes 3145736 | tf_op jit(solution)/shard_map/ppermute | solution.py:30
  60.1 65.6 %collective-permute-start.6 = (bf16[256,2048]{1,0:T(8,128)(2,1)}, bf16[256,2048]{1,0:T(8,128)(2,1)}, u32[]{:S(2)}, u32[]{:S(2)}) collective-permute-start(bf16[256,2048]{1,0:T(8,128)(2,1)} %stack.94.weight), channel_id=1, source_target_pairs={{0,16},{8,24},{16,0},{24,8},{1,17},{9,25},{17,1},{25,9},{2,18},{10... | collective-permute-start | bytes 3145736 | tf_op jit(solution)/shard_map/ppermute | solution.py:30
  61.6 21.8 %collective-permute-start.12 = (bf16[64,2048]{1,0:T(8,128)(2,1)}, bf16[64,2048]{1,0:T(8,128)(2,1)S(1)}, u32[]{:S(2)}, u32[]{:S(2)}) collective-permute-start(bf16[64,2048]{1,0:T(8,128)(2,1)} %get-tuple-element.85.refs_0_), channel_id=1, source_target_pairs={{0,2},{1,3},{2,0},{3,1},{4,6},{5,7},{6,4},{7,5},{8,10},{9,11},{10,... | collective-permute-start | bytes 786440 | tf_op jit(solution)/shard_map/ppermute | solution.py:30
  61.6 21.8 %collective-permute-start.13 = (bf16[64,2048]{1,0:T(8,128)(2,1)}, bf16[64,2048]{1,0:T(8,128)(2,1)S(1)}, u32[]{:S(2)}, u32[]{:S(2)}) collective-permute-start(bf16[64,2048]{1,0:T(8,128)(2,1)} %collective-permute-done.11.refs_1_), channel_id=1, source_target_pairs={{0,2},{1,3},{2,0},{3,1},{4,6},{5,7},{6,4},{7,5},{8,10},{9,11},{10,... | collective-permute-start | bytes 786440 | tf_op jit(solution)/shard_map/ppermute | solution.py:30
  66.5 18.3 %copy-start.7 = (bf16[1,128,4096]{2,1,0:T(8,128)(2,1)S(1)}, bf16[1,128,4096]{2,1,0:T(8,128)(2,1)}, u32[]{:S(2)}) copy-start(bf16[1,128,4096]{2,1,0:T(8,128)(2,1)} %param.9) | copy-start | bytes 3145732
  83.4 15.3 %copy-start.27 = (f32[768,128]{1,0:T(8,128)}, f32[768,128]{1,0:T(8,128)S(1)}, u32[]{:S(2)}) copy-start(f32[768,128]{1,0:T(8,128)S(1)} %get-tuple-element.104.refs_4_) | copy-start | bytes 1179652
  102.6 39.1 %collective-permute-start.22 = (f32[128,2048]{1,0:T(8,128)}, f32[128,2048]{1,0:T(8,128)}, u32[]{:S(2)}, u32[]{:S(2)}) collective-permute-start(f32[128,2048]{1,0:T(8,128)} %get-tuple-element.117), channel_id=1, source_target_pairs={{0,16},{8,24},{16,0},{24,8},{1,17},{9,25},{17,1},{25,9},{2,18},{10... | collective-permute-start | bytes 3145736 | tf_op jit(solution)/shard_map/ppermute | solution.py:30
  103.3 41.9 %collective-permute-start.19 = (f32[128,2048]{1,0:T(8,128)}, f32[128,2048]{1,0:T(8,128)S(1)}, u32[]{:S(2)}, u32[]{:S(2)}) collective-permute-start(f32[128,2048]{1,0:T(8,128)} %copy-done.38), channel_id=1, source_target_pairs={{0,8},{8,0},{16,24},{24,16},{1,9},{9,1},{17,25},{25,17},{2,10},{10... | collective-permute-start | bytes 3145736 | tf_op jit(solution)/shard_map/ppermute | solution.py:30
  139.7 14.9 %collective-permute-start.21 = (f32[128,1024]{1,0:T(8,128)S(1)}, f32[128,1024]{1,0:T(8,128)S(1)}, u32[]{:S(2)}, u32[]{:S(2)}) collective-permute-start(f32[128,1024]{1,0:T(8,128)S(1)} %get-tuple-element.115), channel_id=1, source_target_pairs={{0,16},{8,24},{16,0},{24,8},{1,17},{9,25},{17,1},{25,9},{2,18},{10... | collective-permute-start | bytes 1572872 | tf_op jit(solution)/shard_map/ppermute | solution.py:30
  141.2 21.9 %collective-permute-start.29 = (f32[128,1024]{1,0:T(8,128)S(1)}, f32[128,1024]{1,0:T(8,128)S(1)}, u32[]{:S(2)}, u32[]{:S(2)}) collective-permute-start(f32[128,1024]{1,0:T(8,128)S(1)} %get-tuple-element.120), channel_id=1, source_target_pairs={{0,16},{8,24},{16,0},{24,8},{1,17},{9,25},{17,1},{25,9},{2,18},{10... | collective-permute-start | bytes 1572872 | tf_op jit(solution)/shard_map/ppermute | solution.py:30
  143.0 26.2 %copy-start.20 = (f32[128,2048]{1,0:T(8,128)S(1)}, f32[128,2048]{1,0:T(8,128)}, u32[]{:S(2)}) copy-start(f32[128,2048]{1,0:T(8,128)} %copy-done.19) | copy-start | bytes 3145732
  143.1 21.6 %collective-permute-start.30 = (f32[128,1024]{1,0:T(8,128)S(1)}, f32[128,1024]{1,0:T(8,128)S(1)}, u32[]{:S(2)}, u32[]{:S(2)}) collective-permute-start(f32[128,1024]{1,0:T(8,128)S(1)} %get-tuple-element.146), channel_id=1, source_target_pairs={{0,8},{8,0},{16,24},{24,16},{1,9},{9,1},{17,25},{25,17},{2,10},{10... | collective-permute-start | bytes 1572872 | tf_op jit(solution)/shard_map/ppermute | solution.py:30
  144.6 24.6 %collective-permute-start.23 = (f32[128,1024]{1,0:T(8,128)S(1)}, f32[128,1024]{1,0:T(8,128)S(1)}, u32[]{:S(2)}, u32[]{:S(2)}) collective-permute-start(f32[128,1024]{1,0:T(8,128)S(1)} %get-tuple-element.147), channel_id=1, source_target_pairs={{0,8},{8,0},{16,24},{24,16},{1,9},{9,1},{17,25},{25,17},{2,10},{10... | collective-permute-start | bytes 1572872 | tf_op jit(solution)/shard_map/ppermute | solution.py:30
  145.1 35.3 %collective-permute-start.18 = (f32[128,1024]{1,0:T(8,128)S(1)}, f32[128,1024]{1,0:T(8,128)S(1)}, u32[]{:S(2)}, u32[]{:S(2)}) collective-permute-start(f32[128,1024]{1,0:T(8,128)S(1)} %get-tuple-element.111), channel_id=1, source_target_pairs={{0,8},{8,0},{16,24},{24,16},{1,9},{9,1},{17,25},{25,17},{2,10},{10... | collective-permute-start | bytes 1572872 | tf_op jit(solution)/shard_map/ppermute | solution.py:30
  154.6 34.0 %collective-permute-start.27 = (f32[128,1024]{1,0:T(8,128)}, f32[128,1024]{1,0:T(8,128)}, u32[]{:S(2)}, u32[]{:S(2)}) collective-permute-start(f32[128,1024]{1,0:T(8,128)} %get-tuple-element.118), channel_id=1, source_target_pairs={{0,8},{8,0},{16,24},{24,16},{1,9},{9,1},{17,25},{25,17},{2,10},{10... | collective-permute-start | bytes 1572872 | tf_op jit(solution)/shard_map/ppermute | solution.py:30
  163.1 25.4 %collective-permute-start.28 = (f32[128,1024]{1,0:T(8,128)}, f32[128,1024]{1,0:T(8,128)}, u32[]{:S(2)}, u32[]{:S(2)}) collective-permute-start(f32[128,1024]{1,0:T(8,128)} %get-tuple-element.142), channel_id=1, source_target_pairs={{0,16},{8,24},{16,0},{24,8},{1,17},{9,25},{17,1},{25,9},{2,18},{10... | collective-permute-start | bytes 1572872 | tf_op jit(solution)/shard_map/ppermute | solution.py:30
  164.6 23.9 %collective-permute-start.20 = (f32[128,1024]{1,0:T(8,128)}, f32[128,1024]{1,0:T(8,128)}, u32[]{:S(2)}, u32[]{:S(2)}) collective-permute-start(f32[128,1024]{1,0:T(8,128)} %get-tuple-element.143), channel_id=1, source_target_pairs={{0,16},{8,24},{16,0},{24,8},{1,17},{9,25},{17,1},{25,9},{2,18},{10... | collective-permute-start | bytes 1572872 | tf_op jit(solution)/shard_map/ppermute | solution.py:30
  170.6 18.0 %collective-permute-start.31 = (f32[128,1024]{1,0:T(8,128)}, f32[128,1024]{1,0:T(8,128)}, u32[]{:S(2)}, u32[]{:S(2)}) collective-permute-start(f32[128,1024]{1,0:T(8,128)} %get-tuple-element.144), channel_id=1, source_target_pairs={{0,2},{1,3},{2,0},{3,1},{4,6},{5,7},{6,4},{7,5},{8,10},{9,11},{10,... | collective-permute-start | bytes 1572872 | tf_op jit(solution)/shard_map/ppermute | solution.py:30
  180.4 10.8 %collective-permute-start.24 = (f32[128,1024]{1,0:T(8,128)}, f32[128,1024]{1,0:T(8,128)}, u32[]{:S(2)}, u32[]{:S(2)}) collective-permute-start(f32[128,1024]{1,0:T(8,128)} %get-tuple-element.145), channel_id=1, source_target_pairs={{0,2},{1,3},{2,0},{3,1},{4,6},{5,7},{6,4},{7,5},{8,10},{9,11},{10,... | collective-permute-start | bytes 1572872 | tf_op jit(solution)/shard_map/ppermute | solution.py:30
  188.6 9.6 %collective-permute-start.15 = (f32[432,320]{0,1:T(8,128)}, f32[432,320]{0,1:T(8,128)}, u32[]{:S(2)}, u32[]{:S(2)}) collective-permute-start(f32[432,320]{0,1:T(8,128)} %copy.33), channel_id=1, source_target_pairs={{0,1},{1,0},{2,3},{3,2},{4,5},{5,4},{6,7},{7,6},{8,9},{9,8},{10,11... | collective-permute-start | bytes 1658888 | tf_op jit(solution)/shard_map/ppermute | solution.py:30
  195.1 20.3 %collective-permute-start.25 = (f32[64,1024]{1,0:T(8,128)}, f32[64,1024]{1,0:T(8,128)S(1)}, u32[]{:S(2)}, u32[]{:S(2)}) collective-permute-start(f32[64,1024]{1,0:T(8,128)} %slice.94), channel_id=1, source_target_pairs={{0,4},{1,5},{2,6},{3,7},{4,0},{5,1},{6,2},{7,3},{8,12},{9,13},{10,... | collective-permute-start | bytes 786440 | tf_op jit(solution)/shard_map/ppermute | solution.py:30
  198.1 42.3 %collective-permute-start.14 = (bf16[128,6144]{1,0:T(8,128)(2,1)S(1)}, bf16[128,6144]{1,0:T(8,128)(2,1)S(1)}, u32[]{:S(2)}, u32[]{:S(2)}) collective-permute-start(bf16[128,6144]{1,0:T(8,128)(2,1)S(1)} %copy-done.12), channel_id=1, source_target_pairs={{0,1},{1,0},{2,3},{3,2},{4,5},{5,4},{6,7},{7,6},{8,9},{9,8},{10,11... | collective-permute-start | bytes 4718600 | tf_op jit(solution)/shard_map/ppermute | solution.py:30
  201.8 18.0 %collective-permute-start.32 = (f32[64,1024]{1,0:T(8,128)S(1)}, f32[64,1024]{1,0:T(8,128)S(1)}, u32[]{:S(2)}, u32[]{:S(2)}) collective-permute-start(f32[64,1024]{1,0:T(8,128)S(1)} %slice.100), channel_id=1, source_target_pairs={{0,4},{1,5},{2,6},{3,7},{4,0},{5,1},{6,2},{7,3},{8,12},{9,13},{10,... | collective-permute-start | bytes 786440 | tf_op jit(solution)/shard_map/ppermute | solution.py:30
  215.5 4.4 %collective-permute-start.26 = (f32[32,1024]{1,0:T(8,128)S(1)}, f32[32,1024]{1,0:T(8,128)S(1)}, u32[]{:S(2)}, u32[]{:S(2)}) collective-permute-start(f32[32,1024]{1,0:T(8,128)S(1)} %get-tuple-element.153), channel_id=1, source_target_pairs={{0,1},{1,0},{2,3},{3,2},{4,5},{5,4},{6,7},{7,6},{8,9},{9,8},{10,11... | collective-permute-start | bytes 393224 | tf_op jit(solution)/shard_map/ppermute | solution.py:30
  219.8 5.3 %collective-permute-start.33 = (f32[32,1024]{1,0:T(8,128)S(1)}, f32[32,1024]{1,0:T(8,128)S(1)}, u32[]{:S(2)}, u32[]{:S(2)}) collective-permute-start(f32[32,1024]{1,0:T(8,128)S(1)} %get-tuple-element.151), channel_id=1, source_target_pairs={{0,1},{1,0},{2,3},{3,2},{4,5},{5,4},{6,7},{7,6},{8,9},{9,8},{10,11... | collective-permute-start | bytes 393224 | tf_op jit(solution)/shard_map/ppermute | solution.py:30
  220.0 22.0 %collective-permute-start.38 = (f32[32,2048]{1,0:T(8,128)S(1)}, f32[32,2048]{1,0:T(8,128)S(1)}, u32[]{:S(2)}, u32[]{:S(2)}) collective-permute-start(f32[32,2048]{1,0:T(8,128)S(1)} %maximum_select_fusion.refs_0_), channel_id=1, source_target_pairs={{0,24},{8,16},{16,8},{24,0},{1,25},{9,17},{17,9},{25,1},{2,26},{10... | collective-permute-start | bytes 786440 | tf_op jit(solution)/shard_map/ppermute | solution.py:30
  222.5 9.5 %collective-permute-start.16 = (f32[128,320]{1,0:T(8,128)S(1)}, f32[128,320]{1,0:T(8,128)S(1)}, u32[]{:S(2)}, u32[]{:S(2)}) collective-permute-start(f32[128,320]{1,0:T(8,128)S(1)} %get-tuple-element.148), channel_id=1, source_target_pairs={{2,0},{3,1},{4,2},{5,3},{6,4},{7,5},{10,8},{11,9},{12,10},{13,11},... | collective-permute-start | bytes 491528 | tf_op jit(solution)/shard_map/ppermute | solution.py:25
  223.8 16.2 %collective-permute-start.17 = (f32[128,320]{1,0:T(8,128)S(1)}, f32[128,320]{1,0:T(8,128)S(1)}, u32[]{:S(2)}, u32[]{:S(2)}) collective-permute-start(f32[128,320]{1,0:T(8,128)S(1)} %get-tuple-element.149), channel_id=1, source_target_pairs={{4,0},{5,1},{6,2},{7,3},{12,8},{13,9},{14,10},{15,11},{20,16},{21,... | collective-permute-start | bytes 491528 | tf_op jit(solution)/shard_map/ppermute | solution.py:25
  225.1 22.3 %collective-permute-start.36 = (f32[32,2048]{1,0:T(8,128)S(1)}, f32[32,2048]{1,0:T(8,128)}, u32[]{:S(2)}, u32[]{:S(2)}) collective-permute-start(f32[32,2048]{1,0:T(8,128)S(1)} %maximum_select_fusion.refs_0_), channel_id=1, source_target_pairs={{0,16},{8,24},{16,0},{24,8},{1,17},{9,25},{17,1},{25,9},{2,18},{10... | collective-permute-start | bytes 786440 | tf_op jit(solution)/shard_map/ppermute | solution.py:30
  232.0 15.4 %collective-permute-start.34 = (f32[32,2048]{1,0:T(8,128)S(1)}, f32[32,2048]{1,0:T(8,128)}, u32[]{:S(2)}, u32[]{:S(2)}) collective-permute-start(f32[32,2048]{1,0:T(8,128)S(1)} %maximum_select_fusion.refs_0_), channel_id=1, source_target_pairs={{0,8},{8,0},{16,24},{24,16},{1,9},{9,1},{17,25},{25,17},{2,10},{10... | collective-permute-start | bytes 786440 | tf_op jit(solution)/shard_map/ppermute | solution.py:30
  240.0 10.5 %collective-permute-start.39 = (f32[32,2048]{1,0:T(8,128)}, f32[32,2048]{1,0:T(8,128)}, u32[]{:S(2)}, u32[]{:S(2)}) collective-permute-start(f32[32,2048]{1,0:T(8,128)} %maximum_select_fusion.1.refs_1_), channel_id=1, source_target_pairs={{0,24},{8,16},{16,8},{24,0},{1,25},{9,17},{17,9},{25,1},{2,26},{10... | collective-permute-start | bytes 786440 | tf_op jit(solution)/shard_map/ppermute | solution.py:30
  240.5 13.1 %collective-permute-start.37 = (f32[32,2048]{1,0:T(8,128)}, f32[32,2048]{1,0:T(8,128)S(1)}, u32[]{:S(2)}, u32[]{:S(2)}) collective-permute-start(f32[32,2048]{1,0:T(8,128)} %maximum_select_fusion.1.refs_1_), channel_id=1, source_target_pairs={{0,16},{8,24},{16,0},{24,8},{1,17},{9,25},{17,1},{25,9},{2,18},{10... | collective-permute-start | bytes 786440 | tf_op jit(solution)/shard_map/ppermute | solution.py:30
  242.7 10.9 %collective-permute-start.35 = (f32[32,2048]{1,0:T(8,128)}, f32[32,2048]{1,0:T(8,128)S(1)}, u32[]{:S(2)}, u32[]{:S(2)}) collective-permute-start(f32[32,2048]{1,0:T(8,128)} %maximum_select_fusion.1.refs_1_), channel_id=1, source_target_pairs={{0,8},{8,0},{16,24},{24,16},{1,9},{9,1},{17,25},{25,17},{2,10},{10... | collective-permute-start | bytes 786440 | tf_op jit(solution)/shard_map/ppermute | solution.py:30
  (37 other events, 151.7 us)

commit v2 on v1

--- a/solution.py
+++ b/solution.py
@@ -55,7 +55,6 @@
     scale = 1.0 / jnp.sqrt(jnp.float32(NOPE + ROPE))
     rows = cand.shape[0] // 2
     half = weight_grads[0].shape[0]
-    part = pl.program_id(0) * (len(weight_grads) // 2) // pl.num_programs(0)
     sib_q, sib_rope = sib_grads.at[:, : 2 * NOPE], sib_grads.at[:, 2 * NOPE :]
     lane_half = lax.broadcasted_iota(jnp.int32, (rows, 2 * ROPE), 1) // ROPE
 
@@ -104,15 +103,11 @@
         key_grads = jnp.concatenate(both_grads, axis=0)
         lat_sum[...] += dot(key_grads, head_weight, 1, 1)
         weight_grad = dot(cand_t[...], key_grads, 1, 0)
-        for at in range(len(weight_grads) // 2):
-
-            @pl.when(part == at)
-            def _():
-                weight_grads[2 * at][:, columns] = weight_grad[:half]
-                weight_grads[2 * at + 1][:, columns] = weight_grad[half:]
-
-
-def chunk_backward(place, own, packed, totals, weight, shared, earlier, sizes, parts):
+        weight_grads[0][:, columns] = weight_grad[:half]
+        weight_grads[1][:, columns] = weight_grad[half:]
+
+
+def chunk_backward(place, t, unit, own, packed, totals, weight, shared, earlier, sizes):
     q_own, rope_own, out_own = own
     tot_own, tot_sib = totals
     cand, cand_t, rope_keys, bias = shared
@@ -120,30 +115,26 @@
     chunks, pairs = sizes
     wide, narrow = 2 * NOPE, 2 * ROPE
     span = pairs * (2 * wide + narrow)
-    mine = lambda p, place: (place[0] * 2 + place[1]) * pairs + p
-    theirs = lambda p, place: place[0] * pairs + p
-    part_pairs = pairs // parts
-
-    def part_block(part):
-        return lambda p, place: (0, jnp.clip(p - part * part_pairs, 0, part_pairs - 1))
-
+    first, count = unit
+    mine = lambda p, place: (place[1 + t] * 2 + place[0]) * pairs + first + p
+    theirs = lambda p, place: place[1 + t] * pairs + first + p
     whole = lambda array: pl.BlockSpec(array.shape, lambda p, place: (0, 0))
     in_specs = [
         pl.BlockSpec((tokens, wide), lambda p, place: (0, mine(p, place))),
         pl.BlockSpec((tokens, narrow), lambda p, place: (0, mine(p, place))),
         pl.BlockSpec((tokens, wide), lambda p, place: (0, mine(p, place))),
         pl.BlockSpec((1, 2, tokens), lambda p, place: (mine(p, place), 0, 0)),
-        pl.BlockSpec((tokens, wide), lambda p, place: (0, place[0] * (span // wide) + p)),
+        pl.BlockSpec((tokens, wide), lambda p, place: (0, place[1 + t] * (span // wide) + first + p)),
         pl.BlockSpec(
             (tokens, narrow),
-            lambda p, place: (0, place[0] * (span // narrow) + pairs * wide // narrow + p),
+            lambda p, place: (0, place[1 + t] * (span // narrow) + pairs * wide // narrow + first + p),
         ),
         pl.BlockSpec(
             (tokens, wide),
-            lambda p, place: (0, place[0] * (span // wide) + pairs * (wide + narrow) // wide + p),
+            lambda p, place: (0, place[1 + t] * (span // wide) + pairs * (wide + narrow) // wide + first + p),
         ),
         pl.BlockSpec((1, 2, tokens), lambda p, place: (theirs(p, place), 0, 0)),
-        pl.BlockSpec((LAT, 2 * (NOPE + VDIM)), lambda p, place: (0, p)),
+        pl.BlockSpec((LAT, 2 * (NOPE + VDIM)), lambda p, place: (0, first + p)),
         whole(cand),
         whole(cand_t),
         whole(rope_keys),
@@ -157,13 +148,13 @@
             aliases[1 + len(operands)] = index
             in_specs.append(pl.BlockSpec(memory_space=pl.ANY))
             operands.append(array)
-    columns = weight.shape[1]
+    columns = 2 * (NOPE + VDIM) * count
     bf16, f32 = jnp.bfloat16, jnp.float32
     out_shape = [
         jax.ShapeDtypeStruct(q_own.shape, bf16),
         jax.ShapeDtypeStruct(rope_own.shape, bf16),
         jax.ShapeDtypeStruct((tokens, chunks * pairs * (wide + narrow)), bf16),
-        *[jax.ShapeDtypeStruct((LAT // 2, columns // parts), f32)] * (2 * parts),
+        *[jax.ShapeDtypeStruct((LAT // 2, columns), f32)] * 2,
         jax.ShapeDtypeStruct((cand.shape[0], LAT), f32),
         jax.ShapeDtypeStruct((cand.shape[0], narrow), f32),
     ]
@@ -171,23 +162,20 @@
         pl.BlockSpec((tokens, wide), lambda p, place: (0, mine(p, place))),
         pl.BlockSpec((tokens, narrow), lambda p, place: (0, mine(p, place))),
         pl.BlockSpec((tokens, wide + narrow), lambda p, place: (0, theirs(p, place))),
-        *[
-            pl.BlockSpec((LAT // 2, 2 * (NOPE + VDIM)), part_block(part // 2))
-            for part in range(2 * parts)
-        ],
+        *[pl.BlockSpec((LAT // 2, 2 * (NOPE + VDIM)), lambda p, place: (0, p))] * 2,
         pl.BlockSpec((cand.shape[0], LAT), lambda p, place: (0, 0)),
         pl.BlockSpec((cand.shape[0], narrow), lambda p, place: (0, 0)),
     ]
     return pl.pallas_call(
         functools.partial(heads_kernel, earlier=len(aliases)),
         grid_spec=pltpu.PrefetchScalarGridSpec(
-            num_scalar_prefetch=1, grid=(pairs,), in_specs=in_specs, out_specs=out_specs
+            num_scalar_prefetch=1, grid=(count,), in_specs=in_specs, out_specs=out_specs
         ),
         out_shape=out_shape,
         input_output_aliases=aliases,
         compiler_params=pltpu.CompilerParams(vmem_limit_bytes=KERNEL_BYTES),
         cost_estimate=pl.CostEstimate(
-            flops=pairs * 1_000_000_000, bytes_accessed=pairs * 3_000_000, transcendentals=0
+            flops=count * 100_000_000, bytes_accessed=count * 300_000, transcendentals=0
         ),
         name="heads_backward",
     )(place, *operands)
@@ -206,7 +194,7 @@
 def place_columns(place, received, q_full, rope_full, chunks):
     tokens = q_full.shape[0]
     q_cols, rope_cols = q_full.shape[1] // chunks // 2, rope_full.shape[1] // chunks // 2
-    put = lambda c, place: (0, c * 2 + 1 - place[1])
+    put = lambda c, place: (0, c * 2 + 1 - place[0])
     return pl.pallas_call(
         place_kernel,
         grid_spec=pltpu.PrefetchScalarGridSpec(
@@ -273,7 +261,7 @@
 
     def column_block(t, other):
         def block(i, place):
-            return (0, (place[0] ^ t) * 2 + (1 - place[1] if other else place[1]))
+            return (0, place[1 + t] * 2 + (1 - place[0] if other else place[0]))
 
         return pl.BlockSpec((rows, width), block)
 
@@ -317,7 +305,7 @@
             num_scalar_prefetch=1,
             grid=(count,),
             in_specs=[pl.BlockSpec((rows, columns), lambda t, place: (0, 0))] * len(pieces),
-            out_specs=pl.BlockSpec((rows, 2 * columns), lambda t, place: (0, place[0] ^ t)),
+            out_specs=pl.BlockSpec((rows, 2 * columns), lambda t, place: (0, place[1 + t])),
         ),
         out_shape=jax.ShapeDtypeStruct((rows, count * 2 * columns), pieces[0].dtype),
         compiler_params=pltpu.CompilerParams(vmem_limit_bytes=KERNEL_BYTES),
@@ -326,6 +314,37 @@
     )(place, *pieces)
 
 
+def piece_kernel(place, kept, crossed, out):
+    width = kept.shape[1]
+
+    @pl.when(place[0] == 0)
+    def _():
+        out[:, :width] = kept[...]
+        out[:, width:] = crossed[...]
+
+    @pl.when(place[0] != 0)
+    def _():
+        out[:, :width] = crossed[...]
+        out[:, width:] = kept[...]
+
+
+def join_cores(place, kept, crossed):
+    rows, columns = kept.shape
+    return pl.pallas_call(
+        piece_kernel,
+        grid_spec=pltpu.PrefetchScalarGridSpec(
+            num_scalar_prefetch=1,
+            grid=(1,),
+            in_specs=[pl.BlockSpec((rows, columns), lambda i, place: (0, 0))] * 2,
+            out_specs=pl.BlockSpec((rows, 2 * columns), lambda i, place: (0, 0)),
+        ),
+        out_shape=jax.ShapeDtypeStruct((rows, 2 * columns), kept.dtype),
+        compiler_params=pltpu.CompilerParams(vmem_limit_bytes=KERNEL_BYTES),
+        cost_estimate=pl.CostEstimate(flops=0, bytes_accessed=500_000, transcendentals=0),
+        name="join_cores",
+    )(place, kept, crossed)
+
+
 def pack_kernel(place, q_ref, rope_ref, out_ref, packed):
     q_cols, rope_cols = q_ref.shape[1], rope_ref.shape[1]
     packed[:, :q_cols] = q_ref[...]
@@ -336,7 +355,7 @@
 def pack_columns(place, arrays, chunks):
     tokens = arrays[0].shape[0]
     widths = [array.shape[1] // chunks // 2 for array in arrays]
-    theirs = lambda c, place: (0, c * 2 + 1 - place[1])
+    theirs = lambda c, place: (0, c * 2 + 1 - place[0])
     return pl.pallas_call(
         pack_kernel,
         grid_spec=pltpu.PrefetchScalarGridSpec(
@@ -487,19 +506,36 @@
     far = n_dp - 1
     lat_block = up_weight.shape[0]
 
-    place = jnp.stack([dp, core]).astype(jnp.int32)
+    place = jnp.stack([core] + [dp ^ t for t in range(n_dp)]).astype(jnp.int32)
 
     leaving, *staying = weight_parts(place, up_weight, n_dp, far)
     crossed = exchange(leaving, "ctx", 1)
-    crossed, q_nope, q_rope, grad_out, log_total, kv_latent = lax.optimization_barrier(
-        (crossed, q_nope, q_rope, grad_out, log_total, kv_latent)
-    )
     chip_rows = stack(
         [*staying, crossed], (((0, 0), (2, 0)), ((1, 0), (2, 1))), part_cols
     )
-    chip_rows, q_nope, q_rope, grad_out, log_total, kv_latent = lax.optimization_barrier(
-        (chip_rows, q_nope, q_rope, grad_out, log_total, kv_latent)
-    )
+    chip_rows, place, selected, offered, q_nope, q_rope, grad_out, log_total, kv_latent = (
+        lax.optimization_barrier(
+            (chip_rows, place, selected, offered, q_nope, q_rope, grad_out, log_total, kv_latent)
+        )
+    )
+    partners = halving_order(n_ctx)[::2]
+
+    def over_chips(start):
+        at_step = {0: start}
+        for step in range(2, n_ctx, 4):
+            at_step[step] = exchange(at_step[step - 2], "ctx", 2)
+            if step + 2 < n_ctx:
+                at_step[step + 2] = exchange(start, "ctx", step + 2)
+        return [at_step[partner] for partner in partners], at_step[n_ctx - 2]
+
+    def joined(pieces):
+        return stack(pieces, (tuple((index, 0) for index in range(len(pieces))),), part_cols)[0]
+
+    near_pieces, last = over_chips(chip_rows[0])
+    weights = {0: joined(near_pieces)}
+    weights[far] = joined(over_chips(after(chip_rows[1], last))[0])
+    for t in range(1, far):
+        weights[t] = exchange(weights[0], "dp", t)
     queries, rope_queries, out_grads = q_nope[0], q_rope[0], grad_out[0]
 
     packed = exchange(
@@ -546,42 +582,40 @@
     sib_bundles = exchange(own_bundles, "ctx", 1)
     shared = collect(plan, own_bundles, sib_bundles, tuple(blocks), lat_block)
 
-    partners = halving_order(n_ctx)[::2]
-    weights = {}
-    for order, t in enumerate((0, far)):
-        at_step = {0: chip_rows[order]}
-        if order:
-            at_step[0] = after(at_step[0], packed, tot_sib, sib_bundles)
-        for step in range(4, n_ctx, 4):
-            at_step[step] = exchange(at_step[0], "ctx", step)
-        for step in range(2, n_ctx, 4):
-            at_step[step] = exchange(at_step[step - 2], "ctx", 2)
-        pieces = [at_step[partner] for partner in partners]
-        weights[t] = stack(
-            pieces, (tuple((index, 0) for index in range(len(pieces))),), part_cols
-        )[0]
-    for t in range(1, far):
-        weights[t] = exchange(weights[0], "dp", t)
-
     earlier = None
-    weight_grads, latents, ropes = {}, [], []
-    for t in [0, far] + list(range(1, far)):
-        split = 1 if t in (0, far) else 2
-        rest = chunk_backward(
-            jnp.stack([dp ^ t, core]).astype(jnp.int32),
-            (queries, rope_queries, out_grads),
-            packed,
-            totals,
-            weights[t],
-            shared,
-            earlier,
-            (n_dp, pairs),
-            split,
-        )
-        earlier, rest = rest[:3], rest[3:]
-        weight_grads[t] = (rest[0 : 2 * split : 2], rest[1 : 2 * split : 2])
-        latents.append(rest[-2])
-        ropes.append(rest[-1])
+    weight_grads, latents, ropes, far_arrived = {}, [], [], []
+    bits = [1 << b for b in range(n_dp.bit_length() - 1)]
+    orders = (bits, bits[::-1])
+    order = [0, far] + list(range(1, far))
+    for t in order:
+        weight_grads[t] = ([], [])
+        half_pairs = pairs // 2
+        units = [(0, pairs)] if t != order[-1] else [(0, half_pairs), (half_pairs, half_pairs)]
+        for unit in units:
+            weight = weights[t]
+            if unit[0]:
+                weight = after(weight, *[arrived for arrived, in far_arrived])
+            rest = chunk_backward(
+                place,
+                t,
+                unit,
+                (queries, rope_queries, out_grads),
+                packed,
+                totals,
+                weight,
+                shared,
+                earlier,
+                (n_dp, pairs),
+            )
+            earlier = rest[:3]
+            for side in range(2):
+                weight_grads[t][side].append(rest[3 + side])
+            latents.append(rest[5])
+            ropes.append(rest[6])
+        if t == far:
+            far_arrived = [
+                [exchange(weight_grads[t][side][0], "dp", orders[side][0])] for side in range(2)
+            ]
 
     q_full, rope_full, sib_grads = earlier
     received = exchange(sib_grads, "ctx", 1)
@@ -594,41 +628,44 @@
     for chips in (1, 2):
         grad_rows = grad_rows + from_behind(by_chip[chips], "ctx", -2 * chips)
 
-    bits = [1 << b for b in range(n_dp.bit_length() - 1)]
     half_cols = part_cols // 2
+
+    def columns(pieces, half):
+        if len(pieces) == 2:
+            return pieces[half]
+        return pieces[0][:, half * half_cols : (half + 1) * half_cols]
+
+    def total(addends, half):
+        return functools.reduce(
+            lambda left, right: left + right, [columns(pieces, half) for pieces in addends]
+        )
+
     sums = []
-    for side, order in enumerate((bits, bits[::-1])):
-        parts = {t: list(weight_grads[t][side]) for t in weight_grads}
+    for side, order in enumerate(orders):
+        addends = {t: [weight_grads[t][side]] for t in weight_grads}
         for bit in order:
             arrived = {}
-            for t in sorted((t for t in parts if t & bit), reverse=True):
-                arrived[t ^ bit] = [exchange(part, "dp", bit) for part in parts[t]]
-            summed = {}
-            for t, more in arrived.items():
-                mine = parts[t]
-                pieces = []
-                for half in range(2):
-                    columns = slice(half * half_cols, (half + 1) * half_cols)
-                    pieces.append(
-                        (mine[half] if len(mine) == 2 else mine[0][:, columns])
-                        + (more[half] if len(more) == 2 else more[0][:, columns])
-                    )
-                summed[t] = pieces
-            parts = summed
-        sums.append(parts[0])
+            for t in sorted((t for t in addends if t & bit), reverse=True):
+                if t == far and bit == order[0]:
+                    arrived[t ^ bit] = far_arrived[side]
+                    continue
+                pieces = addends[t][0]
+                if len(addends[t]) > 1:
+                    pieces = [total(addends[t], half) for half in range(2)]
+                if bit == order[-1]:
+                    pieces = [after(piece, *addends[0][-1]) for piece in pieces]
+                arrived[t ^ bit] = [exchange(piece, "dp", bit) for piece in pieces]
+            addends = {t: addends[t] + [more] for t, more in arrived.items()}
+        sums.append([total(addends[0], half) for half in range(2)])
 
     ctx_bits = [1 << b for b in range(1, n_ctx.bit_length() - 1)]
     finished = []
     for half in range(2):
-        rows = sums[0][half] + exchange(sums[1][half], "ctx", ctx_bits[0])
+        leaving = after(sums[1][half], (grad_rows, grad_nope)[half])
+        rows = sums[0][half] + exchange(leaving, "ctx", ctx_bits[0])
         for bit in ctx_bits[1:]:
             rows = halve(rows, "ctx", bit)
-        kept, crossed = rows[:lat_block], exchange(rows[lat_block:], "ctx", 1)
-        piece = jnp.where(
-            core == 0,
-            jnp.concatenate([kept, crossed], axis=1),
-            jnp.concatenate([crossed, kept], axis=1),
-        )
+        piece = join_cores(place, rows[:lat_block], exchange(rows[lat_block:], "ctx", 1))
         finished.append([piece] + [exchange(piece, "dp", t) for t in range(1, n_dp)])
     grad_weight = lay_out(place, [piece for both in zip(*finished) for piece in both])
     return (grad_nope[None], grad_rope[None], grad_rows[None], grad_weight)

time: 258 us -> 274 us (1.062)
  waiting for transfers between devices: 87 us -> 123 us
  local copies, waits for them, and re-layouts: 29.9 us -> 16.9 us
  Pallas kernels: 77 us -> 71.8 us
    ppermute x36 -> x35, waiting for transfers between devices: 71.3 us -> 104 us  [exchange(): lax.ppermute(value, axis, [(source, source ^ bits) for source in range(co...]
    unnamed x91 -> x59, local copies, waits for them, and re-layouts: 23.9 us -> 11.1 us
    pallas_call x4 -> x5, Pallas kernels: 55.6 us -> 51.5 us  [chunk_backward(): pl.pallas_call(functools.partial(heads_kernel, earlier=len(aliases)), gri...]
    ppermute x36 -> x35, starting transfers between devices: 40 us -> 44 us  [exchange(): lax.ppermute(value, axis, [(source, source ^ bits) for source in range(co...]
    ppermute x4, starting transfers between devices: 11.7 us -> 8.28 us  [from_behind(): lax.ppermute(value, axis, [(source, source + steps) for source in range(i...]
    ppermute x4, waiting for transfers between devices: 15.7 us -> 19 us  [from_behind(): lax.ppermute(value, axis, [(source, source + steps) for source in range(i...]
    add x4 -> x5, other arithmetic: 6.94 us -> 6.24 us  [the longest x3 4.62 us: total(): left + right]
  transfers between devices with their start and end apart: 40 -> 39, of which waited for: 16 -> 25; matrix products, arithmetic and copies ran while one was open for 7% -> 5% of each run, Pallas kernels for 25% -> 22%
where the time goes in v2:
time: 274 us; the launch traced here: 273 us
  waiting for transfers between devices  123 us (45%)
  Pallas kernels  71.8 us (26%)
  starting transfers between devices  52.3 us (19%)
  local copies, waits for them, and re-layouts  16.9 us (6%)
  other arithmetic  8.33 us (3%)
    ppermute x35, waiting for transfers between devices, exchange(): lax.ppermute(value, axis, [(source, source ^ bits) for source in range(co...  104 us
    pallas_call x5, Pallas kernels, chunk_backward(): pl.pallas_call(functools.partial(heads_kernel, earlier=len(aliases)), gri...  51.5 us
    ppermute x35, starting transfers between devices, exchange(): lax.ppermute(value, axis, [(source, source ^ bits) for source in range(co...  44 us
    ppermute x4, waiting for transfers between devices, from_behind(): lax.ppermute(value, axis, [(source, source + steps) for source in range(i...  19 us
    unnamed x59, local copies, waits for them, and re-layouts  11.1 us
    ppermute x4, starting transfers between devices, from_behind(): lax.ppermute(value, axis, [(source, source + steps) for source in range(i...  8.28 us
  transfers between devices with their start and end apart: 39, of which 25 were waited for; matrix products, arithmetic and copies ran while one was open for 5% of the time, Pallas kernels for 22%

profile of v2, /device:TPU:0, one launch (start us, length us, event | category | flops | bytes accessed | tf_op | source)
XLA Modules:
  0.0 273.3 jit_solution(12508008717585633243)
XLA Ops:
  1.3 2.6 weight_parts.1
  8.3 4.8 %pack_columns.1 = bf16[128,10240]{1,0:T(8,128)(2,1)} custom-call(s32[5]{0:T(128)} %stack.63.place, bf16[128,8192]{1,0:T(8,128)(2,1)} %bitcast.47, bf16[128,4096]{1,0:T(8,128)(2,1)} %bitcast.59, bf16[128,8192]{1,0:T(8,128)(2,1)} %bitcast.53), custom_call_target="tpu_custom_call" | custom-call | bytes 5000000 | tf_op jit(solution)/shard_map/pack_columns/pallas_call | solution.py:359
  13.8 3.7 %collective-permute-start.3 = (bf16[64,2048]{1,0:T(8,128)(2,1)}, bf16[64,2048]{1,0:T(8,128)(2,1)S(1)}, u32[]{:S(2)}, u32[]{:S(2)}) collective-permute-start(bf16[64,2048]{1,0:T(8,128)(2,1)} %get-tuple-element.80.refs_0_), channel_id=1, source_target_pairs={{0,4},{1,5},{2,6},{3,7},{4,0},{5,1},{6,2},{7,3},{8,12},{9,13},{10,... | collective-permute-start | bytes 786440 | tf_op jit(solution)/shard_map/ppermute | solution.py:30
  18.2 11.9 %collective-permute-done.3.refs_1_ = bf16[64,2048]{1,0:T(8,128)(2,1)S(1)} collective-permute-done((bf16[64,2048]{1,0:T(8,128)(2,1)}, bf16[64,2048]{1,0:T(8,128)(2,1)S(1)}, u32[]{:S(2)}, u32[]{:S(2)}) %collective-permute-start.3) | collective-permute-done | bytes 262176 | tf_op jit(solution)/shard_map/ppermute | solution.py:30
  32.2 6.1 %collective-permute-done.5.refs_3_ = bf16[64,2048]{1,0:T(8,128)(2,1)} collective-permute-done((bf16[64,2048]{1,0:T(8,128)(2,1)S(1)}, bf16[64,2048]{1,0:T(8,128)(2,1)}, u32[]{:S(2)}, u32[]{:S(2)}) %collective-permute-start.5) | collective-permute-done | bytes 262176 | tf_op jit(solution)/shard_map/ppermute | solution.py:30
  38.3 2.6 collective-permute-start.7
  40.9 2.2 collective-permute-start.11
  43.1 3.3 %collective-permute-start.10 = (bf16[144,320]{1,0:T(8,128)(2,1)S(1)}, bf16[144,320]{1,0:T(8,128)(2,1)S(1)}, u32[]{:S(2)}, u32[]{:S(2)}) collective-permute-start(bf16[144,320]{1,0:T(8,128)(2,1)S(1)} %fusion.6.refs_0_), channel_id=1, source_target_pairs={{0,2},{1,3},{2,4},{3,5},{4,6},{5,7},{8,10},{9,11},{10,12},{11,13},... | collective-permute-start | bytes 276488 | tf_op jit(solution)/shard_map/ppermute | solution.py:25
  47.3 2.7 collective-permute-done.11.refs_2_
  50.0 2.4 collective-permute-done.10.refs_1_
  54.0 8.0 %collective-permute-start.8 = (bf16[64,2048]{1,0:T(8,128)(2,1)S(1)}, bf16[64,2048]{1,0:T(8,128)(2,1)}, u32[]{:S(2)}, u32[]{:S(2)}) collective-permute-start(bf16[64,2048]{1,0:T(8,128)(2,1)S(1)} %get-tuple-element.82.refs_0_), channel_id=1, source_target_pairs={{0,2},{1,3},{2,0},{3,1},{4,6},{5,7},{6,4},{7,5},{8,10},{9,11},{10,... | collective-permute-start | bytes 786440 | tf_op jit(solution)/shard_map/ppermute | solution.py:30
  64.9 1.6 collective-permute-start.15
  66.5 2.0 collect.1
  69.3 1.5 collective-permute-start.6
  70.9 3.8 %collective-permute-done.9.refs_3_ = bf16[64,2048]{1,0:T(8,128)(2,1)} collective-permute-done((bf16[64,2048]{1,0:T(8,128)(2,1)}, bf16[64,2048]{1,0:T(8,128)(2,1)}, u32[]{:S(2)}, u32[]{:S(2)}) %collective-permute-start.9) | collective-permute-done | bytes 262176 | tf_op jit(solution)/shard_map/ppermute | solution.py:30
  77.1 12.4 %heads_backward.5 = (bf16[128,8192]{1,0:T(8,128)(2,1)}, bf16[128,4096]{1,0:T(8,128)(2,1)}, bf16[128,6144]{1,0:T(8,128)(2,1)S(1)}, f32[128,2048]{1,0:T(8,128)S(1)...) custom-call(s32[5]{0:T(128)S(1)} %copy-done.23, bf16[128,8192]{1,0:T(8,128)(2,1)S(1)} %bitcast.48, ...), custom_call_target="tpu_custom_call" | custom-call | flops 400000000 | bytes 1200000 | tf_op jit(solution)/shard_map/heads_backward/pallas_call | solution.py:169
  90.6 12.2 %heads_backward.6 = (bf16[128,8192]{1,0:T(8,128)(2,1)}, bf16[128,4096]{1,0:T(8,128)(2,1)}, bf16[128,6144]{1,0:T(8,128)(2,1)S(1)}, f32[128,2048]{1,0:T(8,128)S(1)...) custom-call(s32[5]{0:T(128)S(1)} %copy-done.23, ...), custom_call_target="tpu_custom_call", output_to_operand_aliasing={{0}: (14, {}), {1}: (15, {}), {2}: (16, {})} | custom-call | flops 400000000 | bytes 1200000 | tf_op jit(solution)/shard_map/heads_backward/pallas_call | solution.py:169
  104.3 1.5 collective-permute-start.14
  105.8 12.6 %heads_backward.7 = (bf16[128,8192]{1,0:T(8,128)(2,1)}, bf16[128,4096]{1,0:T(8,128)(2,1)}, bf16[128,6144]{1,0:T(8,128)(2,1)S(1)}, f32[128,2048]{1,0:T(8,128)}, f...) custom-call(s32[5]{0:T(128)S(1)} %copy-done.23, ...), custom_call_target="tpu_custom_call", output_to_operand_aliasing={{0}: (14, {}), {1}: (15, {}), {2}: (16, {})} | custom-call | flops 400000000 | bytes 1200000 | tf_op jit(solution)/shard_map/heads_backward/pallas_call | solution.py:169
  119.0 7.0 %heads_backward.8 = (bf16[128,8192]{1,0:T(8,128)(2,1)}, bf16[128,4096]{1,0:T(8,128)(2,1)}, bf16[128,6144]{1,0:T(8,128)(2,1)S(1)}, f32[128,1024]{1,0:T(8,128)S(1)...) custom-call(s32[5]{0:T(128)S(1)} %copy-done.23, ...), custom_call_target="tpu_custom_call", output_to_operand_aliasing={{0}: (14, {}), {1}: (15, {}), {2}: (16, {})} | custom-call | flops 200000000 | bytes 600000 | tf_op jit(solution)/shard_map/heads_backward/pallas_call | solution.py:169
  126.8 2.1 collective-permute-done.13
  128.9 7.2 %heads_backward.9 = (bf16[128,8192]{1,0:T(8,128)(2,1)}, bf16[128,4096]{1,0:T(8,128)(2,1)}, bf16[128,6144]{1,0:T(8,128)(2,1)S(1)}, f32[128,1024]{1,0:T(8,128)S(1)...) custom-call(s32[5]{0:T(128)S(1)} %copy-done.23, ...), custom_call_target="tpu_custom_call", output_to_operand_aliasing={{0}: (14, {}), {1}: (15, {}), {2}: (16, {})} | custom-call | flops 200000000 | bytes 600000 | tf_op jit(solution)/shard_map/heads_backward/pallas_call | solution.py:169
  137.3 1.6 spread.1
  140.9 1.5 collective-permute-start.22
  142.9 2.7 slice_add_fusion
  145.6 10.3 %collective-permute-done.22 = f32[128,1024]{1,0:T(8,128)} collective-permute-done((f32[128,1024]{1,0:T(8,128)}, f32[128,1024]{1,0:T(8,128)}, u32[]{:S(2)}, u32[]{:S(2)}) %collective-permute-start.22) | collective-permute-done | bytes 524320 | tf_op jit(solution)/shard_map/ppermute | solution.py:30
  155.9 10.9 %collective-permute-done.23 = f32[128,1024]{1,0:T(8,128)} collective-permute-done((f32[128,1024]{1,0:T(8,128)}, f32[128,1024]{1,0:T(8,128)}, u32[]{:S(2)}, u32[]{:S(2)}) %collective-permute-start.23) | collective-permute-done | bytes 524320 | tf_op jit(solution)/shard_map/ppermute | solution.py:30
  168.8 2.2 copy.37
  175.5 5.1 %collective-permute-done.18 = f32[128,320]{1,0:T(8,128)S(1)} collective-permute-done((f32[128,320]{1,0:T(8,128)S(1)}, f32[128,320]{1,0:T(8,128)S(1)}, u32[]{:S(2)}, u32[]{:S(2)}) %collective-permute-start.18) | collective-permute-done | bytes 163872 | tf_op jit(solution)/shard_map/ppermute | solution.py:25
  180.5 1.5 collective-permute-start.21
  182.1 8.8 %collective-permute-done.19 = f32[128,320]{1,0:T(8,128)S(1)} collective-permute-done((f32[128,320]{1,0:T(8,128)S(1)}, f32[128,320]{1,0:T(8,128)S(1)}, u32[]{:S(2)}, u32[]{:S(2)}) %collective-permute-start.19) | collective-permute-done | bytes 163872 | tf_op jit(solution)/shard_map/ppermute | solution.py:25
  190.9 1.5 collective-permute-start.28
  192.5 1.8 add_add_fusion
  195.5 2.4 place_columns.1
  198.7 5.2 %collective-permute-done.28 = f32[128,1024]{1,0:T(8,128)S(1)} collective-permute-done((f32[128,1024]{1,0:T(8,128)S(1)}, f32[128,1024]{1,0:T(8,128)S(1)}, u32[]{:S(2)}, u32[]{:S(2)}) %collective-permute-start.28) | collective-permute-done | bytes 524320 | tf_op jit(solution)/shard_map/ppermute | solution.py:30
  203.9 5.2 %collective-permute-done.25 = f32[128,1024]{1,0:T(8,128)S(1)} collective-permute-done((f32[128,1024]{1,0:T(8,128)S(1)}, f32[128,1024]{1,0:T(8,128)S(1)}, u32[]{:S(2)}, u32[]{:S(2)}) %collective-permute-start.25) | collective-permute-done | bytes 524320 | tf_op jit(solution)/shard_map/ppermute | solution.py:30
  209.2 8.5 %collective-permute-done.30 = f32[128,1024]{1,0:T(8,128)S(1)} collective-permute-done((f32[128,1024]{1,0:T(8,128)S(1)}, f32[128,1024]{1,0:T(8,128)S(1)}, u32[]{:S(2)}, u32[]{:S(2)}) %collective-permute-start.30) | collective-permute-done | bytes 524320 | tf_op jit(solution)/shard_map/ppermute | solution.py:30
  217.6 1.6 fusion.1
  219.2 3.7 %collective-permute-start.26 = (f32[64,1024]{1,0:T(8,128)S(1)}, f32[64,1024]{1,0:T(8,128)S(1)}, u32[]{:S(2)}, u32[]{:S(2)}) collective-permute-start(f32[64,1024]{1,0:T(8,128)S(1)} %slice.111), channel_id=1, source_target_pairs={{0,4},{1,5},{2,6},{3,7},{4,0},{5,1},{6,2},{7,3},{8,12},{9,13},{10,... | collective-permute-start | bytes 786440 | tf_op jit(solution)/shard_map/ppermute | solution.py:30
  223.1 15.8 %collective-permute-done.26 = f32[64,1024]{1,0:T(8,128)S(1)} collective-permute-done((f32[64,1024]{1,0:T(8,128)S(1)}, f32[64,1024]{1,0:T(8,128)S(1)}, u32[]{:S(2)}, u32[]{:S(2)}) %collective-permute-start.26) | collective-permute-done | bytes 262176 | tf_op jit(solution)/shard_map/ppermute | solution.py:30
  239.0 5.2 %collective-permute-done.31 = f32[64,1024]{1,0:T(8,128)S(1)} collective-permute-done((f32[64,1024]{1,0:T(8,128)S(1)}, f32[64,1024]{1,0:T(8,128)S(1)}, u32[]{:S(2)}, u32[]{:S(2)}) %collective-permute-start.31) | collective-permute-done | bytes 262176 | tf_op jit(solution)/shard_map/ppermute | solution.py:30
  244.8 2.5 collective-permute-start.37
  249.3 2.3 collective-permute-start.38
  252.1 2.9 %collective-permute-done.37.refs_6_ = f32[32,2048]{1,0:T(8,128)S(1)} collective-permute-done((f32[32,2048]{1,0:T(8,128)S(1)}, f32[32,2048]{1,0:T(8,128)S(1)}, u32[]{:S(2)}, u32[]{:S(2)}) %collective-permute-start.37) | collective-permute-done | bytes 262176 | tf_op jit(solution)/shard_map/ppermute | solution.py:30
  257.3 3.3 %collective-permute-done.35.refs_4_ = f32[32,2048]{1,0:T(8,128)S(1)} collective-permute-done((f32[32,2048]{1,0:T(8,128)S(1)}, f32[32,2048]{1,0:T(8,128)S(1)}, u32[]{:S(2)}, u32[]{:S(2)}) %collective-permute-start.35) | collective-permute-done | bytes 262176 | tf_op jit(solution)/shard_map/ppermute | solution.py:30
  260.7 5.6 %collective-permute-done.38.refs_7_ = f32[32,2048]{1,0:T(8,128)S(1)} collective-permute-done((f32[32,2048]{1,0:T(8,128)S(1)}, f32[32,2048]{1,0:T(8,128)S(1)}, u32[]{:S(2)}, u32[]{:S(2)}) %collective-permute-start.38) | collective-permute-done | bytes 262176 | tf_op jit(solution)/shard_map/ppermute | solution.py:30
  266.3 4.4 %collective-permute-done.36.refs_5_ = f32[32,2048]{1,0:T(8,128)S(1)} collective-permute-done((f32[32,2048]{1,0:T(8,128)S(1)}, f32[32,2048]{1,0:T(8,128)S(1)}, u32[]{:S(2)}, u32[]{:S(2)}) %collective-permute-start.36) | collective-permute-done | bytes 262176 | tf_op jit(solution)/shard_map/ppermute | solution.py:30
  270.8 2.4 lay_out.1
  (143 shorter events, 38.9 us)
Async XLA Ops:
  0.6 16.9 %copy-start = (s32[1,8,4]{1,2,0:T(4,128)S(1)}, s32[1,8,4]{1,2,0:T(4,128)}, u32[]{:S(2)}) copy-start(s32[1,8,4]{1,2,0:T(4,128)} %param.15) | copy-start | bytes 388
  3.9 1.8 collective-permute-start
  8.3 23.4 %copy-start.28 = (s32[1,2,3]{2,1,0:T(2,128)S(1)}, s32[1,2,3]{2,1,0:T(2,128)}, u32[]{:S(2)}) copy-start(s32[1,2,3]{2,1,0:T(2,128)} %param.14) | copy-start | bytes 76
  8.3 23.8 %copy-start.27 = (bf16[1,128,320]{1,2,0:T(8,128)(2,1)S(1)}, bf16[1,128,320]{1,2,0:T(8,128)(2,1)}, u32[]{:S(2)}) copy-start(bf16[1,128,320]{1,2,0:T(8,128)(2,1)} %param.12) | copy-start | bytes 245764
  13.1 62.8 %collective-permute-start.1 = (bf16[128,10240]{1,0:T(8,128)(2,1)}, bf16[128,10240]{1,0:T(8,128)(2,1)S(1)}, u32[]{:S(2)}, u32[]{:S(2)}) collective-permute-start(bf16[128,10240]{1,0:T(8,128)(2,1)} %pack_columns.1), channel_id=1, source_target_pairs={{0,1},{1,0},{2,3},{3,2},{4,5},{5,4},{6,7},{7,6},{8,9},{9,8},{10,11... | collective-permute-start | bytes 7864328 | tf_op jit(solution)/shard_map/ppermute | solution.py:30
  13.8 16.4 %collective-permute-start.3 = (bf16[64,2048]{1,0:T(8,128)(2,1)}, bf16[64,2048]{1,0:T(8,128)(2,1)S(1)}, u32[]{:S(2)}, u32[]{:S(2)}) collective-permute-start(bf16[64,2048]{1,0:T(8,128)(2,1)} %get-tuple-element.80.refs_0_), channel_id=1, source_target_pairs={{0,4},{1,5},{2,6},{3,7},{4,0},{5,1},{6,2},{7,3},{8,12},{9,13},{10,... | collective-permute-start | bytes 786440 | tf_op jit(solution)/shard_map/ppermute | solution.py:30
  17.5 48.9 %copy-start.11 = (f32[1,64,128]{2,1,0:T(8,128)S(1)}, f32[1,64,128]{2,1,0:T(8,128)}, u32[]{:S(2)}) copy-start(f32[1,64,128]{2,1,0:T(8,128)} %param.11) | copy-start | bytes 98308
  30.2 8.1 %collective-permute-start.5 = (bf16[64,2048]{1,0:T(8,128)(2,1)S(1)}, bf16[64,2048]{1,0:T(8,128)(2,1)}, u32[]{:S(2)}, u32[]{:S(2)}) collective-permute-start(bf16[64,2048]{1,0:T(8,128)(2,1)S(1)} %collective-permute-done.3.refs_1_), channel_id=1, source_target_pairs={{0,2},{1,3},{2,0},{3,1},{4,6},{5,7},{6,4},{7,5},{8,10},{9,11},{10,... | collective-permute-start | bytes 786440 | tf_op jit(solution)/shard_map/ppermute | solution.py:30
  38.3 23.8 %collective-permute-start.7 = (bf16[64,2048]{1,0:T(8,128)(2,1)S(1)}, bf16[64,2048]{1,0:T(8,128)(2,1)}, u32[]{:S(2)}, u32[]{:S(2)}) collective-permute-start(bf16[64,2048]{1,0:T(8,128)(2,1)S(1)} %get-tuple-element.82.refs_0_), channel_id=1, source_target_pairs={{0,4},{1,5},{2,6},{3,7},{4,0},{5,1},{6,2},{7,3},{8,12},{9,13},{10,... | collective-permute-start | bytes 786440 | tf_op jit(solution)/shard_map/ppermute | solution.py:30
  40.9 9.1 %collective-permute-start.11 = (bf16[144,320]{1,0:T(8,128)(2,1)S(1)}, bf16[144,320]{1,0:T(8,128)(2,1)S(1)}, u32[]{:S(2)}, u32[]{:S(2)}) collective-permute-start(bf16[144,320]{1,0:T(8,128)(2,1)S(1)} %fusion.6.refs_0_), channel_id=1, source_target_pairs={{0,4},{1,5},{2,6},{3,7},{8,12},{9,13},{10,14},{11,15},{16,20},{17,... | collective-permute-start | bytes 276488 | tf_op jit(solution)/shard_map/ppermute | solution.py:25
  43.1 9.3 %collective-permute-start.10 = (bf16[144,320]{1,0:T(8,128)(2,1)S(1)}, bf16[144,320]{1,0:T(8,128)(2,1)S(1)}, u32[]{:S(2)}, u32[]{:S(2)}) collective-permute-start(bf16[144,320]{1,0:T(8,128)(2,1)S(1)} %fusion.6.refs_0_), channel_id=1, source_target_pairs={{0,2},{1,3},{2,4},{3,5},{4,6},{5,7},{8,10},{9,11},{10,12},{11,13},... | collective-permute-start | bytes 276488 | tf_op jit(solution)/shard_map/ppermute | solution.py:25
  46.5 15.9 %collective-permute-start.4 = (bf16[64,2048]{1,0:T(8,128)(2,1)}, bf16[64,2048]{1,0:T(8,128)(2,1)}, u32[]{:S(2)}, u32[]{:S(2)}) collective-permute-start(bf16[64,2048]{1,0:T(8,128)(2,1)} %get-tuple-element.80.refs_0_), channel_id=1, source_target_pairs={{0,2},{1,3},{2,0},{3,1},{4,6},{5,7},{6,4},{7,5},{8,10},{9,11},{10,... | collective-permute-start | bytes 786440 | tf_op jit(solution)/shard_map/ppermute | solution.py:30
  54.0 12.5 %collective-permute-start.12 = (bf16[432,320]{1,0:T(8,128)(2,1)S(1)}, bf16[432,320]{1,0:T(8,128)(2,1)}, u32[]{:S(2)}, u32[]{:S(2)}) collective-permute-start(bf16[432,320]{1,0:T(8,128)(2,1)S(1)} %stack.78.own), channel_id=1, source_target_pairs={{0,1},{1,0},{2,3},{3,2},{4,5},{5,4},{6,7},{7,6},{8,9},{9,8},{10,11... | collective-permute-start | bytes 829448 | tf_op jit(solution)/shard_map/ppermute | solution.py:30
  54.0 15.3 %collective-permute-start.8 = (bf16[64,2048]{1,0:T(8,128)(2,1)S(1)}, bf16[64,2048]{1,0:T(8,128)(2,1)}, u32[]{:S(2)}, u32[]{:S(2)}) collective-permute-start(bf16[64,2048]{1,0:T(8,128)(2,1)S(1)} %get-tuple-element.82.refs_0_), channel_id=1, source_target_pairs={{0,2},{1,3},{2,0},{3,1},{4,6},{5,7},{6,4},{7,5},{8,10},{9,11},{10,... | collective-permute-start | bytes 786440 | tf_op jit(solution)/shard_map/ppermute | solution.py:30
  62.1 12.6 %collective-permute-start.9 = (bf16[64,2048]{1,0:T(8,128)(2,1)}, bf16[64,2048]{1,0:T(8,128)(2,1)}, u32[]{:S(2)}, u32[]{:S(2)}) collective-permute-start(bf16[64,2048]{1,0:T(8,128)(2,1)} %collective-permute-done.7.refs_1_), channel_id=1, source_target_pairs={{0,2},{1,3},{2,0},{3,1},{4,6},{5,7},{6,4},{7,5},{8,10},{9,11},{10,... | collective-permute-start | bytes 786440 | tf_op jit(solution)/shard_map/ppermute | solution.py:30
  62.3 13.6 %copy-start.1 = (bf16[1,128,8192]{2,1,0:T(8,128)(2,1)S(1)}, bf16[1,128,8192]{2,1,0:T(8,128)(2,1)}, u32[]{:S(2)}) copy-start(bf16[1,128,8192]{2,1,0:T(8,128)(2,1)} %param.8) | copy-start | bytes 6291460
  62.3 13.6 %copy-start.2 = (bf16[1,128,8192]{2,1,0:T(8,128)(2,1)S(1)}, bf16[1,128,8192]{2,1,0:T(8,128)(2,1)}, u32[]{:S(2)}) copy-start(bf16[1,128,8192]{2,1,0:T(8,128)(2,1)} %param.10) | copy-start | bytes 6291460
  63.4 12.5 %copy-start.23 = (s32[5]{0:T(128)S(1)}, s32[5]{0:T(128)}, u32[]{:S(2)}) copy-start(s32[5]{0:T(128)} %stack.63.place) | copy-start | bytes 64
  64.9 41.0 %collective-permute-start.15 = (bf16[256,2048]{1,0:T(8,128)(2,1)S(1)}, bf16[256,2048]{1,0:T(8,128)(2,1)S(1)}, u32[]{:S(2)}, u32[]{:S(2)}) collective-permute-start(bf16[256,2048]{1,0:T(8,128)(2,1)S(1)} %stack.76.weight), channel_id=1, source_target_pairs={{0,8},{8,0},{16,24},{24,16},{1,9},{9,1},{17,25},{25,17},{2,10},{10... | collective-permute-start | bytes 3145736 | tf_op jit(solution)/shard_map/ppermute | solution.py:30
  66.4 9.4 %collective-permute-start.2 = (f32[4,4,2,128]{3,2,1,0:T(2,128)S(1)}, f32[4,4,2,128]{3,2,1,0:T(2,128)S(1)}, u32[]{:S(2)}, u32[]{:S(2)}) collective-permute-start(f32[4,4,2,128]{3,2,1,0:T(2,128)S(1)} %dynamic-slice_bitcast_fusion), channel_id=1, source_target_pairs={{0,1},{1,0},{2,3},{3,2},{4,5},{5,4},{6,7},{7,6},{8,9},{9,8},{10,11... | collective-permute-start | bytes 49160 | tf_op jit(solution)/shard_map/ppermute | solution.py:30
  69.3 49.6 %collective-permute-start.6 = (bf16[256,2048]{1,0:T(8,128)(2,1)S(1)}, bf16[256,2048]{1,0:T(8,128)(2,1)S(1)}, u32[]{:S(2)}, u32[]{:S(2)}) collective-permute-start(bf16[256,2048]{1,0:T(8,128)(2,1)S(1)} %stack.76.weight), channel_id=1, source_target_pairs={{0,16},{8,24},{16,0},{24,8},{1,17},{9,25},{17,1},{25,9},{2,18},{10... | collective-permute-start | bytes 3145736 | tf_op jit(solution)/shard_map/ppermute | solution.py:30
  102.8 26.1 %collective-permute-start.13 = (f32[128,2048]{1,0:T(8,128)S(1)}, f32[128,2048]{1,0:T(8,128)S(1)}, u32[]{:S(2)}, u32[]{:S(2)}) collective-permute-start(f32[128,2048]{1,0:T(8,128)S(1)} %get-tuple-element.93), channel_id=1, source_target_pairs={{0,8},{8,0},{16,24},{24,16},{1,9},{9,1},{17,25},{25,17},{2,10},{10... | collective-permute-start | bytes 3145736 | tf_op jit(solution)/shard_map/ppermute | solution.py:30
  104.3 24.6 %collective-permute-start.14 = (f32[128,2048]{1,0:T(8,128)S(1)}, f32[128,2048]{1,0:T(8,128)S(1)}, u32[]{:S(2)}, u32[]{:S(2)}) collective-permute-start(f32[128,2048]{1,0:T(8,128)S(1)} %get-tuple-element.94), channel_id=1, source_target_pairs={{0,16},{8,24},{16,0},{24,8},{1,17},{9,25},{17,1},{25,9},{2,18},{10... | collective-permute-start | bytes 3145736 | tf_op jit(solution)/shard_map/ppermute | solution.py:30
  118.4 55.5 %collective-permute-start.20 = (f32[128,2048]{1,0:T(8,128)}, f32[128,2048]{1,0:T(8,128)}, u32[]{:S(2)}, u32[]{:S(2)}) collective-permute-start(f32[128,2048]{1,0:T(8,128)} %get-tuple-element.123), channel_id=1, source_target_pairs={{0,8},{8,0},{16,24},{24,16},{1,9},{9,1},{17,25},{25,17},{2,10},{10... | collective-permute-start | bytes 3145736 | tf_op jit(solution)/shard_map/ppermute | solution.py:30
  140.9 27.9 %collective-permute-start.17 = (f32[432,320]{0,1:T(8,128)}, f32[432,320]{0,1:T(8,128)}, u32[]{:S(2)}, u32[]{:S(2)}) collective-permute-start(f32[432,320]{0,1:T(8,128)} %copy.36), channel_id=1, source_target_pairs={{0,1},{1,0},{2,3},{3,2},{4,5},{5,4},{6,7},{7,6},{8,9},{9,8},{10,11... | collective-permute-start | bytes 1658888 | tf_op jit(solution)/shard_map/ppermute | solution.py:30
  140.9 15.0 %collective-permute-start.22 = (f32[128,1024]{1,0:T(8,128)}, f32[128,1024]{1,0:T(8,128)}, u32[]{:S(2)}, u32[]{:S(2)}) collective-permute-start(f32[128,1024]{1,0:T(8,128)} %get-tuple-element.127), channel_id=1, source_target_pairs={{0,16},{8,24},{16,0},{24,8},{1,17},{9,25},{17,1},{25,9},{2,18},{10... | collective-permute-start | bytes 1572872 | tf_op jit(solution)/shard_map/ppermute | solution.py:30
  142.4 24.4 %collective-permute-start.23 = (f32[128,1024]{1,0:T(8,128)}, f32[128,1024]{1,0:T(8,128)}, u32[]{:S(2)}, u32[]{:S(2)}) collective-permute-start(f32[128,1024]{1,0:T(8,128)} %get-tuple-element.129), channel_id=1, source_target_pairs={{0,16},{8,24},{16,0},{24,8},{1,17},{9,25},{17,1},{25,9},{2,18},{10... | collective-permute-start | bytes 1572872 | tf_op jit(solution)/shard_map/ppermute | solution.py:30
  142.9 52.5 %collective-permute-start.16 = (bf16[128,6144]{1,0:T(8,128)(2,1)S(1)}, bf16[128,6144]{1,0:T(8,128)(2,1)S(1)}, u32[]{:S(2)}, u32[]{:S(2)}) collective-permute-start(bf16[128,6144]{1,0:T(8,128)(2,1)S(1)} %copy-done.5), channel_id=1, source_target_pairs={{0,1},{1,0},{2,3},{3,2},{4,5},{5,4},{6,7},{7,6},{8,9},{9,8},{10,11... | collective-permute-start | bytes 4718600 | tf_op jit(solution)/shard_map/ppermute | solution.py:30
  166.8 25.7 %collective-permute-start.24 = (f32[128,1024]{1,0:T(8,128)}, f32[128,1024]{1,0:T(8,128)}, u32[]{:S(2)}, u32[]{:S(2)}) collective-permute-start(f32[128,1024]{1,0:T(8,128)} %get-tuple-element.130), channel_id=1, source_target_pairs={{0,8},{8,0},{16,24},{24,16},{1,9},{9,1},{17,25},{25,17},{2,10},{10... | collective-permute-start | bytes 1572872 | tf_op jit(solution)/shard_map/ppermute | solution.py:30
  168.2 24.2 %collective-permute-start.29 = (f32[128,1024]{1,0:T(8,128)}, f32[128,1024]{1,0:T(8,128)}, u32[]{:S(2)}, u32[]{:S(2)}) collective-permute-start(f32[128,1024]{1,0:T(8,128)} %get-tuple-element.134), channel_id=1, source_target_pairs={{0,8},{8,0},{16,24},{24,16},{1,9},{9,1},{17,25},{25,17},{2,10},{10... | collective-permute-start | bytes 1572872 | tf_op jit(solution)/shard_map/ppermute | solution.py:30
  172.5 19.9 %copy-start.10 = (f32[128,2048]{1,0:T(8,128)S(1)}, f32[128,2048]{1,0:T(8,128)}, u32[]{:S(2)}) copy-start(f32[128,2048]{1,0:T(8,128)} %copy-done.9) | copy-start | bytes 3145732
  172.5 8.0 %collective-permute-start.18 = (f32[128,320]{1,0:T(8,128)S(1)}, f32[128,320]{1,0:T(8,128)S(1)}, u32[]{:S(2)}, u32[]{:S(2)}) collective-permute-start(f32[128,320]{1,0:T(8,128)S(1)} %get-tuple-element.162), channel_id=1, source_target_pairs={{2,0},{3,1},{4,2},{5,3},{6,4},{7,5},{10,8},{11,9},{12,10},{13,11},... | collective-permute-start | bytes 491528 | tf_op jit(solution)/shard_map/ppermute | solution.py:25
  174.0 16.9 %collective-permute-start.19 = (f32[128,320]{1,0:T(8,128)S(1)}, f32[128,320]{1,0:T(8,128)S(1)}, u32[]{:S(2)}, u32[]{:S(2)}) collective-permute-start(f32[128,320]{1,0:T(8,128)S(1)} %get-tuple-element.163), channel_id=1, source_target_pairs={{4,0},{5,1},{6,2},{7,3},{12,8},{13,9},{14,10},{15,11},{20,16},{21,... | collective-permute-start | bytes 491528 | tf_op jit(solution)/shard_map/ppermute | solution.py:25
  180.5 18.2 %collective-permute-start.21 = (f32[128,1024]{1,0:T(8,128)S(1)}, f32[128,1024]{1,0:T(8,128)S(1)}, u32[]{:S(2)}, u32[]{:S(2)}) collective-permute-start(f32[128,1024]{1,0:T(8,128)S(1)} %get-tuple-element.125), channel_id=1, source_target_pairs={{0,16},{8,24},{16,0},{24,8},{1,17},{9,25},{17,1},{25,9},{2,18},{10... | collective-permute-start | bytes 1572872 | tf_op jit(solution)/shard_map/ppermute | solution.py:30
  190.9 13.1 %collective-permute-start.28 = (f32[128,1024]{1,0:T(8,128)S(1)}, f32[128,1024]{1,0:T(8,128)S(1)}, u32[]{:S(2)}, u32[]{:S(2)}) collective-permute-start(f32[128,1024]{1,0:T(8,128)S(1)} %get-tuple-element.133), channel_id=1, source_target_pairs={{0,16},{8,24},{16,0},{24,8},{1,17},{9,25},{17,1},{25,9},{2,18},{10... | collective-permute-start | bytes 1572872 | tf_op jit(solution)/shard_map/ppermute | solution.py:30
  194.2 14.9 %collective-permute-start.25 = (f32[128,1024]{1,0:T(8,128)S(1)}, f32[128,1024]{1,0:T(8,128)S(1)}, u32[]{:S(2)}, u32[]{:S(2)}) collective-permute-start(f32[128,1024]{1,0:T(8,128)S(1)} %get-tuple-element.131), channel_id=1, source_target_pairs={{0,2},{1,3},{2,0},{3,1},{4,6},{5,7},{6,4},{7,5},{8,10},{9,11},{10,... | collective-permute-start | bytes 1572872 | tf_op jit(solution)/shard_map/ppermute | solution.py:30
  195.5 22.2 %copy-start.7 = (f32[128,2048]{1,0:T(8,128)S(1)}, f32[128,2048]{1,0:T(8,128)}, u32[]{:S(2)}) copy-start(f32[128,2048]{1,0:T(8,128)} %copy-done.6) | copy-start | bytes 3145732
  197.8 19.8 %collective-permute-start.30 = (f32[128,1024]{1,0:T(8,128)S(1)}, f32[128,1024]{1,0:T(8,128)S(1)}, u32[]{:S(2)}, u32[]{:S(2)}) collective-permute-start(f32[128,1024]{1,0:T(8,128)S(1)} %get-tuple-element.135), channel_id=1, source_target_pairs={{0,2},{1,3},{2,0},{3,1},{4,6},{5,7},{6,4},{7,5},{8,10},{9,11},{10,... | collective-permute-start | bytes 1572872 | tf_op jit(solution)/shard_map/ppermute | solution.py:30
  219.2 19.6 %collective-permute-start.26 = (f32[64,1024]{1,0:T(8,128)S(1)}, f32[64,1024]{1,0:T(8,128)S(1)}, u32[]{:S(2)}, u32[]{:S(2)}) collective-permute-start(f32[64,1024]{1,0:T(8,128)S(1)} %slice.111), channel_id=1, source_target_pairs={{0,4},{1,5},{2,6},{3,7},{4,0},{5,1},{6,2},{7,3},{8,12},{9,13},{10,... | collective-permute-start | bytes 786440 | tf_op jit(solution)/shard_map/ppermute | solution.py:30
  223.0 21.2 %collective-permute-start.31 = (f32[64,1024]{1,0:T(8,128)S(1)}, f32[64,1024]{1,0:T(8,128)S(1)}, u32[]{:S(2)}, u32[]{:S(2)}) collective-permute-start(f32[64,1024]{1,0:T(8,128)S(1)} %slice.118), channel_id=1, source_target_pairs={{0,4},{1,5},{2,6},{3,7},{4,0},{5,1},{6,2},{7,3},{8,12},{9,13},{10,... | collective-permute-start | bytes 786440 | tf_op jit(solution)/shard_map/ppermute | solution.py:30
  238.9 5.3 %collective-permute-start.27 = (f32[32,1024]{1,0:T(8,128)S(1)}, f32[32,1024]{1,0:T(8,128)S(1)}, u32[]{:S(2)}, u32[]{:S(2)}) collective-permute-start(f32[32,1024]{1,0:T(8,128)S(1)} %get-tuple-element.166), channel_id=1, source_target_pairs={{0,1},{1,0},{2,3},{3,2},{4,5},{5,4},{6,7},{7,6},{8,9},{9,8},{10,11... | collective-permute-start | bytes 393224 | tf_op jit(solution)/shard_map/ppermute | solution.py:30
  244.8 10.2 %collective-permute-start.37 = (f32[32,2048]{1,0:T(8,128)S(1)}, f32[32,2048]{1,0:T(8,128)S(1)}, u32[]{:S(2)}, u32[]{:S(2)}) collective-permute-start(f32[32,2048]{1,0:T(8,128)S(1)} %join_cores.2.refs_0_), channel_id=1, source_target_pairs={{0,24},{8,16},{16,8},{24,0},{1,25},{9,17},{17,9},{25,1},{2,26},{10... | collective-permute-start | bytes 786440 | tf_op jit(solution)/shard_map/ppermute | solution.py:30
  247.4 1.4 collective-permute-start.32
  247.4 13.2 %collective-permute-start.35 = (f32[32,2048]{1,0:T(8,128)S(1)}, f32[32,2048]{1,0:T(8,128)S(1)}, u32[]{:S(2)}, u32[]{:S(2)}) collective-permute-start(f32[32,2048]{1,0:T(8,128)S(1)} %join_cores.2.refs_0_), channel_id=1, source_target_pairs={{0,16},{8,24},{16,0},{24,8},{1,17},{9,25},{17,1},{25,9},{2,18},{10... | collective-permute-start | bytes 786440 | tf_op jit(solution)/shard_map/ppermute | solution.py:30
  248.0 12.7 %collective-permute-start.33 = (f32[32,2048]{1,0:T(8,128)S(1)}, f32[32,2048]{1,0:T(8,128)S(1)}, u32[]{:S(2)}, u32[]{:S(2)}) collective-permute-start(f32[32,2048]{1,0:T(8,128)S(1)} %join_cores.2.refs_0_), channel_id=1, source_target_pairs={{0,8},{8,0},{16,24},{24,16},{1,9},{9,1},{17,25},{25,17},{2,10},{10... | collective-permute-start | bytes 786440 | tf_op jit(solution)/shard_map/ppermute | solution.py:30
  249.3 17.0 %collective-permute-start.38 = (f32[32,2048]{1,0:T(8,128)S(1)}, f32[32,2048]{1,0:T(8,128)S(1)}, u32[]{:S(2)}, u32[]{:S(2)}) collective-permute-start(f32[32,2048]{1,0:T(8,128)S(1)} %join_cores.3.refs_1_), channel_id=1, source_target_pairs={{0,24},{8,16},{16,8},{24,0},{1,25},{9,17},{17,9},{25,1},{2,26},{10... | collective-permute-start | bytes 786440 | tf_op jit(solution)/shard_map/ppermute | solution.py:30
  251.6 19.1 %collective-permute-start.36 = (f32[32,2048]{1,0:T(8,128)S(1)}, f32[32,2048]{1,0:T(8,128)S(1)}, u32[]{:S(2)}, u32[]{:S(2)}) collective-permute-start(f32[32,2048]{1,0:T(8,128)S(1)} %join_cores.3.refs_1_), channel_id=1, source_target_pairs={{0,16},{8,24},{16,0},{24,8},{1,17},{9,25},{17,1},{25,9},{2,18},{10... | collective-permute-start | bytes 786440 | tf_op jit(solution)/shard_map/ppermute | solution.py:30
  255.0 15.8 %collective-permute-start.34 = (f32[32,2048]{1,0:T(8,128)S(1)}, f32[32,2048]{1,0:T(8,128)S(1)}, u32[]{:S(2)}, u32[]{:S(2)}) collective-permute-start(f32[32,2048]{1,0:T(8,128)S(1)} %join_cores.3.refs_1_), channel_id=1, source_target_pairs={{0,8},{8,0},{16,24},{24,16},{1,9},{9,1},{17,25},{25,17},{2,10},{10... | collective-permute-start | bytes 786440 | tf_op jit(solution)/shard_map/ppermute | solution.py:30
  (20 other events, 64.7 us)

commit v3 on v2

--- a/solution.py
+++ b/solution.py
@@ -107,14 +107,12 @@
         weight_grads[1][:, columns] = weight_grad[half:]
 
 
-def chunk_backward(place, t, unit, own, packed, totals, weight, shared, earlier, sizes):
-    q_own, rope_own, out_own = own
-    tot_own, tot_sib = totals
+def chunk_backward(place, t, unit, own, sibling, weight, shared, earlier, sizes):
+    q_own, rope_own, out_own, tot_own = own
     cand, cand_t, rope_keys, bias = shared
     tokens = q_own.shape[0]
     chunks, pairs = sizes
     wide, narrow = 2 * NOPE, 2 * ROPE
-    span = pairs * (2 * wide + narrow)
     first, count = unit
     mine = lambda p, place: (place[1 + t] * 2 + place[0]) * pairs + first + p
     theirs = lambda p, place: place[1 + t] * pairs + first + p
@@ -124,24 +122,14 @@
         pl.BlockSpec((tokens, narrow), lambda p, place: (0, mine(p, place))),
         pl.BlockSpec((tokens, wide), lambda p, place: (0, mine(p, place))),
         pl.BlockSpec((1, 2, tokens), lambda p, place: (mine(p, place), 0, 0)),
-        pl.BlockSpec((tokens, wide), lambda p, place: (0, place[1 + t] * (span // wide) + first + p)),
-        pl.BlockSpec(
-            (tokens, narrow),
-            lambda p, place: (0, place[1 + t] * (span // narrow) + pairs * wide // narrow + first + p),
-        ),
-        pl.BlockSpec(
-            (tokens, wide),
-            lambda p, place: (0, place[1 + t] * (span // wide) + pairs * (wide + narrow) // wide + first + p),
-        ),
-        pl.BlockSpec((1, 2, tokens), lambda p, place: (theirs(p, place), 0, 0)),
+    ] * 2 + [
         pl.BlockSpec((LAT, 2 * (NOPE + VDIM)), lambda p, place: (0, first + p)),
         whole(cand),
         whole(cand_t),
         whole(rope_keys),
         whole(bias),
     ]
-    operands = [q_own, rope_own, out_own, tot_own, packed, packed, packed, tot_sib, weight]
-    operands += [cand, cand_t, rope_keys, bias]
+    operands = [*own, *sibling, weight, cand, cand_t, rope_keys, bias]
     aliases = {}
     if earlier is not None:
         for index, array in enumerate(earlier):
@@ -246,40 +234,45 @@
     )(*inputs)
 
 
-def leave_kernel(place, *refs):
-    *inputs, leaving, near, distant = refs
-    staying, half = (near, distant), len(inputs) // 2
-    width = inputs[0].shape[1]
-    for at in range(half):
-        leaving[:, at * width : (at + 1) * width] = inputs[at][...]
-        staying[at][...] = inputs[half + at][...]
-
-
-def weight_parts(place, up_weight, chunks, far):
+def leave_kernel(place, near, distant, leaving):
+    width = near.shape[1]
+    leaving[:, :width] = near[...]
+    leaving[:, width:] = distant[...]
+
+
+def join_rows_kernel(place, near, distant, crossed, near_rows, distant_rows):
+    rows, width = near.shape
+    for at, (own, out) in enumerate(((near, near_rows), (distant, distant_rows))):
+        out[:rows, :] = own[...]
+        out[rows:, :] = crossed[:, at * width : (at + 1) * width]
+
+
+def weight_parts(place, up_weight, chunks, far, crossed=None):
     rows = up_weight.shape[0]
     width = up_weight.shape[1] // chunks // 2
-
-    def column_block(t, other):
+    joins = crossed is not None
+
+    def column_block(t):
         def block(i, place):
-            return (0, place[1 + t] * 2 + (1 - place[0] if other else place[0]))
+            return (0, place[1 + t] * 2 + (place[0] if joins else 1 - place[0]))
 
         return pl.BlockSpec((rows, width), block)
 
-    return pl.pallas_call(
-        leave_kernel,
+    whole = lambda shape: pl.BlockSpec(shape, lambda i, place: (0, 0))
+    shapes = [(2 * rows, width)] * 2 if joins else [(rows, 2 * width)]
+    return pl.pallas_call(
+        join_rows_kernel if joins else leave_kernel,
         grid_spec=pltpu.PrefetchScalarGridSpec(
             num_scalar_prefetch=1,
             grid=(1,),
-            in_specs=[column_block(t, other) for other in (True, False) for t in (0, far)],
-            out_specs=[pl.BlockSpec((rows, 2 * width), lambda i, place: (0, 0))]
-            + [pl.BlockSpec((rows, width), lambda i, place: (0, 0))] * 2,
-        ),
-        out_shape=[jax.ShapeDtypeStruct((rows, 2 * width), up_weight.dtype)]
-        + [jax.ShapeDtypeStruct((rows, width), up_weight.dtype)] * 2,
+            in_specs=[column_block(t) for t in (0, far)] + [whole((rows, 2 * width))] * joins,
+            out_specs=[whole(shape) for shape in shapes],
+        ),
+        out_shape=[jax.ShapeDtypeStruct(shape, up_weight.dtype) for shape in shapes],
         compiler_params=pltpu.CompilerParams(vmem_limit_bytes=INPUT_BYTES),
         cost_estimate=pl.CostEstimate(flops=0, bytes_accessed=1_000_000, transcendentals=0),
         name="weight_parts",
-    )(place, *[up_weight] * 4)
+    )(place, up_weight, up_weight, *([crossed] if joins else []))
 
 
 def lay_kernel(place, *refs):
@@ -343,32 +336,6 @@
         cost_estimate=pl.CostEstimate(flops=0, bytes_accessed=500_000, transcendentals=0),
         name="join_cores",
     )(place, kept, crossed)
-
-
-def pack_kernel(place, q_ref, rope_ref, out_ref, packed):
-    q_cols, rope_cols = q_ref.shape[1], rope_ref.shape[1]
-    packed[:, :q_cols] = q_ref[...]
-    packed[:, q_cols : q_cols + rope_cols] = rope_ref[...]
-    packed[:, q_cols + rope_cols :] = out_ref[...]
-
-
-def pack_columns(place, arrays, chunks):
-    tokens = arrays[0].shape[0]
-    widths = [array.shape[1] // chunks // 2 for array in arrays]
-    theirs = lambda c, place: (0, c * 2 + 1 - place[0])
-    return pl.pallas_call(
-        pack_kernel,
-        grid_spec=pltpu.PrefetchScalarGridSpec(
-            num_scalar_prefetch=1,
-            grid=(chunks,),
-            in_specs=[pl.BlockSpec((tokens, width), theirs) for width in widths],
-            out_specs=pl.BlockSpec((tokens, sum(widths)), lambda c, place: (0, c)),
-        ),
-        out_shape=jax.ShapeDtypeStruct((tokens, chunks * sum(widths)), arrays[0].dtype),
-        compiler_params=pltpu.CompilerParams(vmem_limit_bytes=INPUT_BYTES),
-        cost_estimate=pl.CostEstimate(flops=0, bytes_accessed=5_000_000, transcendentals=0),
-        name="pack_columns",
-    )(place, *arrays)
 
 
 def halving_order(count):
@@ -508,45 +475,45 @@
 
     place = jnp.stack([core] + [dp ^ t for t in range(n_dp)]).astype(jnp.int32)
 
-    leaving, *staying = weight_parts(place, up_weight, n_dp, far)
+    leaving, = weight_parts(place, up_weight, n_dp, far)
     crossed = exchange(leaving, "ctx", 1)
-    chip_rows = stack(
-        [*staying, crossed], (((0, 0), (2, 0)), ((1, 0), (2, 1))), part_cols
-    )
-    chip_rows, place, selected, offered, q_nope, q_rope, grad_out, log_total, kv_latent = (
+    crossed, place, selected, offered, q_nope, q_rope, grad_out, log_total, kv_latent = (
         lax.optimization_barrier(
-            (chip_rows, place, selected, offered, q_nope, q_rope, grad_out, log_total, kv_latent)
+            (crossed, place, selected, offered, q_nope, q_rope, grad_out, log_total, kv_latent)
         )
     )
+    chip_rows = weight_parts(place, up_weight, n_dp, far, crossed)
+    own = [q_nope[0], q_rope[0], grad_out[0]]
+    sibling = [exchange(array, "ctx", 1) for array in own]
+
     partners = halving_order(n_ctx)[::2]
 
-    def over_chips(start):
+    def over_chips(start, onward, *earlier):
         at_step = {0: start}
-        for step in range(2, n_ctx, 4):
-            at_step[step] = exchange(at_step[step - 2], "ctx", 2)
-            if step + 2 < n_ctx:
+        for step in range(4, n_ctx, 4):
+            at_step[step] = exchange(start, "ctx", step)
+        at_step[2] = exchange(start, "ctx", 2)
+        for step in range(4, n_ctx, 4):
+            if onward:
+                forwarded = after(at_step[step], at_step[2], *earlier)
+                at_step[step + 2] = exchange(forwarded, "ctx", 2)
+            else:
                 at_step[step + 2] = exchange(start, "ctx", step + 2)
-        return [at_step[partner] for partner in partners], at_step[n_ctx - 2]
+        return [at_step[partner] for partner in partners], at_step[n_ctx - 4]
 
     def joined(pieces):
         return stack(pieces, (tuple((index, 0) for index in range(len(pieces))),), part_cols)[0]
 
-    near_pieces, last = over_chips(chip_rows[0])
+    near_pieces, last = over_chips(chip_rows[0], True, *sibling)
+    far_pieces, _ = over_chips(after(chip_rows[1], last), False)
     weights = {0: joined(near_pieces)}
-    weights[far] = joined(over_chips(after(chip_rows[1], last))[0])
     for t in range(1, far):
         weights[t] = exchange(weights[0], "dp", t)
-    queries, rope_queries, out_grads = q_nope[0], q_rope[0], grad_out[0]
-
-    packed = exchange(
-        pack_columns(place, (queries, rope_queries, out_grads), n_dp), "ctx", 1
-    )
-    totals = log_total[0].reshape(n_dp, 2, pairs, 2, group_len)
-    tot_sib = exchange(lax.dynamic_index_in_dim(totals, 1 - core, 1, keepdims=False), "ctx", 1)
-    totals = (
-        totals.reshape(n_dp * 2 * pairs, 2, group_len),
-        tot_sib.reshape(n_dp * pairs, 2, group_len),
-    )
+    log_total = after(log_total, last)[0]
+    sibling.append(exchange(log_total, "ctx", 1))
+    own.append(log_total)
+    for arrays in (own, sibling):
+        arrays[3] = arrays[3].reshape(heads // 2, 2, group_len)
 
     offer_plan = offered[0]
     span = group_len + 16
@@ -576,93 +543,92 @@
             kinds = jnp.where(picked, 2.0, jnp.where(same, 1.0, 0.0)).reshape(1, -1)
     plan = jnp.concatenate([ctx[None], *starts, *usables]).astype(jnp.int32)
     kinds = jnp.pad(kinds.astype(jnp.bfloat16), ((0, 15), (0, LAT + ROPE - kinds.shape[1])))
-    bundle = jnp.concatenate([kv_latent[0], kinds], axis=0)
+    bundle = after(jnp.concatenate([kv_latent[0], kinds], axis=0), *sibling[:3])
     bundles = [bundle, from_behind(bundle, "ctx", 2), from_behind(bundle, "ctx", 4)]
     own_bundles = stack(bundles, (((0, 0), (1, 0), (2, 0)),), LAT + ROPE)[0]
     sib_bundles = exchange(own_bundles, "ctx", 1)
     shared = collect(plan, own_bundles, sib_bundles, tuple(blocks), lat_block)
 
     earlier = None
-    weight_grads, latents, ropes, far_arrived = {}, [], [], []
+    latents, ropes = [], []
+    weight_grads = {t: ([], []) for t in range(n_dp)}
     bits = [1 << b for b in range(n_dp.bit_length() - 1)]
     orders = (bits, bits[::-1])
-    order = [0, far] + list(range(1, far))
-    for t in order:
-        weight_grads[t] = ([], [])
-        half_pairs = pairs // 2
-        units = [(0, pairs)] if t != order[-1] else [(0, half_pairs), (half_pairs, half_pairs)]
-        for unit in units:
-            weight = weights[t]
-            if unit[0]:
-                weight = after(weight, *[arrived for arrived, in far_arrived])
-            rest = chunk_backward(
-                place,
-                t,
-                unit,
-                (queries, rope_queries, out_grads),
-                packed,
-                totals,
-                weight,
-                shared,
-                earlier,
-                (n_dp, pairs),
-            )
-            earlier = rest[:3]
-            for side in range(2):
-                weight_grads[t][side].append(rest[3 + side])
-            latents.append(rest[5])
-            ropes.append(rest[6])
-        if t == far:
-            far_arrived = [
-                [exchange(weight_grads[t][side][0], "dp", orders[side][0])] for side in range(2)
-            ]
+    first_sums = [{t: [] for t in range(n_dp) if t & order[0]} for order in orders]
+    units = [(0, 0), (0, 1)]
+    units += [(t, half) for half in range(2) for t in [far] + list(range(1, far))]
+    for t, half in units:
+        if (t, half) == (far, 0):
+            weights[far] = joined([after(far_pieces[0], latents[-1])] + far_pieces[1:])
+        weight = weights[t]
+        if (t, half) == (far, 1):
+            weight = after(weight, *[sent[far][0] for sent in first_sums])
+        if (t, half) == (far - 1, 1):
+            weight = after(weight, *[sent[u][0] for sent in first_sums for u in sent if u != far])
+        rest = chunk_backward(
+            place,
+            t,
+            (half * pairs // 2, pairs // 2),
+            own,
+            sibling,
+            weight,
+            shared,
+            earlier,
+            (n_dp, pairs),
+        )
+        earlier = rest[:3]
+        for side, sent in enumerate(first_sums):
+            grad = rest[3 + side]
+            weight_grads[t][side].append(grad)
+            if t in sent:
+                leaving = after(grad, sent[t][0]) if half else grad
+                sent[t].append(exchange(leaving, "dp", orders[side][0]))
+        latents.append(rest[5])
+        ropes.append(rest[6])
+
+    def total(addends, half):
+        return functools.reduce(
+            lambda left, right: left + right, [pieces[half] for pieces in addends]
+        )
+
+    sums = []
+    for side, order in enumerate(orders):
+        addends = {t: [weight_grads[t][side]] for t in weight_grads}
+        arrived = {t ^ order[0]: pieces for t, pieces in first_sums[side].items()}
+        addends = {t: addends[t] + [more] for t, more in arrived.items()}
+        for bit in order[1:]:
+            arrived = {}
+            for t in sorted((t for t in addends if t & bit), reverse=True):
+                behind = first_sums[1 - side].get(bit, first_sums[side][order[0]])
+                arrived[t ^ bit] = [
+                    exchange(after(total(addends[t], half), behind[half]), "dp", bit)
+                    for half in range(2)
+                ]
+            addends = {t: addends[t] + [more] for t, more in arrived.items()}
+        sums.append(addends[0])
 
     q_full, rope_full, sib_grads = earlier
     received = exchange(sib_grads, "ctx", 1)
     grad_nope, grad_rope = place_columns(place, received, q_full, rope_full, n_dp)
 
+    latents[-1] = after(latents[-1], *[sent[far][1] for sent in first_sums])
     own_grads, sib_grads = spread(plan, latents, ropes, 3 * span, tuple(blocks), lat_block)
-    grad_rows = own_grads + exchange(sib_grads, "ctx", 1)
+    swapped = exchange(sib_grads, "ctx", 1)
+    grad_rows = own_grads + swapped
     by_chip = [grad_rows[at * span : at * span + group_len] for at in range(3)]
     grad_rows = by_chip[0]
     for chips in (1, 2):
         grad_rows = grad_rows + from_behind(by_chip[chips], "ctx", -2 * chips)
 
-    half_cols = part_cols // 2
-
-    def columns(pieces, half):
-        if len(pieces) == 2:
-            return pieces[half]
-        return pieces[0][:, half * half_cols : (half + 1) * half_cols]
-
-    def total(addends, half):
-        return functools.reduce(
-            lambda left, right: left + right, [columns(pieces, half) for pieces in addends]
-        )
-
-    sums = []
-    for side, order in enumerate(orders):
-        addends = {t: [weight_grads[t][side]] for t in weight_grads}
-        for bit in order:
-            arrived = {}
-            for t in sorted((t for t in addends if t & bit), reverse=True):
-                if t == far and bit == order[0]:
-                    arrived[t ^ bit] = far_arrived[side]
-                    continue
-                pieces = addends[t][0]
-                if len(addends[t]) > 1:
-                    pieces = [total(addends[t], half) for half in range(2)]
-                if bit == order[-1]:
-                    pieces = [after(piece, *addends[0][-1]) for piece in pieces]
-                arrived[t ^ bit] = [exchange(piece, "dp", bit) for piece in pieces]
-            addends = {t: addends[t] + [more] for t, more in arrived.items()}
-        sums.append([total(addends[0], half) for half in range(2)])
-
     ctx_bits = [1 << b for b in range(1, n_ctx.bit_length() - 1)]
-    finished = []
+    finished, arrived = [], None
     for half in range(2):
-        leaving = after(sums[1][half], (grad_rows, grad_nope)[half])
-        rows = sums[0][half] + exchange(leaving, "ctx", ctx_bits[0])
+        if half:
+            sums = [[[after(piece, arrived) for piece in pieces] for pieces in side] for side in sums]
+        first, second = [total(side, half) for side in sums]
+        second = after(second, *((grad_rows, grad_nope) if half else (received, swapped)))
+        arrived = exchange(second, "ctx", ctx_bits[0])
+        rows = first + arrived
         for bit in ctx_bits[1:]:
             rows = halve(rows, "ctx", bit)
         piece = join_cores(place, rows[:lat_block], exchange(rows[lat_block:], "ctx", 1))

time: 274 us -> 258 us (0.942)
  waiting for transfers between devices: 123 us -> 101 us
  Pallas kernels: 71.8 us -> 78.2 us
  starting transfers between devices: 52.3 us -> 47.2 us
  other arithmetic: 8.33 us -> 12 us
    ppermute x35 -> x40, waiting for transfers between devices: 104 us -> 84.3 us  [exchange(): lax.ppermute(value, axis, [(source, source ^ bits) for source in range(co...]
    pallas_call x5 -> x8, Pallas kernels: 51.5 us -> 59.9 us  [chunk_backward(): pl.pallas_call(functools.partial(heads_kernel, earlier=len(aliases)), gri...]
    ppermute x35 -> x40, starting transfers between devices: 44 us -> 36.7 us  [exchange(): lax.ppermute(value, axis, [(source, source ^ bits) for source in range(co...]
    unnamed x59 -> x83, local copies, waits for them, and re-layouts: 11.1 us -> 9.03 us
    add x3 -> x6, other arithmetic: 4.62 us -> 6.49 us  [total(): left + right]
  transfers between devices with their start and end apart: 39 -> 44, of which waited for: 25 -> 20; matrix products, arithmetic and copies ran while one was open for 5% -> 7% of each run, Pallas kernels for 22% -> 25%
where the time goes in v3:
time: 258 us; the launch traced here: 257 us
  waiting for transfers between devices  101 us (39%)
  Pallas kernels  78.2 us (30%)
  starting transfers between devices  47.2 us (18%)
  local copies, waits for them, and re-layouts  17 us (7%)
  other arithmetic  12 us (5%)
    ppermute x40, waiting for transfers between devices, exchange(): lax.ppermute(value, axis, [(source, source ^ bits) for source in range(co...  84.3 us
    pallas_call x8, Pallas kernels, chunk_backward(): pl.pallas_call(functools.partial(heads_kernel, earlier=len(aliases)), gri...  59.9 us
    ppermute x40, starting transfers between devices, exchange(): lax.ppermute(value, axis, [(source, source ^ bits) for source in range(co...  36.7 us
    ppermute x4, waiting for transfers between devices, from_behind(): lax.ppermute(value, axis, [(source, source + steps) for source in range(i...  16.8 us
    ppermute x4, starting transfers between devices, from_behind(): lax.ppermute(value, axis, [(source, source + steps) for source in range(i...  10.5 us
    unnamed x83, local copies, waits for them, and re-layouts  9.03 us
    add x6, other arithmetic, total(): left + right  6.49 us
  transfers between devices with their start and end apart: 44, of which 20 were waited for; matrix products, arithmetic and copies ran while one was open for 7% of the time, Pallas kernels for 25%

profile of v3, /device:TPU:0, one launch (start us, length us, event | category | flops | bytes accessed | tf_op | source)
XLA Modules:
  0.0 256.7 jit_solution(10252805613481741185)
XLA Ops:
  1.2 2.5 weight_parts.2
  6.6 2.5 weight_parts.3
  9.2 2.7 %collective-permute-start.6 = (bf16[64,2048]{1,0:T(8,128)(2,1)}, bf16[64,2048]{1,0:T(8,128)(2,1)S(1)}, u32[]{:S(2)}, u32[]{:S(2)}) collective-permute-start(bf16[64,2048]{1,0:T(8,128)(2,1)} %get-tuple-element.109.refs_0_), channel_id=1, source_target_pairs={{0,2},{1,3},{2,0},{3,1},{4,6},{5,7},{6,4},{7,5},{8,10},{9,11},{10,... | collective-permute-start | bytes 786440 | tf_op jit(solution)/shard_map/ppermute | solution.py:30
  11.9 2.6 %collective-permute-start.1 = (bf16[64,2048]{1,0:T(8,128)(2,1)}, bf16[64,2048]{1,0:T(8,128)(2,1)}, u32[]{:S(2)}, u32[]{:S(2)}) collective-permute-start(bf16[64,2048]{1,0:T(8,128)(2,1)} %get-tuple-element.109.refs_0_), channel_id=1, source_target_pairs={{0,4},{1,5},{2,6},{3,7},{4,0},{5,1},{6,2},{7,3},{8,12},{9,13},{10,... | collective-permute-start | bytes 786440 | tf_op jit(solution)/shard_map/ppermute | solution.py:30
  15.8 8.6 %collective-permute-done.6.refs_2_ = bf16[64,2048]{1,0:T(8,128)(2,1)S(1)} collective-permute-done((bf16[64,2048]{1,0:T(8,128)(2,1)}, bf16[64,2048]{1,0:T(8,128)(2,1)S(1)}, u32[]{:S(2)}, u32[]{:S(2)}) %collective-permute-start.6) | collective-permute-done | bytes 262176 | tf_op jit(solution)/shard_map/ppermute | solution.py:30
  24.4 2.7 %collective-permute-done.1.refs_1_ = bf16[64,2048]{1,0:T(8,128)(2,1)} collective-permute-done((bf16[64,2048]{1,0:T(8,128)(2,1)}, bf16[64,2048]{1,0:T(8,128)(2,1)}, u32[]{:S(2)}, u32[]{:S(2)}) %collective-permute-start.1) | collective-permute-done | bytes 262176 | tf_op jit(solution)/shard_map/ppermute | solution.py:30
  30.0 4.9 %collective-permute-done.7.refs_3_ = bf16[64,2048]{1,0:T(8,128)(2,1)} collective-permute-done((bf16[64,2048]{1,0:T(8,128)(2,1)}, bf16[64,2048]{1,0:T(8,128)(2,1)}, u32[]{:S(2)}, u32[]{:S(2)}) %collective-permute-start.7) | collective-permute-done | bytes 262176 | tf_op jit(solution)/shard_map/ppermute | solution.py:30
  35.8 2.1 stack.74.weight
  39.4 1.5 collective-permute-start.8
  40.9 4.2 %collective-permute-start.11 = (bf16[144,320]{1,0:T(8,128)(2,1)S(1)}, bf16[144,320]{1,0:T(8,128)(2,1)S(1)}, u32[]{:S(2)}, u32[]{:S(2)}) collective-permute-start(bf16[144,320]{1,0:T(8,128)(2,1)S(1)} %fusion.2.refs_0_), channel_id=1, source_target_pairs={{0,4},{1,5},{2,6},{3,7},{8,12},{9,13},{10,14},{11,15},{16,20},{17,... | collective-permute-start | bytes 276488 | tf_op jit(solution)/shard_map/ppermute | solution.py:25
  45.2 3.7 %collective-permute-start.10 = (bf16[144,320]{1,0:T(8,128)(2,1)S(1)}, bf16[144,320]{1,0:T(8,128)(2,1)S(1)}, u32[]{:S(2)}, u32[]{:S(2)}) collective-permute-start(bf16[144,320]{1,0:T(8,128)(2,1)S(1)} %fusion.2.refs_0_), channel_id=1, source_target_pairs={{0,2},{1,3},{2,4},{3,5},{4,6},{5,7},{8,10},{9,11},{10,12},{11,13},... | collective-permute-start | bytes 276488 | tf_op jit(solution)/shard_map/ppermute | solution.py:25
  49.4 1.7 collective-permute-done.10.refs_1_
  53.0 2.4 collective-permute-start.15
  59.5 2.0 collect.1
  61.5 1.6 copy-done.3
  64.3 7.4 %heads_backward.8 = (bf16[128,8192]{1,0:T(8,128)(2,1)}, bf16[128,4096]{1,0:T(8,128)(2,1)}, bf16[128,6144]{1,0:T(8,128)(2,1)}, f32[128,1024]{1,0:T(8,128)S(1)}, f...) custom-call(s32[5]{0:T(128)S(1)} %copy-done.25, bf16[128,8192]{1,0:T(8,128)(2,1)S(1)} %bitcast.46, ...), custom_call_target="tpu_custom_call" | custom-call | flops 200000000 | bytes 600000 | tf_op jit(solution)/shard_map/heads_backward/pallas_call | solution.py:157
  73.4 7.4 %heads_backward.9 = (bf16[128,8192]{1,0:T(8,128)(2,1)}, bf16[128,4096]{1,0:T(8,128)(2,1)}, bf16[128,6144]{1,0:T(8,128)(2,1)}, f32[128,1024]{1,0:T(8,128)S(1)}, f...) custom-call(s32[5]{0:T(128)S(1)} %copy-done.25, ...), custom_call_target="tpu_custom_call", output_to_operand_aliasing={{0}: (14, {}), {1}: (15, {}), {2}: (16, {})} | custom-call | flops 200000000 | bytes 600000 | tf_op jit(solution)/shard_map/heads_backward/pallas_call | solution.py:157
  80.9 1.5 stack.76.weight
  82.4 7.5 %heads_backward.10 = (bf16[128,8192]{1,0:T(8,128)(2,1)}, bf16[128,4096]{1,0:T(8,128)(2,1)}, bf16[128,6144]{1,0:T(8,128)(2,1)}, f32[128,1024]{1,0:T(8,128)S(1)}, ...) custom-call(s32[5]{0:T(128)S(1)} %copy-done.25, ...), custom_call_target="tpu_custom_call", output_to_operand_aliasing={{0}: (14, {}), {1}: (15, {}), {2}: (16, {})} | custom-call | flops 200000000 | bytes 600000 | tf_op jit(solution)/shard_map/heads_backward/pallas_call | solution.py:157
  91.0 7.4 %heads_backward.11 = (bf16[128,8192]{1,0:T(8,128)(2,1)}, bf16[128,4096]{1,0:T(8,128)(2,1)}, bf16[128,6144]{1,0:T(8,128)(2,1)}, f32[128,1024]{1,0:T(8,128)S(1)}, ...) custom-call(s32[5]{0:T(128)S(1)} %copy-done.25, ...), custom_call_target="tpu_custom_call", output_to_operand_aliasing={{0}: (14, {}), {1}: (15, {}), {2}: (16, {})} | custom-call | flops 200000000 | bytes 600000 | tf_op jit(solution)/shard_map/heads_backward/pallas_call | solution.py:157
  100.0 7.6 %heads_backward.12 = (bf16[128,8192]{1,0:T(8,128)(2,1)}, bf16[128,4096]{1,0:T(8,128)(2,1)}, bf16[128,6144]{1,0:T(8,128)(2,1)}, f32[128,1024]{1,0:T(8,128)S(1)}, ...) custom-call(s32[5]{0:T(128)S(1)} %copy-done.25, ...), custom_call_target="tpu_custom_call", output_to_operand_aliasing={{0}: (14, {}), {1}: (15, {}), {2}: (16, {})} | custom-call | flops 200000000 | bytes 600000 | tf_op jit(solution)/shard_map/heads_backward/pallas_call | solution.py:157
  108.4 1.5 collective-permute-start.17
  110.8 7.3 %heads_backward.13 = (bf16[128,8192]{1,0:T(8,128)(2,1)}, bf16[128,4096]{1,0:T(8,128)(2,1)}, bf16[128,6144]{1,0:T(8,128)(2,1)}, f32[128,1024]{1,0:T(8,128)S(1)}, ...) custom-call(s32[5]{0:T(128)S(1)} %copy-done.25, ...), custom_call_target="tpu_custom_call", output_to_operand_aliasing={{0}: (14, {}), {1}: (15, {}), {2}: (16, {})} | custom-call | flops 200000000 | bytes 600000 | tf_op jit(solution)/shard_map/heads_backward/pallas_call | solution.py:157
  118.1 7.7 %heads_backward.14 = (bf16[128,8192]{1,0:T(8,128)(2,1)}, bf16[128,4096]{1,0:T(8,128)(2,1)}, bf16[128,6144]{1,0:T(8,128)(2,1)}, f32[128,1024]{1,0:T(8,128)}, f32[...) custom-call(s32[5]{0:T(128)S(1)} %copy-done.25, ...), custom_call_target="tpu_custom_call", output_to_operand_aliasing={{0}: (14, {}), {1}: (15, {}), {2}: (16, {})} | custom-call | flops 200000000 | bytes 600000 | tf_op jit(solution)/shard_map/heads_backward/pallas_call | solution.py:157
  125.8 7.5 %heads_backward.15 = (bf16[128,8192]{1,0:T(8,128)(2,1)}, bf16[128,4096]{1,0:T(8,128)(2,1)}, bf16[128,6144]{1,0:T(8,128)(2,1)}, f32[128,1024]{1,0:T(8,128)S(1)}, ...) custom-call(s32[5]{0:T(128)S(1)} %copy-done.25, ...), custom_call_target="tpu_custom_call", output_to_operand_aliasing={{0}: (14, {}), {1}: (15, {}), {2}: (16, {})} | custom-call | flops 200000000 | bytes 600000 | tf_op jit(solution)/shard_map/heads_backward/pallas_call | solution.py:157
  137.4 10.4 %collective-permute-done.22 = f32[128,1024]{1,0:T(8,128)S(1)} collective-permute-done((f32[128,1024]{1,0:T(8,128)S(1)}, f32[128,1024]{1,0:T(8,128)S(1)}, u32[]{:S(2)}, u32[]{:S(2)}) %collective-permute-start.22) | collective-permute-done | bytes 524320 | tf_op jit(solution)/shard_map/ppermute | solution.py:30
  148.7 1.7 spread.1
  151.5 1.5 collective-permute-start.32
  153.1 1.9 add.135
  155.0 5.1 %collective-permute-done.31 = f32[128,1024]{1,0:T(8,128)} collective-permute-done((f32[128,1024]{1,0:T(8,128)}, f32[128,1024]{1,0:T(8,128)}, u32[]{:S(2)}, u32[]{:S(2)}) %collective-permute-start.31) | collective-permute-done | bytes 524320 | tf_op jit(solution)/shard_map/ppermute | solution.py:30
  160.6 10.7 %collective-permute-done.27 = f32[128,1024]{1,0:T(8,128)} collective-permute-done((f32[128,1024]{1,0:T(8,128)}, f32[128,1024]{1,0:T(8,128)}, u32[]{:S(2)}, u32[]{:S(2)}) %collective-permute-start.27) | collective-permute-done | bytes 524320 | tf_op jit(solution)/shard_map/ppermute | solution.py:30
  171.3 2.2 add_add_fusion.2
  173.5 2.3 copy.46
  177.1 1.6 collective-permute-start.28
  181.4 1.6 collective-permute-start.26
  183.1 15.1 %collective-permute-done.24 = f32[128,320]{1,0:T(8,128)S(1)} collective-permute-done((f32[128,320]{1,0:T(8,128)S(1)}, f32[128,320]{1,0:T(8,128)S(1)}, u32[]{:S(2)}, u32[]{:S(2)}) %collective-permute-start.24) | collective-permute-done | bytes 163872 | tf_op jit(solution)/shard_map/ppermute | solution.py:25
  198.2 1.5 collective-permute-start.33
  199.7 2.4 place_columns.1
  204.2 5.5 %collective-permute-done.33 = f32[128,1024]{1,0:T(8,128)S(1)} collective-permute-done((f32[128,1024]{1,0:T(8,128)S(1)}, f32[128,1024]{1,0:T(8,128)S(1)}, u32[]{:S(2)}, u32[]{:S(2)}) %collective-permute-start.33) | collective-permute-done | bytes 524320 | tf_op jit(solution)/shard_map/ppermute | solution.py:30
  209.6 8.6 %collective-permute-done.29 = f32[64,1024]{1,0:T(8,128)S(1)} collective-permute-done((f32[64,1024]{1,0:T(8,128)S(1)}, f32[64,1024]{1,0:T(8,128)S(1)}, u32[]{:S(2)}, u32[]{:S(2)}) %collective-permute-start.29) | collective-permute-done | bytes 262176 | tf_op jit(solution)/shard_map/ppermute | solution.py:30
  218.3 2.2 collective-permute-done.35
  225.0 1.5 collective-permute-start.42
  226.5 7.7 %collective-permute-done.36 = f32[64,1024]{1,0:T(8,128)S(1)} collective-permute-done((f32[64,1024]{1,0:T(8,128)S(1)}, f32[64,1024]{1,0:T(8,128)S(1)}, u32[]{:S(2)}, u32[]{:S(2)}) %collective-permute-start.36) | collective-permute-done | bytes 262176 | tf_op jit(solution)/shard_map/ppermute | solution.py:30
  236.2 2.3 collective-permute-start.43
  240.6 3.0 %collective-permute-done.40.refs_4_ = f32[32,2048]{1,0:T(8,128)S(1)} collective-permute-done((f32[32,2048]{1,0:T(8,128)S(1)}, f32[32,2048]{1,0:T(8,128)S(1)}, u32[]{:S(2)}, u32[]{:S(2)}) %collective-permute-start.40) | collective-permute-done | bytes 262176 | tf_op jit(solution)/shard_map/ppermute | solution.py:30
  243.6 7.1 %collective-permute-done.43.refs_7_ = f32[32,2048]{1,0:T(8,128)S(1)} collective-permute-done((f32[32,2048]{1,0:T(8,128)S(1)}, f32[32,2048]{1,0:T(8,128)S(1)}, u32[]{:S(2)}, u32[]{:S(2)}) %collective-permute-start.43) | collective-permute-done | bytes 262176 | tf_op jit(solution)/shard_map/ppermute | solution.py:30
  250.6 3.6 %collective-permute-done.41.refs_5_ = f32[32,2048]{1,0:T(8,128)S(1)} collective-permute-done((f32[32,2048]{1,0:T(8,128)S(1)}, f32[32,2048]{1,0:T(8,128)S(1)}, u32[]{:S(2)}, u32[]{:S(2)}) %collective-permute-start.41) | collective-permute-done | bytes 262176 | tf_op jit(solution)/shard_map/ppermute | solution.py:30
  254.3 2.4 lay_out.1
  (182 shorter events, 45.2 us)
Async XLA Ops:
  1.2 27.3 %copy-start.40 = (s32[1,2,3]{2,1,0:T(2,128)S(1)}, s32[1,2,3]{2,1,0:T(2,128)}, u32[]{:S(2)}) copy-start(s32[1,2,3]{2,1,0:T(2,128)} %param.14) | copy-start | bytes 76
  3.7 1.8 collective-permute-start
  5.6 22.6 %collective-permute-start.2 = (bf16[128,8192]{1,0:T(8,128)(2,1)S(1)}, bf16[128,8192]{1,0:T(8,128)(2,1)}, u32[]{:S(2)}, u32[]{:S(2)}) collective-permute-start(bf16[128,8192]{1,0:T(8,128)(2,1)S(1)} %bitcast.45), channel_id=1, source_target_pairs={{0,1},{1,0},{2,3},{3,2},{4,5},{5,4},{6,7},{7,6},{8,9},{9,8},{10,11... | collective-permute-start | bytes 6291464 | tf_op jit(solution)/shard_map/ppermute | solution.py:30
  5.9 22.2 %collective-permute-start.4 = (bf16[128,8192]{1,0:T(8,128)(2,1)}, bf16[128,8192]{1,0:T(8,128)(2,1)}, u32[]{:S(2)}, u32[]{:S(2)}) collective-permute-start(bf16[128,8192]{1,0:T(8,128)(2,1)} %bitcast.54), channel_id=1, source_target_pairs={{0,1},{1,0},{2,3},{3,2},{4,5},{5,4},{6,7},{7,6},{8,9},{9,8},{10,11... | collective-permute-start | bytes 6291464 | tf_op jit(solution)/shard_map/ppermute | solution.py:30
  6.1 21.0 %collective-permute-start.3 = (bf16[128,4096]{1,0:T(8,128)(2,1)}, bf16[128,4096]{1,0:T(8,128)(2,1)S(1)}, u32[]{:S(2)}, u32[]{:S(2)}) collective-permute-start(bf16[128,4096]{1,0:T(8,128)(2,1)} %bitcast.63), channel_id=1, source_target_pairs={{0,1},{1,0},{2,3},{3,2},{4,5},{5,4},{6,7},{7,6},{8,9},{9,8},{10,11... | collective-permute-start | bytes 3145736 | tf_op jit(solution)/shard_map/ppermute | solution.py:30
  9.2 42.1 %copy-start.9 = (f32[1,64,128]{2,1,0:T(8,128)S(1)}, f32[1,64,128]{2,1,0:T(8,128)}, u32[]{:S(2)}) copy-start(f32[1,64,128]{2,1,0:T(8,128)} %param.11) | copy-start | bytes 98308
  9.2 15.2 %collective-permute-start.6 = (bf16[64,2048]{1,0:T(8,128)(2,1)}, bf16[64,2048]{1,0:T(8,128)(2,1)S(1)}, u32[]{:S(2)}, u32[]{:S(2)}) collective-permute-start(bf16[64,2048]{1,0:T(8,128)(2,1)} %get-tuple-element.109.refs_0_), channel_id=1, source_target_pairs={{0,2},{1,3},{2,0},{3,1},{4,6},{5,7},{6,4},{7,5},{8,10},{9,11},{10,... | collective-permute-start | bytes 786440 | tf_op jit(solution)/shard_map/ppermute | solution.py:30
  11.9 15.2 %collective-permute-start.1 = (bf16[64,2048]{1,0:T(8,128)(2,1)}, bf16[64,2048]{1,0:T(8,128)(2,1)}, u32[]{:S(2)}, u32[]{:S(2)}) collective-permute-start(bf16[64,2048]{1,0:T(8,128)(2,1)} %get-tuple-element.109.refs_0_), channel_id=1, source_target_pairs={{0,4},{1,5},{2,6},{3,7},{4,0},{5,1},{6,2},{7,3},{8,12},{9,13},{10,... | collective-permute-start | bytes 786440 | tf_op jit(solution)/shard_map/ppermute | solution.py:30
  14.6 36.7 %copy-start.38 = (s32[6]{0:T(128)}, s32[6]{0:T(128)S(1)}, u32[]{:S(2)}) copy-start(s32[6]{0:T(128)S(1)} %stack.73) | copy-start | bytes 76
  28.1 6.7 %collective-permute-start.7 = (bf16[64,2048]{1,0:T(8,128)(2,1)}, bf16[64,2048]{1,0:T(8,128)(2,1)}, u32[]{:S(2)}, u32[]{:S(2)}) collective-permute-start(bf16[64,2048]{1,0:T(8,128)(2,1)} %collective-permute-done.1.refs_1_), channel_id=1, source_target_pairs={{0,2},{1,3},{2,0},{3,1},{4,6},{5,7},{6,4},{7,5},{8,10},{9,11},{10,... | collective-permute-start | bytes 786440 | tf_op jit(solution)/shard_map/ppermute | solution.py:30
  29.9 31.6 %copy-start.5 = (bf16[1,128,4096]{2,1,0:T(8,128)(2,1)S(1)}, bf16[1,128,4096]{2,1,0:T(8,128)(2,1)}, u32[]{:S(2)}) copy-start(bf16[1,128,4096]{2,1,0:T(8,128)(2,1)} %param.9) | copy-start | bytes 3145732
  37.9 53.1 %collective-permute-start.9 = (bf16[256,2048]{1,0:T(8,128)(2,1)}, bf16[256,2048]{1,0:T(8,128)(2,1)}, u32[]{:S(2)}, u32[]{:S(2)}) collective-permute-start(bf16[256,2048]{1,0:T(8,128)(2,1)} %stack.74.weight), channel_id=1, source_target_pairs={{0,8},{8,0},{16,24},{24,16},{1,9},{9,1},{17,25},{25,17},{2,10},{10... | collective-permute-start | bytes 3145736 | tf_op jit(solution)/shard_map/ppermute | solution.py:30
  39.4 60.6 %collective-permute-start.8 = (bf16[256,2048]{1,0:T(8,128)(2,1)}, bf16[256,2048]{1,0:T(8,128)(2,1)}, u32[]{:S(2)}, u32[]{:S(2)}) collective-permute-start(bf16[256,2048]{1,0:T(8,128)(2,1)} %stack.74.weight), channel_id=1, source_target_pairs={{0,16},{8,24},{16,0},{24,8},{1,17},{9,25},{17,1},{25,9},{2,18},{10... | collective-permute-start | bytes 3145736 | tf_op jit(solution)/shard_map/ppermute | solution.py:30
  40.9 8.5 %collective-permute-start.11 = (bf16[144,320]{1,0:T(8,128)(2,1)S(1)}, bf16[144,320]{1,0:T(8,128)(2,1)S(1)}, u32[]{:S(2)}, u32[]{:S(2)}) collective-permute-start(bf16[144,320]{1,0:T(8,128)(2,1)S(1)} %fusion.2.refs_0_), channel_id=1, source_target_pairs={{0,4},{1,5},{2,6},{3,7},{8,12},{9,13},{10,14},{11,15},{16,20},{17,... | collective-permute-start | bytes 276488 | tf_op jit(solution)/shard_map/ppermute | solution.py:25
  45.2 6.0 %collective-permute-start.10 = (bf16[144,320]{1,0:T(8,128)(2,1)S(1)}, bf16[144,320]{1,0:T(8,128)(2,1)S(1)}, u32[]{:S(2)}, u32[]{:S(2)}) collective-permute-start(bf16[144,320]{1,0:T(8,128)(2,1)S(1)} %fusion.2.refs_0_), channel_id=1, source_target_pairs={{0,2},{1,3},{2,4},{3,5},{4,6},{5,7},{8,10},{9,11},{10,12},{11,13},... | collective-permute-start | bytes 276488 | tf_op jit(solution)/shard_map/ppermute | solution.py:25
  51.2 5.1 %collective-permute-start.12 = (bf16[432,320]{1,0:T(8,128)(2,1)S(1)}, bf16[432,320]{1,0:T(8,128)(2,1)}, u32[]{:S(2)}, u32[]{:S(2)}) collective-permute-start(bf16[432,320]{1,0:T(8,128)(2,1)S(1)} %stack.75.own), channel_id=1, source_target_pairs={{0,1},{1,0},{2,3},{3,2},{4,5},{5,4},{6,7},{7,6},{8,9},{9,8},{10,11... | collective-permute-start | bytes 829448 | tf_op jit(solution)/shard_map/ppermute | solution.py:30
  51.3 4.2 %collective-permute-start.5 = (f32[64,128]{1,0:T(8,128)S(1)}, f32[64,128]{1,0:T(8,128)S(1)}, u32[]{:S(2)}, u32[]{:S(2)}) collective-permute-start(f32[64,128]{1,0:T(8,128)S(1)} %bitcast.72), channel_id=1, source_target_pairs={{0,1},{1,0},{2,3},{3,2},{4,5},{5,4},{6,7},{7,6},{8,9},{9,8},{10,11... | collective-permute-start | bytes 98312 | tf_op jit(solution)/shard_map/ppermute | solution.py:30
  53.0 27.8 %collective-permute-start.15 = (bf16[64,2048]{1,0:T(8,128)(2,1)}, bf16[64,2048]{1,0:T(8,128)(2,1)}, u32[]{:S(2)}, u32[]{:S(2)}) collective-permute-start(bf16[64,2048]{1,0:T(8,128)(2,1)} %get-tuple-element.126.refs_0_), channel_id=1, source_target_pairs={{0,6},{1,7},{2,4},{3,5},{4,2},{5,3},{6,0},{7,1},{8,14},{9,15},{10,... | collective-permute-start | bytes 786440 | tf_op jit(solution)/shard_map/ppermute | solution.py:30
  55.5 25.4 %collective-permute-start.14 = (bf16[64,2048]{1,0:T(8,128)(2,1)}, bf16[64,2048]{1,0:T(8,128)(2,1)}, u32[]{:S(2)}, u32[]{:S(2)}) collective-permute-start(bf16[64,2048]{1,0:T(8,128)(2,1)} %get-tuple-element.126.refs_0_), channel_id=1, source_target_pairs={{0,2},{1,3},{2,0},{3,1},{4,6},{5,7},{6,4},{7,5},{8,10},{9,11},{10,... | collective-permute-start | bytes 786440 | tf_op jit(solution)/shard_map/ppermute | solution.py:30
  56.3 24.6 %collective-permute-start.13 = (bf16[64,2048]{1,0:T(8,128)(2,1)}, bf16[64,2048]{1,0:T(8,128)(2,1)}, u32[]{:S(2)}, u32[]{:S(2)}) collective-permute-start(bf16[64,2048]{1,0:T(8,128)(2,1)} %get-tuple-element.126.refs_0_), channel_id=1, source_target_pairs={{0,4},{1,5},{2,6},{3,7},{4,0},{5,1},{6,2},{7,3},{8,12},{9,13},{10,... | collective-permute-start | bytes 786440 | tf_op jit(solution)/shard_map/ppermute | solution.py:30
  90.0 20.0 %collective-permute-start.18 = (f32[128,1024]{1,0:T(8,128)S(1)}, f32[128,1024]{1,0:T(8,128)S(1)}, u32[]{:S(2)}, u32[]{:S(2)}) collective-permute-start(f32[128,1024]{1,0:T(8,128)S(1)} %get-tuple-element.139), channel_id=1, source_target_pairs={{0,8},{8,0},{16,24},{24,16},{1,9},{9,1},{17,25},{25,17},{2,10},{10... | collective-permute-start | bytes 1572872 | tf_op jit(solution)/shard_map/ppermute | solution.py:30
  90.5 19.4 %collective-permute-start.19 = (f32[128,1024]{1,0:T(8,128)S(1)}, f32[128,1024]{1,0:T(8,128)S(1)}, u32[]{:S(2)}, u32[]{:S(2)}) collective-permute-start(f32[128,1024]{1,0:T(8,128)S(1)} %get-tuple-element.140), channel_id=1, source_target_pairs={{0,16},{8,24},{16,0},{24,8},{1,17},{9,25},{17,1},{25,9},{2,18},{10... | collective-permute-start | bytes 1572872 | tf_op jit(solution)/shard_map/ppermute | solution.py:30
  98.5 27.3 %collective-permute-start.16 = (f32[128,1024]{1,0:T(8,128)S(1)}, f32[128,1024]{1,0:T(8,128)S(1)}, u32[]{:S(2)}, u32[]{:S(2)}) collective-permute-start(f32[128,1024]{1,0:T(8,128)S(1)} %get-tuple-element.133), channel_id=1, source_target_pairs={{0,8},{8,0},{16,24},{24,16},{1,9},{9,1},{17,25},{25,17},{2,10},{10... | collective-permute-start | bytes 1572872 | tf_op jit(solution)/shard_map/ppermute | solution.py:30
  108.4 17.4 %collective-permute-start.17 = (f32[128,1024]{1,0:T(8,128)S(1)}, f32[128,1024]{1,0:T(8,128)S(1)}, u32[]{:S(2)}, u32[]{:S(2)}) collective-permute-start(f32[128,1024]{1,0:T(8,128)S(1)} %get-tuple-element.137), channel_id=1, source_target_pairs={{0,16},{8,24},{16,0},{24,8},{1,17},{9,25},{17,1},{25,9},{2,18},{10... | collective-permute-start | bytes 1572872 | tf_op jit(solution)/shard_map/ppermute | solution.py:30
  133.3 43.8 %collective-permute-start.20 = (bf16[128,6144]{1,0:T(8,128)(2,1)}, bf16[128,6144]{1,0:T(8,128)(2,1)S(1)}, u32[]{:S(2)}, u32[]{:S(2)}) collective-permute-start(bf16[128,6144]{1,0:T(8,128)(2,1)} %get-tuple-element.151), channel_id=1, source_target_pairs={{0,1},{1,0},{2,3},{3,2},{4,5},{5,4},{6,7},{7,6},{8,9},{9,8},{10,11... | collective-permute-start | bytes 4718600 | tf_op jit(solution)/shard_map/ppermute | solution.py:30
  133.4 14.3 %collective-permute-start.22 = (f32[128,1024]{1,0:T(8,128)S(1)}, f32[128,1024]{1,0:T(8,128)S(1)}, u32[]{:S(2)}, u32[]{:S(2)}) collective-permute-start(f32[128,1024]{1,0:T(8,128)S(1)} %get-tuple-element.166), channel_id=1, source_target_pairs={{0,16},{8,24},{16,0},{24,8},{1,17},{9,25},{17,1},{25,9},{2,18},{10... | collective-permute-start | bytes 1572872 | tf_op jit(solution)/shard_map/ppermute | solution.py:30
  133.9 14.8 %collective-permute-start.21 = (f32[128,1024]{1,0:T(8,128)S(1)}, f32[128,1024]{1,0:T(8,128)S(1)}, u32[]{:S(2)}, u32[]{:S(2)}) collective-permute-start(f32[128,1024]{1,0:T(8,128)S(1)} %get-tuple-element.164), channel_id=1, source_target_pairs={{0,8},{8,0},{16,24},{24,16},{1,9},{9,1},{17,25},{25,17},{2,10},{10... | collective-permute-start | bytes 1572872 | tf_op jit(solution)/shard_map/ppermute | solution.py:30
  134.5 25.6 %collective-permute-start.31 = (f32[128,1024]{1,0:T(8,128)}, f32[128,1024]{1,0:T(8,128)}, u32[]{:S(2)}, u32[]{:S(2)}) collective-permute-start(f32[128,1024]{1,0:T(8,128)} %get-tuple-element.188), channel_id=1, source_target_pairs={{0,8},{8,0},{16,24},{24,16},{1,9},{9,1},{17,25},{25,17},{2,10},{10... | collective-permute-start | bytes 1572872 | tf_op jit(solution)/shard_map/ppermute | solution.py:30
  136.8 34.5 %collective-permute-start.27 = (f32[128,1024]{1,0:T(8,128)}, f32[128,1024]{1,0:T(8,128)}, u32[]{:S(2)}, u32[]{:S(2)}) collective-permute-start(f32[128,1024]{1,0:T(8,128)} %add.127), channel_id=1, source_target_pairs={{0,8},{8,0},{16,24},{24,16},{1,9},{9,1},{17,25},{25,17},{2,10},{10... | collective-permute-start | bytes 1572872 | tf_op jit(solution)/shard_map/ppermute | solution.py:30
  151.5 22.0 %collective-permute-start.23 = (f32[432,320]{0,1:T(8,128)}, f32[432,320]{0,1:T(8,128)}, u32[]{:S(2)}, u32[]{:S(2)}) collective-permute-start(f32[432,320]{0,1:T(8,128)} %copy.45), channel_id=1, source_target_pairs={{0,1},{1,0},{2,3},{3,2},{4,5},{5,4},{6,7},{7,6},{8,9},{9,8},{10,11... | collective-permute-start | bytes 1658888 | tf_op jit(solution)/shard_map/ppermute | solution.py:30
  151.5 29.8 %collective-permute-start.32 = (f32[128,1024]{1,0:T(8,128)}, f32[128,1024]{1,0:T(8,128)}, u32[]{:S(2)}, u32[]{:S(2)}) collective-permute-start(f32[128,1024]{1,0:T(8,128)} %copy-done.26), channel_id=1, source_target_pairs={{0,16},{8,24},{16,0},{24,8},{1,17},{9,25},{17,1},{25,9},{2,18},{10... | collective-permute-start | bytes 1572872 | tf_op jit(solution)/shard_map/ppermute | solution.py:30
  160.1 42.1 %collective-permute-start.34 = (f32[128,1024]{1,0:T(8,128)}, f32[128,1024]{1,0:T(8,128)}, u32[]{:S(2)}, u32[]{:S(2)}) collective-permute-start(f32[128,1024]{1,0:T(8,128)} %add.135), channel_id=1, source_target_pairs={{0,8},{8,0},{16,24},{24,16},{1,9},{9,1},{17,25},{25,17},{2,10},{10... | collective-permute-start | bytes 1572872 | tf_op jit(solution)/shard_map/ppermute | solution.py:30
  177.1 25.1 %collective-permute-start.28 = (f32[128,1024]{1,0:T(8,128)}, f32[128,1024]{1,0:T(8,128)S(1)}, u32[]{:S(2)}, u32[]{:S(2)}) collective-permute-start(f32[128,1024]{1,0:T(8,128)} %add_add_fusion.2), channel_id=1, source_target_pairs={{0,2},{1,3},{2,0},{3,1},{4,6},{5,7},{6,4},{7,5},{8,10},{9,11},{10,... | collective-permute-start | bytes 1572872 | tf_op jit(solution)/shard_map/ppermute | solution.py:30
  178.7 19.5 %collective-permute-start.24 = (f32[128,320]{1,0:T(8,128)S(1)}, f32[128,320]{1,0:T(8,128)S(1)}, u32[]{:S(2)}, u32[]{:S(2)}) collective-permute-start(f32[128,320]{1,0:T(8,128)S(1)} %get-tuple-element.220), channel_id=1, source_target_pairs={{2,0},{3,1},{4,2},{5,3},{6,4},{7,5},{10,8},{11,9},{12,10},{13,11},... | collective-permute-start | bytes 491528 | tf_op jit(solution)/shard_map/ppermute | solution.py:25
  180.0 19.7 %collective-permute-start.25 = (f32[128,320]{1,0:T(8,128)S(1)}, f32[128,320]{1,0:T(8,128)S(1)}, u32[]{:S(2)}, u32[]{:S(2)}) collective-permute-start(f32[128,320]{1,0:T(8,128)S(1)} %get-tuple-element.221), channel_id=1, source_target_pairs={{4,0},{5,1},{6,2},{7,3},{12,8},{13,9},{14,10},{15,11},{20,16},{21,... | collective-permute-start | bytes 491528 | tf_op jit(solution)/shard_map/ppermute | solution.py:25
  181.4 22.5 %collective-permute-start.26 = (f32[128,1024]{1,0:T(8,128)S(1)}, f32[128,1024]{1,0:T(8,128)S(1)}, u32[]{:S(2)}, u32[]{:S(2)}) collective-permute-start(f32[128,1024]{1,0:T(8,128)S(1)} %add.124), channel_id=1, source_target_pairs={{0,16},{8,24},{16,0},{24,8},{1,17},{9,25},{17,1},{25,9},{2,18},{10... | collective-permute-start | bytes 1572872 | tf_op jit(solution)/shard_map/ppermute | solution.py:30
  198.2 11.5 %collective-permute-start.33 = (f32[128,1024]{1,0:T(8,128)S(1)}, f32[128,1024]{1,0:T(8,128)S(1)}, u32[]{:S(2)}, u32[]{:S(2)}) collective-permute-start(f32[128,1024]{1,0:T(8,128)S(1)} %add.132), channel_id=1, source_target_pairs={{0,16},{8,24},{16,0},{24,8},{1,17},{9,25},{17,1},{25,9},{2,18},{10... | collective-permute-start | bytes 1572872 | tf_op jit(solution)/shard_map/ppermute | solution.py:30
  203.6 16.9 %collective-permute-start.35 = (f32[128,1024]{1,0:T(8,128)S(1)}, f32[128,1024]{1,0:T(8,128)S(1)}, u32[]{:S(2)}, u32[]{:S(2)}) collective-permute-start(f32[128,1024]{1,0:T(8,128)S(1)} %add_add_fusion), channel_id=1, source_target_pairs={{0,2},{1,3},{2,0},{3,1},{4,6},{5,7},{6,4},{7,5},{8,10},{9,11},{10,... | collective-permute-start | bytes 1572872 | tf_op jit(solution)/shard_map/ppermute | solution.py:30
  204.1 14.1 %collective-permute-start.29 = (f32[64,1024]{1,0:T(8,128)S(1)}, f32[64,1024]{1,0:T(8,128)S(1)}, u32[]{:S(2)}, u32[]{:S(2)}) collective-permute-start(f32[64,1024]{1,0:T(8,128)S(1)} %slice.60), channel_id=1, source_target_pairs={{0,4},{1,5},{2,6},{3,7},{4,0},{5,1},{6,2},{7,3},{8,12},{9,13},{10,... | collective-permute-start | bytes 786440 | tf_op jit(solution)/shard_map/ppermute | solution.py:30
  221.6 12.5 %collective-permute-start.36 = (f32[64,1024]{1,0:T(8,128)S(1)}, f32[64,1024]{1,0:T(8,128)S(1)}, u32[]{:S(2)}, u32[]{:S(2)}) collective-permute-start(f32[64,1024]{1,0:T(8,128)S(1)} %slice.64), channel_id=1, source_target_pairs={{0,4},{1,5},{2,6},{3,7},{4,0},{5,1},{6,2},{7,3},{8,12},{9,13},{10,... | collective-permute-start | bytes 786440 | tf_op jit(solution)/shard_map/ppermute | solution.py:30
  223.0 1.4 collective-permute-start.30
  225.0 13.6 %collective-permute-start.42 = (f32[32,2048]{1,0:T(8,128)S(1)}, f32[32,2048]{1,0:T(8,128)S(1)}, u32[]{:S(2)}, u32[]{:S(2)}) collective-permute-start(f32[32,2048]{1,0:T(8,128)S(1)} %join_cores.2.refs_0_), channel_id=1, source_target_pairs={{0,24},{8,16},{16,8},{24,0},{1,25},{9,17},{17,9},{25,1},{2,26},{10... | collective-permute-start | bytes 786440 | tf_op jit(solution)/shard_map/ppermute | solution.py:30
  234.2 1.4 collective-permute-start.37
  234.3 9.2 %collective-permute-start.40 = (f32[32,2048]{1,0:T(8,128)S(1)}, f32[32,2048]{1,0:T(8,128)S(1)}, u32[]{:S(2)}, u32[]{:S(2)}) collective-permute-start(f32[32,2048]{1,0:T(8,128)S(1)} %join_cores.2.refs_0_), channel_id=1, source_target_pairs={{0,16},{8,24},{16,0},{24,8},{1,17},{9,25},{17,1},{25,9},{2,18},{10... | collective-permute-start | bytes 786440 | tf_op jit(solution)/shard_map/ppermute | solution.py:30
  234.4 9.2 %collective-permute-start.38 = (f32[32,2048]{1,0:T(8,128)S(1)}, f32[32,2048]{1,0:T(8,128)S(1)}, u32[]{:S(2)}, u32[]{:S(2)}) collective-permute-start(f32[32,2048]{1,0:T(8,128)S(1)} %join_cores.2.refs_0_), channel_id=1, source_target_pairs={{0,8},{8,0},{16,24},{24,16},{1,9},{9,1},{17,25},{25,17},{2,10},{10... | collective-permute-start | bytes 786440 | tf_op jit(solution)/shard_map/ppermute | solution.py:30
  236.2 14.4 %collective-permute-start.43 = (f32[32,2048]{1,0:T(8,128)S(1)}, f32[32,2048]{1,0:T(8,128)S(1)}, u32[]{:S(2)}, u32[]{:S(2)}) collective-permute-start(f32[32,2048]{1,0:T(8,128)S(1)} %join_cores.3.refs_1_), channel_id=1, source_target_pairs={{0,24},{8,16},{16,8},{24,0},{1,25},{9,17},{17,9},{25,1},{2,26},{10... | collective-permute-start | bytes 786440 | tf_op jit(solution)/shard_map/ppermute | solution.py:30
  238.5 15.8 %collective-permute-start.41 = (f32[32,2048]{1,0:T(8,128)S(1)}, f32[32,2048]{1,0:T(8,128)S(1)}, u32[]{:S(2)}, u32[]{:S(2)}) collective-permute-start(f32[32,2048]{1,0:T(8,128)S(1)} %join_cores.3.refs_1_), channel_id=1, source_target_pairs={{0,16},{8,24},{16,0},{24,8},{1,17},{9,25},{17,1},{25,9},{2,18},{10... | collective-permute-start | bytes 786440 | tf_op jit(solution)/shard_map/ppermute | solution.py:30
  238.6 15.7 %collective-permute-start.39 = (f32[32,2048]{1,0:T(8,128)S(1)}, f32[32,2048]{1,0:T(8,128)S(1)}, u32[]{:S(2)}, u32[]{:S(2)}) collective-permute-start(f32[32,2048]{1,0:T(8,128)S(1)} %join_cores.3.refs_1_), channel_id=1, source_target_pairs={{0,8},{8,0},{16,24},{24,16},{1,9},{9,1},{17,25},{25,17},{2,10},{10... | collective-permute-start | bytes 786440 | tf_op jit(solution)/shard_map/ppermute | solution.py:30
  (37 other events, 266.4 us)

commit v4 on v3

--- a/solution.py
+++ b/solution.py
@@ -485,36 +485,6 @@
     chip_rows = weight_parts(place, up_weight, n_dp, far, crossed)
     own = [q_nope[0], q_rope[0], grad_out[0]]
     sibling = [exchange(array, "ctx", 1) for array in own]
-
-    partners = halving_order(n_ctx)[::2]
-
-    def over_chips(start, onward, *earlier):
-        at_step = {0: start}
-        for step in range(4, n_ctx, 4):
-            at_step[step] = exchange(start, "ctx", step)
-        at_step[2] = exchange(start, "ctx", 2)
-        for step in range(4, n_ctx, 4):
-            if onward:
-                forwarded = after(at_step[step], at_step[2], *earlier)
-                at_step[step + 2] = exchange(forwarded, "ctx", 2)
-            else:
-                at_step[step + 2] = exchange(start, "ctx", step + 2)
-        return [at_step[partner] for partner in partners], at_step[n_ctx - 4]
-
-    def joined(pieces):
-        return stack(pieces, (tuple((index, 0) for index in range(len(pieces))),), part_cols)[0]
-
-    near_pieces, last = over_chips(chip_rows[0], True, *sibling)
-    far_pieces, _ = over_chips(after(chip_rows[1], last), False)
-    weights = {0: joined(near_pieces)}
-    for t in range(1, far):
-        weights[t] = exchange(weights[0], "dp", t)
-    log_total = after(log_total, last)[0]
-    sibling.append(exchange(log_total, "ctx", 1))
-    own.append(log_total)
-    for arrays in (own, sibling):
-        arrays[3] = arrays[3].reshape(heads // 2, 2, group_len)
-
     offer_plan = offered[0]
     span = group_len + 16
     blocks, starts, usables = [], [], []
@@ -543,11 +513,40 @@
             kinds = jnp.where(picked, 2.0, jnp.where(same, 1.0, 0.0)).reshape(1, -1)
     plan = jnp.concatenate([ctx[None], *starts, *usables]).astype(jnp.int32)
     kinds = jnp.pad(kinds.astype(jnp.bfloat16), ((0, 15), (0, LAT + ROPE - kinds.shape[1])))
-    bundle = after(jnp.concatenate([kv_latent[0], kinds], axis=0), *sibling[:3])
+    bundle = after(jnp.concatenate([kv_latent[0], kinds], axis=0), *sibling)
     bundles = [bundle, from_behind(bundle, "ctx", 2), from_behind(bundle, "ctx", 4)]
     own_bundles = stack(bundles, (((0, 0), (1, 0), (2, 0)),), LAT + ROPE)[0]
     sib_bundles = exchange(own_bundles, "ctx", 1)
     shared = collect(plan, own_bundles, sib_bundles, tuple(blocks), lat_block)
+
+    partners = halving_order(n_ctx)[::2]
+
+    def over_chips(start, onward, *earlier):
+        at_step = {0: start}
+        for step in range(4, n_ctx, 4):
+            at_step[step] = exchange(start, "ctx", step)
+        at_step[2] = exchange(start, "ctx", 2)
+        for step in range(4, n_ctx, 4):
+            if onward:
+                forwarded = after(at_step[step], at_step[2], *earlier)
+                at_step[step + 2] = exchange(forwarded, "ctx", 2)
+            else:
+                at_step[step + 2] = exchange(start, "ctx", step + 2)
+        return [at_step[partner] for partner in partners], at_step[n_ctx - 4]
+
+    def joined(pieces):
+        return stack(pieces, (tuple((index, 0) for index in range(len(pieces))),), part_cols)[0]
+
+    near_pieces, last = over_chips(chip_rows[0], True, *bundles[1:])
+    far_pieces, _ = over_chips(after(chip_rows[1], last), False)
+    weights = {0: joined(near_pieces), far: joined(far_pieces)}
+    for t in range(1, far):
+        weights[t] = exchange(weights[0], "dp", t)
+    log_total = after(log_total, last)[0]
+    sibling.append(exchange(log_total, "ctx", 1))
+    own.append(log_total)
+    for arrays in (own, sibling):
+        arrays[3] = arrays[3].reshape(heads // 2, 2, group_len)
 
     earlier = None
     latents, ropes = [], []
@@ -555,20 +554,18 @@
     bits = [1 << b for b in range(n_dp.bit_length() - 1)]
     orders = (bits, bits[::-1])
     first_sums = [{t: [] for t in range(n_dp) if t & order[0]} for order in orders]
-    units = [(0, 0), (0, 1)]
-    units += [(t, half) for half in range(2) for t in [far] + list(range(1, far))]
-    for t, half in units:
-        if (t, half) == (far, 0):
-            weights[far] = joined([after(far_pieces[0], latents[-1])] + far_pieces[1:])
+    units = [(t, 0, pairs) for t in [far] + list(range(1, far - 1))]
+    units += [(t, start, pairs // 2) for t in (far - 1, 0) for start in (0, pairs // 2)]
+    for t, start, count in units:
         weight = weights[t]
-        if (t, half) == (far, 1):
+        if t == 0:
+            weight = after(weight, *[sent[u][-1 if start else 0] for sent in first_sums for u in sent])
+        if t == far - 1 and start:
             weight = after(weight, *[sent[far][0] for sent in first_sums])
-        if (t, half) == (far - 1, 1):
-            weight = after(weight, *[sent[u][0] for sent in first_sums for u in sent if u != far])
         rest = chunk_backward(
             place,
             t,
-            (half * pairs // 2, pairs // 2),
+            (start, count),
             own,
             sibling,
             weight,
@@ -578,20 +575,26 @@
         )
         earlier = rest[:3]
         for side, sent in enumerate(first_sums):
-            grad = rest[3 + side]
-            weight_grads[t][side].append(grad)
+            weight_grads[t][side].append(rest[3 + side])
             if t in sent:
-                leaving = after(grad, sent[t][0]) if half else grad
-                sent[t].append(exchange(leaving, "dp", orders[side][0]))
+                sent[t].append(exchange(rest[3 + side], "dp", orders[side][0]))
         latents.append(rest[5])
         ropes.append(rest[6])
 
+    half_cols = part_cols // 2
+
+    def columns(pieces, half):
+        if len(pieces) == 2:
+            return pieces[half]
+        return pieces[0][:, half * half_cols : (half + 1) * half_cols]
+
     def total(addends, half):
         return functools.reduce(
-            lambda left, right: left + right, [pieces[half] for pieces in addends]
+            lambda left, right: left + right, [columns(pieces, half) for pieces in addends]
         )
 
     sums = []
+    last_sums = first_sums[1][far - 1]
     for side, order in enumerate(orders):
         addends = {t: [weight_grads[t][side]] for t in weight_grads}
         arrived = {t ^ order[0]: pieces for t, pieces in first_sums[side].items()}
@@ -599,11 +602,11 @@
         for bit in order[1:]:
             arrived = {}
             for t in sorted((t for t in addends if t & bit), reverse=True):
-                behind = first_sums[1 - side].get(bit, first_sums[side][order[0]])
-                arrived[t ^ bit] = [
-                    exchange(after(total(addends[t], half), behind[half]), "dp", bit)
-                    for half in range(2)
-                ]
+                leaving = [total(addends[t], half) for half in range(2)]
+                if side == 0:
+                    behind = (first_sums[0][order[0]][0], last_sums[0])
+                    leaving = [after(half, there) for half, there in zip(leaving, behind)]
+                arrived[t ^ bit] = [exchange(half, "dp", bit) for half in leaving]
             addends = {t: addends[t] + [more] for t, more in arrived.items()}
         sums.append(addends[0])
 
@@ -611,7 +614,6 @@
     received = exchange(sib_grads, "ctx", 1)
     grad_nope, grad_rope = place_columns(place, received, q_full, rope_full, n_dp)
 
-    latents[-1] = after(latents[-1], *[sent[far][1] for sent in first_sums])
     own_grads, sib_grads = spread(plan, latents, ropes, 3 * span, tuple(blocks), lat_block)
     swapped = exchange(sib_grads, "ctx", 1)
     grad_rows = own_grads + swapped
@@ -626,12 +628,14 @@
         if half:
             sums = [[[after(piece, arrived) for piece in pieces] for pieces in side] for side in sums]
         first, second = [total(side, half) for side in sums]
-        second = after(second, *((grad_rows, grad_nope) if half else (received, swapped)))
         arrived = exchange(second, "ctx", ctx_bits[0])
         rows = first + arrived
         for bit in ctx_bits[1:]:
             rows = halve(rows, "ctx", bit)
-        piece = join_cores(place, rows[:lat_block], exchange(rows[lat_block:], "ctx", 1))
+        crossing = rows[lat_block:]
+        if half:
+            crossing = after(crossing, grad_rows, grad_nope)
+        piece = join_cores(place, rows[:lat_block], exchange(crossing, "ctx", 1))
         finished.append([piece] + [exchange(piece, "dp", t) for t in range(1, n_dp)])
     grad_weight = lay_out(place, [piece for both in zip(*finished) for piece in both])
     return (grad_nope[None], grad_rope[None], grad_rows[None], grad_weight)

time: 258 us -> 229 us (0.89)
  waiting for transfers between devices: 101 us -> 69.2 us
  other arithmetic: 12 us -> 17.3 us
  starting transfers between devices: 47.2 us -> 52 us
  Pallas kernels: 78.2 us -> 74 us
    ppermute x40 -> x37, waiting for transfers between devices: 84.3 us -> 53 us  [exchange(): lax.ppermute(value, axis, [(source, source ^ bits) for source in range(co...]
    ppermute x40 -> x37, starting transfers between devices: 36.7 us -> 45.1 us  [exchange(): lax.ppermute(value, axis, [(source, source ^ bits) for source in range(co...]
    pallas_call x8 -> x6, Pallas kernels: 59.9 us -> 55.4 us  [chunk_backward(): pl.pallas_call(functools.partial(heads_kernel, earlier=len(aliases)), gri...]
    ppermute x4, starting transfers between devices: 10.5 us -> 6.86 us  [from_behind(): lax.ppermute(value, axis, [(source, source + steps) for source in range(i...]
    unnamed x83 -> x81, local copies, waits for them, and re-layouts: 9.03 us -> 6.55 us
    add x6 -> x4, other arithmetic: 6.49 us -> 5.06 us  [total(): left + right]
  transfers between devices with their start and end apart: 44 -> 41, of which waited for: 20 -> 20; matrix products, arithmetic and copies ran while one was open for 7% -> 11% of each run, Pallas kernels for 25% -> 30%
where the time goes in v4:
time: 229 us; the launch traced here: 228 us
  Pallas kernels  74 us (32%)
  waiting for transfers between devices  69.2 us (30%)
  starting transfers between devices  52 us (23%)
  other arithmetic  17.3 us (8%)
  local copies, waits for them, and re-layouts  14.7 us (6%)
    pallas_call x6, Pallas kernels, chunk_backward(): pl.pallas_call(functools.partial(heads_kernel, earlier=len(aliases)), gri...  55.4 us
    ppermute x37, waiting for transfers between devices, exchange(): lax.ppermute(value, axis, [(source, source ^ bits) for source in range(co...  53 us
    ppermute x37, starting transfers between devices, exchange(): lax.ppermute(value, axis, [(source, source ^ bits) for source in range(co...  45.1 us
    ppermute x4, waiting for transfers between devices, from_behind(): lax.ppermute(value, axis, [(source, source + steps) for source in range(i...  16.2 us
    ppermute x4, starting transfers between devices, from_behind(): lax.ppermute(value, axis, [(source, source + steps) for source in range(i...  6.86 us
    unnamed x81, local copies, waits for them, and re-layouts  6.55 us
    add x4, other arithmetic, total(): left + right  5.06 us
    pallas_call x2, Pallas kernels, weight_parts(): pl.pallas_call(join_rows_kernel if joins else leave_kernel, grid_spec=plt...  4.95 us
  transfers between devices with their start and end apart: 41, of which 20 were waited for; matrix products, arithmetic and copies ran while one was open for 11% of the time, Pallas kernels for 30%

profile of v4, /device:TPU:0, one launch (start us, length us, event | category | flops | bytes accessed | tf_op | source)
XLA Modules:
  0.0 228.3 jit_solution(3607456824362197136)
XLA Ops:
  1.3 2.4 %weight_parts.2 = bf16[32,4096]{1,0:T(8,128)(2,1)} custom-call(s32[5]{0:T(128)} %stack.64.place, bf16[32,16384]{1,0:T(8,128)(2,1)} %distant.3, bf16[32,16384]{1,0:T(8,128)(2,1)} %distant.3), custom_call_target="tpu_custom_call" | custom-call | bytes 1000000 | tf_op jit(solution)/shard_map/weight_parts/pallas_call | solution.py:263
  7.6 2.6 %weight_parts.3 = (bf16[64,2048]{1,0:T(8,128)(2,1)}, bf16[64,2048]{1,0:T(8,128)(2,1)}) custom-call(s32[5]{0:T(128)} %stack.64.place, bf16[32,16384]{1,0:T(8,128)(2,1)} %distant.3, bf16[32,16384]{1,0:T(8,128)(2,1)} %distant.3, bf16[32,4096]{1,0:T(8,128)(2,1)} %copy-done.30), custom_call_target="tpu_custom_call" | custom-call | bytes 1000000 | tf_op jit(solution)/shard_map/weight_parts/pallas_call | solution.py:263
  10.2 2.7 %collective-permute-start.6 = (bf16[64,2048]{1,0:T(8,128)(2,1)}, bf16[64,2048]{1,0:T(8,128)(2,1)}, u32[]{:S(2)}, u32[]{:S(2)}) collective-permute-start(bf16[64,2048]{1,0:T(8,128)(2,1)} %get-tuple-element.87.refs_0_), channel_id=1, source_target_pairs={{0,2},{1,3},{2,0},{3,1},{4,6},{5,7},{6,4},{7,5},{8,10},{9,11},{10,... | collective-permute-start | bytes 786440 | tf_op jit(solution)/shard_map/ppermute | solution.py:30
  12.9 2.6 %collective-permute-start.1 = (bf16[64,2048]{1,0:T(8,128)(2,1)}, bf16[64,2048]{1,0:T(8,128)(2,1)}, u32[]{:S(2)}, u32[]{:S(2)}) collective-permute-start(bf16[64,2048]{1,0:T(8,128)(2,1)} %get-tuple-element.87.refs_0_), channel_id=1, source_target_pairs={{0,4},{1,5},{2,6},{3,7},{4,0},{5,1},{6,2},{7,3},{8,12},{9,13},{10,... | collective-permute-start | bytes 786440 | tf_op jit(solution)/shard_map/ppermute | solution.py:30
  19.9 1.6 copy.37
  23.4 2.2 collective-permute-start.8
  25.7 2.0 collective-permute-start.7
  28.3 2.0 collective-permute-done.7.refs_1_
  30.3 4.4 %collective-permute-start.9 = (bf16[64,2048]{1,0:T(8,128)(2,1)}, bf16[64,2048]{1,0:T(8,128)(2,1)S(1)}, u32[]{:S(2)}, u32[]{:S(2)}) collective-permute-start(bf16[64,2048]{1,0:T(8,128)(2,1)} %collective-permute-done.1.refs_1_), channel_id=1, source_target_pairs={{0,2},{1,3},{2,0},{3,1},{4,6},{5,7},{6,4},{7,5},{8,10},{9,11},{10,... | collective-permute-start | bytes 786440 | tf_op jit(solution)/shard_map/ppermute | solution.py:30
  35.2 3.4 %collective-permute-start.14 = (bf16[64,2048]{1,0:T(8,128)(2,1)}, bf16[64,2048]{1,0:T(8,128)(2,1)}, u32[]{:S(2)}, u32[]{:S(2)}) collective-permute-start(bf16[64,2048]{1,0:T(8,128)(2,1)} %get-tuple-element.99.refs_0_), channel_id=1, source_target_pairs={{0,6},{1,7},{2,4},{3,5},{4,2},{5,3},{6,0},{7,1},{8,14},{9,15},{10,... | collective-permute-start | bytes 786440 | tf_op jit(solution)/shard_map/ppermute | solution.py:30
  42.8 2.1 stack.77.weight
  44.8 1.5 collective-permute-start.10
  47.1 4.3 %collective-permute-done.14.refs_3_ = bf16[64,2048]{1,0:T(8,128)(2,1)} collective-permute-done((bf16[64,2048]{1,0:T(8,128)(2,1)}, bf16[64,2048]{1,0:T(8,128)(2,1)}, u32[]{:S(2)}, u32[]{:S(2)}) %collective-permute-start.14) | collective-permute-done | bytes 262176 | tf_op jit(solution)/shard_map/ppermute | solution.py:30
  52.2 5.4 %collective-permute-done.13.refs_2_ = bf16[64,2048]{1,0:T(8,128)(2,1)} collective-permute-done((bf16[64,2048]{1,0:T(8,128)(2,1)}, bf16[64,2048]{1,0:T(8,128)(2,1)}, u32[]{:S(2)}, u32[]{:S(2)}) %collective-permute-start.13) | collective-permute-done | bytes 262176 | tf_op jit(solution)/shard_map/ppermute | solution.py:30
  58.8 1.6 collective-permute-start.17
  60.4 2.1 collect.1
  63.8 13.0 %heads_backward.6 = (bf16[128,8192]{1,0:T(8,128)(2,1)}, bf16[128,4096]{1,0:T(8,128)(2,1)}, bf16[128,6144]{1,0:T(8,128)(2,1)S(1)}, f32[128,2048]{1,0:T(8,128)S(1)...) custom-call(s32[5]{0:T(128)S(1)} %copy-done.20, bf16[128,8192]{1,0:T(8,128)(2,1)S(1)} %bitcast.46, ...), custom_call_target="tpu_custom_call" | custom-call | flops 400000000 | bytes 1200000 | tf_op jit(solution)/shard_map/heads_backward/pallas_call | solution.py:157
  78.8 13.0 %heads_backward.7 = (bf16[128,8192]{1,0:T(8,128)(2,1)}, bf16[128,4096]{1,0:T(8,128)(2,1)}, bf16[128,6144]{1,0:T(8,128)(2,1)S(1)}, f32[128,2048]{1,0:T(8,128)S(1)...) custom-call(s32[5]{0:T(128)S(1)} %copy-done.20, ...), custom_call_target="tpu_custom_call", output_to_operand_aliasing={{0}: (14, {}), {1}: (15, {}), {2}: (16, {})} | custom-call | flops 400000000 | bytes 1200000 | tf_op jit(solution)/shard_map/heads_backward/pallas_call | solution.py:157
  92.3 7.2 %heads_backward.8 = (bf16[128,8192]{1,0:T(8,128)(2,1)}, bf16[128,4096]{1,0:T(8,128)(2,1)}, bf16[128,6144]{1,0:T(8,128)(2,1)S(1)}, f32[128,1024]{1,0:T(8,128)S(1)...) custom-call(s32[5]{0:T(128)S(1)} %copy-done.20, ...), custom_call_target="tpu_custom_call", output_to_operand_aliasing={{0}: (14, {}), {1}: (15, {}), {2}: (16, {})} | custom-call | flops 200000000 | bytes 600000 | tf_op jit(solution)/shard_map/heads_backward/pallas_call | solution.py:157
  99.5 1.5 collective-permute-start.20
  101.0 6.6 %collective-permute-done.18 = f32[128,2048]{1,0:T(8,128)S(1)} collective-permute-done((f32[128,2048]{1,0:T(8,128)S(1)}, f32[128,2048]{1,0:T(8,128)S(1)}, u32[]{:S(2)}, u32[]{:S(2)}) %collective-permute-start.18) | collective-permute-done | bytes 1048608 | tf_op jit(solution)/shard_map/ppermute | solution.py:30
  108.6 1.5 collective-permute-start.26
  110.6 7.2 %heads_backward.9 = (bf16[128,8192]{1,0:T(8,128)(2,1)}, bf16[128,4096]{1,0:T(8,128)(2,1)}, bf16[128,6144]{1,0:T(8,128)(2,1)S(1)}, f32[128,1024]{1,0:T(8,128)S(1)...) custom-call(s32[5]{0:T(128)S(1)} %copy-done.20, ...), custom_call_target="tpu_custom_call", output_to_operand_aliasing={{0}: (14, {}), {1}: (15, {}), {2}: (16, {})} | custom-call | flops 200000000 | bytes 600000 | tf_op jit(solution)/shard_map/heads_backward/pallas_call | solution.py:157
  117.8 1.5 collective-permute-start.19
  119.3 6.5 %collective-permute-done.15 = f32[128,2048]{1,0:T(8,128)S(1)} collective-permute-done((f32[128,2048]{1,0:T(8,128)S(1)}, f32[128,2048]{1,0:T(8,128)S(1)}, u32[]{:S(2)}, u32[]{:S(2)}) %collective-permute-start.15) | collective-permute-done | bytes 1048608 | tf_op jit(solution)/shard_map/ppermute | solution.py:30
  125.8 7.6 %heads_backward.10 = (bf16[128,8192]{1,0:T(8,128)(2,1)}, bf16[128,4096]{1,0:T(8,128)(2,1)}, bf16[128,6144]{1,0:T(8,128)(2,1)S(1)}, f32[128,1024]{1,0:T(8,128)S(1...) custom-call(s32[5]{0:T(128)S(1)} %copy-done.20, ...), custom_call_target="tpu_custom_call", output_to_operand_aliasing={{0}: (14, {}), {1}: (15, {}), {2}: (16, {})} | custom-call | flops 200000000 | bytes 600000 | tf_op jit(solution)/shard_map/heads_backward/pallas_call | solution.py:157
  133.5 3.6 %collective-permute-done.26 = f32[128,1024]{1,0:T(8,128)S(1)} collective-permute-done((f32[128,1024]{1,0:T(8,128)S(1)}, f32[128,1024]{1,0:T(8,128)S(1)}, u32[]{:S(2)}, u32[]{:S(2)}) %collective-permute-start.26) | collective-permute-done | bytes 524320 | tf_op jit(solution)/shard_map/ppermute | solution.py:30
  138.0 3.7 %collective-permute-start.27 = (f32[128,1024]{1,0:T(8,128)}, f32[128,1024]{1,0:T(8,128)}, u32[]{:S(2)}, u32[]{:S(2)}) collective-permute-start(f32[128,1024]{1,0:T(8,128)} %add_add_fusion.2), channel_id=1, source_target_pairs={{0,2},{1,3},{2,0},{3,1},{4,6},{5,7},{6,4},{7,5},{8,10},{9,11},{10,... | collective-permute-start | bytes 1572872 | tf_op jit(solution)/shard_map/ppermute | solution.py:30
  142.8 1.5 collective-permute-start.25
  144.8 7.4 %heads_backward.11 = (bf16[128,8192]{1,0:T(8,128)(2,1)}, bf16[128,4096]{1,0:T(8,128)(2,1)}, bf16[128,6144]{1,0:T(8,128)(2,1)S(1)}, f32[128,1024]{1,0:T(8,128)S(1...) custom-call(s32[5]{0:T(128)S(1)} %copy-done.20, ...), custom_call_target="tpu_custom_call", output_to_operand_aliasing={{0}: (14, {}), {1}: (15, {}), {2}: (16, {})} | custom-call | flops 200000000 | bytes 600000 | tf_op jit(solution)/shard_map/heads_backward/pallas_call | solution.py:157
  152.3 1.6 spread.1
  155.9 2.1 add_add_fusion
  158.0 1.5 fusion.1
  159.6 2.0 collective-permute-start.28
  161.8 2.2 copy.40
  164.0 1.5 add.120
  168.2 7.8 %collective-permute-done.28 = f32[64,1024]{1,0:T(8,128)} collective-permute-done((f32[64,1024]{1,0:T(8,128)S(1)}, f32[64,1024]{1,0:T(8,128)}, u32[]{:S(2)}, u32[]{:S(2)}) %collective-permute-start.28) | collective-permute-done | bytes 262176 | tf_op jit(solution)/shard_map/ppermute | solution.py:30
  177.0 1.7 collective-permute-done.32
  180.0 1.9 collective-permute-start.33
  182.0 2.7 %collective-permute-done.23 = f32[128,320]{1,0:T(8,128)S(1)} collective-permute-done((f32[128,320]{1,0:T(8,128)S(1)}, f32[128,320]{1,0:T(8,128)S(1)}, u32[]{:S(2)}, u32[]{:S(2)}) %collective-permute-start.23) | collective-permute-done | bytes 163872 | tf_op jit(solution)/shard_map/ppermute | solution.py:25
  184.7 11.3 %collective-permute-done.24 = f32[128,320]{1,0:T(8,128)S(1)} collective-permute-done((f32[128,320]{1,0:T(8,128)S(1)}, f32[128,320]{1,0:T(8,128)S(1)}, u32[]{:S(2)}, u32[]{:S(2)}) %collective-permute-start.24) | collective-permute-done | bytes 163872 | tf_op jit(solution)/shard_map/ppermute | solution.py:25
  197.3 2.5 %collective-permute-start.39 = (f32[32,2048]{1,0:T(8,128)S(1)}, f32[32,2048]{1,0:T(8,128)S(1)}, u32[]{:S(2)}, u32[]{:S(2)}) collective-permute-start(f32[32,2048]{1,0:T(8,128)S(1)} %join_cores.2.refs_0_), channel_id=1, source_target_pairs={{0,24},{8,16},{16,8},{24,0},{1,25},{9,17},{17,9},{25,1},{2,26},{10... | collective-permute-start | bytes 786440 | tf_op jit(solution)/shard_map/ppermute | solution.py:30
  201.3 2.4 %place_columns.1 = (bf16[128,8192]{1,0:T(8,128)(2,1)}, bf16[128,4096]{1,0:T(8,128)(2,1)}) custom-call(s32[5]{0:T(128)S(1)} %copy-done.21, bf16[128,6144]{1,0:T(8,128)(2,1)S(1)} %collective-permute-done.21.received, bf16[128,8192]{1,0:T(8,128)(2,1)} %get-tuple-element.124.q_in, ...), custom_call_target="tpu_custom_call", output_to_operand_aliasing={{0}: (2, {}), {1}: (3, {})} | custom-call | bytes 4000000 | tf_op jit(solution)/shard_map/place_columns/pallas_call | solution.py:186
  203.7 1.5 collective-permute-start.37
  212.8 1.6 collective-permute-done.35.refs_2_
  214.4 5.6 %collective-permute-done.40.refs_7_ = f32[32,2048]{1,0:T(8,128)S(1)} collective-permute-done((f32[32,2048]{1,0:T(8,128)S(1)}, f32[32,2048]{1,0:T(8,128)S(1)}, u32[]{:S(2)}, u32[]{:S(2)}) %collective-permute-start.40) | collective-permute-done | bytes 262176 | tf_op jit(solution)/shard_map/ppermute | solution.py:30
  220.0 3.7 %collective-permute-done.38.refs_5_ = f32[32,2048]{1,0:T(8,128)S(1)} collective-permute-done((f32[32,2048]{1,0:T(8,128)S(1)}, f32[32,2048]{1,0:T(8,128)S(1)}, u32[]{:S(2)}, u32[]{:S(2)}) %collective-permute-start.38) | collective-permute-done | bytes 262176 | tf_op jit(solution)/shard_map/ppermute | solution.py:30
  225.9 2.4 %lay_out.1 = f32[32,16384]{1,0:T(8,128)} custom-call(s32[5]{0:T(128)S(1)} %copy-done.21, f32[32,2048]{1,0:T(8,128)S(1)} %join_cores.2.refs_0_, f32[32,2048]{1,0:T(8,128)S(1)} %join_cores.3.refs_1_, f32[32,2048]{1,0:T(8,128)S(1)} %collective-permute-done.35.refs_2_, f32[32,2048]{1,0:T(8,128)S(1)} %collective-permute-done.36.refs_3_, ...), custom_call_target="tpu_custom_call" | custom-call | bytes 4000000 | tf_op jit(solution)/shard_map/lay_out/pallas_call | solution.py:295
  (170 shorter events, 46.6 us)
Async XLA Ops:
  0.6 14.9 %copy-start = (s32[1,8,4]{1,2,0:T(4,128)S(1)}, s32[1,8,4]{1,2,0:T(4,128)}, u32[]{:S(2)}) copy-start(s32[1,8,4]{1,2,0:T(4,128)} %param.15) | copy-start | bytes 388
  3.7 1.8 collective-permute-start
  5.5 17.9 %collective-permute-start.2 = (bf16[128,8192]{1,0:T(8,128)(2,1)S(1)}, bf16[128,8192]{1,0:T(8,128)(2,1)}, u32[]{:S(2)}, u32[]{:S(2)}) collective-permute-start(bf16[128,8192]{1,0:T(8,128)(2,1)S(1)} %bitcast.45), channel_id=1, source_target_pairs={{0,1},{1,0},{2,3},{3,2},{4,5},{5,4},{6,7},{7,6},{8,9},{9,8},{10,11... | collective-permute-start | bytes 6291464 | tf_op jit(solution)/shard_map/ppermute | solution.py:30
  5.9 17.6 %collective-permute-start.4 = (bf16[128,8192]{1,0:T(8,128)(2,1)}, bf16[128,8192]{1,0:T(8,128)(2,1)}, u32[]{:S(2)}, u32[]{:S(2)}) collective-permute-start(bf16[128,8192]{1,0:T(8,128)(2,1)} %bitcast.52), channel_id=1, source_target_pairs={{0,1},{1,0},{2,3},{3,2},{4,5},{5,4},{6,7},{7,6},{8,9},{9,8},{10,11... | collective-permute-start | bytes 6291464 | tf_op jit(solution)/shard_map/ppermute | solution.py:30
  6.1 16.4 %collective-permute-start.3 = (bf16[128,4096]{1,0:T(8,128)(2,1)}, bf16[128,4096]{1,0:T(8,128)(2,1)S(1)}, u32[]{:S(2)}, u32[]{:S(2)}) collective-permute-start(bf16[128,4096]{1,0:T(8,128)(2,1)} %bitcast.59), channel_id=1, source_target_pairs={{0,1},{1,0},{2,3},{3,2},{4,5},{5,4},{6,7},{7,6},{8,9},{9,8},{10,11... | collective-permute-start | bytes 3145736 | tf_op jit(solution)/shard_map/ppermute | solution.py:30
  10.2 17.7 %collective-permute-start.6 = (bf16[64,2048]{1,0:T(8,128)(2,1)}, bf16[64,2048]{1,0:T(8,128)(2,1)}, u32[]{:S(2)}, u32[]{:S(2)}) collective-permute-start(bf16[64,2048]{1,0:T(8,128)(2,1)} %get-tuple-element.87.refs_0_), channel_id=1, source_target_pairs={{0,2},{1,3},{2,0},{3,1},{4,6},{5,7},{6,4},{7,5},{8,10},{9,11},{10,... | collective-permute-start | bytes 786440 | tf_op jit(solution)/shard_map/ppermute | solution.py:30
  12.9 15.2 %collective-permute-start.1 = (bf16[64,2048]{1,0:T(8,128)(2,1)}, bf16[64,2048]{1,0:T(8,128)(2,1)}, u32[]{:S(2)}, u32[]{:S(2)}) collective-permute-start(bf16[64,2048]{1,0:T(8,128)(2,1)} %get-tuple-element.87.refs_0_), channel_id=1, source_target_pairs={{0,4},{1,5},{2,6},{3,7},{4,0},{5,1},{6,2},{7,3},{8,12},{9,13},{10,... | collective-permute-start | bytes 786440 | tf_op jit(solution)/shard_map/ppermute | solution.py:30
  15.5 35.9 %copy-start.9 = (f32[1,64,128]{2,1,0:T(8,128)S(1)}, f32[1,64,128]{2,1,0:T(8,128)}, u32[]{:S(2)}) copy-start(f32[1,64,128]{2,1,0:T(8,128)} %param.11) | copy-start | bytes 98308
  15.5 42.1 %copy-start.18 = (bf16[64,2048]{1,0:T(8,128)(2,1)S(1)}, bf16[64,2048]{1,0:T(8,128)(2,1)}, u32[]{:S(2)}) copy-start(bf16[64,2048]{1,0:T(8,128)(2,1)} %get-tuple-element.99.refs_0_) | copy-start | bytes 786436
  23.4 4.9 %collective-permute-start.8 = (bf16[144,320]{1,0:T(8,128)(2,1)S(1)}, bf16[144,320]{1,0:T(8,128)(2,1)S(1)}, u32[]{:S(2)}, u32[]{:S(2)}) collective-permute-start(bf16[144,320]{1,0:T(8,128)(2,1)S(1)} %fusion.4.refs_0_), channel_id=1, source_target_pairs={{0,4},{1,5},{2,6},{3,7},{8,12},{9,13},{10,14},{11,15},{16,20},{17,... | collective-permute-start | bytes 276488 | tf_op jit(solution)/shard_map/ppermute | solution.py:25
  25.7 4.7 %collective-permute-start.7 = (bf16[144,320]{1,0:T(8,128)(2,1)S(1)}, bf16[144,320]{1,0:T(8,128)(2,1)S(1)}, u32[]{:S(2)}, u32[]{:S(2)}) collective-permute-start(bf16[144,320]{1,0:T(8,128)(2,1)S(1)} %fusion.4.refs_0_), channel_id=1, source_target_pairs={{0,2},{1,3},{2,4},{3,5},{4,6},{5,7},{8,10},{9,11},{10,12},{11,13},... | collective-permute-start | bytes 276488 | tf_op jit(solution)/shard_map/ppermute | solution.py:25
  30.3 11.5 %collective-permute-start.9 = (bf16[64,2048]{1,0:T(8,128)(2,1)}, bf16[64,2048]{1,0:T(8,128)(2,1)S(1)}, u32[]{:S(2)}, u32[]{:S(2)}) collective-permute-start(bf16[64,2048]{1,0:T(8,128)(2,1)} %collective-permute-done.1.refs_1_), channel_id=1, source_target_pairs={{0,2},{1,3},{2,0},{3,1},{4,6},{5,7},{6,4},{7,5},{8,10},{9,11},{10,... | collective-permute-start | bytes 786440 | tf_op jit(solution)/shard_map/ppermute | solution.py:30
  35.2 16.1 %collective-permute-start.14 = (bf16[64,2048]{1,0:T(8,128)(2,1)}, bf16[64,2048]{1,0:T(8,128)(2,1)}, u32[]{:S(2)}, u32[]{:S(2)}) collective-permute-start(bf16[64,2048]{1,0:T(8,128)(2,1)} %get-tuple-element.99.refs_0_), channel_id=1, source_target_pairs={{0,6},{1,7},{2,4},{3,5},{4,2},{5,3},{6,0},{7,1},{8,14},{9,15},{10,... | collective-permute-start | bytes 786440 | tf_op jit(solution)/shard_map/ppermute | solution.py:30
  38.6 19.0 %collective-permute-start.13 = (bf16[64,2048]{1,0:T(8,128)(2,1)}, bf16[64,2048]{1,0:T(8,128)(2,1)}, u32[]{:S(2)}, u32[]{:S(2)}) collective-permute-start(bf16[64,2048]{1,0:T(8,128)(2,1)} %get-tuple-element.99.refs_0_), channel_id=1, source_target_pairs={{0,2},{1,3},{2,0},{3,1},{4,6},{5,7},{6,4},{7,5},{8,10},{9,11},{10,... | collective-permute-start | bytes 786440 | tf_op jit(solution)/shard_map/ppermute | solution.py:30
  38.6 19.0 %collective-permute-start.12 = (bf16[64,2048]{1,0:T(8,128)(2,1)}, bf16[64,2048]{1,0:T(8,128)(2,1)}, u32[]{:S(2)}, u32[]{:S(2)}) collective-permute-start(bf16[64,2048]{1,0:T(8,128)(2,1)} %get-tuple-element.99.refs_0_), channel_id=1, source_target_pairs={{0,4},{1,5},{2,6},{3,7},{4,0},{5,1},{6,2},{7,3},{8,12},{9,13},{10,... | collective-permute-start | bytes 786440 | tf_op jit(solution)/shard_map/ppermute | solution.py:30
  40.4 20.0 %collective-permute-start.11 = (bf16[432,320]{1,0:T(8,128)(2,1)}, bf16[432,320]{1,0:T(8,128)(2,1)}, u32[]{:S(2)}, u32[]{:S(2)}) collective-permute-start(bf16[432,320]{1,0:T(8,128)(2,1)} %stack.78.own), channel_id=1, source_target_pairs={{0,1},{1,0},{2,3},{3,2},{4,5},{5,4},{6,7},{7,6},{8,9},{9,8},{10,11... | collective-permute-start | bytes 829448 | tf_op jit(solution)/shard_map/ppermute | solution.py:30
  44.8 17.7 %copy-start.5 = (bf16[1,128,4096]{2,1,0:T(8,128)(2,1)S(1)}, bf16[1,128,4096]{2,1,0:T(8,128)(2,1)}, u32[]{:S(2)}) copy-start(bf16[1,128,4096]{2,1,0:T(8,128)(2,1)} %param.9) | copy-start | bytes 3145732
  44.8 17.7 %copy-start.20 = (s32[5]{0:T(128)S(1)}, s32[5]{0:T(128)}, u32[]{:S(2)}) copy-start(s32[5]{0:T(128)} %stack.64.place) | copy-start | bytes 64
  44.8 33.9 %collective-permute-start.10 = (bf16[256,2048]{1,0:T(8,128)(2,1)}, bf16[256,2048]{1,0:T(8,128)(2,1)}, u32[]{:S(2)}, u32[]{:S(2)}) collective-permute-start(bf16[256,2048]{1,0:T(8,128)(2,1)} %stack.77.weight), channel_id=1, source_target_pairs={{0,8},{8,0},{16,24},{24,16},{1,9},{9,1},{17,25},{25,17},{2,10},{10... | collective-permute-start | bytes 3145736 | tf_op jit(solution)/shard_map/ppermute | solution.py:30
  51.3 11.1 %collective-permute-start.5 = (f32[64,128]{1,0:T(8,128)S(1)}, f32[64,128]{1,0:T(8,128)S(1)}, u32[]{:S(2)}, u32[]{:S(2)}) collective-permute-start(f32[64,128]{1,0:T(8,128)S(1)} %bitcast.66), channel_id=1, source_target_pairs={{0,1},{1,0},{2,3},{3,2},{4,5},{5,4},{6,7},{7,6},{8,9},{9,8},{10,11... | collective-permute-start | bytes 98312 | tf_op jit(solution)/shard_map/ppermute | solution.py:30
  58.8 33.5 %collective-permute-start.17 = (bf16[256,2048]{1,0:T(8,128)(2,1)}, bf16[256,2048]{1,0:T(8,128)(2,1)S(1)}, u32[]{:S(2)}, u32[]{:S(2)}) collective-permute-start(bf16[256,2048]{1,0:T(8,128)(2,1)} %stack.77.weight), channel_id=1, source_target_pairs={{0,16},{8,24},{16,0},{24,8},{1,17},{9,25},{17,1},{25,9},{2,18},{10... | collective-permute-start | bytes 3145736 | tf_op jit(solution)/shard_map/ppermute | solution.py:30
  63.8 15.0 %copy-start.8 = (bf16[128,4096]{1,0:T(8,128)(2,1)S(1)}, bf16[128,4096]{1,0:T(8,128)(2,1)}, u32[]{:S(2)}) copy-start(bf16[128,4096]{1,0:T(8,128)(2,1)} %copy-done.6) | copy-start | bytes 3145732
  76.7 30.9 %collective-permute-start.18 = (f32[128,2048]{1,0:T(8,128)S(1)}, f32[128,2048]{1,0:T(8,128)S(1)}, u32[]{:S(2)}, u32[]{:S(2)}) collective-permute-start(f32[128,2048]{1,0:T(8,128)S(1)} %get-tuple-element.105), channel_id=1, source_target_pairs={{0,16},{8,24},{16,0},{24,8},{1,17},{9,25},{17,1},{25,9},{2,18},{10... | collective-permute-start | bytes 3145736 | tf_op jit(solution)/shard_map/ppermute | solution.py:30
  77.3 32.8 %collective-permute-start.16 = (f32[128,2048]{1,0:T(8,128)S(1)}, f32[128,2048]{1,0:T(8,128)S(1)}, u32[]{:S(2)}, u32[]{:S(2)}) collective-permute-start(f32[128,2048]{1,0:T(8,128)S(1)} %get-tuple-element.104), channel_id=1, source_target_pairs={{0,8},{8,0},{16,24},{24,16},{1,9},{9,1},{17,25},{25,17},{2,10},{10... | collective-permute-start | bytes 3145736 | tf_op jit(solution)/shard_map/ppermute | solution.py:30
  91.7 34.1 %collective-permute-start.15 = (f32[128,2048]{1,0:T(8,128)S(1)}, f32[128,2048]{1,0:T(8,128)S(1)}, u32[]{:S(2)}, u32[]{:S(2)}) collective-permute-start(f32[128,2048]{1,0:T(8,128)S(1)} %get-tuple-element.103), channel_id=1, source_target_pairs={{0,8},{8,0},{16,24},{24,16},{1,9},{9,1},{17,25},{25,17},{2,10},{10... | collective-permute-start | bytes 3145736 | tf_op jit(solution)/shard_map/ppermute | solution.py:30
  99.5 19.9 %collective-permute-start.20 = (f32[128,1024]{1,0:T(8,128)S(1)}, f32[128,1024]{1,0:T(8,128)S(1)}, u32[]{:S(2)}, u32[]{:S(2)}) collective-permute-start(f32[128,1024]{1,0:T(8,128)S(1)} %get-tuple-element.115), channel_id=1, source_target_pairs={{0,16},{8,24},{16,0},{24,8},{1,17},{9,25},{17,1},{25,9},{2,18},{10... | collective-permute-start | bytes 1572872 | tf_op jit(solution)/shard_map/ppermute | solution.py:30
  108.6 28.5 %collective-permute-start.26 = (f32[128,1024]{1,0:T(8,128)S(1)}, f32[128,1024]{1,0:T(8,128)S(1)}, u32[]{:S(2)}, u32[]{:S(2)}) collective-permute-start(f32[128,1024]{1,0:T(8,128)S(1)} %get-tuple-element.177), channel_id=1, source_target_pairs={{0,8},{8,0},{16,24},{24,16},{1,9},{9,1},{17,25},{25,17},{2,10},{10... | collective-permute-start | bytes 1572872 | tf_op jit(solution)/shard_map/ppermute | solution.py:30
  110.1 45.8 %collective-permute-start.31 = (f32[128,1024]{1,0:T(8,128)}, f32[128,1024]{1,0:T(8,128)}, u32[]{:S(2)}, u32[]{:S(2)}) collective-permute-start(f32[128,1024]{1,0:T(8,128)} %get-tuple-element.176), channel_id=1, source_target_pairs={{0,8},{8,0},{16,24},{24,16},{1,9},{9,1},{17,25},{25,17},{2,10},{10... | collective-permute-start | bytes 1572872 | tf_op jit(solution)/shard_map/ppermute | solution.py:30
  117.8 27.0 %collective-permute-start.19 = (f32[128,1024]{1,0:T(8,128)S(1)}, f32[128,1024]{1,0:T(8,128)S(1)}, u32[]{:S(2)}, u32[]{:S(2)}) collective-permute-start(f32[128,1024]{1,0:T(8,128)S(1)} %get-tuple-element.113), channel_id=1, source_target_pairs={{0,16},{8,24},{16,0},{24,8},{1,17},{9,25},{17,1},{25,9},{2,18},{10... | collective-permute-start | bytes 1572872 | tf_op jit(solution)/shard_map/ppermute | solution.py:30
  138.0 17.9 %collective-permute-start.27 = (f32[128,1024]{1,0:T(8,128)}, f32[128,1024]{1,0:T(8,128)}, u32[]{:S(2)}, u32[]{:S(2)}) collective-permute-start(f32[128,1024]{1,0:T(8,128)} %add_add_fusion.2), channel_id=1, source_target_pairs={{0,2},{1,3},{2,0},{3,1},{4,6},{5,7},{6,4},{7,5},{8,10},{9,11},{10,... | collective-permute-start | bytes 1572872 | tf_op jit(solution)/shard_map/ppermute | solution.py:30
  142.8 15.2 %collective-permute-start.25 = (f32[128,1024]{1,0:T(8,128)}, f32[128,1024]{1,0:T(8,128)}, u32[]{:S(2)}, u32[]{:S(2)}) collective-permute-start(f32[128,1024]{1,0:T(8,128)} %get-tuple-element.144), channel_id=1, source_target_pairs={{0,16},{8,24},{16,0},{24,8},{1,17},{9,25},{17,1},{25,9},{2,18},{10... | collective-permute-start | bytes 1572872 | tf_op jit(solution)/shard_map/ppermute | solution.py:30
  144.3 17.5 %collective-permute-start.30 = (f32[128,1024]{1,0:T(8,128)}, f32[128,1024]{1,0:T(8,128)}, u32[]{:S(2)}, u32[]{:S(2)}) collective-permute-start(f32[128,1024]{1,0:T(8,128)} %get-tuple-element.151), channel_id=1, source_target_pairs={{0,16},{8,24},{16,0},{24,8},{1,17},{9,25},{17,1},{25,9},{2,18},{10... | collective-permute-start | bytes 1572872 | tf_op jit(solution)/shard_map/ppermute | solution.py:30
  155.9 6.0 %collective-permute-start.22 = (f32[432,320]{0,1:T(8,128)}, f32[432,320]{0,1:T(8,128)}, u32[]{:S(2)}, u32[]{:S(2)}) collective-permute-start(f32[432,320]{0,1:T(8,128)} %copy.39), channel_id=1, source_target_pairs={{0,1},{1,0},{2,3},{3,2},{4,5},{5,4},{6,7},{7,6},{8,9},{9,8},{10,11... | collective-permute-start | bytes 1658888 | tf_op jit(solution)/shard_map/ppermute | solution.py:30
  158.0 20.7 %collective-permute-start.32 = (f32[128,1024]{1,0:T(8,128)}, f32[128,1024]{1,0:T(8,128)}, u32[]{:S(2)}, u32[]{:S(2)}) collective-permute-start(f32[128,1024]{1,0:T(8,128)} %add_add_fusion), channel_id=1, source_target_pairs={{0,2},{1,3},{2,0},{3,1},{4,6},{5,7},{6,4},{7,5},{8,10},{9,11},{10,... | collective-permute-start | bytes 1572872 | tf_op jit(solution)/shard_map/ppermute | solution.py:30
  159.6 16.4 %collective-permute-start.28 = (f32[64,1024]{1,0:T(8,128)S(1)}, f32[64,1024]{1,0:T(8,128)}, u32[]{:S(2)}, u32[]{:S(2)}) collective-permute-start(f32[64,1024]{1,0:T(8,128)S(1)} %slice.95), channel_id=1, source_target_pairs={{0,4},{1,5},{2,6},{3,7},{4,0},{5,1},{6,2},{7,3},{8,12},{9,13},{10,... | collective-permute-start | bytes 786440 | tf_op jit(solution)/shard_map/ppermute | solution.py:30
  161.6 39.7 %collective-permute-start.21 = (bf16[128,6144]{1,0:T(8,128)(2,1)S(1)}, bf16[128,6144]{1,0:T(8,128)(2,1)S(1)}, u32[]{:S(2)}, u32[]{:S(2)}) collective-permute-start(bf16[128,6144]{1,0:T(8,128)(2,1)S(1)} %copy-done.4), channel_id=1, source_target_pairs={{0,1},{1,0},{2,3},{3,2},{4,5},{5,4},{6,7},{7,6},{8,9},{9,8},{10,11... | collective-permute-start | bytes 4718600 | tf_op jit(solution)/shard_map/ppermute | solution.py:30
  165.6 19.1 %collective-permute-start.23 = (f32[128,320]{1,0:T(8,128)S(1)}, f32[128,320]{1,0:T(8,128)S(1)}, u32[]{:S(2)}, u32[]{:S(2)}) collective-permute-start(f32[128,320]{1,0:T(8,128)S(1)} %get-tuple-element.180), channel_id=1, source_target_pairs={{2,0},{3,1},{4,2},{5,3},{6,4},{7,5},{10,8},{11,9},{12,10},{13,11},... | collective-permute-start | bytes 491528 | tf_op jit(solution)/shard_map/ppermute | solution.py:25
  166.9 29.1 %collective-permute-start.24 = (f32[128,320]{1,0:T(8,128)S(1)}, f32[128,320]{1,0:T(8,128)S(1)}, u32[]{:S(2)}, u32[]{:S(2)}) collective-permute-start(f32[128,320]{1,0:T(8,128)S(1)} %get-tuple-element.181), channel_id=1, source_target_pairs={{4,0},{5,1},{6,2},{7,3},{12,8},{13,9},{14,10},{15,11},{20,16},{21,... | collective-permute-start | bytes 491528 | tf_op jit(solution)/shard_map/ppermute | solution.py:25
  177.0 19.8 %copy-start.21 = (s32[5]{0:T(128)S(1)}, s32[5]{0:T(128)}, u32[]{:S(2)}) copy-start(s32[5]{0:T(128)} %stack.64.place) | copy-start | bytes 64
  180.0 21.2 %collective-permute-start.33 = (f32[64,1024]{1,0:T(8,128)S(1)}, f32[64,1024]{1,0:T(8,128)S(1)}, u32[]{:S(2)}, u32[]{:S(2)}) collective-permute-start(f32[64,1024]{1,0:T(8,128)S(1)} %slice.101), channel_id=1, source_target_pairs={{0,4},{1,5},{2,6},{3,7},{4,0},{5,1},{6,2},{7,3},{8,12},{9,13},{10,... | collective-permute-start | bytes 786440 | tf_op jit(solution)/shard_map/ppermute | solution.py:30
  182.0 14.7 %collective-permute-start.29 = (f32[32,1024]{1,0:T(8,128)S(1)}, f32[32,1024]{1,0:T(8,128)S(1)}, u32[]{:S(2)}, u32[]{:S(2)}) collective-permute-start(f32[32,1024]{1,0:T(8,128)S(1)} %get-tuple-element.184), channel_id=1, source_target_pairs={{0,1},{1,0},{2,3},{3,2},{4,5},{5,4},{6,7},{7,6},{8,9},{9,8},{10,11... | collective-permute-start | bytes 393224 | tf_op jit(solution)/shard_map/ppermute | solution.py:30
  197.3 12.1 %collective-permute-start.39 = (f32[32,2048]{1,0:T(8,128)S(1)}, f32[32,2048]{1,0:T(8,128)S(1)}, u32[]{:S(2)}, u32[]{:S(2)}) collective-permute-start(f32[32,2048]{1,0:T(8,128)S(1)} %join_cores.2.refs_0_), channel_id=1, source_target_pairs={{0,24},{8,16},{16,8},{24,0},{1,25},{9,17},{17,9},{25,1},{2,26},{10... | collective-permute-start | bytes 786440 | tf_op jit(solution)/shard_map/ppermute | solution.py:30
  203.7 3.0 %collective-permute-start.34 = (f32[32,1024]{1,0:T(8,128)S(1)}, f32[32,1024]{1,0:T(8,128)S(1)}, u32[]{:S(2)}, u32[]{:S(2)}) collective-permute-start(f32[32,1024]{1,0:T(8,128)S(1)} %get-tuple-element.157), channel_id=1, source_target_pairs={{0,1},{1,0},{2,3},{3,2},{4,5},{5,4},{6,7},{7,6},{8,9},{9,8},{10,11... | collective-permute-start | bytes 393224 | tf_op jit(solution)/shard_map/ppermute | solution.py:30
  203.7 9.1 %collective-permute-start.37 = (f32[32,2048]{1,0:T(8,128)S(1)}, f32[32,2048]{1,0:T(8,128)S(1)}, u32[]{:S(2)}, u32[]{:S(2)}) collective-permute-start(f32[32,2048]{1,0:T(8,128)S(1)} %join_cores.2.refs_0_), channel_id=1, source_target_pairs={{0,16},{8,24},{16,0},{24,8},{1,17},{9,25},{17,1},{25,9},{2,18},{10... | collective-permute-start | bytes 786440 | tf_op jit(solution)/shard_map/ppermute | solution.py:30
  205.2 9.1 %collective-permute-start.35 = (f32[32,2048]{1,0:T(8,128)S(1)}, f32[32,2048]{1,0:T(8,128)S(1)}, u32[]{:S(2)}, u32[]{:S(2)}) collective-permute-start(f32[32,2048]{1,0:T(8,128)S(1)} %join_cores.2.refs_0_), channel_id=1, source_target_pairs={{0,8},{8,0},{16,24},{24,16},{1,9},{9,1},{17,25},{25,17},{2,10},{10... | collective-permute-start | bytes 786440 | tf_op jit(solution)/shard_map/ppermute | solution.py:30
  207.3 12.7 %collective-permute-start.40 = (f32[32,2048]{1,0:T(8,128)S(1)}, f32[32,2048]{1,0:T(8,128)S(1)}, u32[]{:S(2)}, u32[]{:S(2)}) collective-permute-start(f32[32,2048]{1,0:T(8,128)S(1)} %join_cores.3.refs_1_), channel_id=1, source_target_pairs={{0,24},{8,16},{16,8},{24,0},{1,25},{9,17},{17,9},{25,1},{2,26},{10... | collective-permute-start | bytes 786440 | tf_op jit(solution)/shard_map/ppermute | solution.py:30
  208.1 15.5 %collective-permute-start.38 = (f32[32,2048]{1,0:T(8,128)S(1)}, f32[32,2048]{1,0:T(8,128)S(1)}, u32[]{:S(2)}, u32[]{:S(2)}) collective-permute-start(f32[32,2048]{1,0:T(8,128)S(1)} %join_cores.3.refs_1_), channel_id=1, source_target_pairs={{0,16},{8,24},{16,0},{24,8},{1,17},{9,25},{17,1},{25,9},{2,18},{10... | collective-permute-start | bytes 786440 | tf_op jit(solution)/shard_map/ppermute | solution.py:30
  210.1 14.9 %collective-permute-start.36 = (f32[32,2048]{1,0:T(8,128)S(1)}, f32[32,2048]{1,0:T(8,128)S(1)}, u32[]{:S(2)}, u32[]{:S(2)}) collective-permute-start(f32[32,2048]{1,0:T(8,128)S(1)} %join_cores.3.refs_1_), channel_id=1, source_target_pairs={{0,8},{8,0},{16,24},{24,16},{1,9},{9,1},{17,25},{25,17},{2,10},{10... | collective-permute-start | bytes 786440 | tf_op jit(solution)/shard_map/ppermute | solution.py:30
  (33 other events, 191.7 us)

commit v5 on v4

--- a/solution.py
+++ b/solution.py
@@ -521,45 +521,47 @@
 
     partners = halving_order(n_ctx)[::2]
 
-    def over_chips(start, onward, *earlier):
+    def over_chips(start):
         at_step = {0: start}
         for step in range(4, n_ctx, 4):
             at_step[step] = exchange(start, "ctx", step)
         at_step[2] = exchange(start, "ctx", 2)
         for step in range(4, n_ctx, 4):
-            if onward:
-                forwarded = after(at_step[step], at_step[2], *earlier)
-                at_step[step + 2] = exchange(forwarded, "ctx", 2)
-            else:
-                at_step[step + 2] = exchange(start, "ctx", step + 2)
+            at_step[step + 2] = exchange(after(at_step[step], at_step[2]), "ctx", 2)
         return [at_step[partner] for partner in partners], at_step[n_ctx - 4]
 
     def joined(pieces):
         return stack(pieces, (tuple((index, 0) for index in range(len(pieces))),), part_cols)[0]
 
-    near_pieces, last = over_chips(chip_rows[0], True, *bundles[1:])
-    far_pieces, _ = over_chips(after(chip_rows[1], last), False)
-    weights = {0: joined(near_pieces), far: joined(far_pieces)}
-    for t in range(1, far):
-        weights[t] = exchange(weights[0], "dp", t)
+    near_pieces, last = over_chips(chip_rows[0])
+    far_pieces, _ = over_chips(after(chip_rows[1], last))
     log_total = after(log_total, last)[0]
     sibling.append(exchange(log_total, "ctx", 1))
     own.append(log_total)
     for arrays in (own, sibling):
         arrays[3] = arrays[3].reshape(heads // 2, 2, group_len)
 
+    weights = {0: joined([after(near_pieces[0], sib_bundles, sibling[3])] + near_pieces[1:])}
+    for t in range(1, far):
+        weights[t] = exchange(weights[0], "dp", t)
     earlier = None
     latents, ropes = [], []
     weight_grads = {t: ([], []) for t in range(n_dp)}
     bits = [1 << b for b in range(n_dp.bit_length() - 1)]
     orders = (bits, bits[::-1])
     first_sums = [{t: [] for t in range(n_dp) if t & order[0]} for order in orders]
-    units = [(t, 0, pairs) for t in [far] + list(range(1, far - 1))]
-    units += [(t, start, pairs // 2) for t in (far - 1, 0) for start in (0, pairs // 2)]
+    half_pairs = pairs // 2
+    units = [(0, 0, half_pairs)] + [(t, 0, pairs) for t in [far] + list(range(1, far - 1))]
+    units += [(far - 1, 0, half_pairs), (far - 1, half_pairs, half_pairs)]
+    units.append((0, half_pairs, half_pairs))
     for t, start, count in units:
+        if t == far:
+            weights[far] = joined([after(far_pieces[0], latents[-1])] + far_pieces[1:])
         weight = weights[t]
-        if t == 0:
-            weight = after(weight, *[sent[u][-1 if start else 0] for sent in first_sums for u in sent])
+        if t == 0 and start:
+            weight = after(weight, *[piece for sent in first_sums for u in sent for piece in sent[u]])
+        if t == 1 and not start:
+            weight = after(weight, *[weights[near] for near in range(2, far)])
         if t == far - 1 and start:
             weight = after(weight, *[sent[far][0] for sent in first_sums])
         rest = chunk_backward(
@@ -605,7 +607,9 @@
                 leaving = [total(addends[t], half) for half in range(2)]
                 if side == 0:
                     behind = (first_sums[0][order[0]][0], last_sums[0])
-                    leaving = [after(half, there) for half, there in zip(leaving, behind)]
+                else:
+                    behind = [weight_grads[far - 1][side][0]] * 2
+                leaving = [after(half, there) for half, there in zip(leaving, behind)]
                 arrived[t ^ bit] = [exchange(half, "dp", bit) for half in leaving]
             addends = {t: addends[t] + [more] for t, more in arrived.items()}
         sums.append(addends[0])
@@ -628,15 +632,14 @@
         if half:
             sums = [[[after(piece, arrived) for piece in pieces] for pieces in side] for side in sums]
         first, second = [total(side, half) for side in sums]
-        arrived = exchange(second, "ctx", ctx_bits[0])
+        there = (sums[0][-1][half], latents[-1]) if half == 0 else (sums[0][-1][half],)
+        arrived = exchange(after(second, *there), "ctx", ctx_bits[0])
         rows = first + arrived
         for bit in ctx_bits[1:]:
             rows = halve(rows, "ctx", bit)
-        crossing = rows[lat_block:]
-        if half:
-            crossing = after(crossing, grad_rows, grad_nope)
-        piece = join_cores(place, rows[:lat_block], exchange(crossing, "ctx", 1))
+        piece = join_cores(place, rows[:lat_block], exchange(rows[lat_block:], "ctx", 1))
         finished.append([piece] + [exchange(piece, "dp", t) for t in range(1, n_dp)])
+    finished[0][0] = after(finished[0][0], grad_rows, grad_nope)
     grad_weight = lay_out(place, [piece for both in zip(*finished) for piece in both])
     return (grad_nope[None], grad_rope[None], grad_rows[None], grad_weight)
 

time: 229 us -> 229 us (level)
  waiting for transfers between devices: 69.2 us -> 55.9 us
  starting transfers between devices: 52 us -> 58.3 us
  Pallas kernels: 74 us -> 77.4 us
  local copies, waits for them, and re-layouts: 14.7 us -> 17.9 us
    ppermute x4, waiting for transfers between devices: 16.2 us -> 2 us  [from_behind(): lax.ppermute(value, axis, [(source, source + steps) for source in range(i...]
    ppermute x37, starting transfers between devices: 45.1 us -> 50.2 us  [exchange(): lax.ppermute(value, axis, [(source, source ^ bits) for source in range(co...]
    unnamed x81 -> x71, local copies, waits for them, and re-layouts: 6.55 us -> 8.66 us
  transfers between devices with their start and end apart: 41 -> 41, of which waited for: 20 -> 17; matrix products, arithmetic and copies ran while one was open for 11% -> 12% of each run, Pallas kernels for 30% -> 31%
where the time goes in v5:
time: 229 us; the launch traced here: 228 us
  Pallas kernels  77.4 us (34%)
  starting transfers between devices  58.3 us (25%)
  waiting for transfers between devices  55.9 us (24%)
  local copies, waits for them, and re-layouts  17.9 us (8%)
  other arithmetic  17.6 us (8%)
    pallas_call x6, Pallas kernels, chunk_backward(): pl.pallas_call(functools.partial(heads_kernel, earlier=len(aliases)), gri...  56.1 us
    ppermute x37, waiting for transfers between devices, exchange(): lax.ppermute(value, axis, [(source, source ^ bits) for source in range(co...  53.9 us
    ppermute x37, starting transfers between devices, exchange(): lax.ppermute(value, axis, [(source, source ^ bits) for source in range(co...  50.2 us
    unnamed x71, local copies, waits for them, and re-layouts  8.66 us
    ppermute x4, starting transfers between devices, from_behind(): lax.ppermute(value, axis, [(source, source + steps) for source in range(i...  8.12 us
    add x4, other arithmetic, total(): left + right  5.03 us
    pallas_call x2, Pallas kernels, weight_parts(): pl.pallas_call(join_rows_kernel if joins else leave_kernel, grid_spec=plt...  4.91 us
    pallas_call x3, Pallas kernels, stack(): pl.pallas_call(functools.partial(stack_kernel, arrangement=arrangement),...  4.86 us
  transfers between devices with their start and end apart: 41, of which 17 were waited for; matrix products, arithmetic and copies ran while one was open for 12% of the time, Pallas kernels for 31%

profile of v5, /device:TPU:0, one launch (start us, length us, event | category | flops | bytes accessed | tf_op | source)
XLA Modules:
  0.0 228.2 jit_solution(10417991308894493409)
XLA Ops:
  1.3 2.4 %weight_parts.2 = bf16[32,4096]{1,0:T(8,128)(2,1)} custom-call(s32[5]{0:T(128)} %stack.64.place, bf16[32,16384]{1,0:T(8,128)(2,1)} %distant.3, bf16[32,16384]{1,0:T(8,128)(2,1)} %distant.3), custom_call_target="tpu_custom_call" | custom-call | bytes 1000000 | tf_op jit(solution)/shard_map/weight_parts/pallas_call | solution.py:263
  7.6 2.6 %weight_parts.3 = (bf16[64,2048]{1,0:T(8,128)(2,1)}, bf16[64,2048]{1,0:T(8,128)(2,1)}) custom-call(s32[5]{0:T(128)} %stack.64.place, bf16[32,16384]{1,0:T(8,128)(2,1)} %distant.3, bf16[32,16384]{1,0:T(8,128)(2,1)} %distant.3, bf16[32,4096]{1,0:T(8,128)(2,1)} %copy-done.31), custom_call_target="tpu_custom_call" | custom-call | bytes 1000000 | tf_op jit(solution)/shard_map/weight_parts/pallas_call | solution.py:263
  10.1 2.7 %collective-permute-start.9 = (bf16[64,2048]{1,0:T(8,128)(2,1)}, bf16[64,2048]{1,0:T(8,128)(2,1)S(1)}, u32[]{:S(2)}, u32[]{:S(2)}) collective-permute-start(bf16[64,2048]{1,0:T(8,128)(2,1)} %get-tuple-element.100.refs_0_), channel_id=1, source_target_pairs={{0,2},{1,3},{2,0},{3,1},{4,6},{5,7},{6,4},{7,5},{8,10},{9,11},{10,... | collective-permute-start | bytes 786440 | tf_op jit(solution)/shard_map/ppermute | solution.py:30
  12.9 2.6 %collective-permute-start.1 = (bf16[64,2048]{1,0:T(8,128)(2,1)}, bf16[64,2048]{1,0:T(8,128)(2,1)}, u32[]{:S(2)}, u32[]{:S(2)}) collective-permute-start(bf16[64,2048]{1,0:T(8,128)(2,1)} %get-tuple-element.100.refs_0_), channel_id=1, source_target_pairs={{0,4},{1,5},{2,6},{3,7},{4,0},{5,1},{6,2},{7,3},{8,12},{9,13},{10,... | collective-permute-start | bytes 786440 | tf_op jit(solution)/shard_map/ppermute | solution.py:30
  19.7 1.6 copy.37
  23.2 2.9 %collective-permute-start.7 = (bf16[144,320]{1,0:T(8,128)(2,1)S(1)}, bf16[144,320]{1,0:T(8,128)(2,1)}, u32[]{:S(2)}, u32[]{:S(2)}) collective-permute-start(bf16[144,320]{1,0:T(8,128)(2,1)S(1)} %fusion.4.refs_0_), channel_id=1, source_target_pairs={{0,4},{1,5},{2,6},{3,7},{8,12},{9,13},{10,14},{11,15},{16,20},{17,... | collective-permute-start | bytes 276488 | tf_op jit(solution)/shard_map/ppermute | solution.py:25
  26.1 2.7 %collective-permute-start.6 = (bf16[144,320]{1,0:T(8,128)(2,1)S(1)}, bf16[144,320]{1,0:T(8,128)(2,1)}, u32[]{:S(2)}, u32[]{:S(2)}) collective-permute-start(bf16[144,320]{1,0:T(8,128)(2,1)S(1)} %fusion.4.refs_0_), channel_id=1, source_target_pairs={{0,2},{1,3},{2,4},{3,5},{4,6},{5,7},{8,10},{9,11},{10,12},{11,13},... | collective-permute-start | bytes 276488 | tf_op jit(solution)/shard_map/ppermute | solution.py:25
  29.4 1.5 collective-permute-start.10
  31.3 1.7 stack.77.own
  34.1 3.4 %collective-permute-start.14 = (bf16[64,2048]{1,0:T(8,128)(2,1)}, bf16[64,2048]{1,0:T(8,128)(2,1)}, u32[]{:S(2)}, u32[]{:S(2)}) collective-permute-start(bf16[64,2048]{1,0:T(8,128)(2,1)} %get-tuple-element.110.refs_0_), channel_id=1, source_target_pairs={{0,2},{1,3},{2,0},{3,1},{4,6},{5,7},{6,4},{7,5},{8,10},{9,11},{10,... | collective-permute-start | bytes 786440 | tf_op jit(solution)/shard_map/ppermute | solution.py:30
  37.5 2.0 collective-permute-start.13
  41.7 2.1 stack.78.weight
  43.8 1.5 collective-permute-start.12
  47.5 2.9 %collective-permute-done.14.refs_2_ = bf16[64,2048]{1,0:T(8,128)(2,1)} collective-permute-done((bf16[64,2048]{1,0:T(8,128)(2,1)}, bf16[64,2048]{1,0:T(8,128)(2,1)}, u32[]{:S(2)}, u32[]{:S(2)}) %collective-permute-start.14) | collective-permute-done | bytes 262176 | tf_op jit(solution)/shard_map/ppermute | solution.py:30
  50.5 3.8 %collective-permute-start.15 = (bf16[64,2048]{1,0:T(8,128)(2,1)}, bf16[64,2048]{1,0:T(8,128)(2,1)S(1)}, u32[]{:S(2)}, u32[]{:S(2)}) collective-permute-start(bf16[64,2048]{1,0:T(8,128)(2,1)} %collective-permute-done.13.refs_1_), channel_id=1, source_target_pairs={{0,2},{1,3},{2,0},{3,1},{4,6},{5,7},{6,4},{7,5},{8,10},{9,11},{10,... | collective-permute-start | bytes 786440 | tf_op jit(solution)/shard_map/ppermute | solution.py:30
  55.7 2.1 collect.1
  57.8 1.6 copy-done.2
  61.3 7.6 %heads_backward.6 = (bf16[128,8192]{1,0:T(8,128)(2,1)}, bf16[128,4096]{1,0:T(8,128)(2,1)}, bf16[128,6144]{1,0:T(8,128)(2,1)S(1)}, f32[128,1024]{1,0:T(8,128)S(1)...) custom-call(s32[5]{0:T(128)S(1)} %copy-done.21, bf16[128,8192]{1,0:T(8,128)(2,1)S(1)} %bitcast.46, ...), custom_call_target="tpu_custom_call" | custom-call | flops 200000000 | bytes 600000 | tf_op jit(solution)/shard_map/heads_backward/pallas_call | solution.py:157
  70.8 13.1 %heads_backward.7 = (bf16[128,8192]{1,0:T(8,128)(2,1)}, bf16[128,4096]{1,0:T(8,128)(2,1)}, bf16[128,6144]{1,0:T(8,128)(2,1)S(1)}, f32[128,2048]{1,0:T(8,128)S(1)...) custom-call(s32[5]{0:T(128)S(1)} %copy-done.21, ...), custom_call_target="tpu_custom_call", output_to_operand_aliasing={{0}: (14, {}), {1}: (15, {}), {2}: (16, {})} | custom-call | flops 400000000 | bytes 1200000 | tf_op jit(solution)/shard_map/heads_backward/pallas_call | solution.py:157
  85.4 1.5 collective-permute-start.19
  87.0 13.0 %heads_backward.8 = (bf16[128,8192]{1,0:T(8,128)(2,1)}, bf16[128,4096]{1,0:T(8,128)(2,1)}, bf16[128,6144]{1,0:T(8,128)(2,1)S(1)}, f32[128,2048]{1,0:T(8,128)S(1)...) custom-call(s32[5]{0:T(128)S(1)} %copy-done.21, ...), custom_call_target="tpu_custom_call", output_to_operand_aliasing={{0}: (14, {}), {1}: (15, {}), {2}: (16, {})} | custom-call | flops 400000000 | bytes 1200000 | tf_op jit(solution)/shard_map/heads_backward/pallas_call | solution.py:157
  100.5 9.5 %collective-permute-done.17 = f32[128,2048]{1,0:T(8,128)S(1)} collective-permute-done((f32[128,2048]{1,0:T(8,128)S(1)}, f32[128,2048]{1,0:T(8,128)S(1)}, u32[]{:S(2)}, u32[]{:S(2)}) %collective-permute-start.17) | collective-permute-done | bytes 1048608 | tf_op jit(solution)/shard_map/ppermute | solution.py:30
  110.0 7.4 %heads_backward.9 = (bf16[128,8192]{1,0:T(8,128)(2,1)}, bf16[128,4096]{1,0:T(8,128)(2,1)}, bf16[128,6144]{1,0:T(8,128)(2,1)S(1)}, f32[128,1024]{1,0:T(8,128)S(1)...) custom-call(s32[5]{0:T(128)S(1)} %copy-done.21, ...), custom_call_target="tpu_custom_call", output_to_operand_aliasing={{0}: (14, {}), {1}: (15, {}), {2}: (16, {})} | custom-call | flops 200000000 | bytes 600000 | tf_op jit(solution)/shard_map/heads_backward/pallas_call | solution.py:157
  117.4 1.5 collective-permute-start.18
  121.5 7.6 %heads_backward.10 = (bf16[128,8192]{1,0:T(8,128)(2,1)}, bf16[128,4096]{1,0:T(8,128)(2,1)}, bf16[128,6144]{1,0:T(8,128)(2,1)S(1)}, f32[128,1024]{1,0:T(8,128)S(1...) custom-call(s32[5]{0:T(128)S(1)} %copy-done.22, ...), custom_call_target="tpu_custom_call", output_to_operand_aliasing={{0}: (14, {}), {1}: (15, {}), {2}: (16, {})} | custom-call | flops 200000000 | bytes 600000 | tf_op jit(solution)/shard_map/heads_backward/pallas_call | solution.py:157
  130.6 1.9 collective-permute-done.16
  132.5 1.5 collective-permute-start.25
  135.5 8.2 %collective-permute-done.26 = f32[128,1024]{1,0:T(8,128)S(1)} collective-permute-done((f32[128,1024]{1,0:T(8,128)S(1)}, f32[128,1024]{1,0:T(8,128)S(1)}, u32[]{:S(2)}, u32[]{:S(2)}) %collective-permute-start.26) | collective-permute-done | bytes 524320 | tf_op jit(solution)/shard_map/ppermute | solution.py:30
  144.6 7.4 %heads_backward.11 = (bf16[128,8192]{1,0:T(8,128)(2,1)}, bf16[128,4096]{1,0:T(8,128)(2,1)}, bf16[128,6144]{1,0:T(8,128)(2,1)S(1)}, f32[128,1024]{1,0:T(8,128)S(1...) custom-call(s32[5]{0:T(128)S(1)} %copy-done.22, ...), custom_call_target="tpu_custom_call", output_to_operand_aliasing={{0}: (14, {}), {1}: (15, {}), {2}: (16, {})} | custom-call | flops 200000000 | bytes 600000 | tf_op jit(solution)/shard_map/heads_backward/pallas_call | solution.py:157
  152.2 1.6 collective-permute-start.30
  153.8 1.6 spread.1
  157.4 5.9 %collective-permute-done.27 = f32[128,1024]{1,0:T(8,128)} collective-permute-done((f32[128,1024]{1,0:T(8,128)}, f32[128,1024]{1,0:T(8,128)}, u32[]{:S(2)}, u32[]{:S(2)}) %collective-permute-start.27) | collective-permute-done | bytes 524320 | tf_op jit(solution)/shard_map/ppermute | solution.py:30
  163.3 2.2 add_add_fusion
  167.4 2.1 collective-permute-start.28
  169.5 2.2 copy.40
  171.7 1.5 add.120
  173.2 6.6 %collective-permute-done.28 = f32[64,1024]{1,0:T(8,128)} collective-permute-done((f32[64,1024]{1,0:T(8,128)S(1)}, f32[64,1024]{1,0:T(8,128)}, u32[]{:S(2)}, u32[]{:S(2)}) %collective-permute-start.28) | collective-permute-done | bytes 262176 | tf_op jit(solution)/shard_map/ppermute | solution.py:30
  182.6 3.2 %collective-permute-start.33 = (f32[64,1024]{1,0:T(8,128)S(1)}, f32[64,1024]{1,0:T(8,128)S(1)}, u32[]{:S(2)}, u32[]{:S(2)}) collective-permute-start(f32[64,1024]{1,0:T(8,128)S(1)} %slice.101), channel_id=1, source_target_pairs={{0,4},{1,5},{2,6},{3,7},{4,0},{5,1},{6,2},{7,3},{8,12},{9,13},{10,... | collective-permute-start | bytes 786440 | tf_op jit(solution)/shard_map/ppermute | solution.py:30
  189.1 2.5 %collective-permute-start.39 = (f32[32,2048]{1,0:T(8,128)S(1)}, f32[32,2048]{1,0:T(8,128)S(1)}, u32[]{:S(2)}, u32[]{:S(2)}) collective-permute-start(f32[32,2048]{1,0:T(8,128)S(1)} %join_cores.2.refs_0_), channel_id=1, source_target_pairs={{0,24},{8,16},{16,8},{24,0},{1,25},{9,17},{17,9},{25,1},{2,26},{10... | collective-permute-start | bytes 786440 | tf_op jit(solution)/shard_map/ppermute | solution.py:30
  191.6 5.1 %collective-permute-done.33 = f32[64,1024]{1,0:T(8,128)S(1)} collective-permute-done((f32[64,1024]{1,0:T(8,128)S(1)}, f32[64,1024]{1,0:T(8,128)S(1)}, u32[]{:S(2)}, u32[]{:S(2)}) %collective-permute-start.33) | collective-permute-done | bytes 262176 | tf_op jit(solution)/shard_map/ppermute | solution.py:30
  198.2 5.8 %collective-permute-start.37 = (f32[32,2048]{1,0:T(8,128)S(1)}, f32[32,2048]{1,0:T(8,128)}, u32[]{:S(2)}, u32[]{:S(2)}) collective-permute-start(f32[32,2048]{1,0:T(8,128)S(1)} %join_cores.2.refs_0_), channel_id=1, source_target_pairs={{0,16},{8,24},{16,0},{24,8},{1,17},{9,25},{17,1},{25,9},{2,18},{10... | collective-permute-start | bytes 786440 | tf_op jit(solution)/shard_map/ppermute | solution.py:30
  205.3 1.6 collective-permute-done.24
  206.9 1.6 collective-permute-start.40
  211.9 2.4 %place_columns.1 = (bf16[128,8192]{1,0:T(8,128)(2,1)}, bf16[128,4096]{1,0:T(8,128)(2,1)}) custom-call(s32[5]{0:T(128)S(1)} %copy-done.22, bf16[128,6144]{1,0:T(8,128)(2,1)S(1)} %collective-permute-done.21.received, bf16[128,8192]{1,0:T(8,128)(2,1)} %get-tuple-element.135.q_in, ...), custom_call_target="tpu_custom_call", output_to_operand_aliasing={{0}: (2, {}), {1}: (3, {})} | custom-call | bytes 4000000 | tf_op jit(solution)/shard_map/place_columns/pallas_call | solution.py:186
  214.6 5.1 %collective-permute-done.40.refs_7_ = f32[32,2048]{1,0:T(8,128)} collective-permute-done((f32[32,2048]{1,0:T(8,128)}, f32[32,2048]{1,0:T(8,128)}, u32[]{:S(2)}, u32[]{:S(2)}) %collective-permute-start.40) | collective-permute-done | bytes 262176 | tf_op jit(solution)/shard_map/ppermute | solution.py:30
  219.6 2.2 collective-permute-done.38.refs_5_
  221.8 2.8 %collective-permute-done.36.refs_3_ = f32[32,2048]{1,0:T(8,128)S(1)} collective-permute-done((f32[32,2048]{1,0:T(8,128)}, f32[32,2048]{1,0:T(8,128)S(1)}, u32[]{:S(2)}, u32[]{:S(2)}) %collective-permute-start.36) | collective-permute-done | bytes 262176 | tf_op jit(solution)/shard_map/ppermute | solution.py:30
  224.6 3.6 %lay_out.1 = f32[32,16384]{1,0:T(8,128)} custom-call(s32[5]{0:T(128)S(1)} %copy-done.22, f32[32,2048]{1,0:T(8,128)S(1)} %join_cores.2.refs_0_, f32[32,2048]{1,0:T(8,128)} %join_cores.3.refs_1_, f32[32,2048]{1,0:T(8,128)} %collective-permute-done.35.refs_2_, f32[32,2048]{1,0:T(8,128)S(1)} %collective-permute-done.36.refs_3_, ...), custom_call_target="tpu_custom_call" | custom-call | bytes 4000000 | tf_op jit(solution)/shard_map/lay_out/pallas_call | solution.py:295
  (160 shorter events, 47.3 us)
Async XLA Ops:
  0.6 14.8 %copy-start = (s32[1,8,4]{1,2,0:T(4,128)S(1)}, s32[1,8,4]{1,2,0:T(4,128)}, u32[]{:S(2)}) copy-start(s32[1,8,4]{1,2,0:T(4,128)} %param.15) | copy-start | bytes 388
  3.7 35.9 %copy-start.10 = (f32[1,64,128]{2,1,0:T(8,128)S(1)}, f32[1,64,128]{2,1,0:T(8,128)}, u32[]{:S(2)}) copy-start(f32[1,64,128]{2,1,0:T(8,128)} %param.11) | copy-start | bytes 98308
  3.7 1.8 collective-permute-start
  5.5 17.7 %collective-permute-start.2 = (bf16[128,8192]{1,0:T(8,128)(2,1)S(1)}, bf16[128,8192]{1,0:T(8,128)(2,1)}, u32[]{:S(2)}, u32[]{:S(2)}) collective-permute-start(bf16[128,8192]{1,0:T(8,128)(2,1)S(1)} %bitcast.45), channel_id=1, source_target_pairs={{0,1},{1,0},{2,3},{3,2},{4,5},{5,4},{6,7},{7,6},{8,9},{9,8},{10,11... | collective-permute-start | bytes 6291464 | tf_op jit(solution)/shard_map/ppermute | solution.py:30
  5.9 17.4 %collective-permute-start.4 = (bf16[128,8192]{1,0:T(8,128)(2,1)}, bf16[128,8192]{1,0:T(8,128)(2,1)}, u32[]{:S(2)}, u32[]{:S(2)}) collective-permute-start(bf16[128,8192]{1,0:T(8,128)(2,1)} %bitcast.52), channel_id=1, source_target_pairs={{0,1},{1,0},{2,3},{3,2},{4,5},{5,4},{6,7},{7,6},{8,9},{9,8},{10,11... | collective-permute-start | bytes 6291464 | tf_op jit(solution)/shard_map/ppermute | solution.py:30
  6.1 16.1 %collective-permute-start.3 = (bf16[128,4096]{1,0:T(8,128)(2,1)}, bf16[128,4096]{1,0:T(8,128)(2,1)S(1)}, u32[]{:S(2)}, u32[]{:S(2)}) collective-permute-start(bf16[128,4096]{1,0:T(8,128)(2,1)} %bitcast.59), channel_id=1, source_target_pairs={{0,1},{1,0},{2,3},{3,2},{4,5},{5,4},{6,7},{7,6},{8,9},{9,8},{10,11... | collective-permute-start | bytes 3145736 | tf_op jit(solution)/shard_map/ppermute | solution.py:30
  10.1 19.2 %collective-permute-start.9 = (bf16[64,2048]{1,0:T(8,128)(2,1)}, bf16[64,2048]{1,0:T(8,128)(2,1)S(1)}, u32[]{:S(2)}, u32[]{:S(2)}) collective-permute-start(bf16[64,2048]{1,0:T(8,128)(2,1)} %get-tuple-element.100.refs_0_), channel_id=1, source_target_pairs={{0,2},{1,3},{2,0},{3,1},{4,6},{5,7},{6,4},{7,5},{8,10},{9,11},{10,... | collective-permute-start | bytes 786440 | tf_op jit(solution)/shard_map/ppermute | solution.py:30
  12.9 16.5 %collective-permute-start.1 = (bf16[64,2048]{1,0:T(8,128)(2,1)}, bf16[64,2048]{1,0:T(8,128)(2,1)}, u32[]{:S(2)}, u32[]{:S(2)}) collective-permute-start(bf16[64,2048]{1,0:T(8,128)(2,1)} %get-tuple-element.100.refs_0_), channel_id=1, source_target_pairs={{0,4},{1,5},{2,6},{3,7},{4,0},{5,1},{6,2},{7,3},{8,12},{9,13},{10,... | collective-permute-start | bytes 786440 | tf_op jit(solution)/shard_map/ppermute | solution.py:30
  23.2 7.7 %collective-permute-start.7 = (bf16[144,320]{1,0:T(8,128)(2,1)S(1)}, bf16[144,320]{1,0:T(8,128)(2,1)}, u32[]{:S(2)}, u32[]{:S(2)}) collective-permute-start(bf16[144,320]{1,0:T(8,128)(2,1)S(1)} %fusion.4.refs_0_), channel_id=1, source_target_pairs={{0,4},{1,5},{2,6},{3,7},{8,12},{9,13},{10,14},{11,15},{16,20},{17,... | collective-permute-start | bytes 276488 | tf_op jit(solution)/shard_map/ppermute | solution.py:25
  26.1 5.2 %collective-permute-start.6 = (bf16[144,320]{1,0:T(8,128)(2,1)S(1)}, bf16[144,320]{1,0:T(8,128)(2,1)}, u32[]{:S(2)}, u32[]{:S(2)}) collective-permute-start(bf16[144,320]{1,0:T(8,128)(2,1)S(1)} %fusion.4.refs_0_), channel_id=1, source_target_pairs={{0,2},{1,3},{2,4},{3,5},{4,6},{5,7},{8,10},{9,11},{10,12},{11,13},... | collective-permute-start | bytes 276488 | tf_op jit(solution)/shard_map/ppermute | solution.py:25
  29.4 28.5 %copy-start.6 = (bf16[1,128,4096]{2,1,0:T(8,128)(2,1)S(1)}, bf16[1,128,4096]{2,1,0:T(8,128)(2,1)}, u32[]{:S(2)}) copy-start(bf16[1,128,4096]{2,1,0:T(8,128)(2,1)} %param.9) | copy-start | bytes 3145732
  29.4 11.4 %collective-permute-start.10 = (bf16[64,2048]{1,0:T(8,128)(2,1)}, bf16[64,2048]{1,0:T(8,128)(2,1)}, u32[]{:S(2)}, u32[]{:S(2)}) collective-permute-start(bf16[64,2048]{1,0:T(8,128)(2,1)} %collective-permute-done.1.refs_1_), channel_id=1, source_target_pairs={{0,2},{1,3},{2,0},{3,1},{4,6},{5,7},{6,4},{7,5},{8,10},{9,11},{10,... | collective-permute-start | bytes 786440 | tf_op jit(solution)/shard_map/ppermute | solution.py:30
  33.0 7.8 %collective-permute-start.8 = (bf16[432,320]{1,0:T(8,128)(2,1)}, bf16[432,320]{1,0:T(8,128)(2,1)}, u32[]{:S(2)}, u32[]{:S(2)}) collective-permute-start(bf16[432,320]{1,0:T(8,128)(2,1)} %stack.77.own), channel_id=1, source_target_pairs={{0,1},{1,0},{2,3},{3,2},{4,5},{5,4},{6,7},{7,6},{8,9},{9,8},{10,11... | collective-permute-start | bytes 829448 | tf_op jit(solution)/shard_map/ppermute | solution.py:30
  34.1 16.3 %collective-permute-start.14 = (bf16[64,2048]{1,0:T(8,128)(2,1)}, bf16[64,2048]{1,0:T(8,128)(2,1)}, u32[]{:S(2)}, u32[]{:S(2)}) collective-permute-start(bf16[64,2048]{1,0:T(8,128)(2,1)} %get-tuple-element.110.refs_0_), channel_id=1, source_target_pairs={{0,2},{1,3},{2,0},{3,1},{4,6},{5,7},{6,4},{7,5},{8,10},{9,11},{10,... | collective-permute-start | bytes 786440 | tf_op jit(solution)/shard_map/ppermute | solution.py:30
  37.5 12.9 %collective-permute-start.13 = (bf16[64,2048]{1,0:T(8,128)(2,1)}, bf16[64,2048]{1,0:T(8,128)(2,1)}, u32[]{:S(2)}, u32[]{:S(2)}) collective-permute-start(bf16[64,2048]{1,0:T(8,128)(2,1)} %get-tuple-element.110.refs_0_), channel_id=1, source_target_pairs={{0,4},{1,5},{2,6},{3,7},{4,0},{5,1},{6,2},{7,3},{8,12},{9,13},{10,... | collective-permute-start | bytes 786440 | tf_op jit(solution)/shard_map/ppermute | solution.py:30
  39.6 1.2 collective-permute-start.5
  43.8 43.1 %collective-permute-start.12 = (bf16[256,2048]{1,0:T(8,128)(2,1)}, bf16[256,2048]{1,0:T(8,128)(2,1)}, u32[]{:S(2)}, u32[]{:S(2)}) collective-permute-start(bf16[256,2048]{1,0:T(8,128)(2,1)} %stack.78.weight), channel_id=1, source_target_pairs={{0,16},{8,24},{16,0},{24,8},{1,17},{9,25},{17,1},{25,9},{2,18},{10... | collective-permute-start | bytes 3145736 | tf_op jit(solution)/shard_map/ppermute | solution.py:30
  45.3 41.6 %collective-permute-start.11 = (bf16[256,2048]{1,0:T(8,128)(2,1)}, bf16[256,2048]{1,0:T(8,128)(2,1)}, u32[]{:S(2)}, u32[]{:S(2)}) collective-permute-start(bf16[256,2048]{1,0:T(8,128)(2,1)} %stack.78.weight), channel_id=1, source_target_pairs={{0,8},{8,0},{16,24},{24,16},{1,9},{9,1},{17,25},{25,17},{2,10},{10... | collective-permute-start | bytes 3145736 | tf_op jit(solution)/shard_map/ppermute | solution.py:30
  50.5 19.3 %collective-permute-start.15 = (bf16[64,2048]{1,0:T(8,128)(2,1)}, bf16[64,2048]{1,0:T(8,128)(2,1)S(1)}, u32[]{:S(2)}, u32[]{:S(2)}) collective-permute-start(bf16[64,2048]{1,0:T(8,128)(2,1)} %collective-permute-done.13.refs_1_), channel_id=1, source_target_pairs={{0,2},{1,3},{2,0},{3,1},{4,6},{5,7},{6,4},{7,5},{8,10},{9,11},{10,... | collective-permute-start | bytes 786440 | tf_op jit(solution)/shard_map/ppermute | solution.py:30
  70.8 16.1 %copy-start.3 = (bf16[1,128,8192]{2,1,0:T(8,128)(2,1)S(1)}, bf16[1,128,8192]{2,1,0:T(8,128)(2,1)}, u32[]{:S(2)}) copy-start(bf16[1,128,8192]{2,1,0:T(8,128)(2,1)} %param.10) | copy-start | bytes 6291460
  70.8 16.1 %copy-start.9 = (bf16[128,4096]{1,0:T(8,128)(2,1)S(1)}, bf16[128,4096]{1,0:T(8,128)(2,1)}, u32[]{:S(2)}) copy-start(bf16[128,4096]{1,0:T(8,128)(2,1)} %copy-done.7) | copy-start | bytes 3145732
  83.9 26.1 %collective-permute-start.17 = (f32[128,2048]{1,0:T(8,128)S(1)}, f32[128,2048]{1,0:T(8,128)S(1)}, u32[]{:S(2)}, u32[]{:S(2)}) collective-permute-start(f32[128,2048]{1,0:T(8,128)S(1)} %get-tuple-element.119), channel_id=1, source_target_pairs={{0,8},{8,0},{16,24},{24,16},{1,9},{9,1},{17,25},{25,17},{2,10},{10... | collective-permute-start | bytes 3145736 | tf_op jit(solution)/shard_map/ppermute | solution.py:30
  85.4 24.6 %collective-permute-start.19 = (f32[128,2048]{1,0:T(8,128)S(1)}, f32[128,2048]{1,0:T(8,128)S(1)}, u32[]{:S(2)}, u32[]{:S(2)}) collective-permute-start(f32[128,2048]{1,0:T(8,128)S(1)} %get-tuple-element.124), channel_id=1, source_target_pairs={{0,16},{8,24},{16,0},{24,8},{1,17},{9,25},{17,1},{25,9},{2,18},{10... | collective-permute-start | bytes 3145736 | tf_op jit(solution)/shard_map/ppermute | solution.py:30
  99.9 32.6 %collective-permute-start.16 = (f32[128,2048]{1,0:T(8,128)S(1)}, f32[128,2048]{1,0:T(8,128)S(1)}, u32[]{:S(2)}, u32[]{:S(2)}) collective-permute-start(f32[128,2048]{1,0:T(8,128)S(1)} %get-tuple-element.118), channel_id=1, source_target_pairs={{0,8},{8,0},{16,24},{24,16},{1,9},{9,1},{17,25},{25,17},{2,10},{10... | collective-permute-start | bytes 3145736 | tf_op jit(solution)/shard_map/ppermute | solution.py:30
  117.4 26.3 %collective-permute-start.18 = (f32[128,1024]{1,0:T(8,128)S(1)}, f32[128,1024]{1,0:T(8,128)S(1)}, u32[]{:S(2)}, u32[]{:S(2)}) collective-permute-start(f32[128,1024]{1,0:T(8,128)S(1)} %get-tuple-element.123), channel_id=1, source_target_pairs={{0,16},{8,24},{16,0},{24,8},{1,17},{9,25},{17,1},{25,9},{2,18},{10... | collective-permute-start | bytes 1572872 | tf_op jit(solution)/shard_map/ppermute | solution.py:30
  120.0 23.8 %collective-permute-start.26 = (f32[128,1024]{1,0:T(8,128)S(1)}, f32[128,1024]{1,0:T(8,128)S(1)}, u32[]{:S(2)}, u32[]{:S(2)}) collective-permute-start(f32[128,1024]{1,0:T(8,128)S(1)} %get-tuple-element.157), channel_id=1, source_target_pairs={{0,8},{8,0},{16,24},{24,16},{1,9},{9,1},{17,25},{25,17},{2,10},{10... | collective-permute-start | bytes 1572872 | tf_op jit(solution)/shard_map/ppermute | solution.py:30
  129.1 15.5 %collective-permute-start.20 = (f32[128,1024]{1,0:T(8,128)S(1)}, f32[128,1024]{1,0:T(8,128)S(1)}, u32[]{:S(2)}, u32[]{:S(2)}) collective-permute-start(f32[128,1024]{1,0:T(8,128)S(1)} %get-tuple-element.129), channel_id=1, source_target_pairs={{0,16},{8,24},{16,0},{24,8},{1,17},{9,25},{17,1},{25,9},{2,18},{10... | collective-permute-start | bytes 1572872 | tf_op jit(solution)/shard_map/ppermute | solution.py:30
  132.5 19.6 %copy-start.25 = (f32[128,2048]{1,0:T(8,128)}, f32[128,2048]{1,0:T(8,128)S(1)}, u32[]{:S(2)}) copy-start(f32[128,2048]{1,0:T(8,128)S(1)} %collective-permute-done.16) | copy-start | bytes 3145732
  132.5 19.6 %collective-permute-start.25 = (f32[128,1024]{1,0:T(8,128)S(1)}, f32[128,1024]{1,0:T(8,128)S(1)}, u32[]{:S(2)}, u32[]{:S(2)}) collective-permute-start(f32[128,1024]{1,0:T(8,128)S(1)} %get-tuple-element.154), channel_id=1, source_target_pairs={{0,16},{8,24},{16,0},{24,8},{1,17},{9,25},{17,1},{25,9},{2,18},{10... | collective-permute-start | bytes 1572872 | tf_op jit(solution)/shard_map/ppermute | solution.py:30
  134.0 23.4 %collective-permute-start.31 = (f32[128,1024]{1,0:T(8,128)}, f32[128,1024]{1,0:T(8,128)}, u32[]{:S(2)}, u32[]{:S(2)}) collective-permute-start(f32[128,1024]{1,0:T(8,128)} %get-tuple-element.169), channel_id=1, source_target_pairs={{0,8},{8,0},{16,24},{24,16},{1,9},{9,1},{17,25},{25,17},{2,10},{10... | collective-permute-start | bytes 1572872 | tf_op jit(solution)/shard_map/ppermute | solution.py:30
  152.1 11.1 %collective-permute-start.27 = (f32[128,1024]{1,0:T(8,128)}, f32[128,1024]{1,0:T(8,128)}, u32[]{:S(2)}, u32[]{:S(2)}) collective-permute-start(f32[128,1024]{1,0:T(8,128)} %add_add_fusion.2), channel_id=1, source_target_pairs={{0,2},{1,3},{2,0},{3,1},{4,6},{5,7},{6,4},{7,5},{8,10},{9,11},{10,... | collective-permute-start | bytes 1572872 | tf_op jit(solution)/shard_map/ppermute | solution.py:30
  152.2 13.2 %collective-permute-start.30 = (f32[128,1024]{1,0:T(8,128)}, f32[128,1024]{1,0:T(8,128)}, u32[]{:S(2)}, u32[]{:S(2)}) collective-permute-start(f32[128,1024]{1,0:T(8,128)} %get-tuple-element.164), channel_id=1, source_target_pairs={{0,16},{8,24},{16,0},{24,8},{1,17},{9,25},{17,1},{25,9},{2,18},{10... | collective-permute-start | bytes 1572872 | tf_op jit(solution)/shard_map/ppermute | solution.py:30
  157.4 12.2 %collective-permute-start.22 = (f32[432,320]{0,1:T(8,128)}, f32[432,320]{0,1:T(8,128)}, u32[]{:S(2)}, u32[]{:S(2)}) collective-permute-start(f32[432,320]{0,1:T(8,128)} %copy.39), channel_id=1, source_target_pairs={{0,1},{1,0},{2,3},{3,2},{4,5},{5,4},{6,7},{7,6},{8,9},{9,8},{10,11... | collective-permute-start | bytes 1658888 | tf_op jit(solution)/shard_map/ppermute | solution.py:30
  165.4 15.8 %collective-permute-start.32 = (f32[128,1024]{1,0:T(8,128)}, f32[128,1024]{1,0:T(8,128)}, u32[]{:S(2)}, u32[]{:S(2)}) collective-permute-start(f32[128,1024]{1,0:T(8,128)} %add_add_fusion), channel_id=1, source_target_pairs={{0,2},{1,3},{2,0},{3,1},{4,6},{5,7},{6,4},{7,5},{8,10},{9,11},{10,... | collective-permute-start | bytes 1572872 | tf_op jit(solution)/shard_map/ppermute | solution.py:30
  167.4 12.4 %collective-permute-start.28 = (f32[64,1024]{1,0:T(8,128)S(1)}, f32[64,1024]{1,0:T(8,128)}, u32[]{:S(2)}, u32[]{:S(2)}) collective-permute-start(f32[64,1024]{1,0:T(8,128)S(1)} %slice.95), channel_id=1, source_target_pairs={{0,4},{1,5},{2,6},{3,7},{4,0},{5,1},{6,2},{7,3},{8,12},{9,13},{10,... | collective-permute-start | bytes 786440 | tf_op jit(solution)/shard_map/ppermute | solution.py:30
  169.5 39.0 %collective-permute-start.21 = (bf16[128,6144]{1,0:T(8,128)(2,1)S(1)}, bf16[128,6144]{1,0:T(8,128)(2,1)S(1)}, u32[]{:S(2)}, u32[]{:S(2)}) collective-permute-start(bf16[128,6144]{1,0:T(8,128)(2,1)S(1)} %copy-done.5), channel_id=1, source_target_pairs={{0,1},{1,0},{2,3},{3,2},{4,5},{5,4},{6,7},{7,6},{8,9},{9,8},{10,11... | collective-permute-start | bytes 4718600 | tf_op jit(solution)/shard_map/ppermute | solution.py:30
  182.6 14.1 %collective-permute-start.33 = (f32[64,1024]{1,0:T(8,128)S(1)}, f32[64,1024]{1,0:T(8,128)S(1)}, u32[]{:S(2)}, u32[]{:S(2)}) collective-permute-start(f32[64,1024]{1,0:T(8,128)S(1)} %slice.101), channel_id=1, source_target_pairs={{0,4},{1,5},{2,6},{3,7},{4,0},{5,1},{6,2},{7,3},{8,12},{9,13},{10,... | collective-permute-start | bytes 786440 | tf_op jit(solution)/shard_map/ppermute | solution.py:30
  185.8 2.7 %collective-permute-start.29 = (f32[32,1024]{1,0:T(8,128)S(1)}, f32[32,1024]{1,0:T(8,128)S(1)}, u32[]{:S(2)}, u32[]{:S(2)}) collective-permute-start(f32[32,1024]{1,0:T(8,128)S(1)} %get-tuple-element.198), channel_id=1, source_target_pairs={{0,1},{1,0},{2,3},{3,2},{4,5},{5,4},{6,7},{7,6},{8,9},{9,8},{10,11... | collective-permute-start | bytes 393224 | tf_op jit(solution)/shard_map/ppermute | solution.py:30
  185.9 19.3 %collective-permute-start.23 = (f32[128,320]{1,0:T(8,128)S(1)}, f32[128,320]{1,0:T(8,128)S(1)}, u32[]{:S(2)}, u32[]{:S(2)}) collective-permute-start(f32[128,320]{1,0:T(8,128)S(1)} %get-tuple-element.194), channel_id=1, source_target_pairs={{2,0},{3,1},{4,2},{5,3},{6,4},{7,5},{10,8},{11,9},{12,10},{13,11},... | collective-permute-start | bytes 491528 | tf_op jit(solution)/shard_map/ppermute | solution.py:25
  187.2 19.7 %collective-permute-start.24 = (f32[128,320]{1,0:T(8,128)S(1)}, f32[128,320]{1,0:T(8,128)S(1)}, u32[]{:S(2)}, u32[]{:S(2)}) collective-permute-start(f32[128,320]{1,0:T(8,128)S(1)} %get-tuple-element.195), channel_id=1, source_target_pairs={{4,0},{5,1},{6,2},{7,3},{12,8},{13,9},{14,10},{15,11},{20,16},{21,... | collective-permute-start | bytes 491528 | tf_op jit(solution)/shard_map/ppermute | solution.py:25
  189.1 20.7 %collective-permute-start.39 = (f32[32,2048]{1,0:T(8,128)S(1)}, f32[32,2048]{1,0:T(8,128)S(1)}, u32[]{:S(2)}, u32[]{:S(2)}) collective-permute-start(f32[32,2048]{1,0:T(8,128)S(1)} %join_cores.2.refs_0_), channel_id=1, source_target_pairs={{0,24},{8,16},{16,8},{24,0},{1,25},{9,17},{17,9},{25,1},{2,26},{10... | collective-permute-start | bytes 786440 | tf_op jit(solution)/shard_map/ppermute | solution.py:30
  196.7 1.4 collective-permute-start.34
  198.2 16.2 %collective-permute-start.37 = (f32[32,2048]{1,0:T(8,128)S(1)}, f32[32,2048]{1,0:T(8,128)}, u32[]{:S(2)}, u32[]{:S(2)}) collective-permute-start(f32[32,2048]{1,0:T(8,128)S(1)} %join_cores.2.refs_0_), channel_id=1, source_target_pairs={{0,16},{8,24},{16,0},{24,8},{1,17},{9,25},{17,1},{25,9},{2,18},{10... | collective-permute-start | bytes 786440 | tf_op jit(solution)/shard_map/ppermute | solution.py:30
  205.3 9.3 %collective-permute-start.35 = (f32[32,2048]{1,0:T(8,128)S(1)}, f32[32,2048]{1,0:T(8,128)}, u32[]{:S(2)}, u32[]{:S(2)}) collective-permute-start(f32[32,2048]{1,0:T(8,128)S(1)} %join_cores.2.refs_0_), channel_id=1, source_target_pairs={{0,8},{8,0},{16,24},{24,16},{1,9},{9,1},{17,25},{25,17},{2,10},{10... | collective-permute-start | bytes 786440 | tf_op jit(solution)/shard_map/ppermute | solution.py:30
  206.9 12.7 %collective-permute-start.40 = (f32[32,2048]{1,0:T(8,128)}, f32[32,2048]{1,0:T(8,128)}, u32[]{:S(2)}, u32[]{:S(2)}) collective-permute-start(f32[32,2048]{1,0:T(8,128)} %join_cores.3.refs_1_), channel_id=1, source_target_pairs={{0,24},{8,16},{16,8},{24,0},{1,25},{9,17},{17,9},{25,1},{2,26},{10... | collective-permute-start | bytes 786440 | tf_op jit(solution)/shard_map/ppermute | solution.py:30
  208.5 13.3 %collective-permute-start.38 = (f32[32,2048]{1,0:T(8,128)}, f32[32,2048]{1,0:T(8,128)S(1)}, u32[]{:S(2)}, u32[]{:S(2)}) collective-permute-start(f32[32,2048]{1,0:T(8,128)} %join_cores.3.refs_1_), channel_id=1, source_target_pairs={{0,16},{8,24},{16,0},{24,8},{1,17},{9,25},{17,1},{25,9},{2,18},{10... | collective-permute-start | bytes 786440 | tf_op jit(solution)/shard_map/ppermute | solution.py:30
  210.5 14.1 %collective-permute-start.36 = (f32[32,2048]{1,0:T(8,128)}, f32[32,2048]{1,0:T(8,128)S(1)}, u32[]{:S(2)}, u32[]{:S(2)}) collective-permute-start(f32[32,2048]{1,0:T(8,128)} %join_cores.3.refs_1_), channel_id=1, source_target_pairs={{0,8},{8,0},{16,24},{24,16},{1,9},{9,1},{17,25},{25,17},{2,10},{10... | collective-permute-start | bytes 786440 | tf_op jit(solution)/shard_map/ppermute | solution.py:30
  211.9 12.7 %copy-start.18 = (f32[32,2048]{1,0:T(8,128)S(1)}, f32[32,2048]{1,0:T(8,128)}, u32[]{:S(2)}) copy-start(f32[32,2048]{1,0:T(8,128)} %copy-done.17) | copy-start | bytes 786436
  (28 other events, 117.2 us)

commit v6 on v5

--- a/solution.py
+++ b/solution.py
@@ -12,6 +12,7 @@
 NOPE = 128
 VDIM = 128
 BLOCK = 64
+TOPK = 3
 
 partner_offsets = (1, 2, 3, 4)
 HIDDEN = -1e30
@@ -361,26 +362,51 @@
     return channel == (ctx ^ partner) * lat_block + place % lat_block
 
 
-def collect_kernel(plan, own, sib, cand, cand_t, rope_keys, bias, *, blocks, lat_block):
+def block_sources(place, offered, per_block, span):
+    ctx = place[place.shape[0] - 1]
+    sources = []
+    for side in range(2):
+        group = ctx ^ side
+        for at in range(per_block + len(partner_offsets)):
+            matching = at - per_block
+            offset = partner_offsets[matching] if matching >= 0 else 0
+            source = group - offset
+            usable = source >= 0
+            sender = jnp.maximum(source, 0)
+            inner = offered[sender, matching] if matching >= 0 else at
+            start = jnp.where(usable, ((ctx >> 1) - (sender >> 1)) * span + inner * BLOCK, 0)
+            block_id = jnp.where(usable, sender * per_block + inner, -2)
+            sources.append(((offset + side) % 2, start, usable, block_id))
+    return sources
+
+
+def collect_kernel(place, offered, own, sib, cand, cand_t, rope_keys, bias, *, lat_block):
+    ctx = place[place.shape[0] - 1]
+    span = own.shape[0] // 3
+    per_block = (span - 16) // BLOCK
     pieces = []
     key_at = lax.broadcasted_iota(jnp.int32, (BLOCK, 2 * BLOCK), 0)
     query = lax.broadcasted_iota(jnp.int32, (BLOCK, 2 * BLOCK), 1)
-    per_side = len(blocks) // 2
-    for block, other in enumerate(blocks):
+    causal = jnp.where(key_at <= query % BLOCK, 1.0, 0.0)
+    sources = block_sources(place, offered, per_block, span)
+    for block, (other, start, usable, block_id) in enumerate(sources):
         rows_ref = sib if other else own
-        start = pl.multiple_of(plan[1 + block], 16)
-        rows = rows_ref[pl.ds(start, BLOCK), :]
-        usable = plan[1 + len(blocks) + block]
-        pieces.append(jnp.where(usable > 0, rows, jnp.zeros_like(rows)))
-        side, at = divmod(block, per_side)
-        kinds = (sib if side else own)[2 * BLOCK : 2 * BLOCK + 16, :][:1].astype(jnp.float32)
-        kind = jnp.where(
-            query < BLOCK, kinds[:, 2 * at : 2 * at + 1], kinds[:, 2 * at + 1 : 2 * at + 2]
-        )
-        allowed = (kind > 1.5) | (kind > 0.5) & (key_at <= query % BLOCK)
-        bias[block * BLOCK : (block + 1) * BLOCK, :] = jnp.where(allowed, 0.0, HIDDEN)
+        rows = rows_ref[pl.ds(pl.multiple_of(start, 16), BLOCK), :]
+        pieces.append(jnp.where(usable, rows, jnp.zeros_like(rows)))
+        side = block // (len(sources) // 2)
+        lists = (sib if side else own)[span - 16 : span, :][:1].astype(jnp.int32)
+        open_for = []
+        for at in range(per_block):
+            picks = [lists[:, at * TOPK + k : at * TOPK + k + 1] for k in range(TOPK)]
+            picked = functools.reduce(
+                jnp.maximum, [jnp.where(pick == block_id, 1.0, 0.0) for pick in picks]
+            )
+            same = jnp.where(block_id == (ctx ^ side) * per_block + at, 1.0, 0.0)
+            open_for.append(jnp.maximum(picked, same * causal))
+        allowed = jnp.where(query < BLOCK, open_for[0], open_for[1])
+        bias[block * BLOCK : (block + 1) * BLOCK, :] = jnp.where(allowed > 0.5, 0.0, HIDDEN)
     both = jnp.concatenate(pieces, axis=0)
-    order = channel_order(plan[0], lat_block).astype(jnp.bfloat16)
+    order = channel_order(ctx, lat_block).astype(jnp.bfloat16)
     latent = both[:, :LAT]
     cand[...] = dot(latent, order, 1, 0).astype(jnp.bfloat16)
     cand_t[...] = dot(order, latent, 0, 1).astype(jnp.bfloat16)
@@ -389,16 +415,15 @@
     rope_keys[...] = dot(both[:, LAT:], twice.astype(jnp.bfloat16), 1, 0).astype(jnp.bfloat16)
 
 
-def collect(plan, own, sib, blocks, lat_block):
-    rows = len(blocks) * BLOCK
+def collect(place, offered, own, sib, rows, lat_block):
     bf16 = jnp.bfloat16
     shapes = [((rows, LAT), bf16), ((LAT, rows), bf16), ((rows, 2 * ROPE), bf16)]
     shapes.append(((rows, 2 * BLOCK), jnp.float32))
-    whole = lambda shape: pl.BlockSpec(shape, lambda i, plan: (0, 0))
-    return pl.pallas_call(
-        functools.partial(collect_kernel, blocks=blocks, lat_block=lat_block),
+    whole = lambda shape: pl.BlockSpec(shape, lambda i, place, offered: (0, 0))
+    return pl.pallas_call(
+        functools.partial(collect_kernel, lat_block=lat_block),
         grid_spec=pltpu.PrefetchScalarGridSpec(
-            num_scalar_prefetch=1,
+            num_scalar_prefetch=2,
             grid=(1,),
             in_specs=[whole(own.shape), whole(sib.shape)],
             out_specs=[whole(shape) for shape, _ in shapes],
@@ -409,16 +434,16 @@
             flops=250_000_000, bytes_accessed=3_000_000, transcendentals=0
         ),
         name="collect",
-    )(plan, own, sib)
-
-
-def spread_kernel(plan, *refs, blocks, lat_block):
+    )(place, offered, own, sib)
+
+
+def spread_kernel(place, offered, *refs, lat_block):
     *sums, own, sib = refs
     count = len(sums) // 2
     latent, rope = sums[0][...], sums[count][...]
     for index in range(1, count):
         latent, rope = latent + sums[index][...], rope + sums[count + index][...]
-    order = channel_order(plan[0], lat_block).astype(jnp.float32)
+    order = channel_order(place[place.shape[0] - 1], lat_block).astype(jnp.float32)
     latent = lax.dot_general(
         latent,
         order,
@@ -429,22 +454,25 @@
     rows = jnp.concatenate([latent, rope[:, :ROPE] + rope[:, ROPE:]], axis=1)
     own[...] = jnp.zeros_like(own)
     sib[...] = jnp.zeros_like(sib)
-    for block, other in enumerate(blocks):
-        here = pl.ds(pl.multiple_of(plan[1 + block], 16), BLOCK)
+    span = own.shape[0] // 3
+    sources = block_sources(place, offered, (span - 16) // BLOCK, span)
+    for block, (other, start, _, _) in enumerate(sources):
+        here = pl.ds(pl.multiple_of(start, 16), BLOCK)
         target = sib if other else own
         target[here, :] += rows[block * BLOCK : (block + 1) * BLOCK]
 
 
-def spread(plan, latents, ropes, rows, blocks, lat_block):
+def spread(place, offered, latents, ropes, rows, lat_block):
     shape = (rows, LAT + ROPE)
     sums = [*latents, *ropes]
-    return pl.pallas_call(
-        functools.partial(spread_kernel, blocks=blocks, lat_block=lat_block),
+    whole = lambda shape: pl.BlockSpec(shape, lambda i, place, offered: (0, 0))
+    return pl.pallas_call(
+        functools.partial(spread_kernel, lat_block=lat_block),
         grid_spec=pltpu.PrefetchScalarGridSpec(
-            num_scalar_prefetch=1,
+            num_scalar_prefetch=2,
             grid=(1,),
-            in_specs=[pl.BlockSpec(array.shape, lambda i, plan: (0, 0)) for array in sums],
-            out_specs=[pl.BlockSpec(shape, lambda i, plan: (0, 0))] * 2,
+            in_specs=[whole(array.shape) for array in sums],
+            out_specs=[whole(shape)] * 2,
         ),
         out_shape=[jax.ShapeDtypeStruct(shape, jnp.float32)] * 2,
         compiler_params=pltpu.CompilerParams(vmem_limit_bytes=KERNEL_BYTES),
@@ -452,7 +480,7 @@
             flops=700_000_000, bytes_accessed=6_000_000, transcendentals=0
         ),
         name="spread",
-    )(plan, *sums)
+    )(place, offered, *sums)
 
 
 def halve(value, axis, bit):
@@ -473,7 +501,7 @@
     far = n_dp - 1
     lat_block = up_weight.shape[0]
 
-    place = jnp.stack([core] + [dp ^ t for t in range(n_dp)]).astype(jnp.int32)
+    place = jnp.stack([core] + [dp ^ t for t in range(n_dp)] + [ctx]).astype(jnp.int32)
 
     leaving, = weight_parts(place, up_weight, n_dp, far)
     crossed = exchange(leaving, "ctx", 1)
@@ -485,39 +513,16 @@
     chip_rows = weight_parts(place, up_weight, n_dp, far, crossed)
     own = [q_nope[0], q_rope[0], grad_out[0]]
     sibling = [exchange(array, "ctx", 1) for array in own]
-    offer_plan = offered[0]
+    offered = offered[0]
     span = group_len + 16
-    blocks, starts, usables = [], [], []
-    for side in range(2):
-        group = ctx ^ side
-        offsets = [0] * per_block + list(partner_offsets)
-        blocks += [(offset + side) % 2 for offset in offsets]
-        source = jnp.stack([group - offset for offset in offsets])
-        sender = jnp.maximum(source, 0)
-        inner = jnp.concatenate(
-            [
-                jnp.arange(per_block, dtype=jnp.int32),
-                offer_plan[sender[per_block:], jnp.arange(len(partner_offsets))],
-            ]
-        )
-        usable = source >= 0
-        behind = ctx // 2 - sender // 2
-        starts.append(jnp.where(usable, behind * span + inner * BLOCK, 0))
-        usables.append(usable)
-        if side == 0:
-            ids = jnp.where(usable, sender * per_block + inner, -1)
-            query_ids = group * per_block + jnp.arange(per_block, dtype=jnp.int32)
-            picked = jnp.any(selected[0][None, :, :] == ids[:, None, None], axis=2)
-            picked = picked & (ids >= 0)[:, None]
-            same = ids[:, None] == query_ids[None, :]
-            kinds = jnp.where(picked, 2.0, jnp.where(same, 1.0, 0.0)).reshape(1, -1)
-    plan = jnp.concatenate([ctx[None], *starts, *usables]).astype(jnp.int32)
-    kinds = jnp.pad(kinds.astype(jnp.bfloat16), ((0, 15), (0, LAT + ROPE - kinds.shape[1])))
-    bundle = after(jnp.concatenate([kv_latent[0], kinds], axis=0), *sibling)
+    lists = selected[0].reshape(1, -1).astype(jnp.bfloat16)
+    lists = jnp.pad(lists, ((0, 15), (0, LAT + ROPE - lists.shape[1])))
+    bundle = after(jnp.concatenate([kv_latent[0], lists], axis=0), *sibling)
     bundles = [bundle, from_behind(bundle, "ctx", 2), from_behind(bundle, "ctx", 4)]
     own_bundles = stack(bundles, (((0, 0), (1, 0), (2, 0)),), LAT + ROPE)[0]
     sib_bundles = exchange(own_bundles, "ctx", 1)
-    shared = collect(plan, own_bundles, sib_bundles, tuple(blocks), lat_block)
+    key_len = 2 * (group_len + len(partner_offsets) * BLOCK)
+    shared = collect(place, offered, own_bundles, sib_bundles, key_len, lat_block)
 
     partners = halving_order(n_ctx)[::2]
 
@@ -559,11 +564,12 @@
             weights[far] = joined([after(far_pieces[0], latents[-1])] + far_pieces[1:])
         weight = weights[t]
         if t == 0 and start:
-            weight = after(weight, *[piece for sent in first_sums for u in sent for piece in sent[u]])
+            there = [piece for sent in first_sums for u in sent for piece in sent[u]]
+            weight = after(weight, latents[-1], *there)
         if t == 1 and not start:
             weight = after(weight, *[weights[near] for near in range(2, far)])
         if t == far - 1 and start:
-            weight = after(weight, *[sent[far][0] for sent in first_sums])
+            weight = after(weight, latents[-1], *[sent[far][0] for sent in first_sums])
         rest = chunk_backward(
             place,
             t,
@@ -618,7 +624,7 @@
     received = exchange(sib_grads, "ctx", 1)
     grad_nope, grad_rope = place_columns(place, received, q_full, rope_full, n_dp)
 
-    own_grads, sib_grads = spread(plan, latents, ropes, 3 * span, tuple(blocks), lat_block)
+    own_grads, sib_grads = spread(place, offered, latents, ropes, 3 * span, lat_block)
     swapped = exchange(sib_grads, "ctx", 1)
     grad_rows = own_grads + swapped
     by_chip = [grad_rows[at * span : at * span + group_len] for at in range(3)]
@@ -635,6 +641,8 @@
         there = (sums[0][-1][half], latents[-1]) if half == 0 else (sums[0][-1][half],)
         arrived = exchange(after(second, *there), "ctx", ctx_bits[0])
         rows = first + arrived
+        if half:
+            rows = after(rows, received, grad_rows)
         for bit in ctx_bits[1:]:
             rows = halve(rows, "ctx", bit)
         piece = join_cores(place, rows[:lat_block], exchange(rows[lat_block:], "ctx", 1))

time: 229 us -> 228 us (level)
  waiting for transfers between devices: 55.9 us -> 77.1 us
  other arithmetic: 17.6 us -> 10.3 us
  starting transfers between devices: 58.3 us -> 51.3 us
  local copies, waits for them, and re-layouts: 17.9 us -> 13.5 us
  Pallas kernels: 77.4 us -> 74.3 us
    ppermute x37, waiting for transfers between devices: 53.9 us -> 68.8 us  [exchange(): lax.ppermute(value, axis, [(source, source ^ bits) for source in range(co...]
    ppermute x37, starting transfers between devices: 50.2 us -> 39.5 us  [exchange(): lax.ppermute(value, axis, [(source, source ^ bits) for source in range(co...]
    ppermute x4, waiting for transfers between devices: 2 us -> 8.23 us  [from_behind(): lax.ppermute(value, axis, [(source, source + steps) for source in range(i...]
    ppermute x4, starting transfers between devices: 8.12 us -> 11.8 us  [from_behind(): lax.ppermute(value, axis, [(source, source + steps) for source in range(i...]
    unnamed x71 -> x67, local copies, waits for them, and re-layouts: 8.66 us -> 9.21 us
  transfers between devices with their start and end apart: 41 -> 41, of which waited for: 17 -> 18; matrix products, arithmetic and copies ran while one was open for 12% -> 7% of each run, Pallas kernels for 31% -> 30%
where the time goes in v6:
time: 228 us
  waiting for transfers between devices  77.1 us (34%)
  Pallas kernels  74.3 us (33%)
  starting transfers between devices  51.3 us (22%)
  local copies, waits for them, and re-layouts  13.5 us (6%)
  other arithmetic  10.3 us (5%)
    ppermute x37, waiting for transfers between devices, exchange(): lax.ppermute(value, axis, [(source, source ^ bits) for source in range(co...  68.8 us
    pallas_call x6, Pallas kernels, chunk_backward(): pl.pallas_call(functools.partial(heads_kernel, earlier=len(aliases)), gri...  56 us
    ppermute x37, starting transfers between devices, exchange(): lax.ppermute(value, axis, [(source, source ^ bits) for source in range(co...  39.5 us
    ppermute x4, starting transfers between devices, from_behind(): lax.ppermute(value, axis, [(source, source + steps) for source in range(i...  11.8 us
    unnamed x67, local copies, waits for them, and re-layouts  9.21 us
    ppermute x4, waiting for transfers between devices, from_behind(): lax.ppermute(value, axis, [(source, source + steps) for source in range(i...  8.23 us
    add x4, other arithmetic, total(): left + right  5.4 us
    pallas_call x2, Pallas kernels, weight_parts(): pl.pallas_call(join_rows_kernel if joins else leave_kernel, grid_spec=plt...  5.05 us
  transfers between devices with their start and end apart: 41, of which 18 were waited for; matrix products, arithmetic and copies ran while one was open for 7% of the time, Pallas kernels for 30%

profile of v6, /device:TPU:0, one launch (start us, length us, event | category | flops | bytes accessed | tf_op | source)
XLA Modules:
  0.0 227.6 jit_solution(13966994798452448141)
XLA Ops:
  1.3 2.5 %weight_parts.2 = bf16[32,4096]{1,0:T(8,128)(2,1)} custom-call(s32[6]{0:T(128)} %stack.30.place, bf16[32,16384]{1,0:T(8,128)(2,1)} %distant.3, bf16[32,16384]{1,0:T(8,128)(2,1)} %distant.3), custom_call_target="tpu_custom_call" | custom-call | bytes 1000000 | tf_op jit(solution)/shard_map/weight_parts/pallas_call | solution.py:264
  4.2 1.4 collective-permute-done.crossed
  6.5 2.6 %weight_parts.3 = (bf16[64,2048]{1,0:T(8,128)(2,1)}, bf16[64,2048]{1,0:T(8,128)(2,1)}) custom-call(s32[6]{0:T(128)} %stack.30.place, bf16[32,16384]{1,0:T(8,128)(2,1)} %distant.3, bf16[32,16384]{1,0:T(8,128)(2,1)} %distant.3, bf16[32,4096]{1,0:T(8,128)(2,1)} %copy-done.29), custom_call_target="tpu_custom_call" | custom-call | bytes 1000000 | tf_op jit(solution)/shard_map/weight_parts/pallas_call | solution.py:264
  9.0 2.8 %collective-permute-start.9 = (bf16[64,2048]{1,0:T(8,128)(2,1)}, bf16[64,2048]{1,0:T(8,128)(2,1)}, u32[]{:S(2)}, u32[]{:S(2)}) collective-permute-start(bf16[64,2048]{1,0:T(8,128)(2,1)} %get-tuple-element.100.refs_0_), channel_id=1, source_target_pairs={{0,2},{1,3},{2,0},{3,1},{4,6},{5,7},{6,4},{7,5},{8,10},{9,11},{10,... | collective-permute-start | bytes 786440 | tf_op jit(solution)/shard_map/ppermute | solution.py:31
  11.8 2.6 %collective-permute-start.1 = (bf16[64,2048]{1,0:T(8,128)(2,1)}, bf16[64,2048]{1,0:T(8,128)(2,1)}, u32[]{:S(2)}, u32[]{:S(2)}) collective-permute-start(bf16[64,2048]{1,0:T(8,128)(2,1)} %get-tuple-element.100.refs_0_), channel_id=1, source_target_pairs={{0,4},{1,5},{2,6},{3,7},{4,0},{5,1},{6,2},{7,3},{8,12},{9,13},{10,... | collective-permute-start | bytes 786440 | tf_op jit(solution)/shard_map/ppermute | solution.py:31
  14.7 5.7 %collective-permute-start.7 = (bf16[144,320]{1,0:T(8,128)(2,1)S(1)}, bf16[144,320]{1,0:T(8,128)(2,1)S(1)}, u32[]{:S(2)}, u32[]{:S(2)}) collective-permute-start(bf16[144,320]{1,0:T(8,128)(2,1)S(1)} %fusion.4.refs_0_), channel_id=1, source_target_pairs={{0,4},{1,5},{2,6},{3,7},{8,12},{9,13},{10,14},{11,15},{16,20},{17,... | collective-permute-start | bytes 276488 | tf_op jit(solution)/shard_map/ppermute | solution.py:26
  20.4 3.5 %collective-permute-start.6 = (bf16[144,320]{1,0:T(8,128)(2,1)S(1)}, bf16[144,320]{1,0:T(8,128)(2,1)S(1)}, u32[]{:S(2)}, u32[]{:S(2)}) collective-permute-start(bf16[144,320]{1,0:T(8,128)(2,1)S(1)} %fusion.4.refs_0_), channel_id=1, source_target_pairs={{0,2},{1,3},{2,4},{3,5},{4,6},{5,7},{8,10},{9,11},{10,12},{11,13},... | collective-permute-start | bytes 276488 | tf_op jit(solution)/shard_map/ppermute | solution.py:26
  23.9 2.8 %collective-permute-done.7.refs_2_ = bf16[144,320]{1,0:T(8,128)(2,1)S(1)} collective-permute-done((bf16[144,320]{1,0:T(8,128)(2,1)S(1)}, bf16[144,320]{1,0:T(8,128)(2,1)S(1)}, u32[]{:S(2)}, u32[]{:S(2)}) %collective-permute-start.7) | collective-permute-done | bytes 92192 | tf_op jit(solution)/shard_map/ppermute | solution.py:26
  26.7 1.8 collective-permute-done.6.refs_1_
  28.6 5.2 %collective-permute-start.10 = (bf16[64,2048]{1,0:T(8,128)(2,1)}, bf16[64,2048]{1,0:T(8,128)(2,1)S(1)}, u32[]{:S(2)}, u32[]{:S(2)}) collective-permute-start(bf16[64,2048]{1,0:T(8,128)(2,1)} %collective-permute-done.1.refs_1_), channel_id=1, source_target_pairs={{0,2},{1,3},{2,0},{3,1},{4,6},{5,7},{6,4},{7,5},{8,10},{9,11},{10,... | collective-permute-start | bytes 786440 | tf_op jit(solution)/shard_map/ppermute | solution.py:31
  33.9 3.9 %collective-permute-start.13 = (bf16[64,2048]{1,0:T(8,128)(2,1)}, bf16[64,2048]{1,0:T(8,128)(2,1)}, u32[]{:S(2)}, u32[]{:S(2)}) collective-permute-start(bf16[64,2048]{1,0:T(8,128)(2,1)} %get-tuple-element.111.refs_0_), channel_id=1, source_target_pairs={{0,4},{1,5},{2,6},{3,7},{4,0},{5,1},{6,2},{7,3},{8,12},{9,13},{10,... | collective-permute-start | bytes 786440 | tf_op jit(solution)/shard_map/ppermute | solution.py:31
  39.7 7.1 %collective-permute-done.10.refs_3_ = bf16[64,2048]{1,0:T(8,128)(2,1)S(1)} collective-permute-done((bf16[64,2048]{1,0:T(8,128)(2,1)}, bf16[64,2048]{1,0:T(8,128)(2,1)S(1)}, u32[]{:S(2)}, u32[]{:S(2)}) %collective-permute-start.10) | collective-permute-done | bytes 262176 | tf_op jit(solution)/shard_map/ppermute | solution.py:31
  47.8 2.1 stack.32.weight
  49.8 1.5 collective-permute-start.12
  51.3 1.5 collective-permute-start.11
  53.6 2.4 %collective-permute-start.15 = (bf16[64,2048]{1,0:T(8,128)(2,1)}, bf16[64,2048]{1,0:T(8,128)(2,1)}, u32[]{:S(2)}, u32[]{:S(2)}) collective-permute-start(bf16[64,2048]{1,0:T(8,128)(2,1)} %collective-permute-done.13.refs_1_), channel_id=1, source_target_pairs={{0,2},{1,3},{2,0},{3,1},{4,6},{5,7},{6,4},{7,5},{8,10},{9,11},{10,... | collective-permute-start | bytes 786440 | tf_op jit(solution)/shard_map/ppermute | solution.py:31
  58.2 1.6 copy-done.1
  59.8 7.4 %heads_backward.6 = (bf16[128,8192]{1,0:T(8,128)(2,1)}, bf16[128,4096]{1,0:T(8,128)(2,1)}, bf16[128,6144]{1,0:T(8,128)(2,1)S(1)}, f32[128,1024]{1,0:T(8,128)S(1)...) custom-call(s32[6]{0:T(128)S(1)} %copy-done.20, bf16[128,8192]{1,0:T(8,128)(2,1)S(1)} %bitcast.18, ...), custom_call_target="tpu_custom_call" | custom-call | flops 200000000 | bytes 600000 | tf_op jit(solution)/shard_map/heads_backward/pallas_call | solution.py:158
  67.2 1.5 stack.33.weight
  68.7 13.0 %heads_backward.7 = (bf16[128,8192]{1,0:T(8,128)(2,1)}, bf16[128,4096]{1,0:T(8,128)(2,1)}, bf16[128,6144]{1,0:T(8,128)(2,1)S(1)}, f32[128,2048]{1,0:T(8,128)S(1)...) custom-call(s32[6]{0:T(128)S(1)} %copy-done.20, ...), custom_call_target="tpu_custom_call", output_to_operand_aliasing={{0}: (14, {}), {1}: (15, {}), {2}: (16, {})} | custom-call | flops 400000000 | bytes 1200000 | tf_op jit(solution)/shard_map/heads_backward/pallas_call | solution.py:158
  81.7 1.5 collective-permute-start.16
  83.2 1.5 collective-permute-start.17
  84.8 13.0 %heads_backward.8 = (bf16[128,8192]{1,0:T(8,128)(2,1)}, bf16[128,4096]{1,0:T(8,128)(2,1)}, bf16[128,6144]{1,0:T(8,128)(2,1)S(1)}, f32[128,2048]{1,0:T(8,128)S(1)...) custom-call(s32[6]{0:T(128)S(1)} %copy-done.20, ...), custom_call_target="tpu_custom_call", output_to_operand_aliasing={{0}: (14, {}), {1}: (15, {}), {2}: (16, {})} | custom-call | flops 400000000 | bytes 1200000 | tf_op jit(solution)/shard_map/heads_backward/pallas_call | solution.py:158
  98.3 7.4 %heads_backward.9 = (bf16[128,8192]{1,0:T(8,128)(2,1)}, bf16[128,4096]{1,0:T(8,128)(2,1)}, bf16[128,6144]{1,0:T(8,128)(2,1)S(1)}, f32[128,1024]{1,0:T(8,128)S(1)...) custom-call(s32[6]{0:T(128)S(1)} %copy-done.20, ...), custom_call_target="tpu_custom_call", output_to_operand_aliasing={{0}: (14, {}), {1}: (15, {}), {2}: (16, {})} | custom-call | flops 200000000 | bytes 600000 | tf_op jit(solution)/shard_map/heads_backward/pallas_call | solution.py:158
  105.7 2.1 collective-permute-done.16
  107.8 1.5 collective-permute-start.19
  109.3 7.6 %heads_backward.10 = (bf16[128,8192]{1,0:T(8,128)(2,1)}, bf16[128,4096]{1,0:T(8,128)(2,1)}, bf16[128,6144]{1,0:T(8,128)(2,1)S(1)}, f32[128,1024]{1,0:T(8,128)S(1...) custom-call(s32[6]{0:T(128)S(1)} %copy-done.20, ...), custom_call_target="tpu_custom_call", output_to_operand_aliasing={{0}: (14, {}), {1}: (15, {}), {2}: (16, {})} | custom-call | flops 200000000 | bytes 600000 | tf_op jit(solution)/shard_map/heads_backward/pallas_call | solution.py:158
  118.7 1.5 collective-permute-start.26
  121.3 9.0 %collective-permute-done.18 = f32[128,2048]{1,0:T(8,128)S(1)} collective-permute-done((f32[128,2048]{1,0:T(8,128)S(1)}, f32[128,2048]{1,0:T(8,128)S(1)}, u32[]{:S(2)}, u32[]{:S(2)}) %collective-permute-start.18) | collective-permute-done | bytes 1048608 | tf_op jit(solution)/shard_map/ppermute | solution.py:31
  130.3 1.5 collective-permute-start.25
  131.8 1.5 collective-permute-start.31
  134.2 7.5 %heads_backward.11 = (bf16[128,8192]{1,0:T(8,128)(2,1)}, bf16[128,4096]{1,0:T(8,128)(2,1)}, bf16[128,6144]{1,0:T(8,128)(2,1)S(1)}, f32[128,1024]{1,0:T(8,128)S(1...) custom-call(s32[6]{0:T(128)S(1)} %copy-done.20, ...), custom_call_target="tpu_custom_call", output_to_operand_aliasing={{0}: (14, {}), {1}: (15, {}), {2}: (16, {})} | custom-call | flops 200000000 | bytes 600000 | tf_op jit(solution)/shard_map/heads_backward/pallas_call | solution.py:158
  142.4 1.7 spread.1
  146.2 2.0 add_add_fusion.2
  148.9 2.2 copy.37
  151.1 1.5 add.64
  155.2 8.3 %collective-permute-done.27 = f32[128,1024]{1,0:T(8,128)} collective-permute-done((f32[128,1024]{1,0:T(8,128)}, f32[128,1024]{1,0:T(8,128)}, u32[]{:S(2)}, u32[]{:S(2)}) %collective-permute-start.27) | collective-permute-done | bytes 524320 | tf_op jit(solution)/shard_map/ppermute | solution.py:31
  165.8 1.4 fusion.1
  168.1 3.7 %collective-permute-done.23 = f32[128,320]{1,0:T(8,128)S(1)} collective-permute-done((f32[128,320]{1,0:T(8,128)S(1)}, f32[128,320]{1,0:T(8,128)S(1)}, u32[]{:S(2)}, u32[]{:S(2)}) %collective-permute-start.23) | collective-permute-done | bytes 163872 | tf_op jit(solution)/shard_map/ppermute | solution.py:26
  172.5 9.6 %collective-permute-done.28 = f32[64,1024]{1,0:T(8,128)S(1)} collective-permute-done((f32[64,1024]{1,0:T(8,128)S(1)}, f32[64,1024]{1,0:T(8,128)S(1)}, u32[]{:S(2)}, u32[]{:S(2)}) %collective-permute-start.28) | collective-permute-done | bytes 262176 | tf_op jit(solution)/shard_map/ppermute | solution.py:31
  182.2 5.8 %collective-permute-done.32 = f32[128,1024]{1,0:T(8,128)S(1)} collective-permute-done((f32[128,1024]{1,0:T(8,128)S(1)}, f32[128,1024]{1,0:T(8,128)S(1)}, u32[]{:S(2)}, u32[]{:S(2)}) %collective-permute-start.32) | collective-permute-done | bytes 524320 | tf_op jit(solution)/shard_map/ppermute | solution.py:31
  191.8 11.9 %collective-permute-done.33 = f32[64,1024]{1,0:T(8,128)S(1)} collective-permute-done((f32[64,1024]{1,0:T(8,128)S(1)}, f32[64,1024]{1,0:T(8,128)S(1)}, u32[]{:S(2)}, u32[]{:S(2)}) %collective-permute-start.33) | collective-permute-done | bytes 262176 | tf_op jit(solution)/shard_map/ppermute | solution.py:31
  205.8 2.3 %collective-permute-start.40 = (f32[32,2048]{1,0:T(8,128)S(1)}, f32[32,2048]{1,0:T(8,128)S(1)}, u32[]{:S(2)}, u32[]{:S(2)}) collective-permute-start(f32[32,2048]{1,0:T(8,128)S(1)} %join_cores.3.refs_1_), channel_id=1, source_target_pairs={{0,24},{8,16},{16,8},{24,0},{1,25},{9,17},{17,9},{25,1},{2,26},{10... | collective-permute-start | bytes 786440 | tf_op jit(solution)/shard_map/ppermute | solution.py:31
  209.3 1.7 copy.38
  211.0 2.4 %place_columns.1 = (bf16[128,8192]{1,0:T(8,128)(2,1)}, bf16[128,4096]{1,0:T(8,128)(2,1)}) custom-call(s32[6]{0:T(128)S(1)} %copy-done.20, bf16[128,6144]{1,0:T(8,128)(2,1)S(1)} %collective-permute-done.21.received, bf16[128,8192]{1,0:T(8,128)(2,1)} %get-tuple-element.138.q_in, ...), custom_call_target="tpu_custom_call", output_to_operand_aliasing={{0}: (2, {}), {1}: (3, {})} | custom-call | bytes 4000000 | tf_op jit(solution)/shard_map/place_columns/pallas_call | solution.py:187
  213.6 6.6 %collective-permute-done.40.refs_7_ = f32[32,2048]{1,0:T(8,128)S(1)} collective-permute-done((f32[32,2048]{1,0:T(8,128)S(1)}, f32[32,2048]{1,0:T(8,128)S(1)}, u32[]{:S(2)}, u32[]{:S(2)}) %collective-permute-start.40) | collective-permute-done | bytes 262176 | tf_op jit(solution)/shard_map/ppermute | solution.py:31
  220.2 3.6 %collective-permute-done.38.refs_5_ = f32[32,2048]{1,0:T(8,128)S(1)} collective-permute-done((f32[32,2048]{1,0:T(8,128)S(1)}, f32[32,2048]{1,0:T(8,128)S(1)}, u32[]{:S(2)}, u32[]{:S(2)}) %collective-permute-start.38) | collective-permute-done | bytes 262176 | tf_op jit(solution)/shard_map/ppermute | solution.py:31
  224.2 3.4 %lay_out.1 = f32[32,16384]{1,0:T(8,128)} custom-call(s32[6]{0:T(128)S(1)} %copy-done.20, f32[32,2048]{1,0:T(8,128)S(1)} %join_cores.2.refs_0_, f32[32,2048]{1,0:T(8,128)S(1)} %join_cores.3.refs_1_, f32[32,2048]{1,0:T(8,128)S(1)} %collective-permute-done.35.refs_2_, f32[32,2048]{1,0:T(8,128)} %collective-permute-done.36.refs_3_, ...), custom_call_target="tpu_custom_call" | custom-call | bytes 4000000 | tf_op jit(solution)/shard_map/lay_out/pallas_call | solution.py:296
  (141 shorter events, 30.0 us)
Async XLA Ops:
  3.7 34.0 %copy-start.6 = (f32[1,64,128]{2,1,0:T(8,128)S(1)}, f32[1,64,128]{2,1,0:T(8,128)}, u32[]{:S(2)}) copy-start(f32[1,64,128]{2,1,0:T(8,128)} %param.11) | copy-start | bytes 98308
  3.7 1.8 collective-permute-start
  5.6 9.1 %collective-permute-start.2 = (bf16[128,8192]{1,0:T(8,128)(2,1)S(1)}, bf16[128,8192]{1,0:T(8,128)(2,1)}, u32[]{:S(2)}, u32[]{:S(2)}) collective-permute-start(bf16[128,8192]{1,0:T(8,128)(2,1)S(1)} %bitcast.17), channel_id=1, source_target_pairs={{0,1},{1,0},{2,3},{3,2},{4,5},{5,4},{6,7},{7,6},{8,9},{9,8},{10,11... | collective-permute-start | bytes 6291464 | tf_op jit(solution)/shard_map/ppermute | solution.py:31
  5.9 8.8 %collective-permute-start.4 = (bf16[128,8192]{1,0:T(8,128)(2,1)}, bf16[128,8192]{1,0:T(8,128)(2,1)}, u32[]{:S(2)}, u32[]{:S(2)}) collective-permute-start(bf16[128,8192]{1,0:T(8,128)(2,1)} %bitcast.24), channel_id=1, source_target_pairs={{0,1},{1,0},{2,3},{3,2},{4,5},{5,4},{6,7},{7,6},{8,9},{9,8},{10,11... | collective-permute-start | bytes 6291464 | tf_op jit(solution)/shard_map/ppermute | solution.py:31
  6.1 8.6 %collective-permute-start.3 = (bf16[128,4096]{1,0:T(8,128)(2,1)}, bf16[128,4096]{1,0:T(8,128)(2,1)}, u32[]{:S(2)}, u32[]{:S(2)}) collective-permute-start(bf16[128,4096]{1,0:T(8,128)(2,1)} %bitcast.31), channel_id=1, source_target_pairs={{0,1},{1,0},{2,3},{3,2},{4,5},{5,4},{6,7},{7,6},{8,9},{9,8},{10,11... | collective-permute-start | bytes 3145736 | tf_op jit(solution)/shard_map/ppermute | solution.py:31
  9.0 46.9 %copy-start.31 = (s32[1,8,4]{1,2,0:T(4,128)S(1)}, s32[1,8,4]{1,2,0:T(4,128)}, u32[]{:S(2)}) copy-start(s32[1,8,4]{1,2,0:T(4,128)} %param.15) | copy-start | bytes 388
  9.0 47.0 %copy-start.20 = (s32[6]{0:T(128)S(1)}, s32[6]{0:T(128)}, u32[]{:S(2)}) copy-start(s32[6]{0:T(128)} %stack.30.place) | copy-start | bytes 76
  9.0 49.1 %copy-start.5 = (bf16[1,128,4096]{2,1,0:T(8,128)(2,1)S(1)}, bf16[1,128,4096]{2,1,0:T(8,128)(2,1)}, u32[]{:S(2)}) copy-start(bf16[1,128,4096]{2,1,0:T(8,128)(2,1)} %param.9) | copy-start | bytes 3145732
  9.0 19.6 %collective-permute-start.9 = (bf16[64,2048]{1,0:T(8,128)(2,1)}, bf16[64,2048]{1,0:T(8,128)(2,1)}, u32[]{:S(2)}, u32[]{:S(2)}) collective-permute-start(bf16[64,2048]{1,0:T(8,128)(2,1)} %get-tuple-element.100.refs_0_), channel_id=1, source_target_pairs={{0,2},{1,3},{2,0},{3,1},{4,6},{5,7},{6,4},{7,5},{8,10},{9,11},{10,... | collective-permute-start | bytes 786440 | tf_op jit(solution)/shard_map/ppermute | solution.py:31
  11.8 16.8 %collective-permute-start.1 = (bf16[64,2048]{1,0:T(8,128)(2,1)}, bf16[64,2048]{1,0:T(8,128)(2,1)}, u32[]{:S(2)}, u32[]{:S(2)}) collective-permute-start(bf16[64,2048]{1,0:T(8,128)(2,1)} %get-tuple-element.100.refs_0_), channel_id=1, source_target_pairs={{0,4},{1,5},{2,6},{3,7},{4,0},{5,1},{6,2},{7,3},{8,12},{9,13},{10,... | collective-permute-start | bytes 786440 | tf_op jit(solution)/shard_map/ppermute | solution.py:31
  14.7 12.0 %collective-permute-start.7 = (bf16[144,320]{1,0:T(8,128)(2,1)S(1)}, bf16[144,320]{1,0:T(8,128)(2,1)S(1)}, u32[]{:S(2)}, u32[]{:S(2)}) collective-permute-start(bf16[144,320]{1,0:T(8,128)(2,1)S(1)} %fusion.4.refs_0_), channel_id=1, source_target_pairs={{0,4},{1,5},{2,6},{3,7},{8,12},{9,13},{10,14},{11,15},{16,20},{17,... | collective-permute-start | bytes 276488 | tf_op jit(solution)/shard_map/ppermute | solution.py:26
  20.4 8.1 %collective-permute-start.6 = (bf16[144,320]{1,0:T(8,128)(2,1)S(1)}, bf16[144,320]{1,0:T(8,128)(2,1)S(1)}, u32[]{:S(2)}, u32[]{:S(2)}) collective-permute-start(bf16[144,320]{1,0:T(8,128)(2,1)S(1)} %fusion.4.refs_0_), channel_id=1, source_target_pairs={{0,2},{1,3},{2,4},{3,5},{4,6},{5,7},{8,10},{9,11},{10,12},{11,13},... | collective-permute-start | bytes 276488 | tf_op jit(solution)/shard_map/ppermute | solution.py:26
  28.5 10.5 %collective-permute-start.8 = (bf16[432,320]{1,0:T(8,128)(2,1)S(1)}, bf16[432,320]{1,0:T(8,128)(2,1)S(1)}, u32[]{:S(2)}, u32[]{:S(2)}) collective-permute-start(bf16[432,320]{1,0:T(8,128)(2,1)S(1)} %stack.31.own), channel_id=1, source_target_pairs={{0,1},{1,0},{2,3},{3,2},{4,5},{5,4},{6,7},{7,6},{8,9},{9,8},{10,11... | collective-permute-start | bytes 829448 | tf_op jit(solution)/shard_map/ppermute | solution.py:31
  28.6 18.2 %collective-permute-start.10 = (bf16[64,2048]{1,0:T(8,128)(2,1)}, bf16[64,2048]{1,0:T(8,128)(2,1)S(1)}, u32[]{:S(2)}, u32[]{:S(2)}) collective-permute-start(bf16[64,2048]{1,0:T(8,128)(2,1)} %collective-permute-done.1.refs_1_), channel_id=1, source_target_pairs={{0,2},{1,3},{2,0},{3,1},{4,6},{5,7},{6,4},{7,5},{8,10},{9,11},{10,... | collective-permute-start | bytes 786440 | tf_op jit(solution)/shard_map/ppermute | solution.py:31
  33.8 19.0 %collective-permute-start.14 = (bf16[64,2048]{1,0:T(8,128)(2,1)}, bf16[64,2048]{1,0:T(8,128)(2,1)S(1)}, u32[]{:S(2)}, u32[]{:S(2)}) collective-permute-start(bf16[64,2048]{1,0:T(8,128)(2,1)} %get-tuple-element.111.refs_0_), channel_id=1, source_target_pairs={{0,2},{1,3},{2,0},{3,1},{4,6},{5,7},{6,4},{7,5},{8,10},{9,11},{10,... | collective-permute-start | bytes 786440 | tf_op jit(solution)/shard_map/ppermute | solution.py:31
  33.9 19.6 %collective-permute-start.13 = (bf16[64,2048]{1,0:T(8,128)(2,1)}, bf16[64,2048]{1,0:T(8,128)(2,1)}, u32[]{:S(2)}, u32[]{:S(2)}) collective-permute-start(bf16[64,2048]{1,0:T(8,128)(2,1)} %get-tuple-element.111.refs_0_), channel_id=1, source_target_pairs={{0,4},{1,5},{2,6},{3,7},{4,0},{5,1},{6,2},{7,3},{8,12},{9,13},{10,... | collective-permute-start | bytes 786440 | tf_op jit(solution)/shard_map/ppermute | solution.py:31
  37.8 1.2 collective-permute-start.5
  49.8 34.9 %collective-permute-start.12 = (bf16[256,2048]{1,0:T(8,128)(2,1)}, bf16[256,2048]{1,0:T(8,128)(2,1)}, u32[]{:S(2)}, u32[]{:S(2)}) collective-permute-start(bf16[256,2048]{1,0:T(8,128)(2,1)} %stack.32.weight), channel_id=1, source_target_pairs={{0,8},{8,0},{16,24},{24,16},{1,9},{9,1},{17,25},{25,17},{2,10},{10... | collective-permute-start | bytes 3145736 | tf_op jit(solution)/shard_map/ppermute | solution.py:31
  51.3 33.4 %collective-permute-start.11 = (bf16[256,2048]{1,0:T(8,128)(2,1)}, bf16[256,2048]{1,0:T(8,128)(2,1)}, u32[]{:S(2)}, u32[]{:S(2)}) collective-permute-start(bf16[256,2048]{1,0:T(8,128)(2,1)} %stack.32.weight), channel_id=1, source_target_pairs={{0,16},{8,24},{16,0},{24,8},{1,17},{9,25},{17,1},{25,9},{2,18},{10... | collective-permute-start | bytes 3145736 | tf_op jit(solution)/shard_map/ppermute | solution.py:31
  53.6 13.6 %collective-permute-start.15 = (bf16[64,2048]{1,0:T(8,128)(2,1)}, bf16[64,2048]{1,0:T(8,128)(2,1)}, u32[]{:S(2)}, u32[]{:S(2)}) collective-permute-start(bf16[64,2048]{1,0:T(8,128)(2,1)} %collective-permute-done.13.refs_1_), channel_id=1, source_target_pairs={{0,2},{1,3},{2,0},{3,1},{4,6},{5,7},{6,4},{7,5},{8,10},{9,11},{10,... | collective-permute-start | bytes 786440 | tf_op jit(solution)/shard_map/ppermute | solution.py:31
  68.7 16.0 %copy-start.2 = (bf16[1,128,8192]{2,1,0:T(8,128)(2,1)S(1)}, bf16[1,128,8192]{2,1,0:T(8,128)(2,1)}, u32[]{:S(2)}) copy-start(bf16[1,128,8192]{2,1,0:T(8,128)(2,1)} %param.10) | copy-start | bytes 6291460
  81.7 26.1 %collective-permute-start.16 = (f32[128,2048]{1,0:T(8,128)S(1)}, f32[128,2048]{1,0:T(8,128)S(1)}, u32[]{:S(2)}, u32[]{:S(2)}) collective-permute-start(f32[128,2048]{1,0:T(8,128)S(1)} %get-tuple-element.123), channel_id=1, source_target_pairs={{0,8},{8,0},{16,24},{24,16},{1,9},{9,1},{17,25},{25,17},{2,10},{10... | collective-permute-start | bytes 3145736 | tf_op jit(solution)/shard_map/ppermute | solution.py:31
  83.2 24.6 %collective-permute-start.17 = (f32[128,2048]{1,0:T(8,128)S(1)}, f32[128,2048]{1,0:T(8,128)S(1)}, u32[]{:S(2)}, u32[]{:S(2)}) collective-permute-start(f32[128,2048]{1,0:T(8,128)S(1)} %get-tuple-element.124), channel_id=1, source_target_pairs={{0,16},{8,24},{16,0},{24,8},{1,17},{9,25},{17,1},{25,9},{2,18},{10... | collective-permute-start | bytes 3145736 | tf_op jit(solution)/shard_map/ppermute | solution.py:31
  97.8 32.5 %collective-permute-start.18 = (f32[128,2048]{1,0:T(8,128)S(1)}, f32[128,2048]{1,0:T(8,128)S(1)}, u32[]{:S(2)}, u32[]{:S(2)}) collective-permute-start(f32[128,2048]{1,0:T(8,128)S(1)} %get-tuple-element.130), channel_id=1, source_target_pairs={{0,8},{8,0},{16,24},{24,16},{1,9},{9,1},{17,25},{25,17},{2,10},{10... | collective-permute-start | bytes 3145736 | tf_op jit(solution)/shard_map/ppermute | solution.py:31
  107.8 25.5 %collective-permute-start.19 = (f32[128,1024]{1,0:T(8,128)S(1)}, f32[128,1024]{1,0:T(8,128)S(1)}, u32[]{:S(2)}, u32[]{:S(2)}) collective-permute-start(f32[128,1024]{1,0:T(8,128)S(1)} %get-tuple-element.131), channel_id=1, source_target_pairs={{0,16},{8,24},{16,0},{24,8},{1,17},{9,25},{17,1},{25,9},{2,18},{10... | collective-permute-start | bytes 1572872 | tf_op jit(solution)/shard_map/ppermute | solution.py:31
  117.0 16.3 %collective-permute-start.20 = (f32[128,1024]{1,0:T(8,128)S(1)}, f32[128,1024]{1,0:T(8,128)S(1)}, u32[]{:S(2)}, u32[]{:S(2)}) collective-permute-start(f32[128,1024]{1,0:T(8,128)S(1)} %get-tuple-element.132), channel_id=1, source_target_pairs={{0,16},{8,24},{16,0},{24,8},{1,17},{9,25},{17,1},{25,9},{2,18},{10... | collective-permute-start | bytes 1572872 | tf_op jit(solution)/shard_map/ppermute | solution.py:31
  118.7 27.5 %collective-permute-start.26 = (f32[128,1024]{1,0:T(8,128)}, f32[128,1024]{1,0:T(8,128)}, u32[]{:S(2)}, u32[]{:S(2)}) collective-permute-start(f32[128,1024]{1,0:T(8,128)} %get-tuple-element.158), channel_id=1, source_target_pairs={{0,8},{8,0},{16,24},{24,16},{1,9},{9,1},{17,25},{25,17},{2,10},{10... | collective-permute-start | bytes 1572872 | tf_op jit(solution)/shard_map/ppermute | solution.py:31
  130.3 17.9 %collective-permute-start.25 = (f32[128,1024]{1,0:T(8,128)}, f32[128,1024]{1,0:T(8,128)}, u32[]{:S(2)}, u32[]{:S(2)}) collective-permute-start(f32[128,1024]{1,0:T(8,128)} %get-tuple-element.155), channel_id=1, source_target_pairs={{0,16},{8,24},{16,0},{24,8},{1,17},{9,25},{17,1},{25,9},{2,18},{10... | collective-permute-start | bytes 1572872 | tf_op jit(solution)/shard_map/ppermute | solution.py:31
  131.8 22.1 %collective-permute-start.31 = (f32[128,1024]{1,0:T(8,128)}, f32[128,1024]{1,0:T(8,128)}, u32[]{:S(2)}, u32[]{:S(2)}) collective-permute-start(f32[128,1024]{1,0:T(8,128)} %get-tuple-element.170), channel_id=1, source_target_pairs={{0,8},{8,0},{16,24},{24,16},{1,9},{9,1},{17,25},{25,17},{2,10},{10... | collective-permute-start | bytes 1572872 | tf_op jit(solution)/shard_map/ppermute | solution.py:31
  146.2 2.7 %collective-permute-start.22 = (f32[432,320]{0,1:T(8,128)}, f32[432,320]{0,1:T(8,128)}, u32[]{:S(2)}, u32[]{:S(2)}) collective-permute-start(f32[432,320]{0,1:T(8,128)} %copy.36), channel_id=1, source_target_pairs={{0,1},{1,0},{2,3},{3,2},{4,5},{5,4},{6,7},{7,6},{8,9},{9,8},{10,11... | collective-permute-start | bytes 1658888 | tf_op jit(solution)/shard_map/ppermute | solution.py:31
  148.2 15.4 %collective-permute-start.27 = (f32[128,1024]{1,0:T(8,128)}, f32[128,1024]{1,0:T(8,128)}, u32[]{:S(2)}, u32[]{:S(2)}) collective-permute-start(f32[128,1024]{1,0:T(8,128)} %add_add_fusion.2), channel_id=1, source_target_pairs={{0,2},{1,3},{2,0},{3,1},{4,6},{5,7},{6,4},{7,5},{8,10},{9,11},{10,... | collective-permute-start | bytes 1572872 | tf_op jit(solution)/shard_map/ppermute | solution.py:31
  148.2 15.4 %collective-permute-start.30 = (f32[128,1024]{1,0:T(8,128)}, f32[128,1024]{1,0:T(8,128)}, u32[]{:S(2)}, u32[]{:S(2)}) collective-permute-start(f32[128,1024]{1,0:T(8,128)} %get-tuple-element.165), channel_id=1, source_target_pairs={{0,16},{8,24},{16,0},{24,8},{1,17},{9,25},{17,1},{25,9},{2,18},{10... | collective-permute-start | bytes 1572872 | tf_op jit(solution)/shard_map/ppermute | solution.py:31
  148.7 40.5 %collective-permute-start.21 = (bf16[128,6144]{1,0:T(8,128)(2,1)S(1)}, bf16[128,6144]{1,0:T(8,128)(2,1)S(1)}, u32[]{:S(2)}, u32[]{:S(2)}) collective-permute-start(bf16[128,6144]{1,0:T(8,128)(2,1)S(1)} %copy-done.4), channel_id=1, source_target_pairs={{0,1},{1,0},{2,3},{3,2},{4,5},{5,4},{6,7},{7,6},{8,9},{9,8},{10,11... | collective-permute-start | bytes 4718600 | tf_op jit(solution)/shard_map/ppermute | solution.py:31
  151.1 14.7 %copy-start.24 = (f32[128,2048]{1,0:T(8,128)S(1)}, f32[128,2048]{1,0:T(8,128)}, u32[]{:S(2)}) copy-start(f32[128,2048]{1,0:T(8,128)} %copy-done.23) | copy-start | bytes 3145732
  152.6 19.1 %collective-permute-start.23 = (f32[128,320]{1,0:T(8,128)S(1)}, f32[128,320]{1,0:T(8,128)S(1)}, u32[]{:S(2)}, u32[]{:S(2)}) collective-permute-start(f32[128,320]{1,0:T(8,128)S(1)} %get-tuple-element.186), channel_id=1, source_target_pairs={{2,0},{3,1},{4,2},{5,3},{6,4},{7,5},{10,8},{11,9},{12,10},{13,11},... | collective-permute-start | bytes 491528 | tf_op jit(solution)/shard_map/ppermute | solution.py:26
  153.9 17.8 %collective-permute-start.24 = (f32[128,320]{1,0:T(8,128)S(1)}, f32[128,320]{1,0:T(8,128)S(1)}, u32[]{:S(2)}, u32[]{:S(2)}) collective-permute-start(f32[128,320]{1,0:T(8,128)S(1)} %get-tuple-element.187), channel_id=1, source_target_pairs={{4,0},{5,1},{6,2},{7,3},{12,8},{13,9},{14,10},{15,11},{20,16},{21,... | collective-permute-start | bytes 491528 | tf_op jit(solution)/shard_map/ppermute | solution.py:26
  164.7 23.2 %collective-permute-start.32 = (f32[128,1024]{1,0:T(8,128)S(1)}, f32[128,1024]{1,0:T(8,128)S(1)}, u32[]{:S(2)}, u32[]{:S(2)}) collective-permute-start(f32[128,1024]{1,0:T(8,128)S(1)} %add_add_fusion), channel_id=1, source_target_pairs={{0,2},{1,3},{2,0},{3,1},{4,6},{5,7},{6,4},{7,5},{8,10},{9,11},{10,... | collective-permute-start | bytes 1572872 | tf_op jit(solution)/shard_map/ppermute | solution.py:31
  165.8 22.2 %copy-start.11 = (f32[128,1024]{1,0:T(8,128)S(1)}, f32[128,1024]{1,0:T(8,128)}, u32[]{:S(2)}) copy-start(f32[128,1024]{1,0:T(8,128)} %copy-done.10) | copy-start | bytes 1572868
  167.2 14.9 %collective-permute-start.28 = (f32[64,1024]{1,0:T(8,128)S(1)}, f32[64,1024]{1,0:T(8,128)S(1)}, u32[]{:S(2)}, u32[]{:S(2)}) collective-permute-start(f32[64,1024]{1,0:T(8,128)S(1)} %slice.83), channel_id=1, source_target_pairs={{0,4},{1,5},{2,6},{3,7},{4,0},{5,1},{6,2},{7,3},{8,12},{9,13},{10,... | collective-permute-start | bytes 786440 | tf_op jit(solution)/shard_map/ppermute | solution.py:31
  189.2 14.5 %collective-permute-start.33 = (f32[64,1024]{1,0:T(8,128)S(1)}, f32[64,1024]{1,0:T(8,128)S(1)}, u32[]{:S(2)}, u32[]{:S(2)}) collective-permute-start(f32[64,1024]{1,0:T(8,128)S(1)} %slice.73), channel_id=1, source_target_pairs={{0,4},{1,5},{2,6},{3,7},{4,0},{5,1},{6,2},{7,3},{8,12},{9,13},{10,... | collective-permute-start | bytes 786440 | tf_op jit(solution)/shard_map/ppermute | solution.py:31
  189.3 1.4 collective-permute-start.29
  191.3 17.3 %collective-permute-start.39 = (f32[32,2048]{1,0:T(8,128)S(1)}, f32[32,2048]{1,0:T(8,128)S(1)}, u32[]{:S(2)}, u32[]{:S(2)}) collective-permute-start(f32[32,2048]{1,0:T(8,128)S(1)} %join_cores.2.refs_0_), channel_id=1, source_target_pairs={{0,24},{8,16},{16,8},{24,0},{1,25},{9,17},{17,9},{25,1},{2,26},{10... | collective-permute-start | bytes 786440 | tf_op jit(solution)/shard_map/ppermute | solution.py:31
  203.8 1.4 collective-permute-start.34
  203.9 9.6 %collective-permute-start.37 = (f32[32,2048]{1,0:T(8,128)S(1)}, f32[32,2048]{1,0:T(8,128)S(1)}, u32[]{:S(2)}, u32[]{:S(2)}) collective-permute-start(f32[32,2048]{1,0:T(8,128)S(1)} %join_cores.2.refs_0_), channel_id=1, source_target_pairs={{0,16},{8,24},{16,0},{24,8},{1,17},{9,25},{17,1},{25,9},{2,18},{10... | collective-permute-start | bytes 786440 | tf_op jit(solution)/shard_map/ppermute | solution.py:31
  204.4 9.2 %collective-permute-start.35 = (f32[32,2048]{1,0:T(8,128)S(1)}, f32[32,2048]{1,0:T(8,128)S(1)}, u32[]{:S(2)}, u32[]{:S(2)}) collective-permute-start(f32[32,2048]{1,0:T(8,128)S(1)} %join_cores.2.refs_0_), channel_id=1, source_target_pairs={{0,8},{8,0},{16,24},{24,16},{1,9},{9,1},{17,25},{25,17},{2,10},{10... | collective-permute-start | bytes 786440 | tf_op jit(solution)/shard_map/ppermute | solution.py:31
  205.8 14.4 %collective-permute-start.40 = (f32[32,2048]{1,0:T(8,128)S(1)}, f32[32,2048]{1,0:T(8,128)S(1)}, u32[]{:S(2)}, u32[]{:S(2)}) collective-permute-start(f32[32,2048]{1,0:T(8,128)S(1)} %join_cores.3.refs_1_), channel_id=1, source_target_pairs={{0,24},{8,16},{16,8},{24,0},{1,25},{9,17},{17,9},{25,1},{2,26},{10... | collective-permute-start | bytes 786440 | tf_op jit(solution)/shard_map/ppermute | solution.py:31
  208.1 15.8 %collective-permute-start.38 = (f32[32,2048]{1,0:T(8,128)S(1)}, f32[32,2048]{1,0:T(8,128)S(1)}, u32[]{:S(2)}, u32[]{:S(2)}) collective-permute-start(f32[32,2048]{1,0:T(8,128)S(1)} %join_cores.3.refs_1_), channel_id=1, source_target_pairs={{0,16},{8,24},{16,0},{24,8},{1,17},{9,25},{17,1},{25,9},{2,18},{10... | collective-permute-start | bytes 786440 | tf_op jit(solution)/shard_map/ppermute | solution.py:31
  208.6 15.6 %collective-permute-start.36 = (f32[32,2048]{1,0:T(8,128)S(1)}, f32[32,2048]{1,0:T(8,128)}, u32[]{:S(2)}, u32[]{:S(2)}) collective-permute-start(f32[32,2048]{1,0:T(8,128)S(1)} %join_cores.3.refs_1_), channel_id=1, source_target_pairs={{0,8},{8,0},{16,24},{24,16},{1,9},{9,1},{17,25},{25,17},{2,10},{10... | collective-permute-start | bytes 786440 | tf_op jit(solution)/shard_map/ppermute | solution.py:31
  (26 other events, 144.7 us)

commit v7 on v6

--- a/solution.py
+++ b/solution.py
@@ -533,7 +533,7 @@
         at_step[2] = exchange(start, "ctx", 2)
         for step in range(4, n_ctx, 4):
             at_step[step + 2] = exchange(after(at_step[step], at_step[2]), "ctx", 2)
-        return [at_step[partner] for partner in partners], at_step[n_ctx - 4]
+        return [at_step[partner] for partner in partners], at_step[n_ctx - 2]
 
     def joined(pieces):
         return stack(pieces, (tuple((index, 0) for index in range(len(pieces))),), part_cols)[0]
@@ -546,7 +546,7 @@
     for arrays in (own, sibling):
         arrays[3] = arrays[3].reshape(heads // 2, 2, group_len)
 
-    weights = {0: joined([after(near_pieces[0], sib_bundles, sibling[3])] + near_pieces[1:])}
+    weights = {0: joined([after(near_pieces[0], shared[0], sibling[3])] + near_pieces[1:])}
     for t in range(1, far):
         weights[t] = exchange(weights[0], "dp", t)
     earlier = None
@@ -556,16 +556,12 @@
     orders = (bits, bits[::-1])
     first_sums = [{t: [] for t in range(n_dp) if t & order[0]} for order in orders]
     half_pairs = pairs // 2
-    units = [(0, 0, half_pairs)] + [(t, 0, pairs) for t in [far] + list(range(1, far - 1))]
+    units = [(t, 0, pairs) for t in [0, far] + list(range(1, far - 1))]
     units += [(far - 1, 0, half_pairs), (far - 1, half_pairs, half_pairs)]
-    units.append((0, half_pairs, half_pairs))
     for t, start, count in units:
         if t == far:
             weights[far] = joined([after(far_pieces[0], latents[-1])] + far_pieces[1:])
         weight = weights[t]
-        if t == 0 and start:
-            there = [piece for sent in first_sums for u in sent for piece in sent[u]]
-            weight = after(weight, latents[-1], *there)
         if t == 1 and not start:
             weight = after(weight, *[weights[near] for near in range(2, far)])
         if t == far - 1 and start:
@@ -612,10 +608,10 @@
             for t in sorted((t for t in addends if t & bit), reverse=True):
                 leaving = [total(addends[t], half) for half in range(2)]
                 if side == 0:
-                    behind = (first_sums[0][order[0]][0], last_sums[0])
+                    behind = [(first_sums[0][order[0]][0], last_sums[-1])] * 2
                 else:
-                    behind = [weight_grads[far - 1][side][0]] * 2
-                leaving = [after(half, there) for half, there in zip(leaving, behind)]
+                    behind = [(weight_grads[far - 1][side][0],)] * 2
+                leaving = [after(half, *there) for half, there in zip(leaving, behind)]
                 arrived[t ^ bit] = [exchange(half, "dp", bit) for half in leaving]
             addends = {t: addends[t] + [more] for t, more in arrived.items()}
         sums.append(addends[0])
@@ -624,6 +620,8 @@
     received = exchange(sib_grads, "ctx", 1)
     grad_nope, grad_rope = place_columns(place, received, q_full, rope_full, n_dp)
 
+    first_come = [sent[u][0] for sent in first_sums for u in sent if u != far]
+    latents[-1] = after(latents[-1], *first_come)
     own_grads, sib_grads = spread(place, offered, latents, ropes, 3 * span, lat_block)
     swapped = exchange(sib_grads, "ctx", 1)
     grad_rows = own_grads + swapped
@@ -638,14 +636,15 @@
         if half:
             sums = [[[after(piece, arrived) for piece in pieces] for pieces in side] for side in sums]
         first, second = [total(side, half) for side in sums]
-        there = (sums[0][-1][half], latents[-1]) if half == 0 else (sums[0][-1][half],)
+        there = (sums[0][-1][half], received if half else grad_rows)
         arrived = exchange(after(second, *there), "ctx", ctx_bits[0])
         rows = first + arrived
-        if half:
-            rows = after(rows, received, grad_rows)
         for bit in ctx_bits[1:]:
             rows = halve(rows, "ctx", bit)
-        piece = join_cores(place, rows[:lat_block], exchange(rows[lat_block:], "ctx", 1))
+        kept, crossed = rows[:lat_block], exchange(rows[lat_block:], "ctx", 1)
+        if half:
+            kept = after(kept, *finished[0][1:])
+        piece = join_cores(place, kept, crossed)
         finished.append([piece] + [exchange(piece, "dp", t) for t in range(1, n_dp)])
     finished[0][0] = after(finished[0][0], grad_rows, grad_nope)
     grad_weight = lay_out(place, [piece for both in zip(*finished) for piece in both])

time: 228 us -> 248 us (1.088)
  waiting for transfers between devices: 77.1 us -> 97.9 us
  Pallas kernels: 74.3 us -> 71.4 us
  starting transfers between devices: 51.3 us -> 54.1 us
    ppermute x37, waiting for transfers between devices: 68.8 us -> 83.5 us  [exchange(): lax.ppermute(value, axis, [(source, source ^ bits) for source in range(co...]
    ppermute x4, waiting for transfers between devices: 8.23 us -> 14.4 us  [from_behind(): lax.ppermute(value, axis, [(source, source + steps) for source in range(i...]
    ppermute x37, starting transfers between devices: 39.5 us -> 42.1 us  [exchange(): lax.ppermute(value, axis, [(source, source ^ bits) for source in range(co...]
    pallas_call x6 -> x5, Pallas kernels: 56 us -> 54.4 us  [chunk_backward(): pl.pallas_call(functools.partial(heads_kernel, earlier=len(aliases)), gri...]
    unnamed x67 -> x69, local copies, waits for them, and re-layouts: 9.21 us -> 8.74 us
  transfers between devices with their start and end apart: 41 -> 41, of which waited for: 18 -> 20; matrix products, arithmetic and copies ran while one was open for 7% -> 6% of each run, Pallas kernels for 30% -> 26%
where the time goes in v7:
time: 248 us; the launch traced here: 247 us
  waiting for transfers between devices  97.9 us (39%)
  Pallas kernels  71.4 us (29%)
  starting transfers between devices  54.1 us (22%)
  local copies, waits for them, and re-layouts  13.1 us (5%)
  other arithmetic  9.85 us (4%)
    ppermute x37, waiting for transfers between devices, exchange(): lax.ppermute(value, axis, [(source, source ^ bits) for source in range(co...  83.5 us
    pallas_call x5, Pallas kernels, chunk_backward(): pl.pallas_call(functools.partial(heads_kernel, earlier=len(aliases)), gri...  54.4 us
    ppermute x37, starting transfers between devices, exchange(): lax.ppermute(value, axis, [(source, source ^ bits) for source in range(co...  42.1 us
    ppermute x4, waiting for transfers between devices, from_behind(): lax.ppermute(value, axis, [(source, source + steps) for source in range(i...  14.4 us
    ppermute x4, starting transfers between devices, from_behind(): lax.ppermute(value, axis, [(source, source + steps) for source in range(i...  12 us
    unnamed x69, local copies, waits for them, and re-layouts  8.74 us
    add x4, other arithmetic, total(): left + right  6.23 us
    pallas_call x2, Pallas kernels, weight_parts(): pl.pallas_call(join_rows_kernel if joins else leave_kernel, grid_spec=plt...  5.04 us
  transfers between devices with their start and end apart: 41, of which 20 were waited for; matrix products, arithmetic and copies ran while one was open for 6% of the time, Pallas kernels for 26%

profile of v7, /device:TPU:0, one launch (start us, length us, event | category | flops | bytes accessed | tf_op | source)
XLA Modules:
  0.0 247.4 jit_solution(4076088244644052861)
XLA Ops:
  1.3 2.5 %weight_parts.2 = bf16[32,4096]{1,0:T(8,128)(2,1)} custom-call(s32[6]{0:T(128)} %stack.30.place, bf16[32,16384]{1,0:T(8,128)(2,1)} %distant.3, bf16[32,16384]{1,0:T(8,128)(2,1)} %distant.3), custom_call_target="tpu_custom_call" | custom-call | bytes 1000000 | tf_op jit(solution)/shard_map/weight_parts/pallas_call | solution.py:264
  6.5 2.6 %weight_parts.3 = (bf16[64,2048]{1,0:T(8,128)(2,1)}, bf16[64,2048]{1,0:T(8,128)(2,1)}) custom-call(s32[6]{0:T(128)} %stack.30.place, bf16[32,16384]{1,0:T(8,128)(2,1)} %distant.3, bf16[32,16384]{1,0:T(8,128)(2,1)} %distant.3, bf16[32,4096]{1,0:T(8,128)(2,1)} %copy-done.30), custom_call_target="tpu_custom_call" | custom-call | bytes 1000000 | tf_op jit(solution)/shard_map/weight_parts/pallas_call | solution.py:264
  9.1 2.8 %collective-permute-start.2 = (bf16[64,2048]{1,0:T(8,128)(2,1)}, bf16[64,2048]{1,0:T(8,128)(2,1)}, u32[]{:S(2)}, u32[]{:S(2)}) collective-permute-start(bf16[64,2048]{1,0:T(8,128)(2,1)} %get-tuple-element.96.refs_0_), channel_id=1, source_target_pairs={{0,2},{1,3},{2,0},{3,1},{4,6},{5,7},{6,4},{7,5},{8,10},{9,11},{10,... | collective-permute-start | bytes 786440 | tf_op jit(solution)/shard_map/ppermute | solution.py:31
  11.9 2.6 %collective-permute-start.1 = (bf16[64,2048]{1,0:T(8,128)(2,1)}, bf16[64,2048]{1,0:T(8,128)(2,1)}, u32[]{:S(2)}, u32[]{:S(2)}) collective-permute-start(bf16[64,2048]{1,0:T(8,128)(2,1)} %get-tuple-element.96.refs_0_), channel_id=1, source_target_pairs={{0,4},{1,5},{2,6},{3,7},{4,0},{5,1},{6,2},{7,3},{8,12},{9,13},{10,... | collective-permute-start | bytes 786440 | tf_op jit(solution)/shard_map/ppermute | solution.py:31
  14.7 5.8 %collective-permute-start.9 = (bf16[144,320]{1,0:T(8,128)(2,1)S(1)}, bf16[144,320]{1,0:T(8,128)(2,1)S(1)}, u32[]{:S(2)}, u32[]{:S(2)}) collective-permute-start(bf16[144,320]{1,0:T(8,128)(2,1)S(1)} %fusion.4.refs_0_), channel_id=1, source_target_pairs={{0,4},{1,5},{2,6},{3,7},{8,12},{9,13},{10,14},{11,15},{16,20},{17,... | collective-permute-start | bytes 276488 | tf_op jit(solution)/shard_map/ppermute | solution.py:26
  20.5 3.5 %collective-permute-start.8 = (bf16[144,320]{1,0:T(8,128)(2,1)S(1)}, bf16[144,320]{1,0:T(8,128)(2,1)S(1)}, u32[]{:S(2)}, u32[]{:S(2)}) collective-permute-start(bf16[144,320]{1,0:T(8,128)(2,1)S(1)} %fusion.4.refs_0_), channel_id=1, source_target_pairs={{0,2},{1,3},{2,4},{3,5},{4,6},{5,7},{8,10},{9,11},{10,12},{11,13},... | collective-permute-start | bytes 276488 | tf_op jit(solution)/shard_map/ppermute | solution.py:26
  24.0 2.7 %collective-permute-done.9.refs_2_ = bf16[144,320]{1,0:T(8,128)(2,1)S(1)} collective-permute-done((bf16[144,320]{1,0:T(8,128)(2,1)S(1)}, bf16[144,320]{1,0:T(8,128)(2,1)S(1)}, u32[]{:S(2)}, u32[]{:S(2)}) %collective-permute-start.9) | collective-permute-done | bytes 92192 | tf_op jit(solution)/shard_map/ppermute | solution.py:26
  26.7 1.8 collective-permute-done.8.refs_1_
  28.7 5.2 %collective-permute-start.3 = (bf16[64,2048]{1,0:T(8,128)(2,1)}, bf16[64,2048]{1,0:T(8,128)(2,1)S(1)}, u32[]{:S(2)}, u32[]{:S(2)}) collective-permute-start(bf16[64,2048]{1,0:T(8,128)(2,1)} %collective-permute-done.1.refs_1_), channel_id=1, source_target_pairs={{0,2},{1,3},{2,0},{3,1},{4,6},{5,7},{6,4},{7,5},{8,10},{9,11},{10,... | collective-permute-start | bytes 786440 | tf_op jit(solution)/shard_map/ppermute | solution.py:31
  33.9 7.1 %collective-permute-done.3.refs_3_ = bf16[64,2048]{1,0:T(8,128)(2,1)S(1)} collective-permute-done((bf16[64,2048]{1,0:T(8,128)(2,1)}, bf16[64,2048]{1,0:T(8,128)(2,1)S(1)}, u32[]{:S(2)}, u32[]{:S(2)}) %collective-permute-start.3) | collective-permute-done | bytes 262176 | tf_op jit(solution)/shard_map/ppermute | solution.py:31
  41.8 2.2 collect.1
  47.0 1.6 collective-permute-start.12
  48.5 1.5 collective-permute-start.11
  50.1 1.8 collective-permute-start.14
  51.8 2.2 collective-permute-start.13
  54.0 9.8 %collective-permute-done.14.refs_2_ = bf16[64,2048]{1,0:T(8,128)(2,1)S(1)} collective-permute-done((bf16[64,2048]{1,0:T(8,128)(2,1)S(1)}, bf16[64,2048]{1,0:T(8,128)(2,1)S(1)}, u32[]{:S(2)}, u32[]{:S(2)}) %collective-permute-start.14) | collective-permute-done | bytes 262176 | tf_op jit(solution)/shard_map/ppermute | solution.py:31
  63.9 3.7 %collective-permute-start.15 = (bf16[64,2048]{1,0:T(8,128)(2,1)S(1)}, bf16[64,2048]{1,0:T(8,128)(2,1)S(1)}, u32[]{:S(2)}, u32[]{:S(2)}) collective-permute-start(bf16[64,2048]{1,0:T(8,128)(2,1)S(1)} %collective-permute-done.13.refs_1_), channel_id=1, source_target_pairs={{0,2},{1,3},{2,0},{3,1},{4,6},{5,7},{6,4},{7,5},{8,10},{9,11},{10,... | collective-permute-start | bytes 786440 | tf_op jit(solution)/shard_map/ppermute | solution.py:31
  67.5 13.2 %heads_backward.5 = (bf16[128,8192]{1,0:T(8,128)(2,1)}, bf16[128,4096]{1,0:T(8,128)(2,1)}, bf16[128,6144]{1,0:T(8,128)(2,1)S(1)}, f32[128,2048]{1,0:T(8,128)S(1)...) custom-call(s32[6]{0:T(128)S(1)} %copy-done.21, bf16[128,8192]{1,0:T(8,128)(2,1)S(1)} %bitcast.18, ...), custom_call_target="tpu_custom_call" | custom-call | flops 400000000 | bytes 1200000 | tf_op jit(solution)/shard_map/heads_backward/pallas_call | solution.py:158
  82.0 13.0 %heads_backward.6 = (bf16[128,8192]{1,0:T(8,128)(2,1)}, bf16[128,4096]{1,0:T(8,128)(2,1)}, bf16[128,6144]{1,0:T(8,128)(2,1)S(1)}, f32[128,2048]{1,0:T(8,128)S(1)...) custom-call(s32[6]{0:T(128)S(1)} %copy-done.21, ...), custom_call_target="tpu_custom_call", output_to_operand_aliasing={{0}: (14, {}), {1}: (15, {}), {2}: (16, {})} | custom-call | flops 400000000 | bytes 1200000 | tf_op jit(solution)/shard_map/heads_backward/pallas_call | solution.py:158
  96.1 13.0 %heads_backward.7 = (bf16[128,8192]{1,0:T(8,128)(2,1)}, bf16[128,4096]{1,0:T(8,128)(2,1)}, bf16[128,6144]{1,0:T(8,128)(2,1)S(1)}, f32[128,2048]{1,0:T(8,128)S(1)...) custom-call(s32[6]{0:T(128)S(1)} %copy-done.21, ...), custom_call_target="tpu_custom_call", output_to_operand_aliasing={{0}: (14, {}), {1}: (15, {}), {2}: (16, {})} | custom-call | flops 400000000 | bytes 1200000 | tf_op jit(solution)/shard_map/heads_backward/pallas_call | solution.py:158
  109.1 1.5 collective-permute-start.19
  110.6 7.4 %heads_backward.8 = (bf16[128,8192]{1,0:T(8,128)(2,1)}, bf16[128,4096]{1,0:T(8,128)(2,1)}, bf16[128,6144]{1,0:T(8,128)(2,1)S(1)}, f32[128,1024]{1,0:T(8,128)S(1)...) custom-call(s32[6]{0:T(128)S(1)} %copy-done.21, ...), custom_call_target="tpu_custom_call", output_to_operand_aliasing={{0}: (14, {}), {1}: (15, {}), {2}: (16, {})} | custom-call | flops 200000000 | bytes 600000 | tf_op jit(solution)/shard_map/heads_backward/pallas_call | solution.py:158
  118.0 1.6 collective-permute-start.20
  119.6 1.6 collective-permute-done.16
  122.2 7.9 %heads_backward.9 = (bf16[128,8192]{1,0:T(8,128)(2,1)}, bf16[128,4096]{1,0:T(8,128)(2,1)}, bf16[128,6144]{1,0:T(8,128)(2,1)S(1)}, f32[128,1024]{1,0:T(8,128)S(1)...) custom-call(s32[6]{0:T(128)S(1)} %copy-done.21, ...), custom_call_target="tpu_custom_call", output_to_operand_aliasing={{0}: (14, {}), {1}: (15, {}), {2}: (16, {})} | custom-call | flops 200000000 | bytes 600000 | tf_op jit(solution)/shard_map/heads_backward/pallas_call | solution.py:158
  131.7 9.6 %collective-permute-done.19 = f32[128,2048]{1,0:T(8,128)S(1)} collective-permute-done((f32[128,2048]{1,0:T(8,128)S(1)}, f32[128,2048]{1,0:T(8,128)S(1)}, u32[]{:S(2)}, u32[]{:S(2)}) %collective-permute-start.19) | collective-permute-done | bytes 1048608 | tf_op jit(solution)/shard_map/ppermute | solution.py:31
  141.4 1.7 spread.1
  145.1 2.5 %slice_add_fusion = (f32[128,1024]{1,0:T(8,128)}, f32[128,1024]{1,0:T(8,128)}) fusion(f32[128,2048]{1,0:T(8,128)} %copy-done.26, f32[128,2048]{1,0:T(8,128)S(1)} %copy-done.8), kind=kLoop, calls=%fused_computation | loop fusion | flops 262144 | bytes 3145728 | tf_op jit(solution)/shard_map/add | solution.py:597
  148.1 1.5 collective-permute-start.31
  151.4 2.2 copy.34
  153.6 1.5 add.64
  155.1 1.4 collective-permute-start.22
  156.5 6.2 %collective-permute-done.26 = f32[128,1024]{1,0:T(8,128)} collective-permute-done((f32[128,1024]{1,0:T(8,128)}, f32[128,1024]{1,0:T(8,128)}, u32[]{:S(2)}, u32[]{:S(2)}) %collective-permute-start.26) | collective-permute-done | bytes 524320 | tf_op jit(solution)/shard_map/ppermute | solution.py:31
  165.3 9.9 %collective-permute-done.23 = f32[128,320]{1,0:T(8,128)S(1)} collective-permute-done((f32[128,320]{1,0:T(8,128)S(1)}, f32[128,320]{1,0:T(8,128)S(1)}, u32[]{:S(2)}, u32[]{:S(2)}) %collective-permute-start.23) | collective-permute-done | bytes 163872 | tf_op jit(solution)/shard_map/ppermute | solution.py:26
  176.7 13.1 %collective-permute-done.27 = f32[128,1024]{1,0:T(8,128)S(1)} collective-permute-done((f32[128,1024]{1,0:T(8,128)S(1)}, f32[128,1024]{1,0:T(8,128)S(1)}, u32[]{:S(2)}, u32[]{:S(2)}) %collective-permute-start.27) | collective-permute-done | bytes 524320 | tf_op jit(solution)/shard_map/ppermute | solution.py:31
  191.1 1.7 collective-permute-start.32
  194.2 14.5 %collective-permute-done.28 = f32[64,1024]{1,0:T(8,128)S(1)} collective-permute-done((f32[64,1024]{1,0:T(8,128)S(1)}, f32[64,1024]{1,0:T(8,128)S(1)}, u32[]{:S(2)}, u32[]{:S(2)}) %collective-permute-start.28) | collective-permute-done | bytes 262176 | tf_op jit(solution)/shard_map/ppermute | solution.py:31
  210.0 2.5 collective-permute-start.33
  215.0 1.5 collective-permute-start.35
  216.5 1.5 collective-permute-start.34
  218.0 4.0 %collective-permute-done.33 = f32[64,1024]{1,0:T(8,128)S(1)} collective-permute-done((f32[64,1024]{1,0:T(8,128)S(1)}, f32[64,1024]{1,0:T(8,128)S(1)}, u32[]{:S(2)}, u32[]{:S(2)}) %collective-permute-start.33) | collective-permute-done | bytes 262176 | tf_op jit(solution)/shard_map/ppermute | solution.py:31
  222.2 2.4 collective-permute-done.36.refs_6_
  224.6 4.1 %collective-permute-done.35.refs_4_ = f32[32,2048]{1,0:T(8,128)S(1)} collective-permute-done((f32[32,2048]{1,0:T(8,128)S(1)}, f32[32,2048]{1,0:T(8,128)S(1)}, u32[]{:S(2)}, u32[]{:S(2)}) %collective-permute-start.35) | collective-permute-done | bytes 262176 | tf_op jit(solution)/shard_map/ppermute | solution.py:31
  232.9 2.4 place_columns.1
  235.3 1.7 copy.35
  237.0 2.6 %collective-permute-done.40.refs_7_ = f32[32,2048]{1,0:T(8,128)S(1)} collective-permute-done((f32[32,2048]{1,0:T(8,128)S(1)}, f32[32,2048]{1,0:T(8,128)S(1)}, u32[]{:S(2)}, u32[]{:S(2)}) %collective-permute-start.40) | collective-permute-done | bytes 262176 | tf_op jit(solution)/shard_map/ppermute | solution.py:31
  239.6 3.9 %collective-permute-done.39.refs_5_ = f32[32,2048]{1,0:T(8,128)S(1)} collective-permute-done((f32[32,2048]{1,0:T(8,128)S(1)}, f32[32,2048]{1,0:T(8,128)S(1)}, u32[]{:S(2)}, u32[]{:S(2)}) %collective-permute-start.39) | collective-permute-done | bytes 262176 | tf_op jit(solution)/shard_map/ppermute | solution.py:31
  244.1 3.4 %lay_out.1 = f32[32,16384]{1,0:T(8,128)} custom-call(s32[6]{0:T(128)S(1)} %copy-done.21, f32[32,2048]{1,0:T(8,128)S(1)} %join_cores.2.refs_0_, f32[32,2048]{1,0:T(8,128)S(1)} %join_cores.3.refs_1_, f32[32,2048]{1,0:T(8,128)S(1)} %collective-permute-done.34.refs_2_, f32[32,2048]{1,0:T(8,128)} %collective-permute-done.38.refs_3_, ...), custom_call_target="tpu_custom_call" | custom-call | bytes 4000000 | tf_op jit(solution)/shard_map/lay_out/pallas_call | solution.py:296
  (142 shorter events, 32.4 us)
Async XLA Ops:
  3.8 37.8 %copy-start.11 = (f32[1,64,128]{2,1,0:T(8,128)S(1)}, f32[1,64,128]{2,1,0:T(8,128)}, u32[]{:S(2)}) copy-start(f32[1,64,128]{2,1,0:T(8,128)} %param.11) | copy-start | bytes 98308
  3.8 37.8 %copy-start.32 = (s32[1,8,4]{1,2,0:T(4,128)S(1)}, s32[1,8,4]{1,2,0:T(4,128)}, u32[]{:S(2)}) copy-start(s32[1,8,4]{1,2,0:T(4,128)} %param.15) | copy-start | bytes 388
  3.8 37.9 %copy-start.21 = (s32[6]{0:T(128)S(1)}, s32[6]{0:T(128)}, u32[]{:S(2)}) copy-start(s32[6]{0:T(128)} %stack.30.place) | copy-start | bytes 76
  3.8 1.8 collective-permute-start
  5.7 9.1 %collective-permute-start.4 = (bf16[128,8192]{1,0:T(8,128)(2,1)S(1)}, bf16[128,8192]{1,0:T(8,128)(2,1)}, u32[]{:S(2)}, u32[]{:S(2)}) collective-permute-start(bf16[128,8192]{1,0:T(8,128)(2,1)S(1)} %bitcast.17), channel_id=1, source_target_pairs={{0,1},{1,0},{2,3},{3,2},{4,5},{5,4},{6,7},{7,6},{8,9},{9,8},{10,11... | collective-permute-start | bytes 6291464 | tf_op jit(solution)/shard_map/ppermute | solution.py:31
  6.0 8.7 %collective-permute-start.6 = (bf16[128,8192]{1,0:T(8,128)(2,1)}, bf16[128,8192]{1,0:T(8,128)(2,1)}, u32[]{:S(2)}, u32[]{:S(2)}) collective-permute-start(bf16[128,8192]{1,0:T(8,128)(2,1)} %bitcast.23), channel_id=1, source_target_pairs={{0,1},{1,0},{2,3},{3,2},{4,5},{5,4},{6,7},{7,6},{8,9},{9,8},{10,11... | collective-permute-start | bytes 6291464 | tf_op jit(solution)/shard_map/ppermute | solution.py:31
  6.2 8.5 %collective-permute-start.5 = (bf16[128,4096]{1,0:T(8,128)(2,1)}, bf16[128,4096]{1,0:T(8,128)(2,1)}, u32[]{:S(2)}, u32[]{:S(2)}) collective-permute-start(bf16[128,4096]{1,0:T(8,128)(2,1)} %bitcast.29), channel_id=1, source_target_pairs={{0,1},{1,0},{2,3},{3,2},{4,5},{5,4},{6,7},{7,6},{8,9},{9,8},{10,11... | collective-permute-start | bytes 3145736 | tf_op jit(solution)/shard_map/ppermute | solution.py:31
  9.1 58.4 %copy-start.2 = (bf16[1,128,4096]{2,1,0:T(8,128)(2,1)S(1)}, bf16[1,128,4096]{2,1,0:T(8,128)(2,1)}, u32[]{:S(2)}) copy-start(bf16[1,128,4096]{2,1,0:T(8,128)(2,1)} %param.9) | copy-start | bytes 3145732
  9.1 19.5 %collective-permute-start.2 = (bf16[64,2048]{1,0:T(8,128)(2,1)}, bf16[64,2048]{1,0:T(8,128)(2,1)}, u32[]{:S(2)}, u32[]{:S(2)}) collective-permute-start(bf16[64,2048]{1,0:T(8,128)(2,1)} %get-tuple-element.96.refs_0_), channel_id=1, source_target_pairs={{0,2},{1,3},{2,0},{3,1},{4,6},{5,7},{6,4},{7,5},{8,10},{9,11},{10,... | collective-permute-start | bytes 786440 | tf_op jit(solution)/shard_map/ppermute | solution.py:31
  11.9 16.8 %collective-permute-start.1 = (bf16[64,2048]{1,0:T(8,128)(2,1)}, bf16[64,2048]{1,0:T(8,128)(2,1)}, u32[]{:S(2)}, u32[]{:S(2)}) collective-permute-start(bf16[64,2048]{1,0:T(8,128)(2,1)} %get-tuple-element.96.refs_0_), channel_id=1, source_target_pairs={{0,4},{1,5},{2,6},{3,7},{4,0},{5,1},{6,2},{7,3},{8,12},{9,13},{10,... | collective-permute-start | bytes 786440 | tf_op jit(solution)/shard_map/ppermute | solution.py:31
  14.7 12.0 %collective-permute-start.9 = (bf16[144,320]{1,0:T(8,128)(2,1)S(1)}, bf16[144,320]{1,0:T(8,128)(2,1)S(1)}, u32[]{:S(2)}, u32[]{:S(2)}) collective-permute-start(bf16[144,320]{1,0:T(8,128)(2,1)S(1)} %fusion.4.refs_0_), channel_id=1, source_target_pairs={{0,4},{1,5},{2,6},{3,7},{8,12},{9,13},{10,14},{11,15},{16,20},{17,... | collective-permute-start | bytes 276488 | tf_op jit(solution)/shard_map/ppermute | solution.py:26
  20.5 8.0 %collective-permute-start.8 = (bf16[144,320]{1,0:T(8,128)(2,1)S(1)}, bf16[144,320]{1,0:T(8,128)(2,1)S(1)}, u32[]{:S(2)}, u32[]{:S(2)}) collective-permute-start(bf16[144,320]{1,0:T(8,128)(2,1)S(1)} %fusion.4.refs_0_), channel_id=1, source_target_pairs={{0,2},{1,3},{2,4},{3,5},{4,6},{5,7},{8,10},{9,11},{10,12},{11,13},... | collective-permute-start | bytes 276488 | tf_op jit(solution)/shard_map/ppermute | solution.py:26
  28.6 13.2 %collective-permute-start.10 = (bf16[432,320]{1,0:T(8,128)(2,1)S(1)}, bf16[432,320]{1,0:T(8,128)(2,1)}, u32[]{:S(2)}, u32[]{:S(2)}) collective-permute-start(bf16[432,320]{1,0:T(8,128)(2,1)S(1)} %stack.31.own), channel_id=1, source_target_pairs={{0,1},{1,0},{2,3},{3,2},{4,5},{5,4},{6,7},{7,6},{8,9},{9,8},{10,11... | collective-permute-start | bytes 829448 | tf_op jit(solution)/shard_map/ppermute | solution.py:31
  28.7 12.3 %collective-permute-start.3 = (bf16[64,2048]{1,0:T(8,128)(2,1)}, bf16[64,2048]{1,0:T(8,128)(2,1)S(1)}, u32[]{:S(2)}, u32[]{:S(2)}) collective-permute-start(bf16[64,2048]{1,0:T(8,128)(2,1)} %collective-permute-done.1.refs_1_), channel_id=1, source_target_pairs={{0,2},{1,3},{2,0},{3,1},{4,6},{5,7},{6,4},{7,5},{8,10},{9,11},{10,... | collective-permute-start | bytes 786440 | tf_op jit(solution)/shard_map/ppermute | solution.py:31
  41.7 2.3 collective-permute-start.7
  41.8 25.8 %copy-start.1 = (bf16[1,128,8192]{2,1,0:T(8,128)(2,1)S(1)}, bf16[1,128,8192]{2,1,0:T(8,128)(2,1)}, u32[]{:S(2)}) copy-start(bf16[1,128,8192]{2,1,0:T(8,128)(2,1)} %param.10) | copy-start | bytes 6291460
  47.0 49.1 %collective-permute-start.12 = (bf16[256,2048]{1,0:T(8,128)(2,1)S(1)}, bf16[256,2048]{1,0:T(8,128)(2,1)S(1)}, u32[]{:S(2)}, u32[]{:S(2)}) collective-permute-start(bf16[256,2048]{1,0:T(8,128)(2,1)S(1)} %stack.32.weight), channel_id=1, source_target_pairs={{0,8},{8,0},{16,24},{24,16},{1,9},{9,1},{17,25},{25,17},{2,10},{10... | collective-permute-start | bytes 3145736 | tf_op jit(solution)/shard_map/ppermute | solution.py:31
  48.5 47.5 %collective-permute-start.11 = (bf16[256,2048]{1,0:T(8,128)(2,1)S(1)}, bf16[256,2048]{1,0:T(8,128)(2,1)S(1)}, u32[]{:S(2)}, u32[]{:S(2)}) collective-permute-start(bf16[256,2048]{1,0:T(8,128)(2,1)S(1)} %stack.32.weight), channel_id=1, source_target_pairs={{0,16},{8,24},{16,0},{24,8},{1,17},{9,25},{17,1},{25,9},{2,18},{10... | collective-permute-start | bytes 3145736 | tf_op jit(solution)/shard_map/ppermute | solution.py:31
  50.1 13.8 %collective-permute-start.14 = (bf16[64,2048]{1,0:T(8,128)(2,1)S(1)}, bf16[64,2048]{1,0:T(8,128)(2,1)S(1)}, u32[]{:S(2)}, u32[]{:S(2)}) collective-permute-start(bf16[64,2048]{1,0:T(8,128)(2,1)S(1)} %copy-done.17), channel_id=1, source_target_pairs={{0,2},{1,3},{2,0},{3,1},{4,6},{5,7},{6,4},{7,5},{8,10},{9,11},{10,... | collective-permute-start | bytes 786440 | tf_op jit(solution)/shard_map/ppermute | solution.py:31
  51.8 12.0 %collective-permute-start.13 = (bf16[64,2048]{1,0:T(8,128)(2,1)S(1)}, bf16[64,2048]{1,0:T(8,128)(2,1)S(1)}, u32[]{:S(2)}, u32[]{:S(2)}) collective-permute-start(bf16[64,2048]{1,0:T(8,128)(2,1)S(1)} %copy-done.17), channel_id=1, source_target_pairs={{0,4},{1,5},{2,6},{3,7},{4,0},{5,1},{6,2},{7,3},{8,12},{9,13},{10,... | collective-permute-start | bytes 786440 | tf_op jit(solution)/shard_map/ppermute | solution.py:31
  63.9 16.8 %collective-permute-start.15 = (bf16[64,2048]{1,0:T(8,128)(2,1)S(1)}, bf16[64,2048]{1,0:T(8,128)(2,1)S(1)}, u32[]{:S(2)}, u32[]{:S(2)}) collective-permute-start(bf16[64,2048]{1,0:T(8,128)(2,1)S(1)} %collective-permute-done.13.refs_1_), channel_id=1, source_target_pairs={{0,2},{1,3},{2,0},{3,1},{4,6},{5,7},{6,4},{7,5},{8,10},{9,11},{10,... | collective-permute-start | bytes 786440 | tf_op jit(solution)/shard_map/ppermute | solution.py:31
  95.0 26.1 %collective-permute-start.16 = (f32[128,2048]{1,0:T(8,128)S(1)}, f32[128,2048]{1,0:T(8,128)S(1)}, u32[]{:S(2)}, u32[]{:S(2)}) collective-permute-start(f32[128,2048]{1,0:T(8,128)S(1)} %get-tuple-element.116), channel_id=1, source_target_pairs={{0,8},{8,0},{16,24},{24,16},{1,9},{9,1},{17,25},{25,17},{2,10},{10... | collective-permute-start | bytes 3145736 | tf_op jit(solution)/shard_map/ppermute | solution.py:31
  95.6 25.6 %collective-permute-start.17 = (f32[128,2048]{1,0:T(8,128)S(1)}, f32[128,2048]{1,0:T(8,128)S(1)}, u32[]{:S(2)}, u32[]{:S(2)}) collective-permute-start(f32[128,2048]{1,0:T(8,128)S(1)} %get-tuple-element.117), channel_id=1, source_target_pairs={{0,16},{8,24},{16,0},{24,8},{1,17},{9,25},{17,1},{25,9},{2,18},{10... | collective-permute-start | bytes 3145736 | tf_op jit(solution)/shard_map/ppermute | solution.py:31
  109.1 32.3 %collective-permute-start.19 = (f32[128,2048]{1,0:T(8,128)S(1)}, f32[128,2048]{1,0:T(8,128)S(1)}, u32[]{:S(2)}, u32[]{:S(2)}) collective-permute-start(f32[128,2048]{1,0:T(8,128)S(1)} %get-tuple-element.130), channel_id=1, source_target_pairs={{0,8},{8,0},{16,24},{24,16},{1,9},{9,1},{17,25},{25,17},{2,10},{10... | collective-permute-start | bytes 3145736 | tf_op jit(solution)/shard_map/ppermute | solution.py:31
  118.0 13.7 %collective-permute-start.20 = (f32[128,1024]{1,0:T(8,128)S(1)}, f32[128,1024]{1,0:T(8,128)S(1)}, u32[]{:S(2)}, u32[]{:S(2)}) collective-permute-start(f32[128,1024]{1,0:T(8,128)S(1)} %get-tuple-element.131), channel_id=1, source_target_pairs={{0,16},{8,24},{16,0},{24,8},{1,17},{9,25},{17,1},{25,9},{2,18},{10... | collective-permute-start | bytes 1572872 | tf_op jit(solution)/shard_map/ppermute | solution.py:31
  131.2 19.7 %collective-permute-start.24 = (f32[128,1024]{1,0:T(8,128)}, f32[128,1024]{1,0:T(8,128)}, u32[]{:S(2)}, u32[]{:S(2)}) collective-permute-start(f32[128,1024]{1,0:T(8,128)} %get-tuple-element.142), channel_id=1, source_target_pairs={{0,16},{8,24},{16,0},{24,8},{1,17},{9,25},{17,1},{25,9},{2,18},{10... | collective-permute-start | bytes 1572872 | tf_op jit(solution)/shard_map/ppermute | solution.py:31
  145.1 6.3 %collective-permute-start.21 = (f32[432,320]{0,1:T(8,128)}, f32[432,320]{0,1:T(8,128)}, u32[]{:S(2)}, u32[]{:S(2)}) collective-permute-start(f32[432,320]{0,1:T(8,128)} %copy.33), channel_id=1, source_target_pairs={{0,1},{1,0},{2,3},{3,2},{4,5},{5,4},{6,7},{7,6},{8,9},{9,8},{10,11... | collective-permute-start | bytes 1658888 | tf_op jit(solution)/shard_map/ppermute | solution.py:31
  147.6 15.1 %collective-permute-start.26 = (f32[128,1024]{1,0:T(8,128)}, f32[128,1024]{1,0:T(8,128)}, u32[]{:S(2)}, u32[]{:S(2)}) collective-permute-start(f32[128,1024]{1,0:T(8,128)} %get-tuple-element.146), channel_id=1, source_target_pairs={{0,8},{8,0},{16,24},{24,16},{1,9},{9,1},{17,25},{25,17},{2,10},{10... | collective-permute-start | bytes 1572872 | tf_op jit(solution)/shard_map/ppermute | solution.py:31
  148.1 28.5 %collective-permute-start.31 = (f32[128,1024]{1,0:T(8,128)}, f32[128,1024]{1,0:T(8,128)}, u32[]{:S(2)}, u32[]{:S(2)}) collective-permute-start(f32[128,1024]{1,0:T(8,128)} %get-tuple-element.156), channel_id=1, source_target_pairs={{0,8},{8,0},{16,24},{24,16},{1,9},{9,1},{17,25},{25,17},{2,10},{10... | collective-permute-start | bytes 1572872 | tf_op jit(solution)/shard_map/ppermute | solution.py:31
  149.6 41.5 %collective-permute-start.18 = (bf16[128,6144]{1,0:T(8,128)(2,1)S(1)}, bf16[128,6144]{1,0:T(8,128)(2,1)S(1)}, u32[]{:S(2)}, u32[]{:S(2)}) collective-permute-start(bf16[128,6144]{1,0:T(8,128)(2,1)S(1)} %copy-done.4), channel_id=1, source_target_pairs={{0,1},{1,0},{2,3},{3,2},{4,5},{5,4},{6,7},{7,6},{8,9},{9,8},{10,11... | collective-permute-start | bytes 4718600 | tf_op jit(solution)/shard_map/ppermute | solution.py:31
  150.9 25.0 %collective-permute-start.25 = (f32[128,1024]{1,0:T(8,128)}, f32[128,1024]{1,0:T(8,128)}, u32[]{:S(2)}, u32[]{:S(2)}) collective-permute-start(f32[128,1024]{1,0:T(8,128)} %get-tuple-element.143), channel_id=1, source_target_pairs={{0,16},{8,24},{16,0},{24,8},{1,17},{9,25},{17,1},{25,9},{2,18},{10... | collective-permute-start | bytes 1572872 | tf_op jit(solution)/shard_map/ppermute | solution.py:31
  155.1 10.2 %collective-permute-start.22 = (f32[128,320]{1,0:T(8,128)S(1)}, f32[128,320]{1,0:T(8,128)S(1)}, u32[]{:S(2)}, u32[]{:S(2)}) collective-permute-start(f32[128,320]{1,0:T(8,128)S(1)} %get-tuple-element.172), channel_id=1, source_target_pairs={{2,0},{3,1},{4,2},{5,3},{6,4},{7,5},{10,8},{11,9},{12,10},{13,11},... | collective-permute-start | bytes 491528 | tf_op jit(solution)/shard_map/ppermute | solution.py:26
  162.7 12.5 %collective-permute-start.23 = (f32[128,320]{1,0:T(8,128)S(1)}, f32[128,320]{1,0:T(8,128)S(1)}, u32[]{:S(2)}, u32[]{:S(2)}) collective-permute-start(f32[128,320]{1,0:T(8,128)S(1)} %get-tuple-element.173), channel_id=1, source_target_pairs={{4,0},{5,1},{6,2},{7,3},{12,8},{13,9},{14,10},{15,11},{20,16},{21,... | collective-permute-start | bytes 491528 | tf_op jit(solution)/shard_map/ppermute | solution.py:26
  164.0 28.9 %copy-start.6 = (f32[128,2048]{1,0:T(8,128)S(1)}, f32[128,2048]{1,0:T(8,128)}, u32[]{:S(2)}) copy-start(f32[128,2048]{1,0:T(8,128)} %copy-done.5) | copy-start | bytes 3145732
  164.0 28.9 %copy-start.23 = (f32[128,2048]{1,0:T(8,128)S(1)}, f32[128,2048]{1,0:T(8,128)}, u32[]{:S(2)}) copy-start(f32[128,2048]{1,0:T(8,128)} %copy-done.22) | copy-start | bytes 3145732
  175.9 13.8 %collective-permute-start.27 = (f32[128,1024]{1,0:T(8,128)S(1)}, f32[128,1024]{1,0:T(8,128)S(1)}, u32[]{:S(2)}, u32[]{:S(2)}) collective-permute-start(f32[128,1024]{1,0:T(8,128)S(1)} %add_add_fusion.2), channel_id=1, source_target_pairs={{0,2},{1,3},{2,0},{3,1},{4,6},{5,7},{6,4},{7,5},{8,10},{9,11},{10,... | collective-permute-start | bytes 1572872 | tf_op jit(solution)/shard_map/ppermute | solution.py:31
  175.9 13.9 %collective-permute-start.30 = (f32[128,1024]{1,0:T(8,128)S(1)}, f32[128,1024]{1,0:T(8,128)S(1)}, u32[]{:S(2)}, u32[]{:S(2)}) collective-permute-start(f32[128,1024]{1,0:T(8,128)S(1)} %copy-done.29), channel_id=1, source_target_pairs={{0,16},{8,24},{16,0},{24,8},{1,17},{9,25},{17,1},{25,9},{2,18},{10... | collective-permute-start | bytes 1572872 | tf_op jit(solution)/shard_map/ppermute | solution.py:31
  191.1 18.7 %collective-permute-start.32 = (f32[128,1024]{1,0:T(8,128)S(1)}, f32[128,1024]{1,0:T(8,128)S(1)}, u32[]{:S(2)}, u32[]{:S(2)}) collective-permute-start(f32[128,1024]{1,0:T(8,128)S(1)} %add_add_fusion), channel_id=1, source_target_pairs={{0,2},{1,3},{2,0},{3,1},{4,6},{5,7},{6,4},{7,5},{8,10},{9,11},{10,... | collective-permute-start | bytes 1572872 | tf_op jit(solution)/shard_map/ppermute | solution.py:31
  194.1 14.6 %collective-permute-start.28 = (f32[64,1024]{1,0:T(8,128)S(1)}, f32[64,1024]{1,0:T(8,128)S(1)}, u32[]{:S(2)}, u32[]{:S(2)}) collective-permute-start(f32[64,1024]{1,0:T(8,128)S(1)} %slice.99), channel_id=1, source_target_pairs={{0,4},{1,5},{2,6},{3,7},{4,0},{5,1},{6,2},{7,3},{8,12},{9,13},{10,... | collective-permute-start | bytes 786440 | tf_op jit(solution)/shard_map/ppermute | solution.py:31
  210.0 12.1 %collective-permute-start.33 = (f32[64,1024]{1,0:T(8,128)S(1)}, f32[64,1024]{1,0:T(8,128)S(1)}, u32[]{:S(2)}, u32[]{:S(2)}) collective-permute-start(f32[64,1024]{1,0:T(8,128)S(1)} %slice.105), channel_id=1, source_target_pairs={{0,4},{1,5},{2,6},{3,7},{4,0},{5,1},{6,2},{7,3},{8,12},{9,13},{10,... | collective-permute-start | bytes 786440 | tf_op jit(solution)/shard_map/ppermute | solution.py:31
  212.5 1.4 collective-permute-start.29
  214.5 10.2 %collective-permute-start.36 = (f32[32,2048]{1,0:T(8,128)S(1)}, f32[32,2048]{1,0:T(8,128)S(1)}, u32[]{:S(2)}, u32[]{:S(2)}) collective-permute-start(f32[32,2048]{1,0:T(8,128)S(1)} %join_cores.2.refs_0_), channel_id=1, source_target_pairs={{0,24},{8,16},{16,8},{24,0},{1,25},{9,17},{17,9},{25,1},{2,26},{10... | collective-permute-start | bytes 786440 | tf_op jit(solution)/shard_map/ppermute | solution.py:31
  215.0 13.7 %collective-permute-start.35 = (f32[32,2048]{1,0:T(8,128)S(1)}, f32[32,2048]{1,0:T(8,128)S(1)}, u32[]{:S(2)}, u32[]{:S(2)}) collective-permute-start(f32[32,2048]{1,0:T(8,128)S(1)} %join_cores.2.refs_0_), channel_id=1, source_target_pairs={{0,16},{8,24},{16,0},{24,8},{1,17},{9,25},{17,1},{25,9},{2,18},{10... | collective-permute-start | bytes 786440 | tf_op jit(solution)/shard_map/ppermute | solution.py:31
  216.5 12.2 %collective-permute-start.34 = (f32[32,2048]{1,0:T(8,128)S(1)}, f32[32,2048]{1,0:T(8,128)S(1)}, u32[]{:S(2)}, u32[]{:S(2)}) collective-permute-start(f32[32,2048]{1,0:T(8,128)S(1)} %join_cores.2.refs_0_), channel_id=1, source_target_pairs={{0,8},{8,0},{16,24},{24,16},{1,9},{9,1},{17,25},{25,17},{2,10},{10... | collective-permute-start | bytes 786440 | tf_op jit(solution)/shard_map/ppermute | solution.py:31
  222.1 6.6 %collective-permute-start.37 = (f32[32,1024]{1,0:T(8,128)S(1)}, f32[32,1024]{1,0:T(8,128)S(1)}, u32[]{:S(2)}, u32[]{:S(2)}) collective-permute-start(f32[32,1024]{1,0:T(8,128)S(1)} %get-tuple-element.174), channel_id=1, source_target_pairs={{0,1},{1,0},{2,3},{3,2},{4,5},{5,4},{6,7},{7,6},{8,9},{9,8},{10,11... | collective-permute-start | bytes 393224 | tf_op jit(solution)/shard_map/ppermute | solution.py:31
  229.3 10.3 %collective-permute-start.40 = (f32[32,2048]{1,0:T(8,128)S(1)}, f32[32,2048]{1,0:T(8,128)S(1)}, u32[]{:S(2)}, u32[]{:S(2)}) collective-permute-start(f32[32,2048]{1,0:T(8,128)S(1)} %join_cores.3.refs_1_), channel_id=1, source_target_pairs={{0,24},{8,16},{16,8},{24,0},{1,25},{9,17},{17,9},{25,1},{2,26},{10... | collective-permute-start | bytes 786440 | tf_op jit(solution)/shard_map/ppermute | solution.py:31
  230.6 12.8 %collective-permute-start.39 = (f32[32,2048]{1,0:T(8,128)S(1)}, f32[32,2048]{1,0:T(8,128)S(1)}, u32[]{:S(2)}, u32[]{:S(2)}) collective-permute-start(f32[32,2048]{1,0:T(8,128)S(1)} %join_cores.3.refs_1_), channel_id=1, source_target_pairs={{0,16},{8,24},{16,0},{24,8},{1,17},{9,25},{17,1},{25,9},{2,18},{10... | collective-permute-start | bytes 786440 | tf_op jit(solution)/shard_map/ppermute | solution.py:31
  232.1 12.0 %collective-permute-start.38 = (f32[32,2048]{1,0:T(8,128)S(1)}, f32[32,2048]{1,0:T(8,128)}, u32[]{:S(2)}, u32[]{:S(2)}) collective-permute-start(f32[32,2048]{1,0:T(8,128)S(1)} %join_cores.3.refs_1_), channel_id=1, source_target_pairs={{0,8},{8,0},{16,24},{24,16},{1,9},{9,1},{17,25},{25,17},{2,10},{10... | collective-permute-start | bytes 786440 | tf_op jit(solution)/shard_map/ppermute | solution.py:31
  (27 other events, 168.2 us)

commit v8 on v7

--- a/solution.py
+++ b/solution.py
@@ -533,7 +533,7 @@
         at_step[2] = exchange(start, "ctx", 2)
         for step in range(4, n_ctx, 4):
             at_step[step + 2] = exchange(after(at_step[step], at_step[2]), "ctx", 2)
-        return [at_step[partner] for partner in partners], at_step[n_ctx - 2]
+        return [at_step[partner] for partner in partners], at_step[n_ctx - 4]
 
     def joined(pieces):
         return stack(pieces, (tuple((index, 0) for index in range(len(pieces))),), part_cols)[0]
@@ -556,12 +556,16 @@
     orders = (bits, bits[::-1])
     first_sums = [{t: [] for t in range(n_dp) if t & order[0]} for order in orders]
     half_pairs = pairs // 2
-    units = [(t, 0, pairs) for t in [0, far] + list(range(1, far - 1))]
+    units = [(0, 0, half_pairs)] + [(t, 0, pairs) for t in [far] + list(range(1, far - 1))]
     units += [(far - 1, 0, half_pairs), (far - 1, half_pairs, half_pairs)]
+    units.append((0, half_pairs, half_pairs))
     for t, start, count in units:
         if t == far:
             weights[far] = joined([after(far_pieces[0], latents[-1])] + far_pieces[1:])
         weight = weights[t]
+        if t == 0 and start:
+            there = [piece for sent in first_sums for u in sent for piece in sent[u]]
+            weight = after(weight, latents[-1], *there)
         if t == 1 and not start:
             weight = after(weight, *[weights[near] for near in range(2, far)])
         if t == far - 1 and start:
@@ -620,25 +624,19 @@
     received = exchange(sib_grads, "ctx", 1)
     grad_nope, grad_rope = place_columns(place, received, q_full, rope_full, n_dp)
 
-    first_come = [sent[u][0] for sent in first_sums for u in sent if u != far]
-    latents[-1] = after(latents[-1], *first_come)
     own_grads, sib_grads = spread(place, offered, latents, ropes, 3 * span, lat_block)
     swapped = exchange(sib_grads, "ctx", 1)
     grad_rows = own_grads + swapped
-    by_chip = [grad_rows[at * span : at * span + group_len] for at in range(3)]
-    grad_rows = by_chip[0]
-    for chips in (1, 2):
-        grad_rows = grad_rows + from_behind(by_chip[chips], "ctx", -2 * chips)
-
     ctx_bits = [1 << b for b in range(1, n_ctx.bit_length() - 1)]
     finished, arrived = [], None
     for half in range(2):
         if half:
             sums = [[[after(piece, arrived) for piece in pieces] for pieces in side] for side in sums]
         first, second = [total(side, half) for side in sums]
-        there = (sums[0][-1][half], received if half else grad_rows)
-        arrived = exchange(after(second, *there), "ctx", ctx_bits[0])
+        arrived = exchange(after(second, sums[0][-1][half]), "ctx", ctx_bits[0])
         rows = first + arrived
+        if half:
+            rows = after(rows, received, swapped)
         for bit in ctx_bits[1:]:
             rows = halve(rows, "ctx", bit)
         kept, crossed = rows[:lat_block], exchange(rows[lat_block:], "ctx", 1)
@@ -646,6 +644,12 @@
             kept = after(kept, *finished[0][1:])
         piece = join_cores(place, kept, crossed)
         finished.append([piece] + [exchange(piece, "dp", t) for t in range(1, n_dp)])
+
+    grad_rows = after(grad_rows, rows)
+    by_chip = [grad_rows[at * span : at * span + group_len] for at in range(3)]
+    grad_rows = by_chip[0]
+    for chips in (1, 2):
+        grad_rows = grad_rows + from_behind(by_chip[chips], "ctx", -2 * chips)
     finished[0][0] = after(finished[0][0], grad_rows, grad_nope)
     grad_weight = lay_out(place, [piece for both in zip(*finished) for piece in both])
     return (grad_nope[None], grad_rope[None], grad_rows[None], grad_weight)

time: 248 us -> 213 us (0.86)
  waiting for transfers between devices: 97.9 us -> 66 us
  local copies, waits for them, and re-layouts: 13.1 us -> 7.74 us
  starting transfers between devices: 54.1 us -> 58 us
  other arithmetic: 9.85 us -> 6.35 us
    ppermute x37, waiting for transfers between devices: 83.5 us -> 60.4 us  [exchange(): lax.ppermute(value, axis, [(source, source ^ bits) for source in range(co...]
    ppermute x4, waiting for transfers between devices: 14.4 us -> 5.65 us  [from_behind(): lax.ppermute(value, axis, [(source, source + steps) for source in range(i...]
    unnamed x69 -> x35, local copies, waits for them, and re-layouts: 8.74 us -> 1.79 us
    add x4, other arithmetic: 6.23 us -> 1.45 us  [total(): left + right]
    ppermute x37, starting transfers between devices: 42.1 us -> 46.1 us  [exchange(): lax.ppermute(value, axis, [(source, source ^ bits) for source in range(co...]
    pallas_call x5 -> x6, Pallas kernels: 54.4 us -> 54.8 us  [chunk_backward(): pl.pallas_call(functools.partial(heads_kernel, earlier=len(aliases)), gri...]
  transfers between devices with their start and end apart: 41 -> 41, of which waited for: 20 -> 19; matrix products, arithmetic and copies ran while one was open for 6% -> 5% of each run, Pallas kernels for 26% -> 32%
where the time goes in v8:
time: 213 us; the launch traced here: 212 us
  Pallas kernels  72.8 us (34%)
  waiting for transfers between devices  66 us (31%)
  starting transfers between devices  58 us (27%)
  local copies, waits for them, and re-layouts  7.74 us (4%)
  other arithmetic  6.35 us (3%)
    ppermute x37, waiting for transfers between devices, exchange(): lax.ppermute(value, axis, [(source, source ^ bits) for source in range(co...  60.4 us
    pallas_call x6, Pallas kernels, chunk_backward(): pl.pallas_call(functools.partial(heads_kernel, earlier=len(aliases)), gri...  54.8 us
    ppermute x37, starting transfers between devices, exchange(): lax.ppermute(value, axis, [(source, source ^ bits) for source in range(co...  46.1 us
    ppermute x4, starting transfers between devices, from_behind(): lax.ppermute(value, axis, [(source, source + steps) for source in range(i...  11.9 us
    ppermute x4, waiting for transfers between devices, from_behind(): lax.ppermute(value, axis, [(source, source + steps) for source in range(i...  5.65 us
    pallas_call x2, Pallas kernels, weight_parts(): pl.pallas_call(join_rows_kernel if joins else leave_kernel, grid_spec=plt...  5.05 us
  transfers between devices with their start and end apart: 41, of which 19 were waited for; matrix products, arithmetic and copies ran while one was open for 5% of the time, Pallas kernels for 32%

profile of v8, /device:TPU:0, one launch (start us, length us, event | category | flops | bytes accessed | tf_op | source)
XLA Modules:
  0.0 211.9 jit_solution(5382745186122143254)
XLA Ops:
  1.3 2.5 %weight_parts.2 = bf16[32,4096]{1,0:T(8,128)(2,1)} custom-call(s32[6]{0:T(128)} %stack.30.place, bf16[32,16384]{1,0:T(8,128)(2,1)} %distant.3, bf16[32,16384]{1,0:T(8,128)(2,1)} %distant.3), custom_call_target="tpu_custom_call" | custom-call | bytes 1000000 | tf_op jit(solution)/shard_map/weight_parts/pallas_call | solution.py:264
  4.3 1.4 collective-permute-done.crossed
  6.5 2.6 %weight_parts.3 = (bf16[64,2048]{1,0:T(8,128)(2,1)}, bf16[64,2048]{1,0:T(8,128)(2,1)}) custom-call(s32[6]{0:T(128)} %stack.30.place, bf16[32,16384]{1,0:T(8,128)(2,1)} %distant.3, bf16[32,16384]{1,0:T(8,128)(2,1)} %distant.3, bf16[32,4096]{1,0:T(8,128)(2,1)} %copy-done.13), custom_call_target="tpu_custom_call" | custom-call | bytes 1000000 | tf_op jit(solution)/shard_map/weight_parts/pallas_call | solution.py:264
  9.1 2.8 %collective-permute-start.9 = (bf16[64,2048]{1,0:T(8,128)(2,1)}, bf16[64,2048]{1,0:T(8,128)(2,1)}, u32[]{:S(2)}, u32[]{:S(2)}) collective-permute-start(bf16[64,2048]{1,0:T(8,128)(2,1)} %get-tuple-element.104.refs_0_), channel_id=1, source_target_pairs={{0,2},{1,3},{2,0},{3,1},{4,6},{5,7},{6,4},{7,5},{8,10},{9,11},{10,... | collective-permute-start | bytes 786440 | tf_op jit(solution)/shard_map/ppermute | solution.py:31
  11.9 2.6 %collective-permute-start.1 = (bf16[64,2048]{1,0:T(8,128)(2,1)}, bf16[64,2048]{1,0:T(8,128)(2,1)}, u32[]{:S(2)}, u32[]{:S(2)}) collective-permute-start(bf16[64,2048]{1,0:T(8,128)(2,1)} %get-tuple-element.104.refs_0_), channel_id=1, source_target_pairs={{0,4},{1,5},{2,6},{3,7},{4,0},{5,1},{6,2},{7,3},{8,12},{9,13},{10,... | collective-permute-start | bytes 786440 | tf_op jit(solution)/shard_map/ppermute | solution.py:31
  14.7 5.8 %collective-permute-start.7 = (bf16[144,320]{1,0:T(8,128)(2,1)S(1)}, bf16[144,320]{1,0:T(8,128)(2,1)S(1)}, u32[]{:S(2)}, u32[]{:S(2)}) collective-permute-start(bf16[144,320]{1,0:T(8,128)(2,1)S(1)} %fusion.3.refs_0_), channel_id=1, source_target_pairs={{0,4},{1,5},{2,6},{3,7},{8,12},{9,13},{10,14},{11,15},{16,20},{17,... | collective-permute-start | bytes 276488 | tf_op jit(solution)/shard_map/ppermute | solution.py:26
  20.5 3.5 %collective-permute-start.6 = (bf16[144,320]{1,0:T(8,128)(2,1)S(1)}, bf16[144,320]{1,0:T(8,128)(2,1)S(1)}, u32[]{:S(2)}, u32[]{:S(2)}) collective-permute-start(bf16[144,320]{1,0:T(8,128)(2,1)S(1)} %fusion.3.refs_0_), channel_id=1, source_target_pairs={{0,2},{1,3},{2,4},{3,5},{4,6},{5,7},{8,10},{9,11},{10,12},{11,13},... | collective-permute-start | bytes 276488 | tf_op jit(solution)/shard_map/ppermute | solution.py:26
  24.0 2.7 %collective-permute-done.7.refs_2_ = bf16[144,320]{1,0:T(8,128)(2,1)S(1)} collective-permute-done((bf16[144,320]{1,0:T(8,128)(2,1)S(1)}, bf16[144,320]{1,0:T(8,128)(2,1)S(1)}, u32[]{:S(2)}, u32[]{:S(2)}) %collective-permute-start.7) | collective-permute-done | bytes 92192 | tf_op jit(solution)/shard_map/ppermute | solution.py:26
  26.7 1.8 collective-permute-done.6.refs_1_
  28.7 5.2 %collective-permute-start.10 = (bf16[64,2048]{1,0:T(8,128)(2,1)}, bf16[64,2048]{1,0:T(8,128)(2,1)}, u32[]{:S(2)}, u32[]{:S(2)}) collective-permute-start(bf16[64,2048]{1,0:T(8,128)(2,1)} %collective-permute-done.1.refs_1_), channel_id=1, source_target_pairs={{0,2},{1,3},{2,0},{3,1},{4,6},{5,7},{6,4},{7,5},{8,10},{9,11},{10,... | collective-permute-start | bytes 786440 | tf_op jit(solution)/shard_map/ppermute | solution.py:31
  33.9 3.9 %collective-permute-start.13 = (bf16[64,2048]{1,0:T(8,128)(2,1)}, bf16[64,2048]{1,0:T(8,128)(2,1)}, u32[]{:S(2)}, u32[]{:S(2)}) collective-permute-start(bf16[64,2048]{1,0:T(8,128)(2,1)} %get-tuple-element.113.refs_0_), channel_id=1, source_target_pairs={{0,4},{1,5},{2,6},{3,7},{4,0},{5,1},{6,2},{7,3},{8,12},{9,13},{10,... | collective-permute-start | bytes 786440 | tf_op jit(solution)/shard_map/ppermute | solution.py:31
  37.9 2.1 %collect.1 = (bf16[768,256]{1,0:T(8,128)(2,1)S(1)}, bf16[256,768]{1,0:T(8,128)(2,1)S(1)}, bf16[768,128]{1,0:T(8,128)(2,1)S(1)}, f32[768,128]{1,0:T(8,128)S(1)}) custom-call(s32[6]{0:T(128)S(1)} %copy-done.8, s32[8,4]{1,0:T(8,128)S(1)} %copy.34.offered, bf16[432,320]{1,0:T(8,128)(2,1)S(1)} %stack.31.own, bf16[432,320]{1,0:T(8,128)(2,1)} %collective-permute-done.8.sib), custom_call_target="tpu_custom_call" | custom-call | flops 250000000 | bytes 3000000 | tf_op jit(solution)/shard_map/collect/pallas_call | solution.py:423
  40.1 6.9 %collective-permute-done.10.refs_3_ = bf16[64,2048]{1,0:T(8,128)(2,1)} collective-permute-done((bf16[64,2048]{1,0:T(8,128)(2,1)}, bf16[64,2048]{1,0:T(8,128)(2,1)}, u32[]{:S(2)}, u32[]{:S(2)}) %collective-permute-start.10) | collective-permute-done | bytes 262176 | tf_op jit(solution)/shard_map/ppermute | solution.py:31
  49.1 1.6 collective-permute-start.12
  50.6 1.5 collective-permute-start.11
  52.3 3.7 %collective-permute-start.15 = (bf16[64,2048]{1,0:T(8,128)(2,1)}, bf16[64,2048]{1,0:T(8,128)(2,1)S(1)}, u32[]{:S(2)}, u32[]{:S(2)}) collective-permute-start(bf16[64,2048]{1,0:T(8,128)(2,1)} %collective-permute-done.13.refs_1_), channel_id=1, source_target_pairs={{0,2},{1,3},{2,0},{3,1},{4,6},{5,7},{6,4},{7,5},{8,10},{9,11},{10,... | collective-permute-start | bytes 786440 | tf_op jit(solution)/shard_map/ppermute | solution.py:31
  56.0 7.3 %heads_backward.6 = (bf16[128,8192]{1,0:T(8,128)(2,1)}, bf16[128,4096]{1,0:T(8,128)(2,1)}, bf16[128,6144]{1,0:T(8,128)(2,1)}, f32[128,1024]{1,0:T(8,128)S(1)}, f...) custom-call(s32[6]{0:T(128)S(1)} %copy-done.8, bf16[128,8192]{1,0:T(8,128)(2,1)S(1)} %bitcast.18, ...), custom_call_target="tpu_custom_call" | custom-call | flops 200000000 | bytes 600000 | tf_op jit(solution)/shard_map/heads_backward/pallas_call | solution.py:158
  64.4 12.8 %heads_backward.7 = (bf16[128,8192]{1,0:T(8,128)(2,1)}, bf16[128,4096]{1,0:T(8,128)(2,1)}, bf16[128,6144]{1,0:T(8,128)(2,1)}, f32[128,2048]{1,0:T(8,128)S(1)}, f...) custom-call(s32[6]{0:T(128)S(1)} %copy-done.8, ...), custom_call_target="tpu_custom_call", output_to_operand_aliasing={{0}: (14, {}), {1}: (15, {}), {2}: (16, {})} | custom-call | flops 400000000 | bytes 1200000 | tf_op jit(solution)/shard_map/heads_backward/pallas_call | solution.py:158
  77.2 1.5 collective-permute-start.16
  78.6 1.5 collective-permute-start.17
  80.2 12.8 %heads_backward.8 = (bf16[128,8192]{1,0:T(8,128)(2,1)}, bf16[128,4096]{1,0:T(8,128)(2,1)}, bf16[128,6144]{1,0:T(8,128)(2,1)}, f32[128,2048]{1,0:T(8,128)S(1)}, f...) custom-call(s32[6]{0:T(128)S(1)} %copy-done.8, ...), custom_call_target="tpu_custom_call", output_to_operand_aliasing={{0}: (14, {}), {1}: (15, {}), {2}: (16, {})} | custom-call | flops 400000000 | bytes 1200000 | tf_op jit(solution)/shard_map/heads_backward/pallas_call | solution.py:158
  93.5 7.3 %heads_backward.9 = (bf16[128,8192]{1,0:T(8,128)(2,1)}, bf16[128,4096]{1,0:T(8,128)(2,1)}, bf16[128,6144]{1,0:T(8,128)(2,1)}, f32[128,1024]{1,0:T(8,128)S(1)}, f...) custom-call(s32[6]{0:T(128)S(1)} %copy-done.8, ...), custom_call_target="tpu_custom_call", output_to_operand_aliasing={{0}: (14, {}), {1}: (15, {}), {2}: (16, {})} | custom-call | flops 200000000 | bytes 600000 | tf_op jit(solution)/shard_map/heads_backward/pallas_call | solution.py:158
  100.8 2.5 %collective-permute-done.16 = f32[128,2048]{1,0:T(8,128)S(1)} collective-permute-done((f32[128,2048]{1,0:T(8,128)S(1)}, f32[128,2048]{1,0:T(8,128)S(1)}, u32[]{:S(2)}, u32[]{:S(2)}) %collective-permute-start.16) | collective-permute-done | bytes 1048608 | tf_op jit(solution)/shard_map/ppermute | solution.py:31
  103.3 1.5 collective-permute-start.19
  104.8 7.5 %heads_backward.10 = (bf16[128,8192]{1,0:T(8,128)(2,1)}, bf16[128,4096]{1,0:T(8,128)(2,1)}, bf16[128,6144]{1,0:T(8,128)(2,1)}, f32[128,1024]{1,0:T(8,128)S(1)}, ...) custom-call(s32[6]{0:T(128)S(1)} %copy-done.8, ...), custom_call_target="tpu_custom_call", output_to_operand_aliasing={{0}: (14, {}), {1}: (15, {}), {2}: (16, {})} | custom-call | flops 200000000 | bytes 600000 | tf_op jit(solution)/shard_map/heads_backward/pallas_call | solution.py:158
  112.9 1.6 collective-permute-start.23
  114.7 11.3 %collective-permute-done.20 = f32[128,1024]{1,0:T(8,128)S(1)} collective-permute-done((f32[128,1024]{1,0:T(8,128)S(1)}, f32[128,1024]{1,0:T(8,128)S(1)}, u32[]{:S(2)}, u32[]{:S(2)}) %collective-permute-start.20) | collective-permute-done | bytes 524320 | tf_op jit(solution)/shard_map/ppermute | solution.py:31
  126.0 2.1 collective-permute-start.24
  128.7 8.2 %collective-permute-done.23 = f32[128,1024]{1,0:T(8,128)S(1)} collective-permute-done((f32[128,1024]{1,0:T(8,128)S(1)}, f32[128,1024]{1,0:T(8,128)S(1)}, u32[]{:S(2)}, u32[]{:S(2)}) %collective-permute-start.23) | collective-permute-done | bytes 524320 | tf_op jit(solution)/shard_map/ppermute | solution.py:31
  138.2 1.3 collective-permute-start.26
  139.4 7.3 %heads_backward.11 = (bf16[128,8192]{1,0:T(8,128)(2,1)}, bf16[128,4096]{1,0:T(8,128)(2,1)}, bf16[128,6144]{1,0:T(8,128)(2,1)}, f32[128,1024]{1,0:T(8,128)S(1)}, ...) custom-call(s32[6]{0:T(128)S(1)} %copy-done.8, ...), custom_call_target="tpu_custom_call", output_to_operand_aliasing={{0}: (14, {}), {1}: (15, {}), {2}: (16, {})} | custom-call | flops 200000000 | bytes 600000 | tf_op jit(solution)/shard_map/heads_backward/pallas_call | solution.py:158
  152.4 1.6 spread.1
  155.2 12.3 %collective-permute-done.32 = f32[64,1024]{1,0:T(8,128)} collective-permute-done((f32[64,1024]{1,0:T(8,128)}, f32[64,1024]{1,0:T(8,128)}, u32[]{:S(2)}, u32[]{:S(2)}) %collective-permute-start.32) | collective-permute-done | bytes 262176 | tf_op jit(solution)/shard_map/ppermute | solution.py:31
  168.6 1.5 add_add_fusion.1
  170.9 3.4 %collective-permute-start.29 = (f32[64,1024]{1,0:T(8,128)}, f32[64,1024]{1,0:T(8,128)}, u32[]{:S(2)}, u32[]{:S(2)}) collective-permute-start(f32[64,1024]{1,0:T(8,128)} %slice.65), channel_id=1, source_target_pairs={{0,4},{1,5},{2,6},{3,7},{4,0},{5,1},{6,2},{7,3},{8,12},{9,13},{10,... | collective-permute-start | bytes 786440 | tf_op jit(solution)/shard_map/ppermute | solution.py:31
  174.4 2.2 %copy.37 = f32[432,320]{1,0:T(8,128)} copy(f32[432,320]{0,1:T(8,128)} %copy-done.11) | data formatting | bytes 1105920 | tf_op jit(solution)/shard_map/ppermute | solution.py:31
  179.1 1.5 collective-permute-start.35
  180.7 1.2 collective-permute-start.34
  181.9 2.8 %collective-permute-done.29 = f32[64,1024]{1,0:T(8,128)} collective-permute-done((f32[64,1024]{1,0:T(8,128)}, f32[64,1024]{1,0:T(8,128)}, u32[]{:S(2)}, u32[]{:S(2)}) %collective-permute-start.29) | collective-permute-done | bytes 262176 | tf_op jit(solution)/shard_map/ppermute | solution.py:31
  185.7 1.3 collective-permute-start.30
  187.0 1.3 collective-permute-start.31
  188.4 4.7 %collective-permute-done.35.refs_4_ = f32[32,2048]{1,0:T(8,128)S(1)} collective-permute-done((f32[32,2048]{1,0:T(8,128)S(1)}, f32[32,2048]{1,0:T(8,128)S(1)}, u32[]{:S(2)}, u32[]{:S(2)}) %collective-permute-start.35) | collective-permute-done | bytes 262176 | tf_op jit(solution)/shard_map/ppermute | solution.py:31
  193.8 1.3 collective-permute-start.40
  195.1 1.4 collective-permute-start.39
  197.3 2.4 %place_columns.1 = (bf16[128,8192]{1,0:T(8,128)(2,1)}, bf16[128,4096]{1,0:T(8,128)(2,1)}) custom-call(s32[6]{0:T(128)S(1)} %copy-done.8, bf16[128,6144]{1,0:T(8,128)(2,1)S(1)} %collective-permute-done.21.received, bf16[128,8192]{1,0:T(8,128)(2,1)} %get-tuple-element.140.q_in, ...), custom_call_target="tpu_custom_call", output_to_operand_aliasing={{0}: (2, {}), {1}: (3, {})} | custom-call | bytes 4000000 | tf_op jit(solution)/shard_map/place_columns/pallas_call | solution.py:187
  201.7 2.3 %collective-permute-done.40.refs_7_ = f32[32,2048]{1,0:T(8,128)S(1)} collective-permute-done((f32[32,2048]{1,0:T(8,128)S(1)}, f32[32,2048]{1,0:T(8,128)S(1)}, u32[]{:S(2)}, u32[]{:S(2)}) %collective-permute-start.40) | collective-permute-done | bytes 262176 | tf_op jit(solution)/shard_map/ppermute | solution.py:31
  204.0 4.2 %collective-permute-done.39.refs_5_ = f32[32,2048]{1,0:T(8,128)S(1)} collective-permute-done((f32[32,2048]{1,0:T(8,128)S(1)}, f32[32,2048]{1,0:T(8,128)S(1)}, u32[]{:S(2)}, u32[]{:S(2)}) %collective-permute-start.39) | collective-permute-done | bytes 262176 | tf_op jit(solution)/shard_map/ppermute | solution.py:31
  208.6 3.4 %lay_out.1 = f32[32,16384]{1,0:T(8,128)} custom-call(s32[6]{0:T(128)S(1)} %copy-done.8, f32[32,2048]{1,0:T(8,128)S(1)} %join_cores.2.refs_0_, f32[32,2048]{1,0:T(8,128)S(1)} %join_cores.3.refs_1_, f32[32,2048]{1,0:T(8,128)S(1)} %collective-permute-done.34.refs_2_, f32[32,2048]{1,0:T(8,128)} %collective-permute-done.38.refs_3_, ...), custom_call_target="tpu_custom_call" | custom-call | bytes 4000000 | tf_op jit(solution)/shard_map/lay_out/pallas_call | solution.py:296
  (109 shorter events, 25.3 us)
Async XLA Ops:
  3.8 34.0 %copy-start.3 = (f32[1,64,128]{2,1,0:T(8,128)S(1)}, f32[1,64,128]{2,1,0:T(8,128)}, u32[]{:S(2)}) copy-start(f32[1,64,128]{2,1,0:T(8,128)} %param.11) | copy-start | bytes 98308
  3.8 34.0 %copy-start.15 = (s32[1,8,4]{1,2,0:T(4,128)S(1)}, s32[1,8,4]{1,2,0:T(4,128)}, u32[]{:S(2)}) copy-start(s32[1,8,4]{1,2,0:T(4,128)} %param.15) | copy-start | bytes 388
  3.8 34.1 %copy-start.8 = (s32[6]{0:T(128)S(1)}, s32[6]{0:T(128)}, u32[]{:S(2)}) copy-start(s32[6]{0:T(128)} %stack.30.place) | copy-start | bytes 76
  3.8 1.8 collective-permute-start
  5.7 9.1 %collective-permute-start.2 = (bf16[128,8192]{1,0:T(8,128)(2,1)S(1)}, bf16[128,8192]{1,0:T(8,128)(2,1)}, u32[]{:S(2)}, u32[]{:S(2)}) collective-permute-start(bf16[128,8192]{1,0:T(8,128)(2,1)S(1)} %bitcast.17), channel_id=1, source_target_pairs={{0,1},{1,0},{2,3},{3,2},{4,5},{5,4},{6,7},{7,6},{8,9},{9,8},{10,11... | collective-permute-start | bytes 6291464 | tf_op jit(solution)/shard_map/ppermute | solution.py:31
  6.0 8.7 %collective-permute-start.4 = (bf16[128,8192]{1,0:T(8,128)(2,1)}, bf16[128,8192]{1,0:T(8,128)(2,1)}, u32[]{:S(2)}, u32[]{:S(2)}) collective-permute-start(bf16[128,8192]{1,0:T(8,128)(2,1)} %bitcast.24), channel_id=1, source_target_pairs={{0,1},{1,0},{2,3},{3,2},{4,5},{5,4},{6,7},{7,6},{8,9},{9,8},{10,11... | collective-permute-start | bytes 6291464 | tf_op jit(solution)/shard_map/ppermute | solution.py:31
  6.2 8.5 %collective-permute-start.3 = (bf16[128,4096]{1,0:T(8,128)(2,1)}, bf16[128,4096]{1,0:T(8,128)(2,1)}, u32[]{:S(2)}, u32[]{:S(2)}) collective-permute-start(bf16[128,4096]{1,0:T(8,128)(2,1)} %bitcast.31), channel_id=1, source_target_pairs={{0,1},{1,0},{2,3},{3,2},{4,5},{5,4},{6,7},{7,6},{8,9},{9,8},{10,11... | collective-permute-start | bytes 3145736 | tf_op jit(solution)/shard_map/ppermute | solution.py:31
  9.1 46.9 %copy-start.2 = (bf16[1,128,4096]{2,1,0:T(8,128)(2,1)S(1)}, bf16[1,128,4096]{2,1,0:T(8,128)(2,1)}, u32[]{:S(2)}) copy-start(bf16[1,128,4096]{2,1,0:T(8,128)(2,1)} %param.9) | copy-start | bytes 3145732
  9.1 19.5 %collective-permute-start.9 = (bf16[64,2048]{1,0:T(8,128)(2,1)}, bf16[64,2048]{1,0:T(8,128)(2,1)}, u32[]{:S(2)}, u32[]{:S(2)}) collective-permute-start(bf16[64,2048]{1,0:T(8,128)(2,1)} %get-tuple-element.104.refs_0_), channel_id=1, source_target_pairs={{0,2},{1,3},{2,0},{3,1},{4,6},{5,7},{6,4},{7,5},{8,10},{9,11},{10,... | collective-permute-start | bytes 786440 | tf_op jit(solution)/shard_map/ppermute | solution.py:31
  11.9 16.8 %collective-permute-start.1 = (bf16[64,2048]{1,0:T(8,128)(2,1)}, bf16[64,2048]{1,0:T(8,128)(2,1)}, u32[]{:S(2)}, u32[]{:S(2)}) collective-permute-start(bf16[64,2048]{1,0:T(8,128)(2,1)} %get-tuple-element.104.refs_0_), channel_id=1, source_target_pairs={{0,4},{1,5},{2,6},{3,7},{4,0},{5,1},{6,2},{7,3},{8,12},{9,13},{10,... | collective-permute-start | bytes 786440 | tf_op jit(solution)/shard_map/ppermute | solution.py:31
  14.7 12.0 %collective-permute-start.7 = (bf16[144,320]{1,0:T(8,128)(2,1)S(1)}, bf16[144,320]{1,0:T(8,128)(2,1)S(1)}, u32[]{:S(2)}, u32[]{:S(2)}) collective-permute-start(bf16[144,320]{1,0:T(8,128)(2,1)S(1)} %fusion.3.refs_0_), channel_id=1, source_target_pairs={{0,4},{1,5},{2,6},{3,7},{8,12},{9,13},{10,14},{11,15},{16,20},{17,... | collective-permute-start | bytes 276488 | tf_op jit(solution)/shard_map/ppermute | solution.py:26
  20.5 8.0 %collective-permute-start.6 = (bf16[144,320]{1,0:T(8,128)(2,1)S(1)}, bf16[144,320]{1,0:T(8,128)(2,1)S(1)}, u32[]{:S(2)}, u32[]{:S(2)}) collective-permute-start(bf16[144,320]{1,0:T(8,128)(2,1)S(1)} %fusion.3.refs_0_), channel_id=1, source_target_pairs={{0,2},{1,3},{2,4},{3,5},{4,6},{5,7},{8,10},{9,11},{10,12},{11,13},... | collective-permute-start | bytes 276488 | tf_op jit(solution)/shard_map/ppermute | solution.py:26
  28.6 9.3 %collective-permute-start.8 = (bf16[432,320]{1,0:T(8,128)(2,1)S(1)}, bf16[432,320]{1,0:T(8,128)(2,1)}, u32[]{:S(2)}, u32[]{:S(2)}) collective-permute-start(bf16[432,320]{1,0:T(8,128)(2,1)S(1)} %stack.31.own), channel_id=1, source_target_pairs={{0,1},{1,0},{2,3},{3,2},{4,5},{5,4},{6,7},{7,6},{8,9},{9,8},{10,11... | collective-permute-start | bytes 829448 | tf_op jit(solution)/shard_map/ppermute | solution.py:31
  28.7 18.3 %collective-permute-start.10 = (bf16[64,2048]{1,0:T(8,128)(2,1)}, bf16[64,2048]{1,0:T(8,128)(2,1)}, u32[]{:S(2)}, u32[]{:S(2)}) collective-permute-start(bf16[64,2048]{1,0:T(8,128)(2,1)} %collective-permute-done.1.refs_1_), channel_id=1, source_target_pairs={{0,2},{1,3},{2,0},{3,1},{4,6},{5,7},{6,4},{7,5},{8,10},{9,11},{10,... | collective-permute-start | bytes 786440 | tf_op jit(solution)/shard_map/ppermute | solution.py:31
  33.9 18.4 %collective-permute-start.14 = (bf16[64,2048]{1,0:T(8,128)(2,1)}, bf16[64,2048]{1,0:T(8,128)(2,1)}, u32[]{:S(2)}, u32[]{:S(2)}) collective-permute-start(bf16[64,2048]{1,0:T(8,128)(2,1)} %get-tuple-element.113.refs_0_), channel_id=1, source_target_pairs={{0,2},{1,3},{2,0},{3,1},{4,6},{5,7},{6,4},{7,5},{8,10},{9,11},{10,... | collective-permute-start | bytes 786440 | tf_op jit(solution)/shard_map/ppermute | solution.py:31
  33.9 18.4 %collective-permute-start.13 = (bf16[64,2048]{1,0:T(8,128)(2,1)}, bf16[64,2048]{1,0:T(8,128)(2,1)}, u32[]{:S(2)}, u32[]{:S(2)}) collective-permute-start(bf16[64,2048]{1,0:T(8,128)(2,1)} %get-tuple-element.113.refs_0_), channel_id=1, source_target_pairs={{0,4},{1,5},{2,6},{3,7},{4,0},{5,1},{6,2},{7,3},{8,12},{9,13},{10,... | collective-permute-start | bytes 786440 | tf_op jit(solution)/shard_map/ppermute | solution.py:31
  37.8 2.3 %collective-permute-start.5 = (f32[64,128]{1,0:T(8,128)S(1)}, f32[64,128]{1,0:T(8,128)S(1)}, u32[]{:S(2)}, u32[]{:S(2)}) collective-permute-start(f32[64,128]{1,0:T(8,128)S(1)} %bitcast.38), channel_id=1, source_target_pairs={{0,1},{1,0},{2,3},{3,2},{4,5},{5,4},{6,7},{7,6},{8,9},{9,8},{10,11... | collective-permute-start | bytes 98312 | tf_op jit(solution)/shard_map/ppermute | solution.py:31
  37.9 18.1 %copy-start.1 = (bf16[1,128,8192]{2,1,0:T(8,128)(2,1)S(1)}, bf16[1,128,8192]{2,1,0:T(8,128)(2,1)}, u32[]{:S(2)}) copy-start(bf16[1,128,8192]{2,1,0:T(8,128)(2,1)} %param.10) | copy-start | bytes 6291460
  49.1 31.1 %collective-permute-start.12 = (bf16[256,2048]{1,0:T(8,128)(2,1)S(1)}, bf16[256,2048]{1,0:T(8,128)(2,1)S(1)}, u32[]{:S(2)}, u32[]{:S(2)}) collective-permute-start(bf16[256,2048]{1,0:T(8,128)(2,1)S(1)} %stack.32.weight), channel_id=1, source_target_pairs={{0,8},{8,0},{16,24},{24,16},{1,9},{9,1},{17,25},{25,17},{2,10},{10... | collective-permute-start | bytes 3145736 | tf_op jit(solution)/shard_map/ppermute | solution.py:31
  50.6 29.5 %collective-permute-start.11 = (bf16[256,2048]{1,0:T(8,128)(2,1)S(1)}, bf16[256,2048]{1,0:T(8,128)(2,1)S(1)}, u32[]{:S(2)}, u32[]{:S(2)}) collective-permute-start(bf16[256,2048]{1,0:T(8,128)(2,1)S(1)} %stack.32.weight), channel_id=1, source_target_pairs={{0,16},{8,24},{16,0},{24,8},{1,17},{9,25},{17,1},{25,9},{2,18},{10... | collective-permute-start | bytes 3145736 | tf_op jit(solution)/shard_map/ppermute | solution.py:31
  52.3 10.9 %collective-permute-start.15 = (bf16[64,2048]{1,0:T(8,128)(2,1)}, bf16[64,2048]{1,0:T(8,128)(2,1)S(1)}, u32[]{:S(2)}, u32[]{:S(2)}) collective-permute-start(bf16[64,2048]{1,0:T(8,128)(2,1)} %collective-permute-done.13.refs_1_), channel_id=1, source_target_pairs={{0,2},{1,3},{2,0},{3,1},{4,6},{5,7},{6,4},{7,5},{8,10},{9,11},{10,... | collective-permute-start | bytes 786440 | tf_op jit(solution)/shard_map/ppermute | solution.py:31
  77.2 26.1 %collective-permute-start.16 = (f32[128,2048]{1,0:T(8,128)S(1)}, f32[128,2048]{1,0:T(8,128)S(1)}, u32[]{:S(2)}, u32[]{:S(2)}) collective-permute-start(f32[128,2048]{1,0:T(8,128)S(1)} %get-tuple-element.125), channel_id=1, source_target_pairs={{0,8},{8,0},{16,24},{24,16},{1,9},{9,1},{17,25},{25,17},{2,10},{10... | collective-permute-start | bytes 3145736 | tf_op jit(solution)/shard_map/ppermute | solution.py:31
  78.6 24.6 %collective-permute-start.17 = (f32[128,2048]{1,0:T(8,128)S(1)}, f32[128,2048]{1,0:T(8,128)S(1)}, u32[]{:S(2)}, u32[]{:S(2)}) collective-permute-start(f32[128,2048]{1,0:T(8,128)S(1)} %get-tuple-element.126), channel_id=1, source_target_pairs={{0,16},{8,24},{16,0},{24,8},{1,17},{9,25},{17,1},{25,9},{2,18},{10... | collective-permute-start | bytes 3145736 | tf_op jit(solution)/shard_map/ppermute | solution.py:31
  93.0 33.0 %collective-permute-start.18 = (f32[128,2048]{1,0:T(8,128)S(1)}, f32[128,2048]{1,0:T(8,128)S(1)}, u32[]{:S(2)}, u32[]{:S(2)}) collective-permute-start(f32[128,2048]{1,0:T(8,128)S(1)} %get-tuple-element.132), channel_id=1, source_target_pairs={{0,8},{8,0},{16,24},{24,16},{1,9},{9,1},{17,25},{25,17},{2,10},{10... | collective-permute-start | bytes 3145736 | tf_op jit(solution)/shard_map/ppermute | solution.py:31
  103.3 33.7 %collective-permute-start.19 = (f32[128,1024]{1,0:T(8,128)S(1)}, f32[128,1024]{1,0:T(8,128)S(1)}, u32[]{:S(2)}, u32[]{:S(2)}) collective-permute-start(f32[128,1024]{1,0:T(8,128)S(1)} %get-tuple-element.133), channel_id=1, source_target_pairs={{0,16},{8,24},{16,0},{24,8},{1,17},{9,25},{17,1},{25,9},{2,18},{10... | collective-permute-start | bytes 1572872 | tf_op jit(solution)/shard_map/ppermute | solution.py:31
  112.2 13.8 %collective-permute-start.20 = (f32[128,1024]{1,0:T(8,128)S(1)}, f32[128,1024]{1,0:T(8,128)S(1)}, u32[]{:S(2)}, u32[]{:S(2)}) collective-permute-start(f32[128,1024]{1,0:T(8,128)S(1)} %get-tuple-element.134), channel_id=1, source_target_pairs={{0,16},{8,24},{16,0},{24,8},{1,17},{9,25},{17,1},{25,9},{2,18},{10... | collective-permute-start | bytes 1572872 | tf_op jit(solution)/shard_map/ppermute | solution.py:31
  112.9 24.0 %collective-permute-start.23 = (f32[128,1024]{1,0:T(8,128)S(1)}, f32[128,1024]{1,0:T(8,128)S(1)}, u32[]{:S(2)}, u32[]{:S(2)}) collective-permute-start(f32[128,1024]{1,0:T(8,128)S(1)} %get-tuple-element.158), channel_id=1, source_target_pairs={{0,8},{8,0},{16,24},{24,16},{1,9},{9,1},{17,25},{25,17},{2,10},{10... | collective-permute-start | bytes 1572872 | tf_op jit(solution)/shard_map/ppermute | solution.py:31
  126.0 24.7 %copy-start.10 = (f32[128,2048]{1,0:T(8,128)}, f32[128,2048]{1,0:T(8,128)S(1)}, u32[]{:S(2)}) copy-start(f32[128,2048]{1,0:T(8,128)S(1)} %collective-permute-done.18) | copy-start | bytes 3145732
  126.0 12.2 %collective-permute-start.24 = (f32[128,1024]{1,0:T(8,128)S(1)}, f32[128,1024]{1,0:T(8,128)S(1)}, u32[]{:S(2)}, u32[]{:S(2)}) collective-permute-start(f32[128,1024]{1,0:T(8,128)S(1)} %get-tuple-element.160), channel_id=1, source_target_pairs={{0,16},{8,24},{16,0},{24,8},{1,17},{9,25},{17,1},{25,9},{2,18},{10... | collective-permute-start | bytes 1572872 | tf_op jit(solution)/shard_map/ppermute | solution.py:31
  128.1 18.7 %collective-permute-start.27 = (f32[128,1024]{1,0:T(8,128)S(1)}, f32[128,1024]{1,0:T(8,128)S(1)}, u32[]{:S(2)}, u32[]{:S(2)}) collective-permute-start(f32[128,1024]{1,0:T(8,128)S(1)} %get-tuple-element.170), channel_id=1, source_target_pairs={{0,8},{8,0},{16,24},{24,16},{1,9},{9,1},{17,25},{25,17},{2,10},{10... | collective-permute-start | bytes 1572872 | tf_op jit(solution)/shard_map/ppermute | solution.py:31
  138.2 9.8 %collective-permute-start.25 = (f32[128,1024]{1,0:T(8,128)S(1)}, f32[128,1024]{1,0:T(8,128)S(1)}, u32[]{:S(2)}, u32[]{:S(2)}) collective-permute-start(f32[128,1024]{1,0:T(8,128)S(1)} %add_add_fusion.2), channel_id=1, source_target_pairs={{0,2},{1,3},{2,0},{3,1},{4,6},{5,7},{6,4},{7,5},{8,10},{9,11},{10,... | collective-permute-start | bytes 1572872 | tf_op jit(solution)/shard_map/ppermute | solution.py:31
  138.2 10.5 %collective-permute-start.26 = (f32[128,1024]{1,0:T(8,128)S(1)}, f32[128,1024]{1,0:T(8,128)S(1)}, u32[]{:S(2)}, u32[]{:S(2)}) collective-permute-start(f32[128,1024]{1,0:T(8,128)S(1)} %get-tuple-element.165), channel_id=1, source_target_pairs={{0,16},{8,24},{16,0},{24,8},{1,17},{9,25},{17,1},{25,9},{2,18},{10... | collective-permute-start | bytes 1572872 | tf_op jit(solution)/shard_map/ppermute | solution.py:31
  146.7 23.4 %collective-permute-start.21 = (bf16[128,6144]{1,0:T(8,128)(2,1)}, bf16[128,6144]{1,0:T(8,128)(2,1)S(1)}, u32[]{:S(2)}, u32[]{:S(2)}) collective-permute-start(bf16[128,6144]{1,0:T(8,128)(2,1)} %get-tuple-element.139), channel_id=1, source_target_pairs={{0,1},{1,0},{2,3},{3,2},{4,5},{5,4},{6,7},{7,6},{8,9},{9,8},{10,11... | collective-permute-start | bytes 4718600 | tf_op jit(solution)/shard_map/ppermute | solution.py:31
  149.7 18.8 %collective-permute-start.28 = (f32[128,1024]{1,0:T(8,128)}, f32[128,1024]{1,0:T(8,128)}, u32[]{:S(2)}, u32[]{:S(2)}) collective-permute-start(f32[128,1024]{1,0:T(8,128)} %add_add_fusion), channel_id=1, source_target_pairs={{0,2},{1,3},{2,0},{3,1},{4,6},{5,7},{6,4},{7,5},{8,10},{9,11},{10,... | collective-permute-start | bytes 1572872 | tf_op jit(solution)/shard_map/ppermute | solution.py:31
  151.7 15.8 %collective-permute-start.32 = (f32[64,1024]{1,0:T(8,128)}, f32[64,1024]{1,0:T(8,128)}, u32[]{:S(2)}, u32[]{:S(2)}) collective-permute-start(f32[64,1024]{1,0:T(8,128)} %slice.82), channel_id=1, source_target_pairs={{0,4},{1,5},{2,6},{3,7},{4,0},{5,1},{6,2},{7,3},{8,12},{9,13},{10,... | collective-permute-start | bytes 786440 | tf_op jit(solution)/shard_map/ppermute | solution.py:31
  154.1 14.5 %copy-start.5 = (f32[128,1024]{1,0:T(8,128)S(1)}, f32[128,1024]{1,0:T(8,128)}, u32[]{:S(2)}) copy-start(f32[128,1024]{1,0:T(8,128)} %copy-done.4) | copy-start | bytes 1572868
  155.2 14.9 %collective-permute-start.22 = (f32[432,320]{0,1:T(8,128)}, f32[432,320]{0,1:T(8,128)S(1)}, u32[]{:S(2)}, u32[]{:S(2)}) collective-permute-start(f32[432,320]{0,1:T(8,128)} %copy.36), channel_id=1, source_target_pairs={{0,1},{1,0},{2,3},{3,2},{4,5},{5,4},{6,7},{7,6},{8,9},{9,8},{10,11... | collective-permute-start | bytes 1658888 | tf_op jit(solution)/shard_map/ppermute | solution.py:31
  170.9 13.7 %collective-permute-start.29 = (f32[64,1024]{1,0:T(8,128)}, f32[64,1024]{1,0:T(8,128)}, u32[]{:S(2)}, u32[]{:S(2)}) collective-permute-start(f32[64,1024]{1,0:T(8,128)} %slice.65), channel_id=1, source_target_pairs={{0,4},{1,5},{2,6},{3,7},{4,0},{5,1},{6,2},{7,3},{8,12},{9,13},{10,... | collective-permute-start | bytes 786440 | tf_op jit(solution)/shard_map/ppermute | solution.py:31
  174.3 3.4 %collective-permute-start.33 = (f32[32,1024]{1,0:T(8,128)S(1)}, f32[32,1024]{1,0:T(8,128)S(1)}, u32[]{:S(2)}, u32[]{:S(2)}) collective-permute-start(f32[32,1024]{1,0:T(8,128)S(1)} %get-tuple-element.194), channel_id=1, source_target_pairs={{0,1},{1,0},{2,3},{3,2},{4,5},{5,4},{6,7},{7,6},{8,9},{9,8},{10,11... | collective-permute-start | bytes 393224 | tf_op jit(solution)/shard_map/ppermute | solution.py:31
  178.3 10.1 %collective-permute-start.36 = (f32[32,2048]{1,0:T(8,128)S(1)}, f32[32,2048]{1,0:T(8,128)S(1)}, u32[]{:S(2)}, u32[]{:S(2)}) collective-permute-start(f32[32,2048]{1,0:T(8,128)S(1)} %join_cores.2.refs_0_), channel_id=1, source_target_pairs={{0,24},{8,16},{16,8},{24,0},{1,25},{9,17},{17,9},{25,1},{2,26},{10... | collective-permute-start | bytes 786440 | tf_op jit(solution)/shard_map/ppermute | solution.py:31
  179.1 14.0 %collective-permute-start.35 = (f32[32,2048]{1,0:T(8,128)S(1)}, f32[32,2048]{1,0:T(8,128)S(1)}, u32[]{:S(2)}, u32[]{:S(2)}) collective-permute-start(f32[32,2048]{1,0:T(8,128)S(1)} %join_cores.2.refs_0_), channel_id=1, source_target_pairs={{0,16},{8,24},{16,0},{24,8},{1,17},{9,25},{17,1},{25,9},{2,18},{10... | collective-permute-start | bytes 786440 | tf_op jit(solution)/shard_map/ppermute | solution.py:31
  180.7 12.5 %collective-permute-start.34 = (f32[32,2048]{1,0:T(8,128)S(1)}, f32[32,2048]{1,0:T(8,128)S(1)}, u32[]{:S(2)}, u32[]{:S(2)}) collective-permute-start(f32[32,2048]{1,0:T(8,128)S(1)} %join_cores.2.refs_0_), channel_id=1, source_target_pairs={{0,8},{8,0},{16,24},{24,16},{1,9},{9,1},{17,25},{25,17},{2,10},{10... | collective-permute-start | bytes 786440 | tf_op jit(solution)/shard_map/ppermute | solution.py:31
  185.7 14.0 %collective-permute-start.30 = (f32[128,320]{1,0:T(8,128)S(1)}, f32[128,320]{1,0:T(8,128)S(1)}, u32[]{:S(2)}, u32[]{:S(2)}) collective-permute-start(f32[128,320]{1,0:T(8,128)S(1)} %get-tuple-element.190), channel_id=1, source_target_pairs={{2,0},{3,1},{4,2},{5,3},{6,4},{7,5},{10,8},{11,9},{12,10},{13,11},... | collective-permute-start | bytes 491528 | tf_op jit(solution)/shard_map/ppermute | solution.py:26
  187.0 13.9 %collective-permute-start.31 = (f32[128,320]{1,0:T(8,128)S(1)}, f32[128,320]{1,0:T(8,128)S(1)}, u32[]{:S(2)}, u32[]{:S(2)}) collective-permute-start(f32[128,320]{1,0:T(8,128)S(1)} %get-tuple-element.191), channel_id=1, source_target_pairs={{4,0},{5,1},{6,2},{7,3},{12,8},{13,9},{14,10},{15,11},{20,16},{21,... | collective-permute-start | bytes 491528 | tf_op jit(solution)/shard_map/ppermute | solution.py:26
  188.4 4.8 %collective-permute-start.37 = (f32[32,1024]{1,0:T(8,128)S(1)}, f32[32,1024]{1,0:T(8,128)S(1)}, u32[]{:S(2)}, u32[]{:S(2)}) collective-permute-start(f32[32,1024]{1,0:T(8,128)S(1)} %get-tuple-element.192), channel_id=1, source_target_pairs={{0,1},{1,0},{2,3},{3,2},{4,5},{5,4},{6,7},{7,6},{8,9},{9,8},{10,11... | collective-permute-start | bytes 393224 | tf_op jit(solution)/shard_map/ppermute | solution.py:31
  193.8 10.2 %collective-permute-start.40 = (f32[32,2048]{1,0:T(8,128)S(1)}, f32[32,2048]{1,0:T(8,128)S(1)}, u32[]{:S(2)}, u32[]{:S(2)}) collective-permute-start(f32[32,2048]{1,0:T(8,128)S(1)} %join_cores.3.refs_1_), channel_id=1, source_target_pairs={{0,24},{8,16},{16,8},{24,0},{1,25},{9,17},{17,9},{25,1},{2,26},{10... | collective-permute-start | bytes 786440 | tf_op jit(solution)/shard_map/ppermute | solution.py:31
  195.1 13.1 %collective-permute-start.39 = (f32[32,2048]{1,0:T(8,128)S(1)}, f32[32,2048]{1,0:T(8,128)S(1)}, u32[]{:S(2)}, u32[]{:S(2)}) collective-permute-start(f32[32,2048]{1,0:T(8,128)S(1)} %join_cores.3.refs_1_), channel_id=1, source_target_pairs={{0,16},{8,24},{16,0},{24,8},{1,17},{9,25},{17,1},{25,9},{2,18},{10... | collective-permute-start | bytes 786440 | tf_op jit(solution)/shard_map/ppermute | solution.py:31
  196.5 12.0 %collective-permute-start.38 = (f32[32,2048]{1,0:T(8,128)S(1)}, f32[32,2048]{1,0:T(8,128)}, u32[]{:S(2)}, u32[]{:S(2)}) collective-permute-start(f32[32,2048]{1,0:T(8,128)S(1)} %join_cores.3.refs_1_), channel_id=1, source_target_pairs={{0,8},{8,0},{16,24},{24,16},{1,9},{9,1},{17,25},{25,17},{2,10},{10... | collective-permute-start | bytes 786440 | tf_op jit(solution)/shard_map/ppermute | solution.py:31
  (10 other events, 52.6 us)

commit v9 on v8

--- a/solution.py
+++ b/solution.py
@@ -164,7 +164,7 @@
         input_output_aliases=aliases,
         compiler_params=pltpu.CompilerParams(vmem_limit_bytes=KERNEL_BYTES),
         cost_estimate=pl.CostEstimate(
-            flops=count * 100_000_000, bytes_accessed=count * 300_000, transcendentals=0
+            flops=count * 1_500_000_000, bytes_accessed=count * 300_000, transcendentals=0
         ),
         name="heads_backward",
     )(place, *operands)
@@ -235,77 +235,81 @@
     )(*inputs)
 
 
-def leave_kernel(place, near, distant, leaving):
-    width = near.shape[1]
-    leaving[:, :width] = near[...]
-    leaving[:, width:] = distant[...]
-
-
-def join_rows_kernel(place, near, distant, crossed, near_rows, distant_rows):
-    rows, width = near.shape
-    for at, (own, out) in enumerate(((near, near_rows), (distant, distant_rows))):
+def join_rows_kernel(place, near, distant, near_crossed, distant_crossed, near_rows, distant_rows):
+    rows = near.shape[0]
+    for own, crossed, out in (
+        (near, near_crossed, near_rows),
+        (distant, distant_crossed, distant_rows),
+    ):
         out[:rows, :] = own[...]
-        out[rows:, :] = crossed[:, at * width : (at + 1) * width]
-
-
-def weight_parts(place, up_weight, chunks, far, crossed=None):
+        out[rows:, :] = crossed[...]
+
+
+def weight_parts(place, up_weight, crossed, chunks, far):
     rows = up_weight.shape[0]
     width = up_weight.shape[1] // chunks // 2
-    joins = crossed is not None
 
     def column_block(t):
-        def block(i, place):
-            return (0, place[1 + t] * 2 + (place[0] if joins else 1 - place[0]))
-
-        return pl.BlockSpec((rows, width), block)
-
-    whole = lambda shape: pl.BlockSpec(shape, lambda i, place: (0, 0))
-    shapes = [(2 * rows, width)] * 2 if joins else [(rows, 2 * width)]
-    return pl.pallas_call(
-        join_rows_kernel if joins else leave_kernel,
+        return pl.BlockSpec((rows, width), lambda i, place: (0, place[1 + t] * 2 + place[0]))
+
+    shape = (2 * rows, width)
+    return pl.pallas_call(
+        join_rows_kernel,
         grid_spec=pltpu.PrefetchScalarGridSpec(
             num_scalar_prefetch=1,
             grid=(1,),
-            in_specs=[column_block(t) for t in (0, far)] + [whole((rows, 2 * width))] * joins,
-            out_specs=[whole(shape) for shape in shapes],
-        ),
-        out_shape=[jax.ShapeDtypeStruct(shape, up_weight.dtype) for shape in shapes],
+            in_specs=[column_block(t) for t in (0, far)] * 2,
+            out_specs=[pl.BlockSpec(shape, lambda i, place: (0, 0))] * 2,
+        ),
+        out_shape=[jax.ShapeDtypeStruct(shape, up_weight.dtype)] * 2,
         compiler_params=pltpu.CompilerParams(vmem_limit_bytes=INPUT_BYTES),
         cost_estimate=pl.CostEstimate(flops=0, bytes_accessed=1_000_000, transcendentals=0),
         name="weight_parts",
-    )(place, up_weight, up_weight, *([crossed] if joins else []))
-
-
-def lay_kernel(place, *refs):
-    *pieces, out = refs
-    width = out.shape[1] // 4
-    for step in range(len(pieces) // 2):
-        early, late = pieces[2 * step], pieces[2 * step + 1]
-
-        @pl.when(pl.program_id(0) == step)
-        def _():
-            for which in range(2):
-                source = slice(which * width, (which + 1) * width)
-                out[:, 2 * which * width : (2 * which + 1) * width] = early[:, source]
-                out[:, (2 * which + 1) * width : (2 * which + 2) * width] = late[:, source]
-
-
-def lay_out(place, pieces):
+    )(place, up_weight, up_weight, crossed, crossed)
+
+
+def lay_kernel(place, *refs, count):
+    pieces, out = refs[:count], refs[-1]
+    width = out.shape[1]
+    for step, piece in enumerate(pieces):
+        for which in range(2):
+
+            @pl.when(pl.program_id(0) == 2 * step + which)
+            def _():
+                out[...] = piece[:, which * width : (which + 1) * width]
+
+
+def lay_out(place, pieces, half, earlier=None):
     rows, columns = pieces[0].shape
-    count = len(pieces) // 2
-    return pl.pallas_call(
-        lay_kernel,
+    count, width = len(pieces), columns // 2
+    total = 2 * count * columns
+
+    def target(step, place):
+        chunk = place[1]
+        for t in range(1, count):
+            chunk = jnp.where((step >> 1) == t, place[1 + t], chunk)
+        return (0, chunk * 4 + (step & 1) * 2 + half)
+
+    in_specs = [pl.BlockSpec((rows, columns), lambda step, place: (0, 0))] * count
+    operands, aliases = list(pieces), {}
+    if earlier is not None:
+        in_specs.append(pl.BlockSpec(memory_space=pl.ANY))
+        operands.append(earlier)
+        aliases = {count + 1: 0}
+    return pl.pallas_call(
+        functools.partial(lay_kernel, count=count),
         grid_spec=pltpu.PrefetchScalarGridSpec(
             num_scalar_prefetch=1,
-            grid=(count,),
-            in_specs=[pl.BlockSpec((rows, columns), lambda t, place: (0, 0))] * len(pieces),
-            out_specs=pl.BlockSpec((rows, 2 * columns), lambda t, place: (0, place[1 + t])),
-        ),
-        out_shape=jax.ShapeDtypeStruct((rows, count * 2 * columns), pieces[0].dtype),
+            grid=(2 * count,),
+            in_specs=in_specs,
+            out_specs=pl.BlockSpec((rows, width), target),
+        ),
+        out_shape=jax.ShapeDtypeStruct((rows, total), pieces[0].dtype),
+        input_output_aliases=aliases,
         compiler_params=pltpu.CompilerParams(vmem_limit_bytes=KERNEL_BYTES),
-        cost_estimate=pl.CostEstimate(flops=0, bytes_accessed=4_000_000, transcendentals=0),
+        cost_estimate=pl.CostEstimate(flops=0, bytes_accessed=2_000_000, transcendentals=0),
         name="lay_out",
-    )(place, *pieces)
+    )(place, *operands)
 
 
 def piece_kernel(place, kept, crossed, out):
@@ -503,14 +507,13 @@
 
     place = jnp.stack([core] + [dp ^ t for t in range(n_dp)] + [ctx]).astype(jnp.int32)
 
-    leaving, = weight_parts(place, up_weight, n_dp, far)
-    crossed = exchange(leaving, "ctx", 1)
+    crossed = exchange(up_weight, "ctx", 1)
     crossed, place, selected, offered, q_nope, q_rope, grad_out, log_total, kv_latent = (
         lax.optimization_barrier(
             (crossed, place, selected, offered, q_nope, q_rope, grad_out, log_total, kv_latent)
         )
     )
-    chip_rows = weight_parts(place, up_weight, n_dp, far, crossed)
+    chip_rows = weight_parts(place, up_weight, crossed, n_dp, far)
     own = [q_nope[0], q_rope[0], grad_out[0]]
     sibling = [exchange(array, "ctx", 1) for array in own]
     offered = offered[0]
@@ -556,11 +559,11 @@
     orders = (bits, bits[::-1])
     first_sums = [{t: [] for t in range(n_dp) if t & order[0]} for order in orders]
     half_pairs = pairs // 2
-    units = [(0, 0, half_pairs)] + [(t, 0, pairs) for t in [far] + list(range(1, far - 1))]
-    units += [(far - 1, 0, half_pairs), (far - 1, half_pairs, half_pairs)]
-    units.append((0, half_pairs, half_pairs))
+    halved = lambda t: [(t, 0, half_pairs), (t, half_pairs, half_pairs)]
+    units = [(0, 0, half_pairs), *halved(far)] + [(t, 0, pairs) for t in range(1, far - 1)]
+    units += [*halved(far - 1), (0, half_pairs, half_pairs)]
     for t, start, count in units:
-        if t == far:
+        if t == far and not start:
             weights[far] = joined([after(far_pieces[0], latents[-1])] + far_pieces[1:])
         weight = weights[t]
         if t == 0 and start:
@@ -568,8 +571,9 @@
             weight = after(weight, latents[-1], *there)
         if t == 1 and not start:
             weight = after(weight, *[weights[near] for near in range(2, far)])
-        if t == far - 1 and start:
-            weight = after(weight, latents[-1], *[sent[far][0] for sent in first_sums])
+        if t == far - 1:
+            far_sums = [sent[far][1 if start else 0] for sent in first_sums]
+            weight = after(weight, latents[-1], *far_sums)
         rest = chunk_backward(
             place,
             t,
@@ -585,7 +589,10 @@
         for side, sent in enumerate(first_sums):
             weight_grads[t][side].append(rest[3 + side])
             if t in sent:
-                sent[t].append(exchange(rest[3 + side], "dp", orders[side][0]))
+                leaving = rest[3 + side]
+                if t == far - 1 and start:
+                    leaving = after(leaving, sent[t][0])
+                sent[t].append(exchange(leaving, "dp", orders[side][0]))
         latents.append(rest[5])
         ropes.append(rest[6])
 
@@ -650,8 +657,9 @@
     grad_rows = by_chip[0]
     for chips in (1, 2):
         grad_rows = grad_rows + from_behind(by_chip[chips], "ctx", -2 * chips)
-    finished[0][0] = after(finished[0][0], grad_rows, grad_nope)
-    grad_weight = lay_out(place, [piece for both in zip(*finished) for piece in both])
+    grad_weight = lay_out(place, finished[0], 0)
+    finished[1][0] = after(finished[1][0], grad_rows, grad_nope)
+    grad_weight = lay_out(place, finished[1], 1, grad_weight)
     return (grad_nope[None], grad_rope[None], grad_rows[None], grad_weight)
 
 

time: 213 us -> 215 us (level)
  Pallas kernels: 72.8 us -> 75.5 us
  waiting for transfers between devices: 66 us -> 63.5 us
  starting transfers between devices: 58 us -> 60.2 us
    ppermute x37 -> x39, starting transfers between devices: 46.1 us -> 48.7 us  [exchange(): lax.ppermute(value, axis, [(source, source ^ bits) for source in range(co...]
    pallas_call x6 -> x7, Pallas kernels: 54.8 us -> 56.6 us  [chunk_backward(): pl.pallas_call(functools.partial(heads_kernel, earlier=len(aliases)), gri...]
    ppermute x37 -> x39, waiting for transfers between devices: 60.4 us -> 58.9 us  [exchange(): lax.ppermute(value, axis, [(source, source ^ bits) for source in range(co...]
  transfers between devices with their start and end apart: 41 -> 43, of which waited for: 19 -> 18; matrix products, arithmetic and copies ran while one was open for 5% -> 5% of each run, Pallas kernels for 32% -> 34%
where the time goes in v9:
time: 215 us; the launch traced here: 214 us
  Pallas kernels  75.5 us (35%)
  waiting for transfers between devices  63.5 us (30%)
  starting transfers between devices  60.2 us (28%)
  local copies, waits for them, and re-layouts  8.32 us (4%)
  other arithmetic  5.21 us (2%)
    ppermute x39, waiting for transfers between devices, exchange(): lax.ppermute(value, axis, [(source, source ^ bits) for source in range(co...  58.9 us
    pallas_call x7, Pallas kernels, chunk_backward(): pl.pallas_call(functools.partial(heads_kernel, earlier=len(aliases)), gri...  56.6 us
    ppermute x39, starting transfers between devices, exchange(): lax.ppermute(value, axis, [(source, source ^ bits) for source in range(co...  48.7 us
    ppermute x4, starting transfers between devices, from_behind(): lax.ppermute(value, axis, [(source, source + steps) for source in range(i...  11.6 us
    pallas_call x2, Pallas kernels, lay_out(): pl.pallas_call(functools.partial(lay_kernel, count=count), grid_spec=pltp...  6.75 us
    ppermute x4, waiting for transfers between devices, from_behind(): lax.ppermute(value, axis, [(source, source + steps) for source in range(i...  4.62 us
  transfers between devices with their start and end apart: 43, of which 18 were waited for; matrix products, arithmetic and copies ran while one was open for 5% of the time, Pallas kernels for 34%

profile of v9, /device:TPU:0, one launch (start us, length us, event | category | flops | bytes accessed | tf_op | source)
XLA Modules:
  0.0 213.9 jit_solution(2253688837985297420)
XLA Ops:
  1.8 1.9 collective-permute-done.near_crossed.distant_crossed
  4.6 2.6 %weight_parts.1 = (bf16[64,2048]{1,0:T(8,128)(2,1)}, bf16[64,2048]{1,0:T(8,128)(2,1)}) custom-call(s32[6]{0:T(128)} %stack.30.place, bf16[32,16384]{1,0:T(8,128)(2,1)} %distant.1, bf16[32,16384]{1,0:T(8,128)(2,1)} %distant.1, bf16[32,16384]{1,0:T(8,128)(2,1)} %copy-done.10, bf16[32,16384]{1,0:T(8,128)(2,1)} %copy-done.10), custom_call_target="tpu_custom_call" | custom-call | bytes 1000000 | tf_op jit(solution)/shard_map/weight_parts/pallas_call | solution.py:256
  7.2 2.9 %collective-permute-start.9 = (bf16[64,2048]{1,0:T(8,128)(2,1)}, bf16[64,2048]{1,0:T(8,128)(2,1)}, u32[]{:S(2)}, u32[]{:S(2)}) collective-permute-start(bf16[64,2048]{1,0:T(8,128)(2,1)} %get-tuple-element.113.refs_0_), channel_id=1, source_target_pairs={{0,2},{1,3},{2,0},{3,1},{4,6},{5,7},{6,4},{7,5},{8,10},{9,11},{10,... | collective-permute-start | bytes 786440 | tf_op jit(solution)/shard_map/ppermute | solution.py:31
  10.2 2.6 %collective-permute-start.1 = (bf16[64,2048]{1,0:T(8,128)(2,1)}, bf16[64,2048]{1,0:T(8,128)(2,1)}, u32[]{:S(2)}, u32[]{:S(2)}) collective-permute-start(bf16[64,2048]{1,0:T(8,128)(2,1)} %get-tuple-element.113.refs_0_), channel_id=1, source_target_pairs={{0,4},{1,5},{2,6},{3,7},{4,0},{5,1},{6,2},{7,3},{8,12},{9,13},{10,... | collective-permute-start | bytes 786440 | tf_op jit(solution)/shard_map/ppermute | solution.py:31
  13.0 5.5 %collective-permute-start.7 = (bf16[144,320]{1,0:T(8,128)(2,1)S(1)}, bf16[144,320]{1,0:T(8,128)(2,1)S(1)}, u32[]{:S(2)}, u32[]{:S(2)}) collective-permute-start(bf16[144,320]{1,0:T(8,128)(2,1)S(1)} %fusion.3.refs_0_), channel_id=1, source_target_pairs={{0,4},{1,5},{2,6},{3,7},{8,12},{9,13},{10,14},{11,15},{16,20},{17,... | collective-permute-start | bytes 276488 | tf_op jit(solution)/shard_map/ppermute | solution.py:26
  18.5 3.5 %collective-permute-start.6 = (bf16[144,320]{1,0:T(8,128)(2,1)S(1)}, bf16[144,320]{1,0:T(8,128)(2,1)S(1)}, u32[]{:S(2)}, u32[]{:S(2)}) collective-permute-start(bf16[144,320]{1,0:T(8,128)(2,1)S(1)} %fusion.3.refs_0_), channel_id=1, source_target_pairs={{0,2},{1,3},{2,4},{3,5},{4,6},{5,7},{8,10},{9,11},{10,12},{11,13},... | collective-permute-start | bytes 276488 | tf_op jit(solution)/shard_map/ppermute | solution.py:26
  22.0 3.0 %collective-permute-done.7.refs_2_ = bf16[144,320]{1,0:T(8,128)(2,1)S(1)} collective-permute-done((bf16[144,320]{1,0:T(8,128)(2,1)S(1)}, bf16[144,320]{1,0:T(8,128)(2,1)S(1)}, u32[]{:S(2)}, u32[]{:S(2)}) %collective-permute-start.7) | collective-permute-done | bytes 92192 | tf_op jit(solution)/shard_map/ppermute | solution.py:26
  25.1 1.6 collective-permute-done.6.refs_1_
  26.8 5.2 %collective-permute-start.10 = (bf16[64,2048]{1,0:T(8,128)(2,1)}, bf16[64,2048]{1,0:T(8,128)(2,1)}, u32[]{:S(2)}, u32[]{:S(2)}) collective-permute-start(bf16[64,2048]{1,0:T(8,128)(2,1)} %collective-permute-done.1.refs_1_), channel_id=1, source_target_pairs={{0,2},{1,3},{2,0},{3,1},{4,6},{5,7},{6,4},{7,5},{8,10},{9,11},{10,... | collective-permute-start | bytes 786440 | tf_op jit(solution)/shard_map/ppermute | solution.py:31
  32.0 3.9 %collective-permute-start.13 = (bf16[64,2048]{1,0:T(8,128)(2,1)}, bf16[64,2048]{1,0:T(8,128)(2,1)}, u32[]{:S(2)}, u32[]{:S(2)}) collective-permute-start(bf16[64,2048]{1,0:T(8,128)(2,1)} %get-tuple-element.122.refs_0_), channel_id=1, source_target_pairs={{0,4},{1,5},{2,6},{3,7},{4,0},{5,1},{6,2},{7,3},{8,12},{9,13},{10,... | collective-permute-start | bytes 786440 | tf_op jit(solution)/shard_map/ppermute | solution.py:31
  36.0 2.1 collect.1
  38.1 6.9 %collective-permute-done.10.refs_3_ = bf16[64,2048]{1,0:T(8,128)(2,1)} collective-permute-done((bf16[64,2048]{1,0:T(8,128)(2,1)}, bf16[64,2048]{1,0:T(8,128)(2,1)}, u32[]{:S(2)}, u32[]{:S(2)}) %collective-permute-start.10) | collective-permute-done | bytes 262176 | tf_op jit(solution)/shard_map/ppermute | solution.py:31
  47.2 1.6 collective-permute-start.12
  48.7 1.5 collective-permute-start.11
  50.4 3.7 %collective-permute-start.15 = (bf16[64,2048]{1,0:T(8,128)(2,1)}, bf16[64,2048]{1,0:T(8,128)(2,1)S(1)}, u32[]{:S(2)}, u32[]{:S(2)}) collective-permute-start(bf16[64,2048]{1,0:T(8,128)(2,1)} %collective-permute-done.13.refs_1_), channel_id=1, source_target_pairs={{0,2},{1,3},{2,0},{3,1},{4,6},{5,7},{6,4},{7,5},{8,10},{9,11},{10,... | collective-permute-start | bytes 786440 | tf_op jit(solution)/shard_map/ppermute | solution.py:31
  54.1 1.6 copy-done.1
  55.7 7.3 %heads_backward.7 = (bf16[128,8192]{1,0:T(8,128)(2,1)}, bf16[128,4096]{1,0:T(8,128)(2,1)}, bf16[128,6144]{1,0:T(8,128)(2,1)}, f32[128,1024]{1,0:T(8,128)S(1)}, f...) custom-call(s32[6]{0:T(128)S(1)} %copy-done.9, bf16[128,8192]{1,0:T(8,128)(2,1)S(1)} %bitcast.18, ...), custom_call_target="tpu_custom_call" | custom-call | flops 3000000000 | bytes 600000 | tf_op jit(solution)/shard_map/heads_backward/pallas_call | solution.py:158
  64.0 7.3 %heads_backward.8 = (bf16[128,8192]{1,0:T(8,128)(2,1)}, bf16[128,4096]{1,0:T(8,128)(2,1)}, bf16[128,6144]{1,0:T(8,128)(2,1)}, f32[128,1024]{1,0:T(8,128)S(1)}, f...) custom-call(s32[6]{0:T(128)S(1)} %copy-done.9, ...), custom_call_target="tpu_custom_call", output_to_operand_aliasing={{0}: (14, {}), {1}: (15, {}), {2}: (16, {})} | custom-call | flops 3000000000 | bytes 600000 | tf_op jit(solution)/shard_map/heads_backward/pallas_call | solution.py:158
  71.3 1.5 collective-permute-start.16
  72.8 1.5 collective-permute-start.17
  74.3 7.3 %heads_backward.9 = (bf16[128,8192]{1,0:T(8,128)(2,1)}, bf16[128,4096]{1,0:T(8,128)(2,1)}, bf16[128,6144]{1,0:T(8,128)(2,1)}, f32[128,1024]{1,0:T(8,128)S(1)}, f...) custom-call(s32[6]{0:T(128)S(1)} %copy-done.9, ...), custom_call_target="tpu_custom_call", output_to_operand_aliasing={{0}: (14, {}), {1}: (15, {}), {2}: (16, {})} | custom-call | flops 3000000000 | bytes 600000 | tf_op jit(solution)/shard_map/heads_backward/pallas_call | solution.py:158
  82.7 12.8 %heads_backward.10 = (bf16[128,8192]{1,0:T(8,128)(2,1)}, bf16[128,4096]{1,0:T(8,128)(2,1)}, bf16[128,6144]{1,0:T(8,128)(2,1)}, f32[128,2048]{1,0:T(8,128)S(1)}, ...) custom-call(s32[6]{0:T(128)S(1)} %copy-done.9, ...), custom_call_target="tpu_custom_call", output_to_operand_aliasing={{0}: (14, {}), {1}: (15, {}), {2}: (16, {})} | custom-call | flops 6000000000 | bytes 1200000 | tf_op jit(solution)/shard_map/heads_backward/pallas_call | solution.py:158
  95.5 7.5 %heads_backward.11 = (bf16[128,8192]{1,0:T(8,128)(2,1)}, bf16[128,4096]{1,0:T(8,128)(2,1)}, bf16[128,6144]{1,0:T(8,128)(2,1)}, f32[128,1024]{1,0:T(8,128)S(1)}, ...) custom-call(s32[6]{0:T(128)S(1)} %copy-done.9, ...), custom_call_target="tpu_custom_call", output_to_operand_aliasing={{0}: (14, {}), {1}: (15, {}), {2}: (16, {})} | custom-call | flops 3000000000 | bytes 600000 | tf_op jit(solution)/shard_map/heads_backward/pallas_call | solution.py:158
  102.9 1.5 collective-permute-start.21
  104.5 1.5 collective-permute-start.20
  105.9 7.3 %heads_backward.12 = (bf16[128,8192]{1,0:T(8,128)(2,1)}, bf16[128,4096]{1,0:T(8,128)(2,1)}, bf16[128,6144]{1,0:T(8,128)(2,1)}, f32[128,1024]{1,0:T(8,128)S(1)}, ...) custom-call(s32[6]{0:T(128)S(1)} %copy-done.9, ...), custom_call_target="tpu_custom_call", output_to_operand_aliasing={{0}: (14, {}), {1}: (15, {}), {2}: (16, {})} | custom-call | flops 3000000000 | bytes 600000 | tf_op jit(solution)/shard_map/heads_backward/pallas_call | solution.py:158
  113.2 1.8 collective-permute-done.21
  115.0 1.5 collective-permute-start.22
  116.7 1.6 collective-permute-start.25
  118.3 7.9 %collective-permute-done.22 = f32[128,1024]{1,0:T(8,128)S(1)} collective-permute-done((f32[128,1024]{1,0:T(8,128)S(1)}, f32[128,1024]{1,0:T(8,128)S(1)}, u32[]{:S(2)}, u32[]{:S(2)}) %collective-permute-start.22) | collective-permute-done | bytes 524320 | tf_op jit(solution)/shard_map/ppermute | solution.py:31
  126.2 4.3 %collective-permute-done.20 = f32[128,2048]{1,0:T(8,128)S(1)} collective-permute-done((f32[128,2048]{1,0:T(8,128)S(1)}, f32[128,2048]{1,0:T(8,128)S(1)}, u32[]{:S(2)}, u32[]{:S(2)}) %collective-permute-start.20) | collective-permute-done | bytes 1048608 | tf_op jit(solution)/shard_map/ppermute | solution.py:31
  131.1 1.5 collective-permute-start.29
  132.5 9.2 %collective-permute-done.25 = f32[128,1024]{1,0:T(8,128)S(1)} collective-permute-done((f32[128,1024]{1,0:T(8,128)S(1)}, f32[128,1024]{1,0:T(8,128)S(1)}, u32[]{:S(2)}, u32[]{:S(2)}) %collective-permute-start.25) | collective-permute-done | bytes 524320 | tf_op jit(solution)/shard_map/ppermute | solution.py:31
  142.6 7.3 %heads_backward.13 = (bf16[128,8192]{1,0:T(8,128)(2,1)}, bf16[128,4096]{1,0:T(8,128)(2,1)}, bf16[128,6144]{1,0:T(8,128)(2,1)}, f32[128,1024]{1,0:T(8,128)S(1)}, ...) custom-call(s32[6]{0:T(128)S(1)} %copy-done.9, ...), custom_call_target="tpu_custom_call", output_to_operand_aliasing={{0}: (14, {}), {1}: (15, {}), {2}: (16, {})} | custom-call | flops 3000000000 | bytes 600000 | tf_op jit(solution)/shard_map/heads_backward/pallas_call | solution.py:158
  152.3 2.0 collective-permute-start.30
  155.5 1.6 spread.1
  158.2 12.5 %collective-permute-done.34 = f32[64,1024]{1,0:T(8,128)} collective-permute-done((f32[64,1024]{1,0:T(8,128)}, f32[64,1024]{1,0:T(8,128)}, u32[]{:S(2)}, u32[]{:S(2)}) %collective-permute-start.34) | collective-permute-done | bytes 262176 | tf_op jit(solution)/shard_map/ppermute | solution.py:31
  171.8 1.5 add_add_fusion.1
  174.1 3.4 %collective-permute-start.31 = (f32[64,1024]{1,0:T(8,128)}, f32[64,1024]{1,0:T(8,128)}, u32[]{:S(2)}, u32[]{:S(2)}) collective-permute-start(f32[64,1024]{1,0:T(8,128)} %slice.49), channel_id=1, source_target_pairs={{0,4},{1,5},{2,6},{3,7},{4,0},{5,1},{6,2},{7,3},{8,12},{9,13},{10,... | collective-permute-start | bytes 786440 | tf_op jit(solution)/shard_map/ppermute | solution.py:31
  177.6 1.3 copy.41
  179.7 2.5 %collective-permute-start.38 = (f32[32,2048]{1,0:T(8,128)S(1)}, f32[32,2048]{1,0:T(8,128)S(1)}, u32[]{:S(2)}, u32[]{:S(2)}) collective-permute-start(f32[32,2048]{1,0:T(8,128)S(1)} %join_cores.2.refs_0_), channel_id=1, source_target_pairs={{0,24},{8,16},{16,8},{24,0},{1,25},{9,17},{17,9},{25,1},{2,26},{10... | collective-permute-start | bytes 786440 | tf_op jit(solution)/shard_map/ppermute | solution.py:31
  183.2 4.9 %collective-permute-done.31 = f32[64,1024]{1,0:T(8,128)} collective-permute-done((f32[64,1024]{1,0:T(8,128)}, f32[64,1024]{1,0:T(8,128)}, u32[]{:S(2)}, u32[]{:S(2)}) %collective-permute-start.31) | collective-permute-done | bytes 262176 | tf_op jit(solution)/shard_map/ppermute | solution.py:31
  191.9 3.0 %collective-permute-done.37.refs_2_ = f32[32,2048]{1,0:T(8,128)S(1)} collective-permute-done((f32[32,2048]{1,0:T(8,128)S(1)}, f32[32,2048]{1,0:T(8,128)S(1)}, u32[]{:S(2)}, u32[]{:S(2)}) %collective-permute-start.37) | collective-permute-done | bytes 262176 | tf_op jit(solution)/shard_map/ppermute | solution.py:31
  195.6 1.8 collective-permute-start.42
  199.2 2.4 %place_columns.1 = (bf16[128,8192]{1,0:T(8,128)(2,1)}, bf16[128,4096]{1,0:T(8,128)(2,1)}) custom-call(s32[6]{0:T(128)S(1)} %copy-done.9, bf16[128,6144]{1,0:T(8,128)(2,1)S(1)} %collective-permute-done.23.received, bf16[128,8192]{1,0:T(8,128)(2,1)} %get-tuple-element.157.q_in, ...), custom_call_target="tpu_custom_call", output_to_operand_aliasing={{0}: (2, {}), {1}: (3, {})} | custom-call | bytes 4000000 | tf_op jit(solution)/shard_map/place_columns/pallas_call | solution.py:187
  201.6 3.4 %lay_out.2.refs_4_ = f32[32,16384]{1,0:T(8,128)} custom-call(s32[6]{0:T(128)S(1)} %copy-done.9, f32[32,2048]{1,0:T(8,128)S(1)} %join_cores.2.refs_0_, f32[32,2048]{1,0:T(8,128)S(1)} %collective-permute-done.36.refs_1_, f32[32,2048]{1,0:T(8,128)S(1)} %collective-permute-done.37.refs_2_, f32[32,2048]{1,0:T(8,128)S(1)} %collective-permute-done.38.refs_3_), custom_call_target="tpu_custom_call" | custom-call | bytes 2000000 | tf_op jit(solution)/shard_map/lay_out/pallas_call | solution.py:299
  205.8 4.6 %collective-permute-done.41.refs_2_ = f32[32,2048]{1,0:T(8,128)S(1)} collective-permute-done((f32[32,2048]{1,0:T(8,128)S(1)}, f32[32,2048]{1,0:T(8,128)S(1)}, u32[]{:S(2)}, u32[]{:S(2)}) %collective-permute-start.41) | collective-permute-done | bytes 262176 | tf_op jit(solution)/shard_map/ppermute | solution.py:31
  210.5 3.4 %lay_out.3 = f32[32,16384]{1,0:T(8,128)} custom-call(s32[6]{0:T(128)S(1)} %copy-done.9, f32[32,2048]{1,0:T(8,128)S(1)} %join_cores.3.refs_0_, f32[32,2048]{1,0:T(8,128)S(1)} %collective-permute-done.40.refs_1_, f32[32,2048]{1,0:T(8,128)S(1)} %collective-permute-done.41.refs_2_, ...), custom_call_target="tpu_custom_call", output_to_operand_aliasing={{}: (5, {})} | custom-call | bytes 2000000 | tf_op jit(solution)/shard_map/lay_out/pallas_call | solution.py:299
  (119 shorter events, 24.0 us)
Async XLA Ops:
  0.6 3.0 %collective-permute-start = (bf16[32,16384]{1,0:T(8,128)(2,1)}, bf16[32,16384]{1,0:T(8,128)(2,1)S(1)}, u32[]{:S(2)}, u32[]{:S(2)}) collective-permute-start(bf16[32,16384]{1,0:T(8,128)(2,1)} %distant.1), channel_id=1, source_target_pairs={{0,1},{1,0},{2,3},{3,2},{4,5},{5,4},{6,7},{7,6},{8,9},{9,8},{10,11... | collective-permute-start | bytes 3145736 | tf_op jit(solution)/shard_map/ppermute | solution.py:31
  3.6 9.4 %collective-permute-start.2 = (bf16[128,8192]{1,0:T(8,128)(2,1)}, bf16[128,8192]{1,0:T(8,128)(2,1)}, u32[]{:S(2)}, u32[]{:S(2)}) collective-permute-start(bf16[128,8192]{1,0:T(8,128)(2,1)} %bitcast.17), channel_id=1, source_target_pairs={{0,1},{1,0},{2,3},{3,2},{4,5},{5,4},{6,7},{7,6},{8,9},{9,8},{10,11... | collective-permute-start | bytes 6291464 | tf_op jit(solution)/shard_map/ppermute | solution.py:31
  4.0 9.0 %collective-permute-start.4 = (bf16[128,8192]{1,0:T(8,128)(2,1)}, bf16[128,8192]{1,0:T(8,128)(2,1)}, u32[]{:S(2)}, u32[]{:S(2)}) collective-permute-start(bf16[128,8192]{1,0:T(8,128)(2,1)} %bitcast.25), channel_id=1, source_target_pairs={{0,1},{1,0},{2,3},{3,2},{4,5},{5,4},{6,7},{7,6},{8,9},{9,8},{10,11... | collective-permute-start | bytes 6291464 | tf_op jit(solution)/shard_map/ppermute | solution.py:31
  4.2 31.7 %copy-start.4 = (f32[1,64,128]{2,1,0:T(8,128)S(1)}, f32[1,64,128]{2,1,0:T(8,128)}, u32[]{:S(2)}) copy-start(f32[1,64,128]{2,1,0:T(8,128)} %param.11) | copy-start | bytes 98308
  4.2 31.8 %copy-start.17 = (s32[1,8,4]{1,2,0:T(4,128)S(1)}, s32[1,8,4]{1,2,0:T(4,128)}, u32[]{:S(2)}) copy-start(s32[1,8,4]{1,2,0:T(4,128)} %param.15) | copy-start | bytes 388
  4.2 31.8 %copy-start.9 = (s32[6]{0:T(128)S(1)}, s32[6]{0:T(128)}, u32[]{:S(2)}) copy-start(s32[6]{0:T(128)} %stack.30.place) | copy-start | bytes 76
  4.2 8.8 %collective-permute-start.3 = (bf16[128,4096]{1,0:T(8,128)(2,1)}, bf16[128,4096]{1,0:T(8,128)(2,1)}, u32[]{:S(2)}, u32[]{:S(2)}) collective-permute-start(bf16[128,4096]{1,0:T(8,128)(2,1)} %bitcast.33), channel_id=1, source_target_pairs={{0,1},{1,0},{2,3},{3,2},{4,5},{5,4},{6,7},{7,6},{8,9},{9,8},{10,11... | collective-permute-start | bytes 3145736 | tf_op jit(solution)/shard_map/ppermute | solution.py:31
  7.2 46.9 %copy-start = (bf16[1,128,8192]{2,1,0:T(8,128)(2,1)S(1)}, bf16[1,128,8192]{2,1,0:T(8,128)(2,1)}, u32[]{:S(2)}) copy-start(bf16[1,128,8192]{2,1,0:T(8,128)(2,1)} %param.8) | copy-start | bytes 6291460
  7.2 46.9 %copy-start.3 = (bf16[1,128,4096]{2,1,0:T(8,128)(2,1)S(1)}, bf16[1,128,4096]{2,1,0:T(8,128)(2,1)}, u32[]{:S(2)}) copy-start(bf16[1,128,4096]{2,1,0:T(8,128)(2,1)} %param.9) | copy-start | bytes 3145732
  7.2 19.5 %collective-permute-start.9 = (bf16[64,2048]{1,0:T(8,128)(2,1)}, bf16[64,2048]{1,0:T(8,128)(2,1)}, u32[]{:S(2)}, u32[]{:S(2)}) collective-permute-start(bf16[64,2048]{1,0:T(8,128)(2,1)} %get-tuple-element.113.refs_0_), channel_id=1, source_target_pairs={{0,2},{1,3},{2,0},{3,1},{4,6},{5,7},{6,4},{7,5},{8,10},{9,11},{10,... | collective-permute-start | bytes 786440 | tf_op jit(solution)/shard_map/ppermute | solution.py:31
  10.2 16.6 %collective-permute-start.1 = (bf16[64,2048]{1,0:T(8,128)(2,1)}, bf16[64,2048]{1,0:T(8,128)(2,1)}, u32[]{:S(2)}, u32[]{:S(2)}) collective-permute-start(bf16[64,2048]{1,0:T(8,128)(2,1)} %get-tuple-element.113.refs_0_), channel_id=1, source_target_pairs={{0,4},{1,5},{2,6},{3,7},{4,0},{5,1},{6,2},{7,3},{8,12},{9,13},{10,... | collective-permute-start | bytes 786440 | tf_op jit(solution)/shard_map/ppermute | solution.py:31
  13.0 12.0 %collective-permute-start.7 = (bf16[144,320]{1,0:T(8,128)(2,1)S(1)}, bf16[144,320]{1,0:T(8,128)(2,1)S(1)}, u32[]{:S(2)}, u32[]{:S(2)}) collective-permute-start(bf16[144,320]{1,0:T(8,128)(2,1)S(1)} %fusion.3.refs_0_), channel_id=1, source_target_pairs={{0,4},{1,5},{2,6},{3,7},{8,12},{9,13},{10,14},{11,15},{16,20},{17,... | collective-permute-start | bytes 276488 | tf_op jit(solution)/shard_map/ppermute | solution.py:26
  18.5 8.1 %collective-permute-start.6 = (bf16[144,320]{1,0:T(8,128)(2,1)S(1)}, bf16[144,320]{1,0:T(8,128)(2,1)S(1)}, u32[]{:S(2)}, u32[]{:S(2)}) collective-permute-start(bf16[144,320]{1,0:T(8,128)(2,1)S(1)} %fusion.3.refs_0_), channel_id=1, source_target_pairs={{0,2},{1,3},{2,4},{3,5},{4,6},{5,7},{8,10},{9,11},{10,12},{11,13},... | collective-permute-start | bytes 276488 | tf_op jit(solution)/shard_map/ppermute | solution.py:26
  26.7 9.3 %collective-permute-start.8 = (bf16[432,320]{1,0:T(8,128)(2,1)S(1)}, bf16[432,320]{1,0:T(8,128)(2,1)}, u32[]{:S(2)}, u32[]{:S(2)}) collective-permute-start(bf16[432,320]{1,0:T(8,128)(2,1)S(1)} %stack.31.own), channel_id=1, source_target_pairs={{0,1},{1,0},{2,3},{3,2},{4,5},{5,4},{6,7},{7,6},{8,9},{9,8},{10,11... | collective-permute-start | bytes 829448 | tf_op jit(solution)/shard_map/ppermute | solution.py:31
  26.8 18.3 %collective-permute-start.10 = (bf16[64,2048]{1,0:T(8,128)(2,1)}, bf16[64,2048]{1,0:T(8,128)(2,1)}, u32[]{:S(2)}, u32[]{:S(2)}) collective-permute-start(bf16[64,2048]{1,0:T(8,128)(2,1)} %collective-permute-done.1.refs_1_), channel_id=1, source_target_pairs={{0,2},{1,3},{2,0},{3,1},{4,6},{5,7},{6,4},{7,5},{8,10},{9,11},{10,... | collective-permute-start | bytes 786440 | tf_op jit(solution)/shard_map/ppermute | solution.py:31
  32.0 18.4 %collective-permute-start.14 = (bf16[64,2048]{1,0:T(8,128)(2,1)}, bf16[64,2048]{1,0:T(8,128)(2,1)}, u32[]{:S(2)}, u32[]{:S(2)}) collective-permute-start(bf16[64,2048]{1,0:T(8,128)(2,1)} %get-tuple-element.122.refs_0_), channel_id=1, source_target_pairs={{0,2},{1,3},{2,0},{3,1},{4,6},{5,7},{6,4},{7,5},{8,10},{9,11},{10,... | collective-permute-start | bytes 786440 | tf_op jit(solution)/shard_map/ppermute | solution.py:31
  32.0 18.4 %collective-permute-start.13 = (bf16[64,2048]{1,0:T(8,128)(2,1)}, bf16[64,2048]{1,0:T(8,128)(2,1)}, u32[]{:S(2)}, u32[]{:S(2)}) collective-permute-start(bf16[64,2048]{1,0:T(8,128)(2,1)} %get-tuple-element.122.refs_0_), channel_id=1, source_target_pairs={{0,4},{1,5},{2,6},{3,7},{4,0},{5,1},{6,2},{7,3},{8,12},{9,13},{10,... | collective-permute-start | bytes 786440 | tf_op jit(solution)/shard_map/ppermute | solution.py:31
  35.9 2.2 %collective-permute-start.5 = (f32[64,128]{1,0:T(8,128)S(1)}, f32[64,128]{1,0:T(8,128)S(1)}, u32[]{:S(2)}, u32[]{:S(2)}) collective-permute-start(f32[64,128]{1,0:T(8,128)S(1)} %bitcast.41), channel_id=1, source_target_pairs={{0,1},{1,0},{2,3},{3,2},{4,5},{5,4},{6,7},{7,6},{8,9},{9,8},{10,11... | collective-permute-start | bytes 98312 | tf_op jit(solution)/shard_map/ppermute | solution.py:31
  47.2 35.0 %collective-permute-start.12 = (bf16[256,2048]{1,0:T(8,128)(2,1)S(1)}, bf16[256,2048]{1,0:T(8,128)(2,1)S(1)}, u32[]{:S(2)}, u32[]{:S(2)}) collective-permute-start(bf16[256,2048]{1,0:T(8,128)(2,1)S(1)} %stack.32.weight), channel_id=1, source_target_pairs={{0,8},{8,0},{16,24},{24,16},{1,9},{9,1},{17,25},{25,17},{2,10},{10... | collective-permute-start | bytes 3145736 | tf_op jit(solution)/shard_map/ppermute | solution.py:31
  48.7 33.9 %collective-permute-start.11 = (bf16[256,2048]{1,0:T(8,128)(2,1)S(1)}, bf16[256,2048]{1,0:T(8,128)(2,1)S(1)}, u32[]{:S(2)}, u32[]{:S(2)}) collective-permute-start(bf16[256,2048]{1,0:T(8,128)(2,1)S(1)} %stack.32.weight), channel_id=1, source_target_pairs={{0,16},{8,24},{16,0},{24,8},{1,17},{9,25},{17,1},{25,9},{2,18},{10... | collective-permute-start | bytes 3145736 | tf_op jit(solution)/shard_map/ppermute | solution.py:31
  50.4 12.5 %collective-permute-start.15 = (bf16[64,2048]{1,0:T(8,128)(2,1)}, bf16[64,2048]{1,0:T(8,128)(2,1)S(1)}, u32[]{:S(2)}, u32[]{:S(2)}) collective-permute-start(bf16[64,2048]{1,0:T(8,128)(2,1)} %collective-permute-done.13.refs_1_), channel_id=1, source_target_pairs={{0,2},{1,3},{2,0},{3,1},{4,6},{5,7},{6,4},{7,5},{8,10},{9,11},{10,... | collective-permute-start | bytes 786440 | tf_op jit(solution)/shard_map/ppermute | solution.py:31
  71.3 24.1 %collective-permute-start.16 = (f32[128,1024]{1,0:T(8,128)S(1)}, f32[128,1024]{1,0:T(8,128)S(1)}, u32[]{:S(2)}, u32[]{:S(2)}) collective-permute-start(f32[128,1024]{1,0:T(8,128)S(1)} %get-tuple-element.134), channel_id=1, source_target_pairs={{0,8},{8,0},{16,24},{24,16},{1,9},{9,1},{17,25},{25,17},{2,10},{10... | collective-permute-start | bytes 1572872 | tf_op jit(solution)/shard_map/ppermute | solution.py:31
  72.8 22.6 %collective-permute-start.17 = (f32[128,1024]{1,0:T(8,128)S(1)}, f32[128,1024]{1,0:T(8,128)S(1)}, u32[]{:S(2)}, u32[]{:S(2)}) collective-permute-start(f32[128,1024]{1,0:T(8,128)S(1)} %get-tuple-element.135), channel_id=1, source_target_pairs={{0,16},{8,24},{16,0},{24,8},{1,17},{9,25},{17,1},{25,9},{2,18},{10... | collective-permute-start | bytes 1572872 | tf_op jit(solution)/shard_map/ppermute | solution.py:31
  81.6 24.3 %collective-permute-start.18 = (f32[128,1024]{1,0:T(8,128)S(1)}, f32[128,1024]{1,0:T(8,128)S(1)}, u32[]{:S(2)}, u32[]{:S(2)}) collective-permute-start(f32[128,1024]{1,0:T(8,128)S(1)} %get-tuple-element.141), channel_id=1, source_target_pairs={{0,8},{8,0},{16,24},{24,16},{1,9},{9,1},{17,25},{25,17},{2,10},{10... | collective-permute-start | bytes 1572872 | tf_op jit(solution)/shard_map/ppermute | solution.py:31
  82.2 23.8 %collective-permute-start.19 = (f32[128,1024]{1,0:T(8,128)S(1)}, f32[128,1024]{1,0:T(8,128)S(1)}, u32[]{:S(2)}, u32[]{:S(2)}) collective-permute-start(f32[128,1024]{1,0:T(8,128)S(1)} %get-tuple-element.142), channel_id=1, source_target_pairs={{0,16},{8,24},{16,0},{24,8},{1,17},{9,25},{17,1},{25,9},{2,18},{10... | collective-permute-start | bytes 1572872 | tf_op jit(solution)/shard_map/ppermute | solution.py:31
  102.9 12.1 %collective-permute-start.21 = (f32[128,1024]{1,0:T(8,128)S(1)}, f32[128,1024]{1,0:T(8,128)S(1)}, u32[]{:S(2)}, u32[]{:S(2)}) collective-permute-start(f32[128,1024]{1,0:T(8,128)S(1)} %get-tuple-element.149), channel_id=1, source_target_pairs={{0,16},{8,24},{16,0},{24,8},{1,17},{9,25},{17,1},{25,9},{2,18},{10... | collective-permute-start | bytes 1572872 | tf_op jit(solution)/shard_map/ppermute | solution.py:31
  104.5 26.1 %collective-permute-start.20 = (f32[128,2048]{1,0:T(8,128)S(1)}, f32[128,2048]{1,0:T(8,128)S(1)}, u32[]{:S(2)}, u32[]{:S(2)}) collective-permute-start(f32[128,2048]{1,0:T(8,128)S(1)} %get-tuple-element.148), channel_id=1, source_target_pairs={{0,8},{8,0},{16,24},{24,16},{1,9},{9,1},{17,25},{25,17},{2,10},{10... | collective-permute-start | bytes 3145736 | tf_op jit(solution)/shard_map/ppermute | solution.py:31
  115.0 11.2 %collective-permute-start.22 = (f32[128,1024]{1,0:T(8,128)S(1)}, f32[128,1024]{1,0:T(8,128)S(1)}, u32[]{:S(2)}, u32[]{:S(2)}) collective-permute-start(f32[128,1024]{1,0:T(8,128)S(1)} %get-tuple-element.151), channel_id=1, source_target_pairs={{0,16},{8,24},{16,0},{24,8},{1,17},{9,25},{17,1},{25,9},{2,18},{10... | collective-permute-start | bytes 1572872 | tf_op jit(solution)/shard_map/ppermute | solution.py:31
  116.7 25.1 %collective-permute-start.25 = (f32[128,1024]{1,0:T(8,128)S(1)}, f32[128,1024]{1,0:T(8,128)S(1)}, u32[]{:S(2)}, u32[]{:S(2)}) collective-permute-start(f32[128,1024]{1,0:T(8,128)S(1)} %get-tuple-element.176), channel_id=1, source_target_pairs={{0,8},{8,0},{16,24},{24,16},{1,9},{9,1},{17,25},{25,17},{2,10},{10... | collective-permute-start | bytes 1572872 | tf_op jit(solution)/shard_map/ppermute | solution.py:31
  130.6 11.3 %collective-permute-start.26 = (f32[128,1024]{1,0:T(8,128)S(1)}, f32[128,1024]{1,0:T(8,128)S(1)}, u32[]{:S(2)}, u32[]{:S(2)}) collective-permute-start(f32[128,1024]{1,0:T(8,128)S(1)} %add.68), channel_id=1, source_target_pairs={{0,16},{8,24},{16,0},{24,8},{1,17},{9,25},{17,1},{25,9},{2,18},{10... | collective-permute-start | bytes 1572872 | tf_op jit(solution)/shard_map/ppermute | solution.py:31
  131.1 18.9 %collective-permute-start.29 = (f32[128,1024]{1,0:T(8,128)S(1)}, f32[128,1024]{1,0:T(8,128)S(1)}, u32[]{:S(2)}, u32[]{:S(2)}) collective-permute-start(f32[128,1024]{1,0:T(8,128)S(1)} %get-tuple-element.188), channel_id=1, source_target_pairs={{0,8},{8,0},{16,24},{24,16},{1,9},{9,1},{17,25},{25,17},{2,10},{10... | collective-permute-start | bytes 1572872 | tf_op jit(solution)/shard_map/ppermute | solution.py:31
  141.9 9.2 %collective-permute-start.27 = (f32[128,1024]{1,0:T(8,128)S(1)}, f32[128,1024]{1,0:T(8,128)S(1)}, u32[]{:S(2)}, u32[]{:S(2)}) collective-permute-start(f32[128,1024]{1,0:T(8,128)S(1)} %add_add_fusion.2), channel_id=1, source_target_pairs={{0,2},{1,3},{2,0},{3,1},{4,6},{5,7},{6,4},{7,5},{8,10},{9,11},{10,... | collective-permute-start | bytes 1572872 | tf_op jit(solution)/shard_map/ppermute | solution.py:31
  142.0 9.2 %collective-permute-start.28 = (f32[128,1024]{1,0:T(8,128)S(1)}, f32[128,1024]{1,0:T(8,128)S(1)}, u32[]{:S(2)}, u32[]{:S(2)}) collective-permute-start(f32[128,1024]{1,0:T(8,128)S(1)} %add.70), channel_id=1, source_target_pairs={{0,16},{8,24},{16,0},{24,8},{1,17},{9,25},{17,1},{25,9},{2,18},{10... | collective-permute-start | bytes 1572872 | tf_op jit(solution)/shard_map/ppermute | solution.py:31
  149.9 23.4 %collective-permute-start.23 = (bf16[128,6144]{1,0:T(8,128)(2,1)}, bf16[128,6144]{1,0:T(8,128)(2,1)S(1)}, u32[]{:S(2)}, u32[]{:S(2)}) collective-permute-start(bf16[128,6144]{1,0:T(8,128)(2,1)} %get-tuple-element.156), channel_id=1, source_target_pairs={{0,1},{1,0},{2,3},{3,2},{4,5},{5,4},{6,7},{7,6},{8,9},{9,8},{10,11... | collective-permute-start | bytes 4718600 | tf_op jit(solution)/shard_map/ppermute | solution.py:31
  152.3 19.5 %collective-permute-start.30 = (f32[128,1024]{1,0:T(8,128)}, f32[128,1024]{1,0:T(8,128)}, u32[]{:S(2)}, u32[]{:S(2)}) collective-permute-start(f32[128,1024]{1,0:T(8,128)} %add_add_fusion), channel_id=1, source_target_pairs={{0,2},{1,3},{2,0},{3,1},{4,6},{5,7},{6,4},{7,5},{8,10},{9,11},{10,... | collective-permute-start | bytes 1572872 | tf_op jit(solution)/shard_map/ppermute | solution.py:31
  155.2 15.5 %collective-permute-start.34 = (f32[64,1024]{1,0:T(8,128)}, f32[64,1024]{1,0:T(8,128)}, u32[]{:S(2)}, u32[]{:S(2)}) collective-permute-start(f32[64,1024]{1,0:T(8,128)} %slice.63), channel_id=1, source_target_pairs={{0,4},{1,5},{2,6},{3,7},{4,0},{5,1},{6,2},{7,3},{8,12},{9,13},{10,... | collective-permute-start | bytes 786440 | tf_op jit(solution)/shard_map/ppermute | solution.py:31
  158.2 15.1 %collective-permute-start.24 = (f32[432,320]{0,1:T(8,128)}, f32[432,320]{0,1:T(8,128)}, u32[]{:S(2)}, u32[]{:S(2)}) collective-permute-start(f32[432,320]{0,1:T(8,128)} %copy.40), channel_id=1, source_target_pairs={{0,1},{1,0},{2,3},{3,2},{4,5},{5,4},{6,7},{7,6},{8,9},{9,8},{10,11... | collective-permute-start | bytes 1658888 | tf_op jit(solution)/shard_map/ppermute | solution.py:31
  174.1 14.0 %collective-permute-start.31 = (f32[64,1024]{1,0:T(8,128)}, f32[64,1024]{1,0:T(8,128)}, u32[]{:S(2)}, u32[]{:S(2)}) collective-permute-start(f32[64,1024]{1,0:T(8,128)} %slice.49), channel_id=1, source_target_pairs={{0,4},{1,5},{2,6},{3,7},{4,0},{5,1},{6,2},{7,3},{8,12},{9,13},{10,... | collective-permute-start | bytes 786440 | tf_op jit(solution)/shard_map/ppermute | solution.py:31
  177.6 1.5 collective-permute-start.35
  179.7 12.2 %collective-permute-start.38 = (f32[32,2048]{1,0:T(8,128)S(1)}, f32[32,2048]{1,0:T(8,128)S(1)}, u32[]{:S(2)}, u32[]{:S(2)}) collective-permute-start(f32[32,2048]{1,0:T(8,128)S(1)} %join_cores.2.refs_0_), channel_id=1, source_target_pairs={{0,24},{8,16},{16,8},{24,0},{1,25},{9,17},{17,9},{25,1},{2,26},{10... | collective-permute-start | bytes 786440 | tf_op jit(solution)/shard_map/ppermute | solution.py:31
  182.2 12.8 %collective-permute-start.37 = (f32[32,2048]{1,0:T(8,128)S(1)}, f32[32,2048]{1,0:T(8,128)S(1)}, u32[]{:S(2)}, u32[]{:S(2)}) collective-permute-start(f32[32,2048]{1,0:T(8,128)S(1)} %join_cores.2.refs_0_), channel_id=1, source_target_pairs={{0,16},{8,24},{16,0},{24,8},{1,17},{9,25},{17,1},{25,9},{2,18},{10... | collective-permute-start | bytes 786440 | tf_op jit(solution)/shard_map/ppermute | solution.py:31
  182.7 12.4 %collective-permute-start.36 = (f32[32,2048]{1,0:T(8,128)S(1)}, f32[32,2048]{1,0:T(8,128)S(1)}, u32[]{:S(2)}, u32[]{:S(2)}) collective-permute-start(f32[32,2048]{1,0:T(8,128)S(1)} %join_cores.2.refs_0_), channel_id=1, source_target_pairs={{0,8},{8,0},{16,24},{24,16},{1,9},{9,1},{17,25},{25,17},{2,10},{10... | collective-permute-start | bytes 786440 | tf_op jit(solution)/shard_map/ppermute | solution.py:31
  189.2 15.8 %collective-permute-start.32 = (f32[128,320]{1,0:T(8,128)S(1)}, f32[128,320]{1,0:T(8,128)S(1)}, u32[]{:S(2)}, u32[]{:S(2)}) collective-permute-start(f32[128,320]{1,0:T(8,128)S(1)} %get-tuple-element.206), channel_id=1, source_target_pairs={{2,0},{3,1},{4,2},{5,3},{6,4},{7,5},{10,8},{11,9},{12,10},{13,11},... | collective-permute-start | bytes 491528 | tf_op jit(solution)/shard_map/ppermute | solution.py:26
  190.5 14.5 %collective-permute-start.33 = (f32[128,320]{1,0:T(8,128)S(1)}, f32[128,320]{1,0:T(8,128)S(1)}, u32[]{:S(2)}, u32[]{:S(2)}) collective-permute-start(f32[128,320]{1,0:T(8,128)S(1)} %get-tuple-element.207), channel_id=1, source_target_pairs={{4,0},{5,1},{6,2},{7,3},{12,8},{13,9},{14,10},{15,11},{20,16},{21,... | collective-permute-start | bytes 491528 | tf_op jit(solution)/shard_map/ppermute | solution.py:26
  191.8 3.2 %collective-permute-start.39 = (f32[32,1024]{1,0:T(8,128)S(1)}, f32[32,1024]{1,0:T(8,128)S(1)}, u32[]{:S(2)}, u32[]{:S(2)}) collective-permute-start(f32[32,1024]{1,0:T(8,128)S(1)} %get-tuple-element.208), channel_id=1, source_target_pairs={{0,1},{1,0},{2,3},{3,2},{4,5},{5,4},{6,7},{7,6},{8,9},{9,8},{10,11... | collective-permute-start | bytes 393224 | tf_op jit(solution)/shard_map/ppermute | solution.py:31
  195.6 10.2 %collective-permute-start.42 = (f32[32,2048]{1,0:T(8,128)S(1)}, f32[32,2048]{1,0:T(8,128)S(1)}, u32[]{:S(2)}, u32[]{:S(2)}) collective-permute-start(f32[32,2048]{1,0:T(8,128)S(1)} %join_cores.3.refs_0_), channel_id=1, source_target_pairs={{0,24},{8,16},{16,8},{24,0},{1,25},{9,17},{17,9},{25,1},{2,26},{10... | collective-permute-start | bytes 786440 | tf_op jit(solution)/shard_map/ppermute | solution.py:31
  197.4 12.9 %collective-permute-start.41 = (f32[32,2048]{1,0:T(8,128)S(1)}, f32[32,2048]{1,0:T(8,128)S(1)}, u32[]{:S(2)}, u32[]{:S(2)}) collective-permute-start(f32[32,2048]{1,0:T(8,128)S(1)} %join_cores.3.refs_0_), channel_id=1, source_target_pairs={{0,16},{8,24},{16,0},{24,8},{1,17},{9,25},{17,1},{25,9},{2,18},{10... | collective-permute-start | bytes 786440 | tf_op jit(solution)/shard_map/ppermute | solution.py:31
  198.7 11.8 %collective-permute-start.40 = (f32[32,2048]{1,0:T(8,128)S(1)}, f32[32,2048]{1,0:T(8,128)S(1)}, u32[]{:S(2)}, u32[]{:S(2)}) collective-permute-start(f32[32,2048]{1,0:T(8,128)S(1)} %join_cores.3.refs_0_), channel_id=1, source_target_pairs={{0,8},{8,0},{16,24},{24,16},{1,9},{9,1},{17,25},{25,17},{2,10},{10... | collective-permute-start | bytes 786440 | tf_op jit(solution)/shard_map/ppermute | solution.py:31
  (14 other events, 96.9 us)

commit v10 on v9

--- a/solution.py
+++ b/solution.py
@@ -164,7 +164,7 @@
         input_output_aliases=aliases,
         compiler_params=pltpu.CompilerParams(vmem_limit_bytes=KERNEL_BYTES),
         cost_estimate=pl.CostEstimate(
-            flops=count * 1_500_000_000, bytes_accessed=count * 300_000, transcendentals=0
+            flops=count * 100_000_000, bytes_accessed=count * 300_000, transcendentals=0
         ),
         name="heads_backward",
     )(place, *operands)
@@ -269,47 +269,43 @@
 
 
 def lay_kernel(place, *refs, count):
-    pieces, out = refs[:count], refs[-1]
-    width = out.shape[1]
-    for step, piece in enumerate(pieces):
+    pieces, out, sems = refs[:count], refs[count], refs[count + 1]
+    width = pieces[0].shape[1] // 2
+    copies = []
+    for index, piece in enumerate(pieces):
+        t, half = divmod(index, 2)
         for which in range(2):
-
-            @pl.when(pl.program_id(0) == 2 * step + which)
-            def _():
-                out[...] = piece[:, which * width : (which + 1) * width]
-
-
-def lay_out(place, pieces, half, earlier=None):
+            start = (place[1 + t] * 4 + which * 2 + half) * width
+            copies.append(
+                pltpu.make_async_copy(
+                    piece.at[:, pl.ds(which * width, width)],
+                    out.at[:, pl.ds(pl.multiple_of(start, width), width)],
+                    sems.at[2 * index + which],
+                )
+            )
+    for copy in copies:
+        copy.start()
+    for copy in copies:
+        copy.wait()
+
+
+def lay_out(place, pieces):
     rows, columns = pieces[0].shape
-    count, width = len(pieces), columns // 2
-    total = 2 * count * columns
-
-    def target(step, place):
-        chunk = place[1]
-        for t in range(1, count):
-            chunk = jnp.where((step >> 1) == t, place[1 + t], chunk)
-        return (0, chunk * 4 + (step & 1) * 2 + half)
-
-    in_specs = [pl.BlockSpec((rows, columns), lambda step, place: (0, 0))] * count
-    operands, aliases = list(pieces), {}
-    if earlier is not None:
-        in_specs.append(pl.BlockSpec(memory_space=pl.ANY))
-        operands.append(earlier)
-        aliases = {count + 1: 0}
+    count = len(pieces)
     return pl.pallas_call(
         functools.partial(lay_kernel, count=count),
         grid_spec=pltpu.PrefetchScalarGridSpec(
             num_scalar_prefetch=1,
-            grid=(2 * count,),
-            in_specs=in_specs,
-            out_specs=pl.BlockSpec((rows, width), target),
-        ),
-        out_shape=jax.ShapeDtypeStruct((rows, total), pieces[0].dtype),
-        input_output_aliases=aliases,
+            grid=(1,),
+            in_specs=[pl.BlockSpec(memory_space=pl.ANY)] * count,
+            out_specs=pl.BlockSpec(memory_space=pl.ANY),
+            scratch_shapes=[pltpu.SemaphoreType.DMA((2 * count,))],
+        ),
+        out_shape=jax.ShapeDtypeStruct((rows, count * columns), pieces[0].dtype),
         compiler_params=pltpu.CompilerParams(vmem_limit_bytes=KERNEL_BYTES),
-        cost_estimate=pl.CostEstimate(flops=0, bytes_accessed=2_000_000, transcendentals=0),
+        cost_estimate=pl.CostEstimate(flops=0, bytes_accessed=4_000_000, transcendentals=0),
         name="lay_out",
-    )(place, *operands)
+    )(place, *pieces)
 
 
 def piece_kernel(place, kept, crossed, out):
@@ -559,21 +555,19 @@
     orders = (bits, bits[::-1])
     first_sums = [{t: [] for t in range(n_dp) if t & order[0]} for order in orders]
     half_pairs = pairs // 2
-    halved = lambda t: [(t, 0, half_pairs), (t, half_pairs, half_pairs)]
-    units = [(0, 0, half_pairs), *halved(far)] + [(t, 0, pairs) for t in range(1, far - 1)]
-    units += [*halved(far - 1), (0, half_pairs, half_pairs)]
+    units = [(t, 0, pairs) for t in [far] + list(range(1, far - 1))]
+    units += [(t, start, half_pairs) for t in (far - 1, 0) for start in (0, half_pairs)]
     for t, start, count in units:
-        if t == far and not start:
-            weights[far] = joined([after(far_pieces[0], latents[-1])] + far_pieces[1:])
+        if t == far:
+            weights[far] = joined(far_pieces)
         weight = weights[t]
         if t == 0 and start:
             there = [piece for sent in first_sums for u in sent for piece in sent[u]]
             weight = after(weight, latents[-1], *there)
         if t == 1 and not start:
             weight = after(weight, *[weights[near] for near in range(2, far)])
-        if t == far - 1:
-            far_sums = [sent[far][1 if start else 0] for sent in first_sums]
-            weight = after(weight, latents[-1], *far_sums)
+        if t == far - 1 and start:
+            weight = after(weight, latents[-1], *[sent[far][0] for sent in first_sums])
         rest = chunk_backward(
             place,
             t,
@@ -589,10 +583,7 @@
         for side, sent in enumerate(first_sums):
             weight_grads[t][side].append(rest[3 + side])
             if t in sent:
-                leaving = rest[3 + side]
-                if t == far - 1 and start:
-                    leaving = after(leaving, sent[t][0])
-                sent[t].append(exchange(leaving, "dp", orders[side][0]))
+                sent[t].append(exchange(rest[3 + side], "dp", orders[side][0]))
         latents.append(rest[5])
         ropes.append(rest[6])
 
@@ -619,7 +610,7 @@
             for t in sorted((t for t in addends if t & bit), reverse=True):
                 leaving = [total(addends[t], half) for half in range(2)]
                 if side == 0:
-                    behind = [(first_sums[0][order[0]][0], last_sums[-1])] * 2
+                    behind = [(first_sums[0][order[0]][0], last_sums[-1], latents[-2])] * 2
                 else:
                     behind = [(weight_grads[far - 1][side][0],)] * 2
                 leaving = [after(half, *there) for half, there in zip(leaving, behind)]
@@ -657,9 +648,8 @@
     grad_rows = by_chip[0]
     for chips in (1, 2):
         grad_rows = grad_rows + from_behind(by_chip[chips], "ctx", -2 * chips)
-    grad_weight = lay_out(place, finished[0], 0)
-    finished[1][0] = after(finished[1][0], grad_rows, grad_nope)
-    grad_weight = lay_out(place, finished[1], 1, grad_weight)
+    finished[0][0] = after(finished[0][0], grad_rows, grad_nope)
+    grad_weight = lay_out(place, [piece for both in zip(*finished) for piece in both])
     return (grad_nope[None], grad_rope[None], grad_rows[None], grad_weight)
 
 

time: 215 us -> 217 us (level)
    ppermute x39 -> x37, waiting for transfers between devices: 58.9 us -> 55.8 us  [exchange(): lax.ppermute(value, axis, [(source, source ^ bits) for source in range(co...]
    pallas_call x2 -> x1, Pallas kernels: 6.75 us -> 9.75 us  [lay_out(): pl.pallas_call(functools.partial(lay_kernel, count=count), grid_spec=pltp...]
    ppermute x4, waiting for transfers between devices: 4.62 us -> 7.4 us  [from_behind(): lax.ppermute(value, axis, [(source, source + steps) for source in range(i...]
    pallas_call x7 -> x6, Pallas kernels: 56.6 us -> 55 us  [chunk_backward(): pl.pallas_call(functools.partial(heads_kernel, earlier=len(aliases)), gri...]
    unnamed x39 -> x43, local copies, waits for them, and re-layouts: 3.39 us -> 4.96 us
    ppermute x39 -> x37, starting transfers between devices: 48.7 us -> 47.6 us  [exchange(): lax.ppermute(value, axis, [(source, source ^ bits) for source in range(co...]
  transfers between devices with their start and end apart: 43 -> 41, of which waited for: 18 -> 17; matrix products, arithmetic and copies ran while one was open for 5% -> 5% of each run, Pallas kernels for 34% -> 31%
where the time goes in v10:
time: 217 us; the launch traced here: 216 us
  Pallas kernels  77 us (35%)
  waiting for transfers between devices  63.2 us (29%)
  starting transfers between devices  59.3 us (27%)
  local copies, waits for them, and re-layouts  9.94 us (5%)
  other arithmetic  5.3 us (2%)
    ppermute x37, waiting for transfers between devices, exchange(): lax.ppermute(value, axis, [(source, source ^ bits) for source in range(co...  55.8 us
    pallas_call x6, Pallas kernels, chunk_backward(): pl.pallas_call(functools.partial(heads_kernel, earlier=len(aliases)), gri...  55 us
    ppermute x37, starting transfers between devices, exchange(): lax.ppermute(value, axis, [(source, source ^ bits) for source in range(co...  47.6 us
    ppermute x4, starting transfers between devices, from_behind(): lax.ppermute(value, axis, [(source, source + steps) for source in range(i...  11.7 us
    pallas_call x1, Pallas kernels, lay_out(): pl.pallas_call(functools.partial(lay_kernel, count=count), grid_spec=pltp...  9.75 us
    ppermute x4, waiting for transfers between devices, from_behind(): lax.ppermute(value, axis, [(source, source + steps) for source in range(i...  7.4 us
    unnamed x43, local copies, waits for them, and re-layouts  4.96 us
  transfers between devices with their start and end apart: 41, of which 17 were waited for; matrix products, arithmetic and copies ran while one was open for 5% of the time, Pallas kernels for 31%

profile of v10, /device:TPU:0, one launch (start us, length us, event | category | flops | bytes accessed | tf_op | source)
XLA Modules:
  0.0 215.9 jit_solution(13095648027443800216)
XLA Ops:
  1.8 1.9 collective-permute-done.near_crossed.distant_crossed
  5.6 2.6 %weight_parts.1 = (bf16[64,2048]{1,0:T(8,128)(2,1)}, bf16[64,2048]{1,0:T(8,128)(2,1)}) custom-call(s32[6]{0:T(128)} %stack.30.place, bf16[32,16384]{1,0:T(8,128)(2,1)} %distant.1, bf16[32,16384]{1,0:T(8,128)(2,1)} %distant.1, bf16[32,16384]{1,0:T(8,128)(2,1)} %copy-done.11, bf16[32,16384]{1,0:T(8,128)(2,1)} %copy-done.11), custom_call_target="tpu_custom_call" | custom-call | bytes 1000000 | tf_op jit(solution)/shard_map/weight_parts/pallas_call | solution.py:256
  8.2 2.7 %collective-permute-start.9 = (bf16[64,2048]{1,0:T(8,128)(2,1)}, bf16[64,2048]{1,0:T(8,128)(2,1)}, u32[]{:S(2)}, u32[]{:S(2)}) collective-permute-start(bf16[64,2048]{1,0:T(8,128)(2,1)} %get-tuple-element.103.refs_0_), channel_id=1, source_target_pairs={{0,2},{1,3},{2,0},{3,1},{4,6},{5,7},{6,4},{7,5},{8,10},{9,11},{10,... | collective-permute-start | bytes 786440 | tf_op jit(solution)/shard_map/ppermute | solution.py:31
  10.9 2.6 %collective-permute-start.1 = (bf16[64,2048]{1,0:T(8,128)(2,1)}, bf16[64,2048]{1,0:T(8,128)(2,1)}, u32[]{:S(2)}, u32[]{:S(2)}) collective-permute-start(bf16[64,2048]{1,0:T(8,128)(2,1)} %get-tuple-element.103.refs_0_), channel_id=1, source_target_pairs={{0,4},{1,5},{2,6},{3,7},{4,0},{5,1},{6,2},{7,3},{8,12},{9,13},{10,... | collective-permute-start | bytes 786440 | tf_op jit(solution)/shard_map/ppermute | solution.py:31
  14.7 5.6 %collective-permute-start.7 = (bf16[144,320]{1,0:T(8,128)(2,1)S(1)}, bf16[144,320]{1,0:T(8,128)(2,1)S(1)}, u32[]{:S(2)}, u32[]{:S(2)}) collective-permute-start(bf16[144,320]{1,0:T(8,128)(2,1)S(1)} %fusion.3.refs_0_), channel_id=1, source_target_pairs={{0,4},{1,5},{2,6},{3,7},{8,12},{9,13},{10,14},{11,15},{16,20},{17,... | collective-permute-start | bytes 276488 | tf_op jit(solution)/shard_map/ppermute | solution.py:26
  20.3 3.5 %collective-permute-start.6 = (bf16[144,320]{1,0:T(8,128)(2,1)S(1)}, bf16[144,320]{1,0:T(8,128)(2,1)S(1)}, u32[]{:S(2)}, u32[]{:S(2)}) collective-permute-start(bf16[144,320]{1,0:T(8,128)(2,1)S(1)} %fusion.3.refs_0_), channel_id=1, source_target_pairs={{0,2},{1,3},{2,4},{3,5},{4,6},{5,7},{8,10},{9,11},{10,12},{11,13},... | collective-permute-start | bytes 276488 | tf_op jit(solution)/shard_map/ppermute | solution.py:26
  23.8 1.9 collective-permute-done.7.refs_2_
  25.8 1.8 collective-permute-done.6.refs_1_
  27.7 5.2 %collective-permute-start.10 = (bf16[64,2048]{1,0:T(8,128)(2,1)}, bf16[64,2048]{1,0:T(8,128)(2,1)}, u32[]{:S(2)}, u32[]{:S(2)}) collective-permute-start(bf16[64,2048]{1,0:T(8,128)(2,1)} %collective-permute-done.1.refs_1_), channel_id=1, source_target_pairs={{0,2},{1,3},{2,0},{3,1},{4,6},{5,7},{6,4},{7,5},{8,10},{9,11},{10,... | collective-permute-start | bytes 786440 | tf_op jit(solution)/shard_map/ppermute | solution.py:31
  33.0 3.9 %collective-permute-start.13 = (bf16[64,2048]{1,0:T(8,128)(2,1)}, bf16[64,2048]{1,0:T(8,128)(2,1)}, u32[]{:S(2)}, u32[]{:S(2)}) collective-permute-start(bf16[64,2048]{1,0:T(8,128)(2,1)} %get-tuple-element.110.refs_0_), channel_id=1, source_target_pairs={{0,4},{1,5},{2,6},{3,7},{4,0},{5,1},{6,2},{7,3},{8,12},{9,13},{10,... | collective-permute-start | bytes 786440 | tf_op jit(solution)/shard_map/ppermute | solution.py:31
  37.0 2.1 collect.1
  39.1 6.9 %collective-permute-done.10.refs_3_ = bf16[64,2048]{1,0:T(8,128)(2,1)} collective-permute-done((bf16[64,2048]{1,0:T(8,128)(2,1)}, bf16[64,2048]{1,0:T(8,128)(2,1)}, u32[]{:S(2)}, u32[]{:S(2)}) %collective-permute-start.10) | collective-permute-done | bytes 262176 | tf_op jit(solution)/shard_map/ppermute | solution.py:31
  48.1 1.6 collective-permute-start.12
  49.7 1.5 collective-permute-start.11
  51.4 3.7 %collective-permute-start.15 = (bf16[64,2048]{1,0:T(8,128)(2,1)}, bf16[64,2048]{1,0:T(8,128)(2,1)S(1)}, u32[]{:S(2)}, u32[]{:S(2)}) collective-permute-start(bf16[64,2048]{1,0:T(8,128)(2,1)} %collective-permute-done.13.refs_1_), channel_id=1, source_target_pairs={{0,2},{1,3},{2,0},{3,1},{4,6},{5,7},{6,4},{7,5},{8,10},{9,11},{10,... | collective-permute-start | bytes 786440 | tf_op jit(solution)/shard_map/ppermute | solution.py:31
  55.0 6.3 %collective-permute-done.15.refs_3_ = bf16[64,2048]{1,0:T(8,128)(2,1)S(1)} collective-permute-done((bf16[64,2048]{1,0:T(8,128)(2,1)}, bf16[64,2048]{1,0:T(8,128)(2,1)S(1)}, u32[]{:S(2)}, u32[]{:S(2)}) %collective-permute-start.15) | collective-permute-done | bytes 262176 | tf_op jit(solution)/shard_map/ppermute | solution.py:31
  63.7 13.0 %heads_backward.6 = (bf16[128,8192]{1,0:T(8,128)(2,1)}, bf16[128,4096]{1,0:T(8,128)(2,1)}, bf16[128,6144]{1,0:T(8,128)(2,1)}, f32[128,2048]{1,0:T(8,128)S(1)}, f...) custom-call(s32[6]{0:T(128)S(1)} %copy-done.10, bf16[128,8192]{1,0:T(8,128)(2,1)S(1)} %bitcast.18, ...), custom_call_target="tpu_custom_call" | custom-call | flops 400000000 | bytes 1200000 | tf_op jit(solution)/shard_map/heads_backward/pallas_call | solution.py:158
  76.7 1.5 collective-permute-start.16
  78.2 1.5 collective-permute-start.17
  79.7 12.8 %heads_backward.7 = (bf16[128,8192]{1,0:T(8,128)(2,1)}, bf16[128,4096]{1,0:T(8,128)(2,1)}, bf16[128,6144]{1,0:T(8,128)(2,1)}, f32[128,2048]{1,0:T(8,128)S(1)}, f...) custom-call(s32[6]{0:T(128)S(1)} %copy-done.10, ...), custom_call_target="tpu_custom_call", output_to_operand_aliasing={{0}: (14, {}), {1}: (15, {}), {2}: (16, {})} | custom-call | flops 400000000 | bytes 1200000 | tf_op jit(solution)/shard_map/heads_backward/pallas_call | solution.py:158
  93.1 7.2 %heads_backward.8 = (bf16[128,8192]{1,0:T(8,128)(2,1)}, bf16[128,4096]{1,0:T(8,128)(2,1)}, bf16[128,6144]{1,0:T(8,128)(2,1)}, f32[128,1024]{1,0:T(8,128)S(1)}, f...) custom-call(s32[6]{0:T(128)S(1)} %copy-done.10, ...), custom_call_target="tpu_custom_call", output_to_operand_aliasing={{0}: (14, {}), {1}: (15, {}), {2}: (16, {})} | custom-call | flops 200000000 | bytes 600000 | tf_op jit(solution)/shard_map/heads_backward/pallas_call | solution.py:158
  100.3 2.5 %collective-permute-done.16 = f32[128,2048]{1,0:T(8,128)S(1)} collective-permute-done((f32[128,2048]{1,0:T(8,128)S(1)}, f32[128,2048]{1,0:T(8,128)S(1)}, u32[]{:S(2)}, u32[]{:S(2)}) %collective-permute-start.16) | collective-permute-done | bytes 1048608 | tf_op jit(solution)/shard_map/ppermute | solution.py:31
  102.8 1.5 collective-permute-start.19
  104.3 7.3 %heads_backward.9 = (bf16[128,8192]{1,0:T(8,128)(2,1)}, bf16[128,4096]{1,0:T(8,128)(2,1)}, bf16[128,6144]{1,0:T(8,128)(2,1)}, f32[128,1024]{1,0:T(8,128)S(1)}, f...) custom-call(s32[6]{0:T(128)S(1)} %copy-done.10, ...), custom_call_target="tpu_custom_call", output_to_operand_aliasing={{0}: (14, {}), {1}: (15, {}), {2}: (16, {})} | custom-call | flops 200000000 | bytes 600000 | tf_op jit(solution)/shard_map/heads_backward/pallas_call | solution.py:158
  112.3 1.6 collective-permute-start.23
  113.8 7.5 %heads_backward.10 = (bf16[128,8192]{1,0:T(8,128)(2,1)}, bf16[128,4096]{1,0:T(8,128)(2,1)}, bf16[128,6144]{1,0:T(8,128)(2,1)}, f32[128,1024]{1,0:T(8,128)S(1)}, ...) custom-call(s32[6]{0:T(128)S(1)} %copy-done.10, ...), custom_call_target="tpu_custom_call", output_to_operand_aliasing={{0}: (14, {}), {1}: (15, {}), {2}: (16, {})} | custom-call | flops 200000000 | bytes 600000 | tf_op jit(solution)/shard_map/heads_backward/pallas_call | solution.py:158
  121.5 3.5 %collective-permute-done.20 = f32[128,1024]{1,0:T(8,128)S(1)} collective-permute-done((f32[128,1024]{1,0:T(8,128)S(1)}, f32[128,1024]{1,0:T(8,128)S(1)}, u32[]{:S(2)}, u32[]{:S(2)}) %collective-permute-start.20) | collective-permute-done | bytes 524320 | tf_op jit(solution)/shard_map/ppermute | solution.py:31
  125.3 2.1 collective-permute-start.24
  128.3 8.2 %collective-permute-done.23 = f32[128,1024]{1,0:T(8,128)S(1)} collective-permute-done((f32[128,1024]{1,0:T(8,128)S(1)}, f32[128,1024]{1,0:T(8,128)S(1)}, u32[]{:S(2)}, u32[]{:S(2)}) %collective-permute-start.23) | collective-permute-done | bytes 524320 | tf_op jit(solution)/shard_map/ppermute | solution.py:31
  136.6 1.8 collective-permute-start.25
  138.4 1.5 collective-permute-start.26
  140.0 7.3 %heads_backward.11 = (bf16[128,8192]{1,0:T(8,128)(2,1)}, bf16[128,4096]{1,0:T(8,128)(2,1)}, bf16[128,6144]{1,0:T(8,128)(2,1)}, f32[128,1024]{1,0:T(8,128)S(1)}, ...) custom-call(s32[6]{0:T(128)S(1)} %copy-done.10, ...), custom_call_target="tpu_custom_call", output_to_operand_aliasing={{0}: (14, {}), {1}: (15, {}), {2}: (16, {})} | custom-call | flops 200000000 | bytes 600000 | tf_op jit(solution)/shard_map/heads_backward/pallas_call | solution.py:158
  151.4 1.7 spread.1
  154.2 12.1 %collective-permute-done.32 = f32[64,1024]{1,0:T(8,128)} collective-permute-done((f32[64,1024]{1,0:T(8,128)}, f32[64,1024]{1,0:T(8,128)}, u32[]{:S(2)}, u32[]{:S(2)}) %collective-permute-start.32) | collective-permute-done | bytes 262176 | tf_op jit(solution)/shard_map/ppermute | solution.py:31
  168.5 1.6 add_add_fusion.1
  170.9 2.3 %collective-permute-start.29 = (f32[64,1024]{1,0:T(8,128)}, f32[64,1024]{1,0:T(8,128)}, u32[]{:S(2)}, u32[]{:S(2)}) collective-permute-start(f32[64,1024]{1,0:T(8,128)} %slice.65), channel_id=1, source_target_pairs={{0,4},{1,5},{2,6},{3,7},{4,0},{5,1},{6,2},{7,3},{8,12},{9,13},{10,... | collective-permute-start | bytes 786440 | tf_op jit(solution)/shard_map/ppermute | solution.py:31
  173.3 1.3 copy.37
  175.3 1.5 collective-permute-start.36
  176.8 1.5 collective-permute-start.35
  178.8 6.4 %collective-permute-done.29 = f32[64,1024]{1,0:T(8,128)} collective-permute-done((f32[64,1024]{1,0:T(8,128)}, f32[64,1024]{1,0:T(8,128)}, u32[]{:S(2)}, u32[]{:S(2)}) %collective-permute-start.29) | collective-permute-done | bytes 262176 | tf_op jit(solution)/shard_map/ppermute | solution.py:31
  186.2 1.3 collective-permute-start.30
  187.5 1.3 collective-permute-start.31
  188.9 1.6 collective-permute-done.35.refs_4_
  191.2 1.6 collective-permute-start.40
  194.7 2.4 %place_columns.1 = (bf16[128,8192]{1,0:T(8,128)(2,1)}, bf16[128,4096]{1,0:T(8,128)(2,1)}) custom-call(s32[6]{0:T(128)S(1)} %copy-done.10, bf16[128,6144]{1,0:T(8,128)(2,1)S(1)} %collective-permute-done.21.received, bf16[128,8192]{1,0:T(8,128)(2,1)} %get-tuple-element.137.q_in, ...), custom_call_target="tpu_custom_call", output_to_operand_aliasing={{0}: (2, {}), {1}: (3, {})} | custom-call | bytes 4000000 | tf_op jit(solution)/shard_map/place_columns/pallas_call | solution.py:187
  197.1 3.6 %collective-permute-done.31 = f32[128,320]{1,0:T(8,128)S(1)} collective-permute-done((f32[128,320]{1,0:T(8,128)S(1)}, f32[128,320]{1,0:T(8,128)S(1)}, u32[]{:S(2)}, u32[]{:S(2)}) %collective-permute-start.31) | collective-permute-done | bytes 163872 | tf_op jit(solution)/shard_map/ppermute | solution.py:26
  201.6 4.4 %collective-permute-done.39.refs_5_ = f32[32,2048]{1,0:T(8,128)S(1)} collective-permute-done((f32[32,2048]{1,0:T(8,128)S(1)}, f32[32,2048]{1,0:T(8,128)S(1)}, u32[]{:S(2)}, u32[]{:S(2)}) %collective-permute-start.39) | collective-permute-done | bytes 262176 | tf_op jit(solution)/shard_map/ppermute | solution.py:31
  206.0 9.8 %lay_out.1 = f32[32,16384]{1,0:T(8,128)} custom-call(s32[6]{0:T(128)S(1)} %copy-done.10, f32[32,2048]{1,0:T(8,128)S(1)} %join_cores.2.refs_0_, f32[32,2048]{1,0:T(8,128)S(1)} %join_cores.3.refs_1_, f32[32,2048]{1,0:T(8,128)S(1)} %collective-permute-done.34.refs_2_, f32[32,2048]{1,0:T(8,128)} %collective-permute-done.38.refs_3_, ...), custom_call_target="tpu_custom_call" | custom-call | bytes 4000000 | tf_op jit(solution)/shard_map/lay_out/pallas_call | solution.py:295
  (116 shorter events, 26.0 us)
Async XLA Ops:
  0.6 3.0 %collective-permute-start = (bf16[32,16384]{1,0:T(8,128)(2,1)}, bf16[32,16384]{1,0:T(8,128)(2,1)S(1)}, u32[]{:S(2)}, u32[]{:S(2)}) collective-permute-start(bf16[32,16384]{1,0:T(8,128)(2,1)} %distant.1), channel_id=1, source_target_pairs={{0,1},{1,0},{2,3},{3,2},{4,5},{5,4},{6,7},{7,6},{8,9},{9,8},{10,11... | collective-permute-start | bytes 3145736 | tf_op jit(solution)/shard_map/ppermute | solution.py:31
  4.6 10.1 %collective-permute-start.2 = (bf16[128,8192]{1,0:T(8,128)(2,1)}, bf16[128,8192]{1,0:T(8,128)(2,1)S(1)}, u32[]{:S(2)}, u32[]{:S(2)}) collective-permute-start(bf16[128,8192]{1,0:T(8,128)(2,1)} %bitcast.17), channel_id=1, source_target_pairs={{0,1},{1,0},{2,3},{3,2},{4,5},{5,4},{6,7},{7,6},{8,9},{9,8},{10,11... | collective-permute-start | bytes 6291464 | tf_op jit(solution)/shard_map/ppermute | solution.py:31
  5.0 9.7 %collective-permute-start.4 = (bf16[128,8192]{1,0:T(8,128)(2,1)}, bf16[128,8192]{1,0:T(8,128)(2,1)}, u32[]{:S(2)}, u32[]{:S(2)}) collective-permute-start(bf16[128,8192]{1,0:T(8,128)(2,1)} %bitcast.24), channel_id=1, source_target_pairs={{0,1},{1,0},{2,3},{3,2},{4,5},{5,4},{6,7},{7,6},{8,9},{9,8},{10,11... | collective-permute-start | bytes 6291464 | tf_op jit(solution)/shard_map/ppermute | solution.py:31
  5.1 31.7 %copy-start.5 = (f32[1,64,128]{2,1,0:T(8,128)S(1)}, f32[1,64,128]{2,1,0:T(8,128)}, u32[]{:S(2)}) copy-start(f32[1,64,128]{2,1,0:T(8,128)} %param.11) | copy-start | bytes 98308
  5.1 31.7 %copy-start.19 = (s32[1,8,4]{1,2,0:T(4,128)S(1)}, s32[1,8,4]{1,2,0:T(4,128)}, u32[]{:S(2)}) copy-start(s32[1,8,4]{1,2,0:T(4,128)} %param.15) | copy-start | bytes 388
  5.1 31.8 %copy-start.10 = (s32[6]{0:T(128)S(1)}, s32[6]{0:T(128)}, u32[]{:S(2)}) copy-start(s32[6]{0:T(128)} %stack.30.place) | copy-start | bytes 76
  5.1 8.6 %collective-permute-start.3 = (bf16[128,4096]{1,0:T(8,128)(2,1)}, bf16[128,4096]{1,0:T(8,128)(2,1)S(1)}, u32[]{:S(2)}, u32[]{:S(2)}) collective-permute-start(bf16[128,4096]{1,0:T(8,128)(2,1)} %bitcast.31), channel_id=1, source_target_pairs={{0,1},{1,0},{2,3},{3,2},{4,5},{5,4},{6,7},{7,6},{8,9},{9,8},{10,11... | collective-permute-start | bytes 3145736 | tf_op jit(solution)/shard_map/ppermute | solution.py:31
  8.2 19.5 %collective-permute-start.9 = (bf16[64,2048]{1,0:T(8,128)(2,1)}, bf16[64,2048]{1,0:T(8,128)(2,1)}, u32[]{:S(2)}, u32[]{:S(2)}) collective-permute-start(bf16[64,2048]{1,0:T(8,128)(2,1)} %get-tuple-element.103.refs_0_), channel_id=1, source_target_pairs={{0,2},{1,3},{2,0},{3,1},{4,6},{5,7},{6,4},{7,5},{8,10},{9,11},{10,... | collective-permute-start | bytes 786440 | tf_op jit(solution)/shard_map/ppermute | solution.py:31
  10.9 16.8 %collective-permute-start.1 = (bf16[64,2048]{1,0:T(8,128)(2,1)}, bf16[64,2048]{1,0:T(8,128)(2,1)}, u32[]{:S(2)}, u32[]{:S(2)}) collective-permute-start(bf16[64,2048]{1,0:T(8,128)(2,1)} %get-tuple-element.103.refs_0_), channel_id=1, source_target_pairs={{0,4},{1,5},{2,6},{3,7},{4,0},{5,1},{6,2},{7,3},{8,12},{9,13},{10,... | collective-permute-start | bytes 786440 | tf_op jit(solution)/shard_map/ppermute | solution.py:31
  14.7 11.1 %collective-permute-start.7 = (bf16[144,320]{1,0:T(8,128)(2,1)S(1)}, bf16[144,320]{1,0:T(8,128)(2,1)S(1)}, u32[]{:S(2)}, u32[]{:S(2)}) collective-permute-start(bf16[144,320]{1,0:T(8,128)(2,1)S(1)} %fusion.3.refs_0_), channel_id=1, source_target_pairs={{0,4},{1,5},{2,6},{3,7},{8,12},{9,13},{10,14},{11,15},{16,20},{17,... | collective-permute-start | bytes 276488 | tf_op jit(solution)/shard_map/ppermute | solution.py:26
  20.3 7.3 %collective-permute-start.6 = (bf16[144,320]{1,0:T(8,128)(2,1)S(1)}, bf16[144,320]{1,0:T(8,128)(2,1)S(1)}, u32[]{:S(2)}, u32[]{:S(2)}) collective-permute-start(bf16[144,320]{1,0:T(8,128)(2,1)S(1)} %fusion.3.refs_0_), channel_id=1, source_target_pairs={{0,2},{1,3},{2,4},{3,5},{4,6},{5,7},{8,10},{9,11},{10,12},{11,13},... | collective-permute-start | bytes 276488 | tf_op jit(solution)/shard_map/ppermute | solution.py:26
  27.6 34.9 %copy-start.2 = (bf16[1,128,4096]{2,1,0:T(8,128)(2,1)S(1)}, bf16[1,128,4096]{2,1,0:T(8,128)(2,1)}, u32[]{:S(2)}) copy-start(bf16[1,128,4096]{2,1,0:T(8,128)(2,1)} %param.9) | copy-start | bytes 3145732
  27.6 9.3 %collective-permute-start.8 = (bf16[432,320]{1,0:T(8,128)(2,1)S(1)}, bf16[432,320]{1,0:T(8,128)(2,1)}, u32[]{:S(2)}, u32[]{:S(2)}) collective-permute-start(bf16[432,320]{1,0:T(8,128)(2,1)S(1)} %stack.31.own), channel_id=1, source_target_pairs={{0,1},{1,0},{2,3},{3,2},{4,5},{5,4},{6,7},{7,6},{8,9},{9,8},{10,11... | collective-permute-start | bytes 829448 | tf_op jit(solution)/shard_map/ppermute | solution.py:31
  27.7 18.3 %collective-permute-start.10 = (bf16[64,2048]{1,0:T(8,128)(2,1)}, bf16[64,2048]{1,0:T(8,128)(2,1)}, u32[]{:S(2)}, u32[]{:S(2)}) collective-permute-start(bf16[64,2048]{1,0:T(8,128)(2,1)} %collective-permute-done.1.refs_1_), channel_id=1, source_target_pairs={{0,2},{1,3},{2,0},{3,1},{4,6},{5,7},{6,4},{7,5},{8,10},{9,11},{10,... | collective-permute-start | bytes 786440 | tf_op jit(solution)/shard_map/ppermute | solution.py:31
  32.9 18.4 %collective-permute-start.14 = (bf16[64,2048]{1,0:T(8,128)(2,1)}, bf16[64,2048]{1,0:T(8,128)(2,1)}, u32[]{:S(2)}, u32[]{:S(2)}) collective-permute-start(bf16[64,2048]{1,0:T(8,128)(2,1)} %get-tuple-element.110.refs_0_), channel_id=1, source_target_pairs={{0,2},{1,3},{2,0},{3,1},{4,6},{5,7},{6,4},{7,5},{8,10},{9,11},{10,... | collective-permute-start | bytes 786440 | tf_op jit(solution)/shard_map/ppermute | solution.py:31
  33.0 18.4 %collective-permute-start.13 = (bf16[64,2048]{1,0:T(8,128)(2,1)}, bf16[64,2048]{1,0:T(8,128)(2,1)}, u32[]{:S(2)}, u32[]{:S(2)}) collective-permute-start(bf16[64,2048]{1,0:T(8,128)(2,1)} %get-tuple-element.110.refs_0_), channel_id=1, source_target_pairs={{0,4},{1,5},{2,6},{3,7},{4,0},{5,1},{6,2},{7,3},{8,12},{9,13},{10,... | collective-permute-start | bytes 786440 | tf_op jit(solution)/shard_map/ppermute | solution.py:31
  36.9 2.2 %collective-permute-start.5 = (f32[64,128]{1,0:T(8,128)S(1)}, f32[64,128]{1,0:T(8,128)S(1)}, u32[]{:S(2)}, u32[]{:S(2)}) collective-permute-start(f32[64,128]{1,0:T(8,128)S(1)} %bitcast.38), channel_id=1, source_target_pairs={{0,1},{1,0},{2,3},{3,2},{4,5},{5,4},{6,7},{7,6},{8,9},{9,8},{10,11... | collective-permute-start | bytes 98312 | tf_op jit(solution)/shard_map/ppermute | solution.py:31
  36.9 24.4 %copy-start.8 = (bf16[64,2048]{1,0:T(8,128)(2,1)S(1)}, bf16[64,2048]{1,0:T(8,128)(2,1)}, u32[]{:S(2)}) copy-start(bf16[64,2048]{1,0:T(8,128)(2,1)} %get-tuple-element.110.refs_0_) | copy-start | bytes 786436
  39.1 23.4 %copy-start = (bf16[1,128,8192]{2,1,0:T(8,128)(2,1)S(1)}, bf16[1,128,8192]{2,1,0:T(8,128)(2,1)}, u32[]{:S(2)}) copy-start(bf16[1,128,8192]{2,1,0:T(8,128)(2,1)} %param.8) | copy-start | bytes 6291460
  48.1 31.6 %collective-permute-start.12 = (bf16[256,2048]{1,0:T(8,128)(2,1)S(1)}, bf16[256,2048]{1,0:T(8,128)(2,1)S(1)}, u32[]{:S(2)}, u32[]{:S(2)}) collective-permute-start(bf16[256,2048]{1,0:T(8,128)(2,1)S(1)} %stack.32.weight), channel_id=1, source_target_pairs={{0,8},{8,0},{16,24},{24,16},{1,9},{9,1},{17,25},{25,17},{2,10},{10... | collective-permute-start | bytes 3145736 | tf_op jit(solution)/shard_map/ppermute | solution.py:31
  49.7 30.0 %collective-permute-start.11 = (bf16[256,2048]{1,0:T(8,128)(2,1)S(1)}, bf16[256,2048]{1,0:T(8,128)(2,1)S(1)}, u32[]{:S(2)}, u32[]{:S(2)}) collective-permute-start(bf16[256,2048]{1,0:T(8,128)(2,1)S(1)} %stack.32.weight), channel_id=1, source_target_pairs={{0,16},{8,24},{16,0},{24,8},{1,17},{9,25},{17,1},{25,9},{2,18},{10... | collective-permute-start | bytes 3145736 | tf_op jit(solution)/shard_map/ppermute | solution.py:31
  51.4 10.0 %collective-permute-start.15 = (bf16[64,2048]{1,0:T(8,128)(2,1)}, bf16[64,2048]{1,0:T(8,128)(2,1)S(1)}, u32[]{:S(2)}, u32[]{:S(2)}) collective-permute-start(bf16[64,2048]{1,0:T(8,128)(2,1)} %collective-permute-done.13.refs_1_), channel_id=1, source_target_pairs={{0,2},{1,3},{2,0},{3,1},{4,6},{5,7},{6,4},{7,5},{8,10},{9,11},{10,... | collective-permute-start | bytes 786440 | tf_op jit(solution)/shard_map/ppermute | solution.py:31
  76.7 26.1 %collective-permute-start.16 = (f32[128,2048]{1,0:T(8,128)S(1)}, f32[128,2048]{1,0:T(8,128)S(1)}, u32[]{:S(2)}, u32[]{:S(2)}) collective-permute-start(f32[128,2048]{1,0:T(8,128)S(1)} %get-tuple-element.119), channel_id=1, source_target_pairs={{0,8},{8,0},{16,24},{24,16},{1,9},{9,1},{17,25},{25,17},{2,10},{10... | collective-permute-start | bytes 3145736 | tf_op jit(solution)/shard_map/ppermute | solution.py:31
  78.2 24.6 %collective-permute-start.17 = (f32[128,2048]{1,0:T(8,128)S(1)}, f32[128,2048]{1,0:T(8,128)S(1)}, u32[]{:S(2)}, u32[]{:S(2)}) collective-permute-start(f32[128,2048]{1,0:T(8,128)S(1)} %get-tuple-element.120), channel_id=1, source_target_pairs={{0,16},{8,24},{16,0},{24,8},{1,17},{9,25},{17,1},{25,9},{2,18},{10... | collective-permute-start | bytes 3145736 | tf_op jit(solution)/shard_map/ppermute | solution.py:31
  92.6 32.7 %collective-permute-start.18 = (f32[128,2048]{1,0:T(8,128)S(1)}, f32[128,2048]{1,0:T(8,128)S(1)}, u32[]{:S(2)}, u32[]{:S(2)}) collective-permute-start(f32[128,2048]{1,0:T(8,128)S(1)} %get-tuple-element.129), channel_id=1, source_target_pairs={{0,8},{8,0},{16,24},{24,16},{1,9},{9,1},{17,25},{25,17},{2,10},{10... | collective-permute-start | bytes 3145736 | tf_op jit(solution)/shard_map/ppermute | solution.py:31
  102.8 33.7 %collective-permute-start.19 = (f32[128,1024]{1,0:T(8,128)S(1)}, f32[128,1024]{1,0:T(8,128)S(1)}, u32[]{:S(2)}, u32[]{:S(2)}) collective-permute-start(f32[128,1024]{1,0:T(8,128)S(1)} %get-tuple-element.130), channel_id=1, source_target_pairs={{0,16},{8,24},{16,0},{24,8},{1,17},{9,25},{17,1},{25,9},{2,18},{10... | collective-permute-start | bytes 1572872 | tf_op jit(solution)/shard_map/ppermute | solution.py:31
  111.6 13.4 %collective-permute-start.20 = (f32[128,1024]{1,0:T(8,128)S(1)}, f32[128,1024]{1,0:T(8,128)S(1)}, u32[]{:S(2)}, u32[]{:S(2)}) collective-permute-start(f32[128,1024]{1,0:T(8,128)S(1)} %get-tuple-element.131), channel_id=1, source_target_pairs={{0,16},{8,24},{16,0},{24,8},{1,17},{9,25},{17,1},{25,9},{2,18},{10... | collective-permute-start | bytes 1572872 | tf_op jit(solution)/shard_map/ppermute | solution.py:31
  112.3 24.2 %collective-permute-start.23 = (f32[128,1024]{1,0:T(8,128)S(1)}, f32[128,1024]{1,0:T(8,128)S(1)}, u32[]{:S(2)}, u32[]{:S(2)}) collective-permute-start(f32[128,1024]{1,0:T(8,128)S(1)} %get-tuple-element.156), channel_id=1, source_target_pairs={{0,8},{8,0},{16,24},{24,16},{1,9},{9,1},{17,25},{25,17},{2,10},{10... | collective-permute-start | bytes 1572872 | tf_op jit(solution)/shard_map/ppermute | solution.py:31
  125.3 24.3 %copy-start.15 = (f32[128,2048]{1,0:T(8,128)}, f32[128,2048]{1,0:T(8,128)S(1)}, u32[]{:S(2)}) copy-start(f32[128,2048]{1,0:T(8,128)S(1)} %collective-permute-done.18) | copy-start | bytes 3145732
  125.3 11.3 %collective-permute-start.24 = (f32[128,1024]{1,0:T(8,128)S(1)}, f32[128,1024]{1,0:T(8,128)S(1)}, u32[]{:S(2)}, u32[]{:S(2)}) collective-permute-start(f32[128,1024]{1,0:T(8,128)S(1)} %get-tuple-element.158), channel_id=1, source_target_pairs={{0,16},{8,24},{16,0},{24,8},{1,17},{9,25},{17,1},{25,9},{2,18},{10... | collective-permute-start | bytes 1572872 | tf_op jit(solution)/shard_map/ppermute | solution.py:31
  127.3 19.9 %collective-permute-start.27 = (f32[128,1024]{1,0:T(8,128)S(1)}, f32[128,1024]{1,0:T(8,128)S(1)}, u32[]{:S(2)}, u32[]{:S(2)}) collective-permute-start(f32[128,1024]{1,0:T(8,128)S(1)} %get-tuple-element.168), channel_id=1, source_target_pairs={{0,8},{8,0},{16,24},{24,16},{1,9},{9,1},{17,25},{25,17},{2,10},{10... | collective-permute-start | bytes 1572872 | tf_op jit(solution)/shard_map/ppermute | solution.py:31
  136.6 10.6 %collective-permute-start.25 = (f32[128,1024]{1,0:T(8,128)S(1)}, f32[128,1024]{1,0:T(8,128)S(1)}, u32[]{:S(2)}, u32[]{:S(2)}) collective-permute-start(f32[128,1024]{1,0:T(8,128)S(1)} %add_add_fusion.2), channel_id=1, source_target_pairs={{0,2},{1,3},{2,0},{3,1},{4,6},{5,7},{6,4},{7,5},{8,10},{9,11},{10,... | collective-permute-start | bytes 1572872 | tf_op jit(solution)/shard_map/ppermute | solution.py:31
  138.4 9.2 %collective-permute-start.26 = (f32[128,1024]{1,0:T(8,128)S(1)}, f32[128,1024]{1,0:T(8,128)S(1)}, u32[]{:S(2)}, u32[]{:S(2)}) collective-permute-start(f32[128,1024]{1,0:T(8,128)S(1)} %get-tuple-element.163), channel_id=1, source_target_pairs={{0,16},{8,24},{16,0},{24,8},{1,17},{9,25},{17,1},{25,9},{2,18},{10... | collective-permute-start | bytes 1572872 | tf_op jit(solution)/shard_map/ppermute | solution.py:31
  147.2 22.8 %collective-permute-start.21 = (bf16[128,6144]{1,0:T(8,128)(2,1)}, bf16[128,6144]{1,0:T(8,128)(2,1)S(1)}, u32[]{:S(2)}, u32[]{:S(2)}) collective-permute-start(bf16[128,6144]{1,0:T(8,128)(2,1)} %get-tuple-element.136), channel_id=1, source_target_pairs={{0,1},{1,0},{2,3},{3,2},{4,5},{5,4},{6,7},{7,6},{8,9},{9,8},{10,11... | collective-permute-start | bytes 4718600 | tf_op jit(solution)/shard_map/ppermute | solution.py:31
  148.6 19.9 %collective-permute-start.28 = (f32[128,1024]{1,0:T(8,128)}, f32[128,1024]{1,0:T(8,128)}, u32[]{:S(2)}, u32[]{:S(2)}) collective-permute-start(f32[128,1024]{1,0:T(8,128)} %add_add_fusion), channel_id=1, source_target_pairs={{0,2},{1,3},{2,0},{3,1},{4,6},{5,7},{6,4},{7,5},{8,10},{9,11},{10,... | collective-permute-start | bytes 1572872 | tf_op jit(solution)/shard_map/ppermute | solution.py:31
  150.5 15.8 %collective-permute-start.32 = (f32[64,1024]{1,0:T(8,128)}, f32[64,1024]{1,0:T(8,128)}, u32[]{:S(2)}, u32[]{:S(2)}) collective-permute-start(f32[64,1024]{1,0:T(8,128)} %slice.82), channel_id=1, source_target_pairs={{0,4},{1,5},{2,6},{3,7},{4,0},{5,1},{6,2},{7,3},{8,12},{9,13},{10,... | collective-permute-start | bytes 786440 | tf_op jit(solution)/shard_map/ppermute | solution.py:31
  154.2 15.8 %collective-permute-start.22 = (f32[432,320]{0,1:T(8,128)}, f32[432,320]{0,1:T(8,128)S(1)}, u32[]{:S(2)}, u32[]{:S(2)}) collective-permute-start(f32[432,320]{0,1:T(8,128)} %copy.36), channel_id=1, source_target_pairs={{0,1},{1,0},{2,3},{3,2},{4,5},{5,4},{6,7},{7,6},{8,9},{9,8},{10,11... | collective-permute-start | bytes 1658888 | tf_op jit(solution)/shard_map/ppermute | solution.py:31
  170.9 14.3 %collective-permute-start.29 = (f32[64,1024]{1,0:T(8,128)}, f32[64,1024]{1,0:T(8,128)}, u32[]{:S(2)}, u32[]{:S(2)}) collective-permute-start(f32[64,1024]{1,0:T(8,128)} %slice.65), channel_id=1, source_target_pairs={{0,4},{1,5},{2,6},{3,7},{4,0},{5,1},{6,2},{7,3},{8,12},{9,13},{10,... | collective-permute-start | bytes 786440 | tf_op jit(solution)/shard_map/ppermute | solution.py:31
  173.2 1.5 collective-permute-start.33
  175.3 13.6 %collective-permute-start.36 = (f32[32,2048]{1,0:T(8,128)S(1)}, f32[32,2048]{1,0:T(8,128)S(1)}, u32[]{:S(2)}, u32[]{:S(2)}) collective-permute-start(f32[32,2048]{1,0:T(8,128)S(1)} %join_cores.2.refs_0_), channel_id=1, source_target_pairs={{0,24},{8,16},{16,8},{24,0},{1,25},{9,17},{17,9},{25,1},{2,26},{10... | collective-permute-start | bytes 786440 | tf_op jit(solution)/shard_map/ppermute | solution.py:31
  176.8 13.8 %collective-permute-start.35 = (f32[32,2048]{1,0:T(8,128)S(1)}, f32[32,2048]{1,0:T(8,128)S(1)}, u32[]{:S(2)}, u32[]{:S(2)}) collective-permute-start(f32[32,2048]{1,0:T(8,128)S(1)} %join_cores.2.refs_0_), channel_id=1, source_target_pairs={{0,16},{8,24},{16,0},{24,8},{1,17},{9,25},{17,1},{25,9},{2,18},{10... | collective-permute-start | bytes 786440 | tf_op jit(solution)/shard_map/ppermute | solution.py:31
  178.3 12.3 %collective-permute-start.34 = (f32[32,2048]{1,0:T(8,128)S(1)}, f32[32,2048]{1,0:T(8,128)S(1)}, u32[]{:S(2)}, u32[]{:S(2)}) collective-permute-start(f32[32,2048]{1,0:T(8,128)S(1)} %join_cores.2.refs_0_), channel_id=1, source_target_pairs={{0,8},{8,0},{16,24},{24,16},{1,9},{9,1},{17,25},{25,17},{2,10},{10... | collective-permute-start | bytes 786440 | tf_op jit(solution)/shard_map/ppermute | solution.py:31
  186.2 10.9 %collective-permute-start.30 = (f32[128,320]{1,0:T(8,128)S(1)}, f32[128,320]{1,0:T(8,128)S(1)}, u32[]{:S(2)}, u32[]{:S(2)}) collective-permute-start(f32[128,320]{1,0:T(8,128)S(1)} %get-tuple-element.188), channel_id=1, source_target_pairs={{2,0},{3,1},{4,2},{5,3},{6,4},{7,5},{10,8},{11,9},{12,10},{13,11},... | collective-permute-start | bytes 491528 | tf_op jit(solution)/shard_map/ppermute | solution.py:26
  187.5 13.2 %collective-permute-start.31 = (f32[128,320]{1,0:T(8,128)S(1)}, f32[128,320]{1,0:T(8,128)S(1)}, u32[]{:S(2)}, u32[]{:S(2)}) collective-permute-start(f32[128,320]{1,0:T(8,128)S(1)} %get-tuple-element.189), channel_id=1, source_target_pairs={{4,0},{5,1},{6,2},{7,3},{12,8},{13,9},{14,10},{15,11},{20,16},{21,... | collective-permute-start | bytes 491528 | tf_op jit(solution)/shard_map/ppermute | solution.py:26
  188.9 1.7 collective-permute-start.37
  191.2 10.4 %collective-permute-start.40 = (f32[32,2048]{1,0:T(8,128)S(1)}, f32[32,2048]{1,0:T(8,128)S(1)}, u32[]{:S(2)}, u32[]{:S(2)}) collective-permute-start(f32[32,2048]{1,0:T(8,128)S(1)} %join_cores.3.refs_1_), channel_id=1, source_target_pairs={{0,24},{8,16},{16,8},{24,0},{1,25},{9,17},{17,9},{25,1},{2,26},{10... | collective-permute-start | bytes 786440 | tf_op jit(solution)/shard_map/ppermute | solution.py:31
  192.8 13.2 %collective-permute-start.39 = (f32[32,2048]{1,0:T(8,128)S(1)}, f32[32,2048]{1,0:T(8,128)S(1)}, u32[]{:S(2)}, u32[]{:S(2)}) collective-permute-start(f32[32,2048]{1,0:T(8,128)S(1)} %join_cores.3.refs_1_), channel_id=1, source_target_pairs={{0,16},{8,24},{16,0},{24,8},{1,17},{9,25},{17,1},{25,9},{2,18},{10... | collective-permute-start | bytes 786440 | tf_op jit(solution)/shard_map/ppermute | solution.py:31
  193.9 12.1 %collective-permute-start.38 = (f32[32,2048]{1,0:T(8,128)S(1)}, f32[32,2048]{1,0:T(8,128)}, u32[]{:S(2)}, u32[]{:S(2)}) collective-permute-start(f32[32,2048]{1,0:T(8,128)S(1)} %join_cores.3.refs_1_), channel_id=1, source_target_pairs={{0,8},{8,0},{16,24},{24,16},{1,9},{9,1},{17,25},{25,17},{2,10},{10... | collective-permute-start | bytes 786440 | tf_op jit(solution)/shard_map/ppermute | solution.py:31
  (14 other events, 82.6 us)

commit v11 on v10

--- a/solution.py
+++ b/solution.py
@@ -268,40 +268,32 @@
     )(place, up_weight, up_weight, crossed, crossed)
 
 
-def lay_kernel(place, *refs, count):
-    pieces, out, sems = refs[:count], refs[count], refs[count + 1]
-    width = pieces[0].shape[1] // 2
-    copies = []
-    for index, piece in enumerate(pieces):
-        t, half = divmod(index, 2)
-        for which in range(2):
-            start = (place[1 + t] * 4 + which * 2 + half) * width
-            copies.append(
-                pltpu.make_async_copy(
-                    piece.at[:, pl.ds(which * width, width)],
-                    out.at[:, pl.ds(pl.multiple_of(start, width), width)],
-                    sems.at[2 * index + which],
-                )
-            )
-    for copy in copies:
-        copy.start()
-    for copy in copies:
-        copy.wait()
+def lay_kernel(place, *refs):
+    *pieces, out = refs
+    width = out.shape[1] // 4
+    for step in range(len(pieces) // 2):
+        early, late = pieces[2 * step], pieces[2 * step + 1]
+
+        @pl.when(pl.program_id(0) == step)
+        def _():
+            for which in range(2):
+                source = slice(which * width, (which + 1) * width)
+                out[:, 2 * which * width : (2 * which + 1) * width] = early[:, source]
+                out[:, (2 * which + 1) * width : (2 * which + 2) * width] = late[:, source]
 
 
 def lay_out(place, pieces):
     rows, columns = pieces[0].shape
-    count = len(pieces)
-    return pl.pallas_call(
-        functools.partial(lay_kernel, count=count),
+    count = len(pieces) // 2
+    return pl.pallas_call(
+        lay_kernel,
         grid_spec=pltpu.PrefetchScalarGridSpec(
             num_scalar_prefetch=1,
-            grid=(1,),
-            in_specs=[pl.BlockSpec(memory_space=pl.ANY)] * count,
-            out_specs=pl.BlockSpec(memory_space=pl.ANY),
-            scratch_shapes=[pltpu.SemaphoreType.DMA((2 * count,))],
-        ),
-        out_shape=jax.ShapeDtypeStruct((rows, count * columns), pieces[0].dtype),
+            grid=(count,),
+            in_specs=[pl.BlockSpec(memory_space=pltpu.VMEM)] * len(pieces),
+            out_specs=pl.BlockSpec((rows, 2 * columns), lambda t, place: (0, place[1 + t])),
+        ),
+        out_shape=jax.ShapeDtypeStruct((rows, count * 2 * columns), pieces[0].dtype),
         compiler_params=pltpu.CompilerParams(vmem_limit_bytes=KERNEL_BYTES),
         cost_estimate=pl.CostEstimate(flops=0, bytes_accessed=4_000_000, transcendentals=0),
         name="lay_out",

time: 217 us -> 211 us (0.972)
  Pallas kernels: 77 us -> 70.6 us
    pallas_call x1, Pallas kernels: 9.75 us -> 3.36 us  [lay_out(): pl.pallas_call(lay_kernel, grid_spec=pltpu.PrefetchScalarGridSpec(num_sca...]
  transfers between devices with their start and end apart: 41 -> 41, of which waited for: 17 -> 17; matrix products, arithmetic and copies ran while one was open for 5% -> 5% of each run, Pallas kernels for 31% -> 32%
where the time goes in v11:
time: 211 us; the launch traced here: 209 us
  Pallas kernels  70.6 us (33%)
  waiting for transfers between devices  63.2 us (30%)
  starting transfers between devices  59.3 us (28%)
  local copies, waits for them, and re-layouts  9.94 us (5%)
  other arithmetic  5.3 us (3%)
    ppermute x37, waiting for transfers between devices, exchange(): lax.ppermute(value, axis, [(source, source ^ bits) for source in range(co...  55.8 us
    pallas_call x6, Pallas kernels, chunk_backward(): pl.pallas_call(functools.partial(heads_kernel, earlier=len(aliases)), gri...  55 us
    ppermute x37, starting transfers between devices, exchange(): lax.ppermute(value, axis, [(source, source ^ bits) for source in range(co...  47.6 us
    ppermute x4, starting transfers between devices, from_behind(): lax.ppermute(value, axis, [(source, source + steps) for source in range(i...  11.7 us
    ppermute x4, waiting for transfers between devices, from_behind(): lax.ppermute(value, axis, [(source, source + steps) for source in range(i...  7.4 us
    unnamed x43, local copies, waits for them, and re-layouts  4.96 us
  transfers between devices with their start and end apart: 41, of which 17 were waited for; matrix products, arithmetic and copies ran while one was open for 5% of the time, Pallas kernels for 32%

profile of v11, /device:TPU:0, one launch (start us, length us, event | category | flops | bytes accessed | tf_op | source)
XLA Modules:
  0.0 209.4 jit_solution(17432079858504166396)
XLA Ops:
  1.8 1.9 collective-permute-done.near_crossed.distant_crossed
  5.6 2.6 %weight_parts.1 = (bf16[64,2048]{1,0:T(8,128)(2,1)}, bf16[64,2048]{1,0:T(8,128)(2,1)}) custom-call(s32[6]{0:T(128)} %stack.30.place, bf16[32,16384]{1,0:T(8,128)(2,1)} %distant.1, bf16[32,16384]{1,0:T(8,128)(2,1)} %distant.1, bf16[32,16384]{1,0:T(8,128)(2,1)} %copy-done.11, bf16[32,16384]{1,0:T(8,128)(2,1)} %copy-done.11), custom_call_target="tpu_custom_call" | custom-call | bytes 1000000 | tf_op jit(solution)/shard_map/weight_parts/pallas_call | solution.py:256
  8.2 2.7 %collective-permute-start.9 = (bf16[64,2048]{1,0:T(8,128)(2,1)}, bf16[64,2048]{1,0:T(8,128)(2,1)}, u32[]{:S(2)}, u32[]{:S(2)}) collective-permute-start(bf16[64,2048]{1,0:T(8,128)(2,1)} %get-tuple-element.103.refs_0_), channel_id=1, source_target_pairs={{0,2},{1,3},{2,0},{3,1},{4,6},{5,7},{6,4},{7,5},{8,10},{9,11},{10,... | collective-permute-start | bytes 786440 | tf_op jit(solution)/shard_map/ppermute | solution.py:31
  10.9 2.6 %collective-permute-start.1 = (bf16[64,2048]{1,0:T(8,128)(2,1)}, bf16[64,2048]{1,0:T(8,128)(2,1)}, u32[]{:S(2)}, u32[]{:S(2)}) collective-permute-start(bf16[64,2048]{1,0:T(8,128)(2,1)} %get-tuple-element.103.refs_0_), channel_id=1, source_target_pairs={{0,4},{1,5},{2,6},{3,7},{4,0},{5,1},{6,2},{7,3},{8,12},{9,13},{10,... | collective-permute-start | bytes 786440 | tf_op jit(solution)/shard_map/ppermute | solution.py:31
  14.7 5.6 %collective-permute-start.7 = (bf16[144,320]{1,0:T(8,128)(2,1)S(1)}, bf16[144,320]{1,0:T(8,128)(2,1)S(1)}, u32[]{:S(2)}, u32[]{:S(2)}) collective-permute-start(bf16[144,320]{1,0:T(8,128)(2,1)S(1)} %fusion.3.refs_0_), channel_id=1, source_target_pairs={{0,4},{1,5},{2,6},{3,7},{8,12},{9,13},{10,14},{11,15},{16,20},{17,... | collective-permute-start | bytes 276488 | tf_op jit(solution)/shard_map/ppermute | solution.py:26
  20.3 3.5 %collective-permute-start.6 = (bf16[144,320]{1,0:T(8,128)(2,1)S(1)}, bf16[144,320]{1,0:T(8,128)(2,1)S(1)}, u32[]{:S(2)}, u32[]{:S(2)}) collective-permute-start(bf16[144,320]{1,0:T(8,128)(2,1)S(1)} %fusion.3.refs_0_), channel_id=1, source_target_pairs={{0,2},{1,3},{2,4},{3,5},{4,6},{5,7},{8,10},{9,11},{10,12},{11,13},... | collective-permute-start | bytes 276488 | tf_op jit(solution)/shard_map/ppermute | solution.py:26
  23.8 1.9 collective-permute-done.7.refs_2_
  25.8 1.8 collective-permute-done.6.refs_1_
  27.7 5.2 %collective-permute-start.10 = (bf16[64,2048]{1,0:T(8,128)(2,1)}, bf16[64,2048]{1,0:T(8,128)(2,1)}, u32[]{:S(2)}, u32[]{:S(2)}) collective-permute-start(bf16[64,2048]{1,0:T(8,128)(2,1)} %collective-permute-done.1.refs_1_), channel_id=1, source_target_pairs={{0,2},{1,3},{2,0},{3,1},{4,6},{5,7},{6,4},{7,5},{8,10},{9,11},{10,... | collective-permute-start | bytes 786440 | tf_op jit(solution)/shard_map/ppermute | solution.py:31
  33.0 3.9 %collective-permute-start.13 = (bf16[64,2048]{1,0:T(8,128)(2,1)}, bf16[64,2048]{1,0:T(8,128)(2,1)}, u32[]{:S(2)}, u32[]{:S(2)}) collective-permute-start(bf16[64,2048]{1,0:T(8,128)(2,1)} %get-tuple-element.110.refs_0_), channel_id=1, source_target_pairs={{0,4},{1,5},{2,6},{3,7},{4,0},{5,1},{6,2},{7,3},{8,12},{9,13},{10,... | collective-permute-start | bytes 786440 | tf_op jit(solution)/shard_map/ppermute | solution.py:31
  37.0 2.1 %collect.1 = (bf16[768,256]{1,0:T(8,128)(2,1)S(1)}, bf16[256,768]{1,0:T(8,128)(2,1)S(1)}, bf16[768,128]{1,0:T(8,128)(2,1)S(1)}, f32[768,128]{1,0:T(8,128)S(1)}) custom-call(s32[6]{0:T(128)S(1)} %copy-done.10, s32[8,4]{1,0:T(8,128)S(1)} %copy.34.offered, bf16[432,320]{1,0:T(8,128)(2,1)S(1)} %stack.31.own, bf16[432,320]{1,0:T(8,128)(2,1)} %collective-permute-done.8.sib), custom_call_target="tpu_custom_call" | custom-call | flops 250000000 | bytes 3000000 | tf_op jit(solution)/shard_map/collect/pallas_call | solution.py:415
  39.1 6.9 %collective-permute-done.10.refs_3_ = bf16[64,2048]{1,0:T(8,128)(2,1)} collective-permute-done((bf16[64,2048]{1,0:T(8,128)(2,1)}, bf16[64,2048]{1,0:T(8,128)(2,1)}, u32[]{:S(2)}, u32[]{:S(2)}) %collective-permute-start.10) | collective-permute-done | bytes 262176 | tf_op jit(solution)/shard_map/ppermute | solution.py:31
  48.1 1.6 collective-permute-start.12
  49.7 1.5 collective-permute-start.11
  51.4 3.7 %collective-permute-start.15 = (bf16[64,2048]{1,0:T(8,128)(2,1)}, bf16[64,2048]{1,0:T(8,128)(2,1)S(1)}, u32[]{:S(2)}, u32[]{:S(2)}) collective-permute-start(bf16[64,2048]{1,0:T(8,128)(2,1)} %collective-permute-done.13.refs_1_), channel_id=1, source_target_pairs={{0,2},{1,3},{2,0},{3,1},{4,6},{5,7},{6,4},{7,5},{8,10},{9,11},{10,... | collective-permute-start | bytes 786440 | tf_op jit(solution)/shard_map/ppermute | solution.py:31
  55.0 6.3 %collective-permute-done.15.refs_3_ = bf16[64,2048]{1,0:T(8,128)(2,1)S(1)} collective-permute-done((bf16[64,2048]{1,0:T(8,128)(2,1)}, bf16[64,2048]{1,0:T(8,128)(2,1)S(1)}, u32[]{:S(2)}, u32[]{:S(2)}) %collective-permute-start.15) | collective-permute-done | bytes 262176 | tf_op jit(solution)/shard_map/ppermute | solution.py:31
  63.7 13.0 %heads_backward.6 = (bf16[128,8192]{1,0:T(8,128)(2,1)}, bf16[128,4096]{1,0:T(8,128)(2,1)}, bf16[128,6144]{1,0:T(8,128)(2,1)}, f32[128,2048]{1,0:T(8,128)S(1)}, f...) custom-call(s32[6]{0:T(128)S(1)} %copy-done.10, bf16[128,8192]{1,0:T(8,128)(2,1)S(1)} %bitcast.18, ...), custom_call_target="tpu_custom_call" | custom-call | flops 400000000 | bytes 1200000 | tf_op jit(solution)/shard_map/heads_backward/pallas_call | solution.py:158
  76.7 1.5 collective-permute-start.16
  78.2 1.5 collective-permute-start.17
  79.7 12.8 %heads_backward.7 = (bf16[128,8192]{1,0:T(8,128)(2,1)}, bf16[128,4096]{1,0:T(8,128)(2,1)}, bf16[128,6144]{1,0:T(8,128)(2,1)}, f32[128,2048]{1,0:T(8,128)S(1)}, f...) custom-call(s32[6]{0:T(128)S(1)} %copy-done.10, ...), custom_call_target="tpu_custom_call", output_to_operand_aliasing={{0}: (14, {}), {1}: (15, {}), {2}: (16, {})} | custom-call | flops 400000000 | bytes 1200000 | tf_op jit(solution)/shard_map/heads_backward/pallas_call | solution.py:158
  93.1 7.2 %heads_backward.8 = (bf16[128,8192]{1,0:T(8,128)(2,1)}, bf16[128,4096]{1,0:T(8,128)(2,1)}, bf16[128,6144]{1,0:T(8,128)(2,1)}, f32[128,1024]{1,0:T(8,128)S(1)}, f...) custom-call(s32[6]{0:T(128)S(1)} %copy-done.10, ...), custom_call_target="tpu_custom_call", output_to_operand_aliasing={{0}: (14, {}), {1}: (15, {}), {2}: (16, {})} | custom-call | flops 200000000 | bytes 600000 | tf_op jit(solution)/shard_map/heads_backward/pallas_call | solution.py:158
  100.3 2.5 %collective-permute-done.16 = f32[128,2048]{1,0:T(8,128)S(1)} collective-permute-done((f32[128,2048]{1,0:T(8,128)S(1)}, f32[128,2048]{1,0:T(8,128)S(1)}, u32[]{:S(2)}, u32[]{:S(2)}) %collective-permute-start.16) | collective-permute-done | bytes 1048608 | tf_op jit(solution)/shard_map/ppermute | solution.py:31
  102.8 1.5 collective-permute-start.19
  104.3 7.3 %heads_backward.9 = (bf16[128,8192]{1,0:T(8,128)(2,1)}, bf16[128,4096]{1,0:T(8,128)(2,1)}, bf16[128,6144]{1,0:T(8,128)(2,1)}, f32[128,1024]{1,0:T(8,128)S(1)}, f...) custom-call(s32[6]{0:T(128)S(1)} %copy-done.10, ...), custom_call_target="tpu_custom_call", output_to_operand_aliasing={{0}: (14, {}), {1}: (15, {}), {2}: (16, {})} | custom-call | flops 200000000 | bytes 600000 | tf_op jit(solution)/shard_map/heads_backward/pallas_call | solution.py:158
  112.3 1.6 collective-permute-start.23
  113.8 7.5 %heads_backward.10 = (bf16[128,8192]{1,0:T(8,128)(2,1)}, bf16[128,4096]{1,0:T(8,128)(2,1)}, bf16[128,6144]{1,0:T(8,128)(2,1)}, f32[128,1024]{1,0:T(8,128)S(1)}, ...) custom-call(s32[6]{0:T(128)S(1)} %copy-done.10, ...), custom_call_target="tpu_custom_call", output_to_operand_aliasing={{0}: (14, {}), {1}: (15, {}), {2}: (16, {})} | custom-call | flops 200000000 | bytes 600000 | tf_op jit(solution)/shard_map/heads_backward/pallas_call | solution.py:158
  121.5 3.5 %collective-permute-done.20 = f32[128,1024]{1,0:T(8,128)S(1)} collective-permute-done((f32[128,1024]{1,0:T(8,128)S(1)}, f32[128,1024]{1,0:T(8,128)S(1)}, u32[]{:S(2)}, u32[]{:S(2)}) %collective-permute-start.20) | collective-permute-done | bytes 524320 | tf_op jit(solution)/shard_map/ppermute | solution.py:31
  125.3 2.1 collective-permute-start.24
  128.3 8.2 %collective-permute-done.23 = f32[128,1024]{1,0:T(8,128)S(1)} collective-permute-done((f32[128,1024]{1,0:T(8,128)S(1)}, f32[128,1024]{1,0:T(8,128)S(1)}, u32[]{:S(2)}, u32[]{:S(2)}) %collective-permute-start.23) | collective-permute-done | bytes 524320 | tf_op jit(solution)/shard_map/ppermute | solution.py:31
  136.6 1.8 collective-permute-start.25
  138.4 1.5 collective-permute-start.26
  140.0 7.3 %heads_backward.11 = (bf16[128,8192]{1,0:T(8,128)(2,1)}, bf16[128,4096]{1,0:T(8,128)(2,1)}, bf16[128,6144]{1,0:T(8,128)(2,1)}, f32[128,1024]{1,0:T(8,128)S(1)}, ...) custom-call(s32[6]{0:T(128)S(1)} %copy-done.10, ...), custom_call_target="tpu_custom_call", output_to_operand_aliasing={{0}: (14, {}), {1}: (15, {}), {2}: (16, {})} | custom-call | flops 200000000 | bytes 600000 | tf_op jit(solution)/shard_map/heads_backward/pallas_call | solution.py:158
  151.4 1.7 spread.1
  154.2 12.1 %collective-permute-done.32 = f32[64,1024]{1,0:T(8,128)} collective-permute-done((f32[64,1024]{1,0:T(8,128)}, f32[64,1024]{1,0:T(8,128)}, u32[]{:S(2)}, u32[]{:S(2)}) %collective-permute-start.32) | collective-permute-done | bytes 262176 | tf_op jit(solution)/shard_map/ppermute | solution.py:31
  168.5 1.6 add_add_fusion.1
  170.9 2.3 %collective-permute-start.29 = (f32[64,1024]{1,0:T(8,128)}, f32[64,1024]{1,0:T(8,128)}, u32[]{:S(2)}, u32[]{:S(2)}) collective-permute-start(f32[64,1024]{1,0:T(8,128)} %slice.65), channel_id=1, source_target_pairs={{0,4},{1,5},{2,6},{3,7},{4,0},{5,1},{6,2},{7,3},{8,12},{9,13},{10,... | collective-permute-start | bytes 786440 | tf_op jit(solution)/shard_map/ppermute | solution.py:31
  173.3 1.3 copy.37
  175.3 1.5 collective-permute-start.36
  176.8 1.5 collective-permute-start.35
  178.8 6.4 %collective-permute-done.29 = f32[64,1024]{1,0:T(8,128)} collective-permute-done((f32[64,1024]{1,0:T(8,128)}, f32[64,1024]{1,0:T(8,128)}, u32[]{:S(2)}, u32[]{:S(2)}) %collective-permute-start.29) | collective-permute-done | bytes 262176 | tf_op jit(solution)/shard_map/ppermute | solution.py:31
  186.2 1.3 collective-permute-start.30
  187.5 1.3 collective-permute-start.31
  188.9 1.6 collective-permute-done.35.refs_4_
  191.2 1.6 collective-permute-start.40
  194.7 2.4 %place_columns.1 = (bf16[128,8192]{1,0:T(8,128)(2,1)}, bf16[128,4096]{1,0:T(8,128)(2,1)}) custom-call(s32[6]{0:T(128)S(1)} %copy-done.10, bf16[128,6144]{1,0:T(8,128)(2,1)S(1)} %collective-permute-done.21.received, bf16[128,8192]{1,0:T(8,128)(2,1)} %get-tuple-element.137.q_in, ...), custom_call_target="tpu_custom_call", output_to_operand_aliasing={{0}: (2, {}), {1}: (3, {})} | custom-call | bytes 4000000 | tf_op jit(solution)/shard_map/place_columns/pallas_call | solution.py:187
  197.1 3.6 %collective-permute-done.31 = f32[128,320]{1,0:T(8,128)S(1)} collective-permute-done((f32[128,320]{1,0:T(8,128)S(1)}, f32[128,320]{1,0:T(8,128)S(1)}, u32[]{:S(2)}, u32[]{:S(2)}) %collective-permute-start.31) | collective-permute-done | bytes 163872 | tf_op jit(solution)/shard_map/ppermute | solution.py:26
  201.6 4.4 %collective-permute-done.39.refs_5_ = f32[32,2048]{1,0:T(8,128)S(1)} collective-permute-done((f32[32,2048]{1,0:T(8,128)S(1)}, f32[32,2048]{1,0:T(8,128)S(1)}, u32[]{:S(2)}, u32[]{:S(2)}) %collective-permute-start.39) | collective-permute-done | bytes 262176 | tf_op jit(solution)/shard_map/ppermute | solution.py:31
  206.0 3.4 %lay_out.1 = f32[32,16384]{1,0:T(8,128)} custom-call(s32[6]{0:T(128)S(1)} %copy-done.10, f32[32,2048]{1,0:T(8,128)S(1)} %join_cores.2.refs_0_, f32[32,2048]{1,0:T(8,128)S(1)} %join_cores.3.refs_1_, f32[32,2048]{1,0:T(8,128)S(1)} %collective-permute-done.34.refs_2_, f32[32,2048]{1,0:T(8,128)} %collective-permute-done.38.refs_3_, ...), custom_call_target="tpu_custom_call" | custom-call | bytes 4000000 | tf_op jit(solution)/shard_map/lay_out/pallas_call | solution.py:288
  (116 shorter events, 26.0 us)
Async XLA Ops:
  0.6 3.0 %collective-permute-start = (bf16[32,16384]{1,0:T(8,128)(2,1)}, bf16[32,16384]{1,0:T(8,128)(2,1)S(1)}, u32[]{:S(2)}, u32[]{:S(2)}) collective-permute-start(bf16[32,16384]{1,0:T(8,128)(2,1)} %distant.1), channel_id=1, source_target_pairs={{0,1},{1,0},{2,3},{3,2},{4,5},{5,4},{6,7},{7,6},{8,9},{9,8},{10,11... | collective-permute-start | bytes 3145736 | tf_op jit(solution)/shard_map/ppermute | solution.py:31
  4.6 10.1 %collective-permute-start.2 = (bf16[128,8192]{1,0:T(8,128)(2,1)}, bf16[128,8192]{1,0:T(8,128)(2,1)S(1)}, u32[]{:S(2)}, u32[]{:S(2)}) collective-permute-start(bf16[128,8192]{1,0:T(8,128)(2,1)} %bitcast.17), channel_id=1, source_target_pairs={{0,1},{1,0},{2,3},{3,2},{4,5},{5,4},{6,7},{7,6},{8,9},{9,8},{10,11... | collective-permute-start | bytes 6291464 | tf_op jit(solution)/shard_map/ppermute | solution.py:31
  5.0 9.7 %collective-permute-start.4 = (bf16[128,8192]{1,0:T(8,128)(2,1)}, bf16[128,8192]{1,0:T(8,128)(2,1)}, u32[]{:S(2)}, u32[]{:S(2)}) collective-permute-start(bf16[128,8192]{1,0:T(8,128)(2,1)} %bitcast.24), channel_id=1, source_target_pairs={{0,1},{1,0},{2,3},{3,2},{4,5},{5,4},{6,7},{7,6},{8,9},{9,8},{10,11... | collective-permute-start | bytes 6291464 | tf_op jit(solution)/shard_map/ppermute | solution.py:31
  5.1 31.7 %copy-start.5 = (f32[1,64,128]{2,1,0:T(8,128)S(1)}, f32[1,64,128]{2,1,0:T(8,128)}, u32[]{:S(2)}) copy-start(f32[1,64,128]{2,1,0:T(8,128)} %param.11) | copy-start | bytes 98308
  5.1 31.7 %copy-start.19 = (s32[1,8,4]{1,2,0:T(4,128)S(1)}, s32[1,8,4]{1,2,0:T(4,128)}, u32[]{:S(2)}) copy-start(s32[1,8,4]{1,2,0:T(4,128)} %param.15) | copy-start | bytes 388
  5.1 31.8 %copy-start.10 = (s32[6]{0:T(128)S(1)}, s32[6]{0:T(128)}, u32[]{:S(2)}) copy-start(s32[6]{0:T(128)} %stack.30.place) | copy-start | bytes 76
  5.1 8.6 %collective-permute-start.3 = (bf16[128,4096]{1,0:T(8,128)(2,1)}, bf16[128,4096]{1,0:T(8,128)(2,1)S(1)}, u32[]{:S(2)}, u32[]{:S(2)}) collective-permute-start(bf16[128,4096]{1,0:T(8,128)(2,1)} %bitcast.31), channel_id=1, source_target_pairs={{0,1},{1,0},{2,3},{3,2},{4,5},{5,4},{6,7},{7,6},{8,9},{9,8},{10,11... | collective-permute-start | bytes 3145736 | tf_op jit(solution)/shard_map/ppermute | solution.py:31
  8.2 19.5 %collective-permute-start.9 = (bf16[64,2048]{1,0:T(8,128)(2,1)}, bf16[64,2048]{1,0:T(8,128)(2,1)}, u32[]{:S(2)}, u32[]{:S(2)}) collective-permute-start(bf16[64,2048]{1,0:T(8,128)(2,1)} %get-tuple-element.103.refs_0_), channel_id=1, source_target_pairs={{0,2},{1,3},{2,0},{3,1},{4,6},{5,7},{6,4},{7,5},{8,10},{9,11},{10,... | collective-permute-start | bytes 786440 | tf_op jit(solution)/shard_map/ppermute | solution.py:31
  10.9 16.8 %collective-permute-start.1 = (bf16[64,2048]{1,0:T(8,128)(2,1)}, bf16[64,2048]{1,0:T(8,128)(2,1)}, u32[]{:S(2)}, u32[]{:S(2)}) collective-permute-start(bf16[64,2048]{1,0:T(8,128)(2,1)} %get-tuple-element.103.refs_0_), channel_id=1, source_target_pairs={{0,4},{1,5},{2,6},{3,7},{4,0},{5,1},{6,2},{7,3},{8,12},{9,13},{10,... | collective-permute-start | bytes 786440 | tf_op jit(solution)/shard_map/ppermute | solution.py:31
  14.7 11.1 %collective-permute-start.7 = (bf16[144,320]{1,0:T(8,128)(2,1)S(1)}, bf16[144,320]{1,0:T(8,128)(2,1)S(1)}, u32[]{:S(2)}, u32[]{:S(2)}) collective-permute-start(bf16[144,320]{1,0:T(8,128)(2,1)S(1)} %fusion.3.refs_0_), channel_id=1, source_target_pairs={{0,4},{1,5},{2,6},{3,7},{8,12},{9,13},{10,14},{11,15},{16,20},{17,... | collective-permute-start | bytes 276488 | tf_op jit(solution)/shard_map/ppermute | solution.py:26
  20.3 7.3 %collective-permute-start.6 = (bf16[144,320]{1,0:T(8,128)(2,1)S(1)}, bf16[144,320]{1,0:T(8,128)(2,1)S(1)}, u32[]{:S(2)}, u32[]{:S(2)}) collective-permute-start(bf16[144,320]{1,0:T(8,128)(2,1)S(1)} %fusion.3.refs_0_), channel_id=1, source_target_pairs={{0,2},{1,3},{2,4},{3,5},{4,6},{5,7},{8,10},{9,11},{10,12},{11,13},... | collective-permute-start | bytes 276488 | tf_op jit(solution)/shard_map/ppermute | solution.py:26
  27.6 34.9 %copy-start.2 = (bf16[1,128,4096]{2,1,0:T(8,128)(2,1)S(1)}, bf16[1,128,4096]{2,1,0:T(8,128)(2,1)}, u32[]{:S(2)}) copy-start(bf16[1,128,4096]{2,1,0:T(8,128)(2,1)} %param.9) | copy-start | bytes 3145732
  27.6 9.3 %collective-permute-start.8 = (bf16[432,320]{1,0:T(8,128)(2,1)S(1)}, bf16[432,320]{1,0:T(8,128)(2,1)}, u32[]{:S(2)}, u32[]{:S(2)}) collective-permute-start(bf16[432,320]{1,0:T(8,128)(2,1)S(1)} %stack.31.own), channel_id=1, source_target_pairs={{0,1},{1,0},{2,3},{3,2},{4,5},{5,4},{6,7},{7,6},{8,9},{9,8},{10,11... | collective-permute-start | bytes 829448 | tf_op jit(solution)/shard_map/ppermute | solution.py:31
  27.7 18.3 %collective-permute-start.10 = (bf16[64,2048]{1,0:T(8,128)(2,1)}, bf16[64,2048]{1,0:T(8,128)(2,1)}, u32[]{:S(2)}, u32[]{:S(2)}) collective-permute-start(bf16[64,2048]{1,0:T(8,128)(2,1)} %collective-permute-done.1.refs_1_), channel_id=1, source_target_pairs={{0,2},{1,3},{2,0},{3,1},{4,6},{5,7},{6,4},{7,5},{8,10},{9,11},{10,... | collective-permute-start | bytes 786440 | tf_op jit(solution)/shard_map/ppermute | solution.py:31
  32.9 18.4 %collective-permute-start.14 = (bf16[64,2048]{1,0:T(8,128)(2,1)}, bf16[64,2048]{1,0:T(8,128)(2,1)}, u32[]{:S(2)}, u32[]{:S(2)}) collective-permute-start(bf16[64,2048]{1,0:T(8,128)(2,1)} %get-tuple-element.110.refs_0_), channel_id=1, source_target_pairs={{0,2},{1,3},{2,0},{3,1},{4,6},{5,7},{6,4},{7,5},{8,10},{9,11},{10,... | collective-permute-start | bytes 786440 | tf_op jit(solution)/shard_map/ppermute | solution.py:31
  33.0 18.4 %collective-permute-start.13 = (bf16[64,2048]{1,0:T(8,128)(2,1)}, bf16[64,2048]{1,0:T(8,128)(2,1)}, u32[]{:S(2)}, u32[]{:S(2)}) collective-permute-start(bf16[64,2048]{1,0:T(8,128)(2,1)} %get-tuple-element.110.refs_0_), channel_id=1, source_target_pairs={{0,4},{1,5},{2,6},{3,7},{4,0},{5,1},{6,2},{7,3},{8,12},{9,13},{10,... | collective-permute-start | bytes 786440 | tf_op jit(solution)/shard_map/ppermute | solution.py:31
  36.9 2.2 %collective-permute-start.5 = (f32[64,128]{1,0:T(8,128)S(1)}, f32[64,128]{1,0:T(8,128)S(1)}, u32[]{:S(2)}, u32[]{:S(2)}) collective-permute-start(f32[64,128]{1,0:T(8,128)S(1)} %bitcast.38), channel_id=1, source_target_pairs={{0,1},{1,0},{2,3},{3,2},{4,5},{5,4},{6,7},{7,6},{8,9},{9,8},{10,11... | collective-permute-start | bytes 98312 | tf_op jit(solution)/shard_map/ppermute | solution.py:31
  36.9 24.4 %copy-start.8 = (bf16[64,2048]{1,0:T(8,128)(2,1)S(1)}, bf16[64,2048]{1,0:T(8,128)(2,1)}, u32[]{:S(2)}) copy-start(bf16[64,2048]{1,0:T(8,128)(2,1)} %get-tuple-element.110.refs_0_) | copy-start | bytes 786436
  39.1 23.4 %copy-start = (bf16[1,128,8192]{2,1,0:T(8,128)(2,1)S(1)}, bf16[1,128,8192]{2,1,0:T(8,128)(2,1)}, u32[]{:S(2)}) copy-start(bf16[1,128,8192]{2,1,0:T(8,128)(2,1)} %param.8) | copy-start | bytes 6291460
  48.1 31.6 %collective-permute-start.12 = (bf16[256,2048]{1,0:T(8,128)(2,1)S(1)}, bf16[256,2048]{1,0:T(8,128)(2,1)S(1)}, u32[]{:S(2)}, u32[]{:S(2)}) collective-permute-start(bf16[256,2048]{1,0:T(8,128)(2,1)S(1)} %stack.32.weight), channel_id=1, source_target_pairs={{0,8},{8,0},{16,24},{24,16},{1,9},{9,1},{17,25},{25,17},{2,10},{10... | collective-permute-start | bytes 3145736 | tf_op jit(solution)/shard_map/ppermute | solution.py:31
  49.7 30.0 %collective-permute-start.11 = (bf16[256,2048]{1,0:T(8,128)(2,1)S(1)}, bf16[256,2048]{1,0:T(8,128)(2,1)S(1)}, u32[]{:S(2)}, u32[]{:S(2)}) collective-permute-start(bf16[256,2048]{1,0:T(8,128)(2,1)S(1)} %stack.32.weight), channel_id=1, source_target_pairs={{0,16},{8,24},{16,0},{24,8},{1,17},{9,25},{17,1},{25,9},{2,18},{10... | collective-permute-start | bytes 3145736 | tf_op jit(solution)/shard_map/ppermute | solution.py:31
  51.4 10.0 %collective-permute-start.15 = (bf16[64,2048]{1,0:T(8,128)(2,1)}, bf16[64,2048]{1,0:T(8,128)(2,1)S(1)}, u32[]{:S(2)}, u32[]{:S(2)}) collective-permute-start(bf16[64,2048]{1,0:T(8,128)(2,1)} %collective-permute-done.13.refs_1_), channel_id=1, source_target_pairs={{0,2},{1,3},{2,0},{3,1},{4,6},{5,7},{6,4},{7,5},{8,10},{9,11},{10,... | collective-permute-start | bytes 786440 | tf_op jit(solution)/shard_map/ppermute | solution.py:31
  76.7 26.1 %collective-permute-start.16 = (f32[128,2048]{1,0:T(8,128)S(1)}, f32[128,2048]{1,0:T(8,128)S(1)}, u32[]{:S(2)}, u32[]{:S(2)}) collective-permute-start(f32[128,2048]{1,0:T(8,128)S(1)} %get-tuple-element.119), channel_id=1, source_target_pairs={{0,8},{8,0},{16,24},{24,16},{1,9},{9,1},{17,25},{25,17},{2,10},{10... | collective-permute-start | bytes 3145736 | tf_op jit(solution)/shard_map/ppermute | solution.py:31
  78.2 24.6 %collective-permute-start.17 = (f32[128,2048]{1,0:T(8,128)S(1)}, f32[128,2048]{1,0:T(8,128)S(1)}, u32[]{:S(2)}, u32[]{:S(2)}) collective-permute-start(f32[128,2048]{1,0:T(8,128)S(1)} %get-tuple-element.120), channel_id=1, source_target_pairs={{0,16},{8,24},{16,0},{24,8},{1,17},{9,25},{17,1},{25,9},{2,18},{10... | collective-permute-start | bytes 3145736 | tf_op jit(solution)/shard_map/ppermute | solution.py:31
  92.6 32.7 %collective-permute-start.18 = (f32[128,2048]{1,0:T(8,128)S(1)}, f32[128,2048]{1,0:T(8,128)S(1)}, u32[]{:S(2)}, u32[]{:S(2)}) collective-permute-start(f32[128,2048]{1,0:T(8,128)S(1)} %get-tuple-element.129), channel_id=1, source_target_pairs={{0,8},{8,0},{16,24},{24,16},{1,9},{9,1},{17,25},{25,17},{2,10},{10... | collective-permute-start | bytes 3145736 | tf_op jit(solution)/shard_map/ppermute | solution.py:31
  102.8 33.7 %collective-permute-start.19 = (f32[128,1024]{1,0:T(8,128)S(1)}, f32[128,1024]{1,0:T(8,128)S(1)}, u32[]{:S(2)}, u32[]{:S(2)}) collective-permute-start(f32[128,1024]{1,0:T(8,128)S(1)} %get-tuple-element.130), channel_id=1, source_target_pairs={{0,16},{8,24},{16,0},{24,8},{1,17},{9,25},{17,1},{25,9},{2,18},{10... | collective-permute-start | bytes 1572872 | tf_op jit(solution)/shard_map/ppermute | solution.py:31
  111.6 13.4 %collective-permute-start.20 = (f32[128,1024]{1,0:T(8,128)S(1)}, f32[128,1024]{1,0:T(8,128)S(1)}, u32[]{:S(2)}, u32[]{:S(2)}) collective-permute-start(f32[128,1024]{1,0:T(8,128)S(1)} %get-tuple-element.131), channel_id=1, source_target_pairs={{0,16},{8,24},{16,0},{24,8},{1,17},{9,25},{17,1},{25,9},{2,18},{10... | collective-permute-start | bytes 1572872 | tf_op jit(solution)/shard_map/ppermute | solution.py:31
  112.3 24.2 %collective-permute-start.23 = (f32[128,1024]{1,0:T(8,128)S(1)}, f32[128,1024]{1,0:T(8,128)S(1)}, u32[]{:S(2)}, u32[]{:S(2)}) collective-permute-start(f32[128,1024]{1,0:T(8,128)S(1)} %get-tuple-element.156), channel_id=1, source_target_pairs={{0,8},{8,0},{16,24},{24,16},{1,9},{9,1},{17,25},{25,17},{2,10},{10... | collective-permute-start | bytes 1572872 | tf_op jit(solution)/shard_map/ppermute | solution.py:31
  125.3 24.3 %copy-start.15 = (f32[128,2048]{1,0:T(8,128)}, f32[128,2048]{1,0:T(8,128)S(1)}, u32[]{:S(2)}) copy-start(f32[128,2048]{1,0:T(8,128)S(1)} %collective-permute-done.18) | copy-start | bytes 3145732
  125.3 11.3 %collective-permute-start.24 = (f32[128,1024]{1,0:T(8,128)S(1)}, f32[128,1024]{1,0:T(8,128)S(1)}, u32[]{:S(2)}, u32[]{:S(2)}) collective-permute-start(f32[128,1024]{1,0:T(8,128)S(1)} %get-tuple-element.158), channel_id=1, source_target_pairs={{0,16},{8,24},{16,0},{24,8},{1,17},{9,25},{17,1},{25,9},{2,18},{10... | collective-permute-start | bytes 1572872 | tf_op jit(solution)/shard_map/ppermute | solution.py:31
  127.3 19.9 %collective-permute-start.27 = (f32[128,1024]{1,0:T(8,128)S(1)}, f32[128,1024]{1,0:T(8,128)S(1)}, u32[]{:S(2)}, u32[]{:S(2)}) collective-permute-start(f32[128,1024]{1,0:T(8,128)S(1)} %get-tuple-element.168), channel_id=1, source_target_pairs={{0,8},{8,0},{16,24},{24,16},{1,9},{9,1},{17,25},{25,17},{2,10},{10... | collective-permute-start | bytes 1572872 | tf_op jit(solution)/shard_map/ppermute | solution.py:31
  136.6 10.6 %collective-permute-start.25 = (f32[128,1024]{1,0:T(8,128)S(1)}, f32[128,1024]{1,0:T(8,128)S(1)}, u32[]{:S(2)}, u32[]{:S(2)}) collective-permute-start(f32[128,1024]{1,0:T(8,128)S(1)} %add_add_fusion.2), channel_id=1, source_target_pairs={{0,2},{1,3},{2,0},{3,1},{4,6},{5,7},{6,4},{7,5},{8,10},{9,11},{10,... | collective-permute-start | bytes 1572872 | tf_op jit(solution)/shard_map/ppermute | solution.py:31
  138.4 9.2 %collective-permute-start.26 = (f32[128,1024]{1,0:T(8,128)S(1)}, f32[128,1024]{1,0:T(8,128)S(1)}, u32[]{:S(2)}, u32[]{:S(2)}) collective-permute-start(f32[128,1024]{1,0:T(8,128)S(1)} %get-tuple-element.163), channel_id=1, source_target_pairs={{0,16},{8,24},{16,0},{24,8},{1,17},{9,25},{17,1},{25,9},{2,18},{10... | collective-permute-start | bytes 1572872 | tf_op jit(solution)/shard_map/ppermute | solution.py:31
  147.2 22.8 %collective-permute-start.21 = (bf16[128,6144]{1,0:T(8,128)(2,1)}, bf16[128,6144]{1,0:T(8,128)(2,1)S(1)}, u32[]{:S(2)}, u32[]{:S(2)}) collective-permute-start(bf16[128,6144]{1,0:T(8,128)(2,1)} %get-tuple-element.136), channel_id=1, source_target_pairs={{0,1},{1,0},{2,3},{3,2},{4,5},{5,4},{6,7},{7,6},{8,9},{9,8},{10,11... | collective-permute-start | bytes 4718600 | tf_op jit(solution)/shard_map/ppermute | solution.py:31
  148.6 19.9 %collective-permute-start.28 = (f32[128,1024]{1,0:T(8,128)}, f32[128,1024]{1,0:T(8,128)}, u32[]{:S(2)}, u32[]{:S(2)}) collective-permute-start(f32[128,1024]{1,0:T(8,128)} %add_add_fusion), channel_id=1, source_target_pairs={{0,2},{1,3},{2,0},{3,1},{4,6},{5,7},{6,4},{7,5},{8,10},{9,11},{10,... | collective-permute-start | bytes 1572872 | tf_op jit(solution)/shard_map/ppermute | solution.py:31
  150.5 15.8 %collective-permute-start.32 = (f32[64,1024]{1,0:T(8,128)}, f32[64,1024]{1,0:T(8,128)}, u32[]{:S(2)}, u32[]{:S(2)}) collective-permute-start(f32[64,1024]{1,0:T(8,128)} %slice.82), channel_id=1, source_target_pairs={{0,4},{1,5},{2,6},{3,7},{4,0},{5,1},{6,2},{7,3},{8,12},{9,13},{10,... | collective-permute-start | bytes 786440 | tf_op jit(solution)/shard_map/ppermute | solution.py:31
  154.2 15.8 %collective-permute-start.22 = (f32[432,320]{0,1:T(8,128)}, f32[432,320]{0,1:T(8,128)S(1)}, u32[]{:S(2)}, u32[]{:S(2)}) collective-permute-start(f32[432,320]{0,1:T(8,128)} %copy.36), channel_id=1, source_target_pairs={{0,1},{1,0},{2,3},{3,2},{4,5},{5,4},{6,7},{7,6},{8,9},{9,8},{10,11... | collective-permute-start | bytes 1658888 | tf_op jit(solution)/shard_map/ppermute | solution.py:31
  170.9 14.3 %collective-permute-start.29 = (f32[64,1024]{1,0:T(8,128)}, f32[64,1024]{1,0:T(8,128)}, u32[]{:S(2)}, u32[]{:S(2)}) collective-permute-start(f32[64,1024]{1,0:T(8,128)} %slice.65), channel_id=1, source_target_pairs={{0,4},{1,5},{2,6},{3,7},{4,0},{5,1},{6,2},{7,3},{8,12},{9,13},{10,... | collective-permute-start | bytes 786440 | tf_op jit(solution)/shard_map/ppermute | solution.py:31
  173.2 1.5 collective-permute-start.33
  175.3 13.6 %collective-permute-start.36 = (f32[32,2048]{1,0:T(8,128)S(1)}, f32[32,2048]{1,0:T(8,128)S(1)}, u32[]{:S(2)}, u32[]{:S(2)}) collective-permute-start(f32[32,2048]{1,0:T(8,128)S(1)} %join_cores.2.refs_0_), channel_id=1, source_target_pairs={{0,24},{8,16},{16,8},{24,0},{1,25},{9,17},{17,9},{25,1},{2,26},{10... | collective-permute-start | bytes 786440 | tf_op jit(solution)/shard_map/ppermute | solution.py:31
  176.8 13.8 %collective-permute-start.35 = (f32[32,2048]{1,0:T(8,128)S(1)}, f32[32,2048]{1,0:T(8,128)S(1)}, u32[]{:S(2)}, u32[]{:S(2)}) collective-permute-start(f32[32,2048]{1,0:T(8,128)S(1)} %join_cores.2.refs_0_), channel_id=1, source_target_pairs={{0,16},{8,24},{16,0},{24,8},{1,17},{9,25},{17,1},{25,9},{2,18},{10... | collective-permute-start | bytes 786440 | tf_op jit(solution)/shard_map/ppermute | solution.py:31
  178.3 12.3 %collective-permute-start.34 = (f32[32,2048]{1,0:T(8,128)S(1)}, f32[32,2048]{1,0:T(8,128)S(1)}, u32[]{:S(2)}, u32[]{:S(2)}) collective-permute-start(f32[32,2048]{1,0:T(8,128)S(1)} %join_cores.2.refs_0_), channel_id=1, source_target_pairs={{0,8},{8,0},{16,24},{24,16},{1,9},{9,1},{17,25},{25,17},{2,10},{10... | collective-permute-start | bytes 786440 | tf_op jit(solution)/shard_map/ppermute | solution.py:31
  186.2 10.9 %collective-permute-start.30 = (f32[128,320]{1,0:T(8,128)S(1)}, f32[128,320]{1,0:T(8,128)S(1)}, u32[]{:S(2)}, u32[]{:S(2)}) collective-permute-start(f32[128,320]{1,0:T(8,128)S(1)} %get-tuple-element.188), channel_id=1, source_target_pairs={{2,0},{3,1},{4,2},{5,3},{6,4},{7,5},{10,8},{11,9},{12,10},{13,11},... | collective-permute-start | bytes 491528 | tf_op jit(solution)/shard_map/ppermute | solution.py:26
  187.5 13.2 %collective-permute-start.31 = (f32[128,320]{1,0:T(8,128)S(1)}, f32[128,320]{1,0:T(8,128)S(1)}, u32[]{:S(2)}, u32[]{:S(2)}) collective-permute-start(f32[128,320]{1,0:T(8,128)S(1)} %get-tuple-element.189), channel_id=1, source_target_pairs={{4,0},{5,1},{6,2},{7,3},{12,8},{13,9},{14,10},{15,11},{20,16},{21,... | collective-permute-start | bytes 491528 | tf_op jit(solution)/shard_map/ppermute | solution.py:26
  188.9 1.7 collective-permute-start.37
  191.2 10.4 %collective-permute-start.40 = (f32[32,2048]{1,0:T(8,128)S(1)}, f32[32,2048]{1,0:T(8,128)S(1)}, u32[]{:S(2)}, u32[]{:S(2)}) collective-permute-start(f32[32,2048]{1,0:T(8,128)S(1)} %join_cores.3.refs_1_), channel_id=1, source_target_pairs={{0,24},{8,16},{16,8},{24,0},{1,25},{9,17},{17,9},{25,1},{2,26},{10... | collective-permute-start | bytes 786440 | tf_op jit(solution)/shard_map/ppermute | solution.py:31
  192.8 13.2 %collective-permute-start.39 = (f32[32,2048]{1,0:T(8,128)S(1)}, f32[32,2048]{1,0:T(8,128)S(1)}, u32[]{:S(2)}, u32[]{:S(2)}) collective-permute-start(f32[32,2048]{1,0:T(8,128)S(1)} %join_cores.3.refs_1_), channel_id=1, source_target_pairs={{0,16},{8,24},{16,0},{24,8},{1,17},{9,25},{17,1},{25,9},{2,18},{10... | collective-permute-start | bytes 786440 | tf_op jit(solution)/shard_map/ppermute | solution.py:31
  193.9 12.1 %collective-permute-start.38 = (f32[32,2048]{1,0:T(8,128)S(1)}, f32[32,2048]{1,0:T(8,128)}, u32[]{:S(2)}, u32[]{:S(2)}) collective-permute-start(f32[32,2048]{1,0:T(8,128)S(1)} %join_cores.3.refs_1_), channel_id=1, source_target_pairs={{0,8},{8,0},{16,24},{24,16},{1,9},{9,1},{17,25},{25,17},{2,10},{10... | collective-permute-start | bytes 786440 | tf_op jit(solution)/shard_map/ppermute | solution.py:31
  (14 other events, 82.6 us)

commit v12 on v11

--- a/solution.py
+++ b/solution.py
@@ -164,7 +164,7 @@
         input_output_aliases=aliases,
         compiler_params=pltpu.CompilerParams(vmem_limit_bytes=KERNEL_BYTES),
         cost_estimate=pl.CostEstimate(
-            flops=count * 100_000_000, bytes_accessed=count * 300_000, transcendentals=0
+            flops=count * 1_500_000_000, bytes_accessed=count * 300_000, transcendentals=0
         ),
         name="heads_backward",
     )(place, *operands)
@@ -547,10 +547,11 @@
     orders = (bits, bits[::-1])
     first_sums = [{t: [] for t in range(n_dp) if t & order[0]} for order in orders]
     half_pairs = pairs // 2
-    units = [(t, 0, pairs) for t in [far] + list(range(1, far - 1))]
-    units += [(t, start, half_pairs) for t in (far - 1, 0) for start in (0, half_pairs)]
+    halved = lambda t: [(t, 0, half_pairs), (t, half_pairs, half_pairs)]
+    units = [*halved(far)]
+    units += [halved(t)[half] for half in range(2) for t in range(1, far)] + halved(0)
     for t, start, count in units:
-        if t == far:
+        if t == far and not start:
             weights[far] = joined(far_pieces)
         weight = weights[t]
         if t == 0 and start:
@@ -558,8 +559,9 @@
             weight = after(weight, latents[-1], *there)
         if t == 1 and not start:
             weight = after(weight, *[weights[near] for near in range(2, far)])
-        if t == far - 1 and start:
-            weight = after(weight, latents[-1], *[sent[far][0] for sent in first_sums])
+        if t == far - 1:
+            far_sums = [sent[far][1 if start else 0] for sent in first_sums]
+            weight = after(weight, latents[-1], *far_sums)
         rest = chunk_backward(
             place,
             t,
@@ -575,7 +577,10 @@
         for side, sent in enumerate(first_sums):
             weight_grads[t][side].append(rest[3 + side])
             if t in sent:
-                sent[t].append(exchange(rest[3 + side], "dp", orders[side][0]))
+                leaving = rest[3 + side]
+                if t != far and start:
+                    leaving = after(leaving, sent[t][0])
+                sent[t].append(exchange(leaving, "dp", orders[side][0]))
         latents.append(rest[5])
         ropes.append(rest[6])
 
@@ -602,7 +607,7 @@
             for t in sorted((t for t in addends if t & bit), reverse=True):
                 leaving = [total(addends[t], half) for half in range(2)]
                 if side == 0:
-                    behind = [(first_sums[0][order[0]][0], last_sums[-1], latents[-2])] * 2
+                    behind = [(*first_sums[0][order[0]], last_sums[-1], latents[-2])] * 2
                 else:
                     behind = [(weight_grads[far - 1][side][0],)] * 2
                 leaving = [after(half, *there) for half, there in zip(leaving, behind)]

time: 211 us -> 215 us (1.019)
  Pallas kernels: 70.6 us -> 74.1 us
    pallas_call x6 -> x8, Pallas kernels: 55 us -> 58.5 us  [chunk_backward(): pl.pallas_call(functools.partial(heads_kernel, earlier=len(aliases)), gri...]
    ppermute x37 -> x40, waiting for transfers between devices: 55.8 us -> 58.7 us  [exchange(): lax.ppermute(value, axis, [(source, source ^ bits) for source in range(co...]
    ppermute x37 -> x40, starting transfers between devices: 47.6 us -> 46.6 us  [exchange(): lax.ppermute(value, axis, [(source, source ^ bits) for source in range(co...]
  transfers between devices with their start and end apart: 41 -> 44, of which waited for: 17 -> 18; matrix products, arithmetic and copies ran while one was open for 5% -> 5% of each run, Pallas kernels for 32% -> 33%
where the time goes in v12:
time: 215 us; the launch traced here: 213 us
  Pallas kernels  74.1 us (34%)
  waiting for transfers between devices  64.5 us (30%)
  starting transfers between devices  58.3 us (27%)
  local copies, waits for them, and re-layouts  9.92 us (5%)
  other arithmetic  5.19 us (2%)
    ppermute x40, waiting for transfers between devices, exchange(): lax.ppermute(value, axis, [(source, source ^ bits) for source in range(co...  58.7 us
    pallas_call x8, Pallas kernels, chunk_backward(): pl.pallas_call(functools.partial(heads_kernel, earlier=len(aliases)), gri...  58.5 us
    ppermute x40, starting transfers between devices, exchange(): lax.ppermute(value, axis, [(source, source ^ bits) for source in range(co...  46.6 us
    ppermute x4, starting transfers between devices, from_behind(): lax.ppermute(value, axis, [(source, source + steps) for source in range(i...  11.7 us
    ppermute x4, waiting for transfers between devices, from_behind(): lax.ppermute(value, axis, [(source, source + steps) for source in range(i...  5.85 us
    unnamed x43, local copies, waits for them, and re-layouts  4.96 us
  transfers between devices with their start and end apart: 44, of which 18 were waited for; matrix products, arithmetic and copies ran while one was open for 5% of the time, Pallas kernels for 33%

profile of v12, /device:TPU:0, one launch (start us, length us, event | category | flops | bytes accessed | tf_op | source)
XLA Modules:
  0.0 213.1 jit_solution(2081548514525829)
XLA Ops:
  1.7 1.9 collective-permute-done.near_crossed.distant_crossed
  5.6 2.6 %weight_parts.1 = (bf16[64,2048]{1,0:T(8,128)(2,1)}, bf16[64,2048]{1,0:T(8,128)(2,1)}) custom-call(s32[6]{0:T(128)} %stack.30.place, bf16[32,16384]{1,0:T(8,128)(2,1)} %distant.1, bf16[32,16384]{1,0:T(8,128)(2,1)} %distant.1, bf16[32,16384]{1,0:T(8,128)(2,1)} %copy-done.11, bf16[32,16384]{1,0:T(8,128)(2,1)} %copy-done.11), custom_call_target="tpu_custom_call" | custom-call | bytes 1000000 | tf_op jit(solution)/shard_map/weight_parts/pallas_call | solution.py:256
  8.2 2.7 %collective-permute-start.9 = (bf16[64,2048]{1,0:T(8,128)(2,1)}, bf16[64,2048]{1,0:T(8,128)(2,1)}, u32[]{:S(2)}, u32[]{:S(2)}) collective-permute-start(bf16[64,2048]{1,0:T(8,128)(2,1)} %get-tuple-element.120.refs_0_), channel_id=1, source_target_pairs={{0,2},{1,3},{2,0},{3,1},{4,6},{5,7},{6,4},{7,5},{8,10},{9,11},{10,... | collective-permute-start | bytes 786440 | tf_op jit(solution)/shard_map/ppermute | solution.py:31
  10.9 2.6 %collective-permute-start.1 = (bf16[64,2048]{1,0:T(8,128)(2,1)}, bf16[64,2048]{1,0:T(8,128)(2,1)}, u32[]{:S(2)}, u32[]{:S(2)}) collective-permute-start(bf16[64,2048]{1,0:T(8,128)(2,1)} %get-tuple-element.120.refs_0_), channel_id=1, source_target_pairs={{0,4},{1,5},{2,6},{3,7},{4,0},{5,1},{6,2},{7,3},{8,12},{9,13},{10,... | collective-permute-start | bytes 786440 | tf_op jit(solution)/shard_map/ppermute | solution.py:31
  14.7 5.6 %collective-permute-start.7 = (bf16[144,320]{1,0:T(8,128)(2,1)S(1)}, bf16[144,320]{1,0:T(8,128)(2,1)S(1)}, u32[]{:S(2)}, u32[]{:S(2)}) collective-permute-start(bf16[144,320]{1,0:T(8,128)(2,1)S(1)} %fusion.1.refs_0_), channel_id=1, source_target_pairs={{0,4},{1,5},{2,6},{3,7},{8,12},{9,13},{10,14},{11,15},{16,20},{17,... | collective-permute-start | bytes 276488 | tf_op jit(solution)/shard_map/ppermute | solution.py:26
  20.3 3.5 %collective-permute-start.6 = (bf16[144,320]{1,0:T(8,128)(2,1)S(1)}, bf16[144,320]{1,0:T(8,128)(2,1)S(1)}, u32[]{:S(2)}, u32[]{:S(2)}) collective-permute-start(bf16[144,320]{1,0:T(8,128)(2,1)S(1)} %fusion.1.refs_0_), channel_id=1, source_target_pairs={{0,2},{1,3},{2,4},{3,5},{4,6},{5,7},{8,10},{9,11},{10,12},{11,13},... | collective-permute-start | bytes 276488 | tf_op jit(solution)/shard_map/ppermute | solution.py:26
  23.8 1.9 collective-permute-done.7.refs_2_
  25.8 1.8 collective-permute-done.6.refs_1_
  27.7 5.2 %collective-permute-start.10 = (bf16[64,2048]{1,0:T(8,128)(2,1)}, bf16[64,2048]{1,0:T(8,128)(2,1)}, u32[]{:S(2)}, u32[]{:S(2)}) collective-permute-start(bf16[64,2048]{1,0:T(8,128)(2,1)} %collective-permute-done.1.refs_1_), channel_id=1, source_target_pairs={{0,2},{1,3},{2,0},{3,1},{4,6},{5,7},{6,4},{7,5},{8,10},{9,11},{10,... | collective-permute-start | bytes 786440 | tf_op jit(solution)/shard_map/ppermute | solution.py:31
  33.0 3.9 %collective-permute-start.13 = (bf16[64,2048]{1,0:T(8,128)(2,1)}, bf16[64,2048]{1,0:T(8,128)(2,1)}, u32[]{:S(2)}, u32[]{:S(2)}) collective-permute-start(bf16[64,2048]{1,0:T(8,128)(2,1)} %get-tuple-element.127.refs_0_), channel_id=1, source_target_pairs={{0,4},{1,5},{2,6},{3,7},{4,0},{5,1},{6,2},{7,3},{8,12},{9,13},{10,... | collective-permute-start | bytes 786440 | tf_op jit(solution)/shard_map/ppermute | solution.py:31
  37.0 2.1 collect.1
  39.1 6.9 %collective-permute-done.10.refs_3_ = bf16[64,2048]{1,0:T(8,128)(2,1)} collective-permute-done((bf16[64,2048]{1,0:T(8,128)(2,1)}, bf16[64,2048]{1,0:T(8,128)(2,1)}, u32[]{:S(2)}, u32[]{:S(2)}) %collective-permute-start.10) | collective-permute-done | bytes 262176 | tf_op jit(solution)/shard_map/ppermute | solution.py:31
  48.1 1.6 collective-permute-start.12
  49.7 1.5 collective-permute-start.11
  51.4 3.7 %collective-permute-start.15 = (bf16[64,2048]{1,0:T(8,128)(2,1)}, bf16[64,2048]{1,0:T(8,128)(2,1)S(1)}, u32[]{:S(2)}, u32[]{:S(2)}) collective-permute-start(bf16[64,2048]{1,0:T(8,128)(2,1)} %collective-permute-done.13.refs_1_), channel_id=1, source_target_pairs={{0,2},{1,3},{2,0},{3,1},{4,6},{5,7},{6,4},{7,5},{8,10},{9,11},{10,... | collective-permute-start | bytes 786440 | tf_op jit(solution)/shard_map/ppermute | solution.py:31
  55.0 6.3 %collective-permute-done.15.refs_3_ = bf16[64,2048]{1,0:T(8,128)(2,1)S(1)} collective-permute-done((bf16[64,2048]{1,0:T(8,128)(2,1)}, bf16[64,2048]{1,0:T(8,128)(2,1)S(1)}, u32[]{:S(2)}, u32[]{:S(2)}) %collective-permute-start.15) | collective-permute-done | bytes 262176 | tf_op jit(solution)/shard_map/ppermute | solution.py:31
  63.7 7.4 %heads_backward.8 = (bf16[128,8192]{1,0:T(8,128)(2,1)}, bf16[128,4096]{1,0:T(8,128)(2,1)}, bf16[128,6144]{1,0:T(8,128)(2,1)}, f32[128,1024]{1,0:T(8,128)S(1)}, f...) custom-call(s32[6]{0:T(128)S(1)} %copy-done.10, bf16[128,8192]{1,0:T(8,128)(2,1)S(1)} %bitcast.18, ...), custom_call_target="tpu_custom_call" | custom-call | flops 3000000000 | bytes 600000 | tf_op jit(solution)/shard_map/heads_backward/pallas_call | solution.py:158
  71.1 1.5 collective-permute-start.16
  72.6 1.5 collective-permute-start.17
  74.1 7.3 %heads_backward.9 = (bf16[128,8192]{1,0:T(8,128)(2,1)}, bf16[128,4096]{1,0:T(8,128)(2,1)}, bf16[128,6144]{1,0:T(8,128)(2,1)}, f32[128,1024]{1,0:T(8,128)S(1)}, f...) custom-call(s32[6]{0:T(128)S(1)} %copy-done.10, ...), custom_call_target="tpu_custom_call", output_to_operand_aliasing={{0}: (14, {}), {1}: (15, {}), {2}: (16, {})} | custom-call | flops 3000000000 | bytes 600000 | tf_op jit(solution)/shard_map/heads_backward/pallas_call | solution.py:158
  82.4 7.2 %heads_backward.10 = (bf16[128,8192]{1,0:T(8,128)(2,1)}, bf16[128,4096]{1,0:T(8,128)(2,1)}, bf16[128,6144]{1,0:T(8,128)(2,1)}, f32[128,1024]{1,0:T(8,128)S(1)}, ...) custom-call(s32[6]{0:T(128)S(1)} %copy-done.10, ...), custom_call_target="tpu_custom_call", output_to_operand_aliasing={{0}: (14, {}), {1}: (15, {}), {2}: (16, {})} | custom-call | flops 3000000000 | bytes 600000 | tf_op jit(solution)/shard_map/heads_backward/pallas_call | solution.py:158
  89.7 1.6 collective-permute-start.20
  91.3 7.2 %heads_backward.11 = (bf16[128,8192]{1,0:T(8,128)(2,1)}, bf16[128,4096]{1,0:T(8,128)(2,1)}, bf16[128,6144]{1,0:T(8,128)(2,1)}, f32[128,1024]{1,0:T(8,128)S(1)}, ...) custom-call(s32[6]{0:T(128)S(1)} %copy-done.10, ...), custom_call_target="tpu_custom_call", output_to_operand_aliasing={{0}: (14, {}), {1}: (15, {}), {2}: (16, {})} | custom-call | flops 3000000000 | bytes 600000 | tf_op jit(solution)/shard_map/heads_backward/pallas_call | solution.py:158
  98.5 1.5 collective-permute-start.22
  100.0 7.5 %heads_backward.12 = (bf16[128,8192]{1,0:T(8,128)(2,1)}, bf16[128,4096]{1,0:T(8,128)(2,1)}, bf16[128,6144]{1,0:T(8,128)(2,1)}, f32[128,1024]{1,0:T(8,128)S(1)}, ...) custom-call(s32[6]{0:T(128)S(1)} %copy-done.10, ...), custom_call_target="tpu_custom_call", output_to_operand_aliasing={{0}: (14, {}), {1}: (15, {}), {2}: (16, {})} | custom-call | flops 3000000000 | bytes 600000 | tf_op jit(solution)/shard_map/heads_backward/pallas_call | solution.py:158
  107.5 7.3 %heads_backward.13 = (bf16[128,8192]{1,0:T(8,128)(2,1)}, bf16[128,4096]{1,0:T(8,128)(2,1)}, bf16[128,6144]{1,0:T(8,128)(2,1)}, f32[128,1024]{1,0:T(8,128)S(1)}, ...) custom-call(s32[6]{0:T(128)S(1)} %copy-done.10, ...), custom_call_target="tpu_custom_call", output_to_operand_aliasing={{0}: (14, {}), {1}: (15, {}), {2}: (16, {})} | custom-call | flops 3000000000 | bytes 600000 | tf_op jit(solution)/shard_map/heads_backward/pallas_call | solution.py:158
  115.9 1.6 collective-permute-start.26
  117.5 7.3 %heads_backward.14 = (bf16[128,8192]{1,0:T(8,128)(2,1)}, bf16[128,4096]{1,0:T(8,128)(2,1)}, bf16[128,6144]{1,0:T(8,128)(2,1)}, f32[128,1024]{1,0:T(8,128)S(1)}, ...) custom-call(s32[6]{0:T(128)S(1)} %copy-done.10, ...), custom_call_target="tpu_custom_call", output_to_operand_aliasing={{0}: (14, {}), {1}: (15, {}), {2}: (16, {})} | custom-call | flops 3000000000 | bytes 600000 | tf_op jit(solution)/shard_map/heads_backward/pallas_call | solution.py:158
  124.8 4.9 %collective-permute-done.21 = f32[128,1024]{1,0:T(8,128)S(1)} collective-permute-done((f32[128,1024]{1,0:T(8,128)S(1)}, f32[128,1024]{1,0:T(8,128)S(1)}, u32[]{:S(2)}, u32[]{:S(2)}) %collective-permute-start.21) | collective-permute-done | bytes 524320 | tf_op jit(solution)/shard_map/ppermute | solution.py:31
  130.9 10.0 %collective-permute-done.26 = f32[128,1024]{1,0:T(8,128)S(1)} collective-permute-done((f32[128,1024]{1,0:T(8,128)S(1)}, f32[128,1024]{1,0:T(8,128)S(1)}, u32[]{:S(2)}, u32[]{:S(2)}) %collective-permute-start.26) | collective-permute-done | bytes 524320 | tf_op jit(solution)/shard_map/ppermute | solution.py:31
  141.0 1.8 collective-permute-start.28
  143.5 7.3 %heads_backward.15 = (bf16[128,8192]{1,0:T(8,128)(2,1)}, bf16[128,4096]{1,0:T(8,128)(2,1)}, bf16[128,6144]{1,0:T(8,128)(2,1)}, f32[128,1024]{1,0:T(8,128)S(1)}, ...) custom-call(s32[6]{0:T(128)S(1)} %copy-done.10, ...), custom_call_target="tpu_custom_call", output_to_operand_aliasing={{0}: (14, {}), {1}: (15, {}), {2}: (16, {})} | custom-call | flops 3000000000 | bytes 600000 | tf_op jit(solution)/shard_map/heads_backward/pallas_call | solution.py:158
  155.1 1.7 spread.1
  158.0 11.9 %collective-permute-done.35 = f32[64,1024]{1,0:T(8,128)} collective-permute-done((f32[64,1024]{1,0:T(8,128)}, f32[64,1024]{1,0:T(8,128)}, u32[]{:S(2)}, u32[]{:S(2)}) %collective-permute-start.35) | collective-permute-done | bytes 262176 | tf_op jit(solution)/shard_map/ppermute | solution.py:31
  172.1 1.6 add_add_fusion.2
  174.5 2.3 %collective-permute-start.32 = (f32[64,1024]{1,0:T(8,128)}, f32[64,1024]{1,0:T(8,128)}, u32[]{:S(2)}, u32[]{:S(2)}) collective-permute-start(f32[64,1024]{1,0:T(8,128)} %slice.34), channel_id=1, source_target_pairs={{0,4},{1,5},{2,6},{3,7},{4,0},{5,1},{6,2},{7,3},{8,12},{9,13},{10,... | collective-permute-start | bytes 786440 | tf_op jit(solution)/shard_map/ppermute | solution.py:31
  176.9 1.3 copy.43
  178.9 1.6 collective-permute-start.39
  181.0 1.5 collective-permute-start.37
  182.5 5.3 %collective-permute-done.32 = f32[64,1024]{1,0:T(8,128)} collective-permute-done((f32[64,1024]{1,0:T(8,128)}, f32[64,1024]{1,0:T(8,128)}, u32[]{:S(2)}, u32[]{:S(2)}) %collective-permute-start.32) | collective-permute-done | bytes 262176 | tf_op jit(solution)/shard_map/ppermute | solution.py:31
  191.5 2.7 %collective-permute-done.38.refs_4_ = f32[32,2048]{1,0:T(8,128)S(1)} collective-permute-done((f32[32,2048]{1,0:T(8,128)S(1)}, f32[32,2048]{1,0:T(8,128)S(1)}, u32[]{:S(2)}, u32[]{:S(2)}) %collective-permute-start.38) | collective-permute-done | bytes 262176 | tf_op jit(solution)/shard_map/ppermute | solution.py:31
  194.9 1.5 collective-permute-start.43
  197.0 1.5 collective-permute-start.41
  198.4 2.4 %place_columns.1 = (bf16[128,8192]{1,0:T(8,128)(2,1)}, bf16[128,4096]{1,0:T(8,128)(2,1)}) custom-call(s32[6]{0:T(128)S(1)} %copy-done.10, bf16[128,6144]{1,0:T(8,128)(2,1)S(1)} %collective-permute-done.24.received, bf16[128,8192]{1,0:T(8,128)(2,1)} %get-tuple-element.167.q_in, ...), custom_call_target="tpu_custom_call", output_to_operand_aliasing={{0}: (2, {}), {1}: (3, {})} | custom-call | bytes 4000000 | tf_op jit(solution)/shard_map/place_columns/pallas_call | solution.py:187
  200.8 2.1 collective-permute-done.34
  203.7 1.3 collective-permute-done.43.refs_7_
  205.1 4.6 %collective-permute-done.42.refs_5_ = f32[32,2048]{1,0:T(8,128)S(1)} collective-permute-done((f32[32,2048]{1,0:T(8,128)S(1)}, f32[32,2048]{1,0:T(8,128)S(1)}, u32[]{:S(2)}, u32[]{:S(2)}) %collective-permute-start.42) | collective-permute-done | bytes 262176 | tf_op jit(solution)/shard_map/ppermute | solution.py:31
  209.7 3.4 %lay_out.1 = f32[32,16384]{1,0:T(8,128)} custom-call(s32[6]{0:T(128)S(1)} %copy-done.10, f32[32,2048]{1,0:T(8,128)S(1)} %join_cores.2.refs_0_, f32[32,2048]{1,0:T(8,128)S(1)} %join_cores.3.refs_1_, f32[32,2048]{1,0:T(8,128)S(1)} %collective-permute-done.37.refs_2_, f32[32,2048]{1,0:T(8,128)} %collective-permute-done.41.refs_3_, ...), custom_call_target="tpu_custom_call" | custom-call | bytes 4000000 | tf_op jit(solution)/shard_map/lay_out/pallas_call | solution.py:288
  (126 shorter events, 28.8 us)
Async XLA Ops:
  0.6 3.0 %collective-permute-start = (bf16[32,16384]{1,0:T(8,128)(2,1)}, bf16[32,16384]{1,0:T(8,128)(2,1)S(1)}, u32[]{:S(2)}, u32[]{:S(2)}) collective-permute-start(bf16[32,16384]{1,0:T(8,128)(2,1)} %distant.1), channel_id=1, source_target_pairs={{0,1},{1,0},{2,3},{3,2},{4,5},{5,4},{6,7},{7,6},{8,9},{9,8},{10,11... | collective-permute-start | bytes 3145736 | tf_op jit(solution)/shard_map/ppermute | solution.py:31
  4.6 10.1 %collective-permute-start.2 = (bf16[128,8192]{1,0:T(8,128)(2,1)}, bf16[128,8192]{1,0:T(8,128)(2,1)S(1)}, u32[]{:S(2)}, u32[]{:S(2)}) collective-permute-start(bf16[128,8192]{1,0:T(8,128)(2,1)} %bitcast.17), channel_id=1, source_target_pairs={{0,1},{1,0},{2,3},{3,2},{4,5},{5,4},{6,7},{7,6},{8,9},{9,8},{10,11... | collective-permute-start | bytes 6291464 | tf_op jit(solution)/shard_map/ppermute | solution.py:31
  5.0 9.7 %collective-permute-start.4 = (bf16[128,8192]{1,0:T(8,128)(2,1)}, bf16[128,8192]{1,0:T(8,128)(2,1)}, u32[]{:S(2)}, u32[]{:S(2)}) collective-permute-start(bf16[128,8192]{1,0:T(8,128)(2,1)} %bitcast.26), channel_id=1, source_target_pairs={{0,1},{1,0},{2,3},{3,2},{4,5},{5,4},{6,7},{7,6},{8,9},{9,8},{10,11... | collective-permute-start | bytes 6291464 | tf_op jit(solution)/shard_map/ppermute | solution.py:31
  5.1 31.7 %copy-start.5 = (f32[1,64,128]{2,1,0:T(8,128)S(1)}, f32[1,64,128]{2,1,0:T(8,128)}, u32[]{:S(2)}) copy-start(f32[1,64,128]{2,1,0:T(8,128)} %param.11) | copy-start | bytes 98308
  5.1 31.7 %copy-start.19 = (s32[1,8,4]{1,2,0:T(4,128)S(1)}, s32[1,8,4]{1,2,0:T(4,128)}, u32[]{:S(2)}) copy-start(s32[1,8,4]{1,2,0:T(4,128)} %param.15) | copy-start | bytes 388
  5.1 31.8 %copy-start.10 = (s32[6]{0:T(128)S(1)}, s32[6]{0:T(128)}, u32[]{:S(2)}) copy-start(s32[6]{0:T(128)} %stack.30.place) | copy-start | bytes 76
  5.1 8.6 %collective-permute-start.3 = (bf16[128,4096]{1,0:T(8,128)(2,1)}, bf16[128,4096]{1,0:T(8,128)(2,1)S(1)}, u32[]{:S(2)}, u32[]{:S(2)}) collective-permute-start(bf16[128,4096]{1,0:T(8,128)(2,1)} %bitcast.35), channel_id=1, source_target_pairs={{0,1},{1,0},{2,3},{3,2},{4,5},{5,4},{6,7},{7,6},{8,9},{9,8},{10,11... | collective-permute-start | bytes 3145736 | tf_op jit(solution)/shard_map/ppermute | solution.py:31
  8.2 19.5 %collective-permute-start.9 = (bf16[64,2048]{1,0:T(8,128)(2,1)}, bf16[64,2048]{1,0:T(8,128)(2,1)}, u32[]{:S(2)}, u32[]{:S(2)}) collective-permute-start(bf16[64,2048]{1,0:T(8,128)(2,1)} %get-tuple-element.120.refs_0_), channel_id=1, source_target_pairs={{0,2},{1,3},{2,0},{3,1},{4,6},{5,7},{6,4},{7,5},{8,10},{9,11},{10,... | collective-permute-start | bytes 786440 | tf_op jit(solution)/shard_map/ppermute | solution.py:31
  10.9 16.8 %collective-permute-start.1 = (bf16[64,2048]{1,0:T(8,128)(2,1)}, bf16[64,2048]{1,0:T(8,128)(2,1)}, u32[]{:S(2)}, u32[]{:S(2)}) collective-permute-start(bf16[64,2048]{1,0:T(8,128)(2,1)} %get-tuple-element.120.refs_0_), channel_id=1, source_target_pairs={{0,4},{1,5},{2,6},{3,7},{4,0},{5,1},{6,2},{7,3},{8,12},{9,13},{10,... | collective-permute-start | bytes 786440 | tf_op jit(solution)/shard_map/ppermute | solution.py:31
  14.7 11.1 %collective-permute-start.7 = (bf16[144,320]{1,0:T(8,128)(2,1)S(1)}, bf16[144,320]{1,0:T(8,128)(2,1)S(1)}, u32[]{:S(2)}, u32[]{:S(2)}) collective-permute-start(bf16[144,320]{1,0:T(8,128)(2,1)S(1)} %fusion.1.refs_0_), channel_id=1, source_target_pairs={{0,4},{1,5},{2,6},{3,7},{8,12},{9,13},{10,14},{11,15},{16,20},{17,... | collective-permute-start | bytes 276488 | tf_op jit(solution)/shard_map/ppermute | solution.py:26
  20.3 7.3 %collective-permute-start.6 = (bf16[144,320]{1,0:T(8,128)(2,1)S(1)}, bf16[144,320]{1,0:T(8,128)(2,1)S(1)}, u32[]{:S(2)}, u32[]{:S(2)}) collective-permute-start(bf16[144,320]{1,0:T(8,128)(2,1)S(1)} %fusion.1.refs_0_), channel_id=1, source_target_pairs={{0,2},{1,3},{2,4},{3,5},{4,6},{5,7},{8,10},{9,11},{10,12},{11,13},... | collective-permute-start | bytes 276488 | tf_op jit(solution)/shard_map/ppermute | solution.py:26
  27.6 34.9 %copy-start.2 = (bf16[1,128,4096]{2,1,0:T(8,128)(2,1)S(1)}, bf16[1,128,4096]{2,1,0:T(8,128)(2,1)}, u32[]{:S(2)}) copy-start(bf16[1,128,4096]{2,1,0:T(8,128)(2,1)} %param.9) | copy-start | bytes 3145732
  27.6 9.3 %collective-permute-start.8 = (bf16[432,320]{1,0:T(8,128)(2,1)S(1)}, bf16[432,320]{1,0:T(8,128)(2,1)}, u32[]{:S(2)}, u32[]{:S(2)}) collective-permute-start(bf16[432,320]{1,0:T(8,128)(2,1)S(1)} %stack.31.own), channel_id=1, source_target_pairs={{0,1},{1,0},{2,3},{3,2},{4,5},{5,4},{6,7},{7,6},{8,9},{9,8},{10,11... | collective-permute-start | bytes 829448 | tf_op jit(solution)/shard_map/ppermute | solution.py:31
  27.7 18.3 %collective-permute-start.10 = (bf16[64,2048]{1,0:T(8,128)(2,1)}, bf16[64,2048]{1,0:T(8,128)(2,1)}, u32[]{:S(2)}, u32[]{:S(2)}) collective-permute-start(bf16[64,2048]{1,0:T(8,128)(2,1)} %collective-permute-done.1.refs_1_), channel_id=1, source_target_pairs={{0,2},{1,3},{2,0},{3,1},{4,6},{5,7},{6,4},{7,5},{8,10},{9,11},{10,... | collective-permute-start | bytes 786440 | tf_op jit(solution)/shard_map/ppermute | solution.py:31
  32.9 18.4 %collective-permute-start.14 = (bf16[64,2048]{1,0:T(8,128)(2,1)}, bf16[64,2048]{1,0:T(8,128)(2,1)}, u32[]{:S(2)}, u32[]{:S(2)}) collective-permute-start(bf16[64,2048]{1,0:T(8,128)(2,1)} %get-tuple-element.127.refs_0_), channel_id=1, source_target_pairs={{0,2},{1,3},{2,0},{3,1},{4,6},{5,7},{6,4},{7,5},{8,10},{9,11},{10,... | collective-permute-start | bytes 786440 | tf_op jit(solution)/shard_map/ppermute | solution.py:31
  33.0 18.4 %collective-permute-start.13 = (bf16[64,2048]{1,0:T(8,128)(2,1)}, bf16[64,2048]{1,0:T(8,128)(2,1)}, u32[]{:S(2)}, u32[]{:S(2)}) collective-permute-start(bf16[64,2048]{1,0:T(8,128)(2,1)} %get-tuple-element.127.refs_0_), channel_id=1, source_target_pairs={{0,4},{1,5},{2,6},{3,7},{4,0},{5,1},{6,2},{7,3},{8,12},{9,13},{10,... | collective-permute-start | bytes 786440 | tf_op jit(solution)/shard_map/ppermute | solution.py:31
  36.9 2.2 %collective-permute-start.5 = (f32[64,128]{1,0:T(8,128)S(1)}, f32[64,128]{1,0:T(8,128)S(1)}, u32[]{:S(2)}, u32[]{:S(2)}) collective-permute-start(f32[64,128]{1,0:T(8,128)S(1)} %bitcast.44), channel_id=1, source_target_pairs={{0,1},{1,0},{2,3},{3,2},{4,5},{5,4},{6,7},{7,6},{8,9},{9,8},{10,11... | collective-permute-start | bytes 98312 | tf_op jit(solution)/shard_map/ppermute | solution.py:31
  48.1 33.8 %collective-permute-start.12 = (bf16[256,2048]{1,0:T(8,128)(2,1)S(1)}, bf16[256,2048]{1,0:T(8,128)(2,1)S(1)}, u32[]{:S(2)}, u32[]{:S(2)}) collective-permute-start(bf16[256,2048]{1,0:T(8,128)(2,1)S(1)} %stack.32.weight), channel_id=1, source_target_pairs={{0,8},{8,0},{16,24},{24,16},{1,9},{9,1},{17,25},{25,17},{2,10},{10... | collective-permute-start | bytes 3145736 | tf_op jit(solution)/shard_map/ppermute | solution.py:31
  49.7 32.8 %collective-permute-start.11 = (bf16[256,2048]{1,0:T(8,128)(2,1)S(1)}, bf16[256,2048]{1,0:T(8,128)(2,1)S(1)}, u32[]{:S(2)}, u32[]{:S(2)}) collective-permute-start(bf16[256,2048]{1,0:T(8,128)(2,1)S(1)} %stack.32.weight), channel_id=1, source_target_pairs={{0,16},{8,24},{16,0},{24,8},{1,17},{9,25},{17,1},{25,9},{2,18},{10... | collective-permute-start | bytes 3145736 | tf_op jit(solution)/shard_map/ppermute | solution.py:31
  51.4 10.0 %collective-permute-start.15 = (bf16[64,2048]{1,0:T(8,128)(2,1)}, bf16[64,2048]{1,0:T(8,128)(2,1)S(1)}, u32[]{:S(2)}, u32[]{:S(2)}) collective-permute-start(bf16[64,2048]{1,0:T(8,128)(2,1)} %collective-permute-done.13.refs_1_), channel_id=1, source_target_pairs={{0,2},{1,3},{2,0},{3,1},{4,6},{5,7},{6,4},{7,5},{8,10},{9,11},{10,... | collective-permute-start | bytes 786440 | tf_op jit(solution)/shard_map/ppermute | solution.py:31
  71.1 18.6 %collective-permute-start.16 = (f32[128,1024]{1,0:T(8,128)S(1)}, f32[128,1024]{1,0:T(8,128)S(1)}, u32[]{:S(2)}, u32[]{:S(2)}) collective-permute-start(f32[128,1024]{1,0:T(8,128)S(1)} %get-tuple-element.136), channel_id=1, source_target_pairs={{0,8},{8,0},{16,24},{24,16},{1,9},{9,1},{17,25},{25,17},{2,10},{10... | collective-permute-start | bytes 1572872 | tf_op jit(solution)/shard_map/ppermute | solution.py:31
  72.6 17.1 %collective-permute-start.17 = (f32[128,1024]{1,0:T(8,128)S(1)}, f32[128,1024]{1,0:T(8,128)S(1)}, u32[]{:S(2)}, u32[]{:S(2)}) collective-permute-start(f32[128,1024]{1,0:T(8,128)S(1)} %get-tuple-element.137), channel_id=1, source_target_pairs={{0,16},{8,24},{16,0},{24,8},{1,17},{9,25},{17,1},{25,9},{2,18},{10... | collective-permute-start | bytes 1572872 | tf_op jit(solution)/shard_map/ppermute | solution.py:31
  81.4 26.1 %collective-permute-start.18 = (f32[128,1024]{1,0:T(8,128)S(1)}, f32[128,1024]{1,0:T(8,128)S(1)}, u32[]{:S(2)}, u32[]{:S(2)}) collective-permute-start(f32[128,1024]{1,0:T(8,128)S(1)} %get-tuple-element.146), channel_id=1, source_target_pairs={{0,8},{8,0},{16,24},{24,16},{1,9},{9,1},{17,25},{25,17},{2,10},{10... | collective-permute-start | bytes 1572872 | tf_op jit(solution)/shard_map/ppermute | solution.py:31
  81.9 25.6 %collective-permute-start.19 = (f32[128,1024]{1,0:T(8,128)S(1)}, f32[128,1024]{1,0:T(8,128)S(1)}, u32[]{:S(2)}, u32[]{:S(2)}) collective-permute-start(f32[128,1024]{1,0:T(8,128)S(1)} %get-tuple-element.147), channel_id=1, source_target_pairs={{0,16},{8,24},{16,0},{24,8},{1,17},{9,25},{17,1},{25,9},{2,18},{10... | collective-permute-start | bytes 1572872 | tf_op jit(solution)/shard_map/ppermute | solution.py:31
  89.7 25.1 %collective-permute-start.20 = (f32[128,1024]{1,0:T(8,128)S(1)}, f32[128,1024]{1,0:T(8,128)S(1)}, u32[]{:S(2)}, u32[]{:S(2)}) collective-permute-start(f32[128,1024]{1,0:T(8,128)S(1)} %get-tuple-element.156), channel_id=1, source_target_pairs={{0,8},{8,0},{16,24},{24,16},{1,9},{9,1},{17,25},{25,17},{2,10},{10... | collective-permute-start | bytes 1572872 | tf_op jit(solution)/shard_map/ppermute | solution.py:31
  98.5 16.9 %collective-permute-start.22 = (f32[128,1024]{1,0:T(8,128)S(1)}, f32[128,1024]{1,0:T(8,128)S(1)}, u32[]{:S(2)}, u32[]{:S(2)}) collective-permute-start(f32[128,1024]{1,0:T(8,128)S(1)} %get-tuple-element.159), channel_id=1, source_target_pairs={{0,16},{8,24},{16,0},{24,8},{1,17},{9,25},{17,1},{25,9},{2,18},{10... | collective-permute-start | bytes 1572872 | tf_op jit(solution)/shard_map/ppermute | solution.py:31
  114.8 14.9 %collective-permute-start.21 = (f32[128,1024]{1,0:T(8,128)S(1)}, f32[128,1024]{1,0:T(8,128)S(1)}, u32[]{:S(2)}, u32[]{:S(2)}) collective-permute-start(f32[128,1024]{1,0:T(8,128)S(1)} %get-tuple-element.158), channel_id=1, source_target_pairs={{0,8},{8,0},{16,24},{24,16},{1,9},{9,1},{17,25},{25,17},{2,10},{10... | collective-permute-start | bytes 1572872 | tf_op jit(solution)/shard_map/ppermute | solution.py:31
  115.4 14.3 %collective-permute-start.23 = (f32[128,1024]{1,0:T(8,128)S(1)}, f32[128,1024]{1,0:T(8,128)S(1)}, u32[]{:S(2)}, u32[]{:S(2)}) collective-permute-start(f32[128,1024]{1,0:T(8,128)S(1)} %get-tuple-element.161), channel_id=1, source_target_pairs={{0,16},{8,24},{16,0},{24,8},{1,17},{9,25},{17,1},{25,9},{2,18},{10... | collective-permute-start | bytes 1572872 | tf_op jit(solution)/shard_map/ppermute | solution.py:31
  115.9 25.0 %collective-permute-start.26 = (f32[128,1024]{1,0:T(8,128)S(1)}, f32[128,1024]{1,0:T(8,128)S(1)}, u32[]{:S(2)}, u32[]{:S(2)}) collective-permute-start(f32[128,1024]{1,0:T(8,128)S(1)} %add.66), channel_id=1, source_target_pairs={{0,8},{8,0},{16,24},{24,16},{1,9},{9,1},{17,25},{25,17},{2,10},{10... | collective-permute-start | bytes 1572872 | tf_op jit(solution)/shard_map/ppermute | solution.py:31
  129.7 11.3 %collective-permute-start.27 = (f32[128,1024]{1,0:T(8,128)S(1)}, f32[128,1024]{1,0:T(8,128)S(1)}, u32[]{:S(2)}, u32[]{:S(2)}) collective-permute-start(f32[128,1024]{1,0:T(8,128)S(1)} %add.68), channel_id=1, source_target_pairs={{0,16},{8,24},{16,0},{24,8},{1,17},{9,25},{17,1},{25,9},{2,18},{10... | collective-permute-start | bytes 1572872 | tf_op jit(solution)/shard_map/ppermute | solution.py:31
  130.3 20.6 %collective-permute-start.30 = (f32[128,1024]{1,0:T(8,128)S(1)}, f32[128,1024]{1,0:T(8,128)S(1)}, u32[]{:S(2)}, u32[]{:S(2)}) collective-permute-start(f32[128,1024]{1,0:T(8,128)S(1)} %add.73), channel_id=1, source_target_pairs={{0,8},{8,0},{16,24},{24,16},{1,9},{9,1},{17,25},{25,17},{2,10},{10... | collective-permute-start | bytes 1572872 | tf_op jit(solution)/shard_map/ppermute | solution.py:31
  141.0 9.8 %collective-permute-start.28 = (f32[128,1024]{1,0:T(8,128)S(1)}, f32[128,1024]{1,0:T(8,128)S(1)}, u32[]{:S(2)}, u32[]{:S(2)}) collective-permute-start(f32[128,1024]{1,0:T(8,128)S(1)} %add_add_fusion.3), channel_id=1, source_target_pairs={{0,2},{1,3},{2,0},{3,1},{4,6},{5,7},{6,4},{7,5},{8,10},{9,11},{10,... | collective-permute-start | bytes 1572872 | tf_op jit(solution)/shard_map/ppermute | solution.py:31
  142.9 9.2 %collective-permute-start.29 = (f32[128,1024]{1,0:T(8,128)S(1)}, f32[128,1024]{1,0:T(8,128)S(1)}, u32[]{:S(2)}, u32[]{:S(2)}) collective-permute-start(f32[128,1024]{1,0:T(8,128)S(1)} %add.70), channel_id=1, source_target_pairs={{0,16},{8,24},{16,0},{24,8},{1,17},{9,25},{17,1},{25,9},{2,18},{10... | collective-permute-start | bytes 1572872 | tf_op jit(solution)/shard_map/ppermute | solution.py:31
  150.7 22.9 %collective-permute-start.24 = (bf16[128,6144]{1,0:T(8,128)(2,1)}, bf16[128,6144]{1,0:T(8,128)(2,1)S(1)}, u32[]{:S(2)}, u32[]{:S(2)}) collective-permute-start(bf16[128,6144]{1,0:T(8,128)(2,1)} %get-tuple-element.166), channel_id=1, source_target_pairs={{0,1},{1,0},{2,3},{3,2},{4,5},{5,4},{6,7},{7,6},{8,9},{9,8},{10,11... | collective-permute-start | bytes 4718600 | tf_op jit(solution)/shard_map/ppermute | solution.py:31
  153.1 18.9 %collective-permute-start.31 = (f32[128,1024]{1,0:T(8,128)}, f32[128,1024]{1,0:T(8,128)}, u32[]{:S(2)}, u32[]{:S(2)}) collective-permute-start(f32[128,1024]{1,0:T(8,128)} %add_add_fusion.1), channel_id=1, source_target_pairs={{0,2},{1,3},{2,0},{3,1},{4,6},{5,7},{6,4},{7,5},{8,10},{9,11},{10,... | collective-permute-start | bytes 1572872 | tf_op jit(solution)/shard_map/ppermute | solution.py:31
  154.4 15.5 %collective-permute-start.35 = (f32[64,1024]{1,0:T(8,128)}, f32[64,1024]{1,0:T(8,128)}, u32[]{:S(2)}, u32[]{:S(2)}) collective-permute-start(f32[64,1024]{1,0:T(8,128)} %slice.45), channel_id=1, source_target_pairs={{0,4},{1,5},{2,6},{3,7},{4,0},{5,1},{6,2},{7,3},{8,12},{9,13},{10,... | collective-permute-start | bytes 786440 | tf_op jit(solution)/shard_map/ppermute | solution.py:31
  157.9 15.7 %collective-permute-start.25 = (f32[432,320]{0,1:T(8,128)}, f32[432,320]{0,1:T(8,128)S(1)}, u32[]{:S(2)}, u32[]{:S(2)}) collective-permute-start(f32[432,320]{0,1:T(8,128)} %copy.42), channel_id=1, source_target_pairs={{0,1},{1,0},{2,3},{3,2},{4,5},{5,4},{6,7},{7,6},{8,9},{9,8},{10,11... | collective-permute-start | bytes 1658888 | tf_op jit(solution)/shard_map/ppermute | solution.py:31
  174.5 13.3 %collective-permute-start.32 = (f32[64,1024]{1,0:T(8,128)}, f32[64,1024]{1,0:T(8,128)}, u32[]{:S(2)}, u32[]{:S(2)}) collective-permute-start(f32[64,1024]{1,0:T(8,128)} %slice.34), channel_id=1, source_target_pairs={{0,4},{1,5},{2,6},{3,7},{4,0},{5,1},{6,2},{7,3},{8,12},{9,13},{10,... | collective-permute-start | bytes 786440 | tf_op jit(solution)/shard_map/ppermute | solution.py:31
  176.8 1.5 collective-permute-start.36
  178.9 12.5 %collective-permute-start.39 = (f32[32,2048]{1,0:T(8,128)S(1)}, f32[32,2048]{1,0:T(8,128)S(1)}, u32[]{:S(2)}, u32[]{:S(2)}) collective-permute-start(f32[32,2048]{1,0:T(8,128)S(1)} %join_cores.2.refs_0_), channel_id=1, source_target_pairs={{0,24},{8,16},{16,8},{24,0},{1,25},{9,17},{17,9},{25,1},{2,26},{10... | collective-permute-start | bytes 786440 | tf_op jit(solution)/shard_map/ppermute | solution.py:31
  180.5 13.7 %collective-permute-start.38 = (f32[32,2048]{1,0:T(8,128)S(1)}, f32[32,2048]{1,0:T(8,128)S(1)}, u32[]{:S(2)}, u32[]{:S(2)}) collective-permute-start(f32[32,2048]{1,0:T(8,128)S(1)} %join_cores.2.refs_0_), channel_id=1, source_target_pairs={{0,16},{8,24},{16,0},{24,8},{1,17},{9,25},{17,1},{25,9},{2,18},{10... | collective-permute-start | bytes 786440 | tf_op jit(solution)/shard_map/ppermute | solution.py:31
  181.0 13.3 %collective-permute-start.37 = (f32[32,2048]{1,0:T(8,128)S(1)}, f32[32,2048]{1,0:T(8,128)S(1)}, u32[]{:S(2)}, u32[]{:S(2)}) collective-permute-start(f32[32,2048]{1,0:T(8,128)S(1)} %join_cores.2.refs_0_), channel_id=1, source_target_pairs={{0,8},{8,0},{16,24},{24,16},{1,9},{9,1},{17,25},{25,17},{2,10},{10... | collective-permute-start | bytes 786440 | tf_op jit(solution)/shard_map/ppermute | solution.py:31
  188.8 12.0 %collective-permute-start.33 = (f32[128,320]{1,0:T(8,128)S(1)}, f32[128,320]{1,0:T(8,128)S(1)}, u32[]{:S(2)}, u32[]{:S(2)}) collective-permute-start(f32[128,320]{1,0:T(8,128)S(1)} %get-tuple-element.218), channel_id=1, source_target_pairs={{2,0},{3,1},{4,2},{5,3},{6,4},{7,5},{10,8},{11,9},{12,10},{13,11},... | collective-permute-start | bytes 491528 | tf_op jit(solution)/shard_map/ppermute | solution.py:26
  190.1 12.8 %collective-permute-start.34 = (f32[128,320]{1,0:T(8,128)S(1)}, f32[128,320]{1,0:T(8,128)S(1)}, u32[]{:S(2)}, u32[]{:S(2)}) collective-permute-start(f32[128,320]{1,0:T(8,128)S(1)} %get-tuple-element.219), channel_id=1, source_target_pairs={{4,0},{5,1},{6,2},{7,3},{12,8},{13,9},{14,10},{15,11},{20,16},{21,... | collective-permute-start | bytes 491528 | tf_op jit(solution)/shard_map/ppermute | solution.py:26
  191.4 2.9 %collective-permute-start.40 = (f32[32,1024]{1,0:T(8,128)S(1)}, f32[32,1024]{1,0:T(8,128)S(1)}, u32[]{:S(2)}, u32[]{:S(2)}) collective-permute-start(f32[32,1024]{1,0:T(8,128)S(1)} %get-tuple-element.220), channel_id=1, source_target_pairs={{0,1},{1,0},{2,3},{3,2},{4,5},{5,4},{6,7},{7,6},{8,9},{9,8},{10,11... | collective-permute-start | bytes 393224 | tf_op jit(solution)/shard_map/ppermute | solution.py:31
  194.9 10.2 %collective-permute-start.43 = (f32[32,2048]{1,0:T(8,128)S(1)}, f32[32,2048]{1,0:T(8,128)S(1)}, u32[]{:S(2)}, u32[]{:S(2)}) collective-permute-start(f32[32,2048]{1,0:T(8,128)S(1)} %join_cores.3.refs_1_), channel_id=1, source_target_pairs={{0,24},{8,16},{16,8},{24,0},{1,25},{9,17},{17,9},{25,1},{2,26},{10... | collective-permute-start | bytes 786440 | tf_op jit(solution)/shard_map/ppermute | solution.py:31
  196.3 13.3 %collective-permute-start.42 = (f32[32,2048]{1,0:T(8,128)S(1)}, f32[32,2048]{1,0:T(8,128)S(1)}, u32[]{:S(2)}, u32[]{:S(2)}) collective-permute-start(f32[32,2048]{1,0:T(8,128)S(1)} %join_cores.3.refs_1_), channel_id=1, source_target_pairs={{0,16},{8,24},{16,0},{24,8},{1,17},{9,25},{17,1},{25,9},{2,18},{10... | collective-permute-start | bytes 786440 | tf_op jit(solution)/shard_map/ppermute | solution.py:31
  197.0 12.7 %collective-permute-start.41 = (f32[32,2048]{1,0:T(8,128)S(1)}, f32[32,2048]{1,0:T(8,128)}, u32[]{:S(2)}, u32[]{:S(2)}) collective-permute-start(f32[32,2048]{1,0:T(8,128)S(1)} %join_cores.3.refs_1_), channel_id=1, source_target_pairs={{0,8},{8,0},{16,24},{24,16},{1,9},{9,1},{17,25},{25,17},{2,10},{10... | collective-permute-start | bytes 786440 | tf_op jit(solution)/shard_map/ppermute | solution.py:31
  (17 other events, 142.1 us)

commit v13 on v11

--- a/solution.py
+++ b/solution.py
@@ -164,7 +164,7 @@
         input_output_aliases=aliases,
         compiler_params=pltpu.CompilerParams(vmem_limit_bytes=KERNEL_BYTES),
         cost_estimate=pl.CostEstimate(
-            flops=count * 100_000_000, bytes_accessed=count * 300_000, transcendentals=0
+            flops=count * 1_000_000_000, bytes_accessed=count * 300_000, transcendentals=0
         ),
         name="heads_backward",
     )(place, *operands)

time: 211 us -> 208 us (0.986)
  starting transfers between devices: 59.3 us -> 55.9 us
  local copies, waits for them, and re-layouts: 9.94 us -> 12.8 us
    ppermute x4, waiting for transfers between devices: 7.4 us -> 3.49 us  [from_behind(): lax.ppermute(value, axis, [(source, source + steps) for source in range(i...]
    ppermute x37, waiting for transfers between devices: 55.8 us -> 58.4 us  [exchange(): lax.ppermute(value, axis, [(source, source ^ bits) for source in range(co...]
    ppermute x37, starting transfers between devices: 47.6 us -> 45.1 us  [exchange(): lax.ppermute(value, axis, [(source, source ^ bits) for source in range(co...]
    unnamed x43 -> x49, local copies, waits for them, and re-layouts: 4.96 us -> 6.91 us
  transfers between devices with their start and end apart: 41 -> 41, of which waited for: 17 -> 19; matrix products, arithmetic and copies ran while one was open for 5% -> 5% of each run, Pallas kernels for 32% -> 32%
where the time goes in v13:
time: 208 us; the launch traced here: 207 us
  Pallas kernels  70.5 us (34%)
  waiting for transfers between devices  61.9 us (30%)
  starting transfers between devices  55.9 us (27%)
  local copies, waits for them, and re-layouts  12.8 us (6%)
  other arithmetic  5.32 us (3%)
    ppermute x37, waiting for transfers between devices, exchange(): lax.ppermute(value, axis, [(source, source ^ bits) for source in range(co...  58.4 us
    pallas_call x6, Pallas kernels, chunk_backward(): pl.pallas_call(functools.partial(heads_kernel, earlier=len(aliases)), gri...  55.1 us
    ppermute x37, starting transfers between devices, exchange(): lax.ppermute(value, axis, [(source, source ^ bits) for source in range(co...  45.1 us
    ppermute x4, starting transfers between devices, from_behind(): lax.ppermute(value, axis, [(source, source + steps) for source in range(i...  10.8 us
    unnamed x49, local copies, waits for them, and re-layouts  6.91 us
  transfers between devices with their start and end apart: 41, of which 19 were waited for; matrix products, arithmetic and copies ran while one was open for 5% of the time, Pallas kernels for 32%

profile of v13, /device:TPU:0, one launch (start us, length us, event | category | flops | bytes accessed | tf_op | source)
XLA Modules:
  0.0 207.5 jit_solution(6387360508580285377)
XLA Ops:
  1.7 1.9 collective-permute-done.near_crossed.distant_crossed
  5.6 2.6 %weight_parts.1 = (bf16[64,2048]{1,0:T(8,128)(2,1)}, bf16[64,2048]{1,0:T(8,128)(2,1)}) custom-call(s32[6]{0:T(128)} %stack.30.place, bf16[32,16384]{1,0:T(8,128)(2,1)} %distant.1, bf16[32,16384]{1,0:T(8,128)(2,1)} %distant.1, bf16[32,16384]{1,0:T(8,128)(2,1)} %copy-done.15, bf16[32,16384]{1,0:T(8,128)(2,1)} %copy-done.15), custom_call_target="tpu_custom_call" | custom-call | bytes 1000000 | tf_op jit(solution)/shard_map/weight_parts/pallas_call | solution.py:256
  8.1 3.7 %collective-permute-start.1 = (bf16[64,2048]{1,0:T(8,128)(2,1)}, bf16[64,2048]{1,0:T(8,128)(2,1)S(1)}, u32[]{:S(2)}, u32[]{:S(2)}) collective-permute-start(bf16[64,2048]{1,0:T(8,128)(2,1)} %get-tuple-element.103.refs_0_), channel_id=1, source_target_pairs={{0,4},{1,5},{2,6},{3,7},{4,0},{5,1},{6,2},{7,3},{8,12},{9,13},{10,... | collective-permute-start | bytes 786440 | tf_op jit(solution)/shard_map/ppermute | solution.py:31
  11.9 1.6 collective-permute-start.9
  15.6 4.8 %collective-permute-start.7 = (bf16[144,320]{1,0:T(8,128)(2,1)S(1)}, bf16[144,320]{1,0:T(8,128)(2,1)S(1)}, u32[]{:S(2)}, u32[]{:S(2)}) collective-permute-start(bf16[144,320]{1,0:T(8,128)(2,1)S(1)} %fusion.3.refs_0_), channel_id=1, source_target_pairs={{0,4},{1,5},{2,6},{3,7},{8,12},{9,13},{10,14},{11,15},{16,20},{17,... | collective-permute-start | bytes 276488 | tf_op jit(solution)/shard_map/ppermute | solution.py:26
  20.3 3.5 %collective-permute-start.6 = (bf16[144,320]{1,0:T(8,128)(2,1)S(1)}, bf16[144,320]{1,0:T(8,128)(2,1)S(1)}, u32[]{:S(2)}, u32[]{:S(2)}) collective-permute-start(bf16[144,320]{1,0:T(8,128)(2,1)S(1)} %fusion.3.refs_0_), channel_id=1, source_target_pairs={{0,2},{1,3},{2,4},{3,5},{4,6},{5,7},{8,10},{9,11},{10,12},{11,13},... | collective-permute-start | bytes 276488 | tf_op jit(solution)/shard_map/ppermute | solution.py:26
  25.8 3.5 %collective-permute-start.13 = (bf16[64,2048]{1,0:T(8,128)(2,1)}, bf16[64,2048]{1,0:T(8,128)(2,1)}, u32[]{:S(2)}, u32[]{:S(2)}) collective-permute-start(bf16[64,2048]{1,0:T(8,128)(2,1)} %get-tuple-element.110.refs_0_), channel_id=1, source_target_pairs={{0,4},{1,5},{2,6},{3,7},{4,0},{5,1},{6,2},{7,3},{8,12},{9,13},{10,... | collective-permute-start | bytes 786440 | tf_op jit(solution)/shard_map/ppermute | solution.py:31
  29.5 3.2 %collective-permute-start.10 = (bf16[64,2048]{1,0:T(8,128)(2,1)}, bf16[64,2048]{1,0:T(8,128)(2,1)}, u32[]{:S(2)}, u32[]{:S(2)}) collective-permute-start(bf16[64,2048]{1,0:T(8,128)(2,1)} %copy-done.10), channel_id=1, source_target_pairs={{0,2},{1,3},{2,0},{3,1},{4,6},{5,7},{6,4},{7,5},{8,10},{9,11},{10,... | collective-permute-start | bytes 786440 | tf_op jit(solution)/shard_map/ppermute | solution.py:31
  32.7 6.8 %collective-permute-done.14.refs_2_ = bf16[64,2048]{1,0:T(8,128)(2,1)S(1)} collective-permute-done((bf16[64,2048]{1,0:T(8,128)(2,1)}, bf16[64,2048]{1,0:T(8,128)(2,1)S(1)}, u32[]{:S(2)}, u32[]{:S(2)}) %collective-permute-start.14) | collective-permute-done | bytes 262176 | tf_op jit(solution)/shard_map/ppermute | solution.py:31
  41.0 2.8 %collective-permute-start.15 = (bf16[64,2048]{1,0:T(8,128)(2,1)}, bf16[64,2048]{1,0:T(8,128)(2,1)}, u32[]{:S(2)}, u32[]{:S(2)}) collective-permute-start(bf16[64,2048]{1,0:T(8,128)(2,1)} %collective-permute-done.13.refs_1_), channel_id=1, source_target_pairs={{0,2},{1,3},{2,0},{3,1},{4,6},{5,7},{6,4},{7,5},{8,10},{9,11},{10,... | collective-permute-start | bytes 786440 | tf_op jit(solution)/shard_map/ppermute | solution.py:31
  43.9 2.1 %collect.1 = (bf16[768,256]{1,0:T(8,128)(2,1)S(1)}, bf16[256,768]{1,0:T(8,128)(2,1)S(1)}, bf16[768,128]{1,0:T(8,128)(2,1)S(1)}, f32[768,128]{1,0:T(8,128)S(1)}) custom-call(s32[6]{0:T(128)S(1)} %copy-done.14, s32[8,4]{1,0:T(8,128)S(1)} %copy.34.offered, bf16[432,320]{1,0:T(8,128)(2,1)S(1)} %stack.31.own, bf16[432,320]{1,0:T(8,128)(2,1)} %collective-permute-done.8.sib), custom_call_target="tpu_custom_call" | custom-call | flops 250000000 | bytes 3000000 | tf_op jit(solution)/shard_map/collect/pallas_call | solution.py:415
  49.5 1.6 collective-permute-start.12
  51.0 1.5 collective-permute-start.11
  53.7 1.2 copy-done.4
  54.9 13.0 %heads_backward.6 = (bf16[128,8192]{1,0:T(8,128)(2,1)}, bf16[128,4096]{1,0:T(8,128)(2,1)}, bf16[128,6144]{1,0:T(8,128)(2,1)}, f32[128,2048]{1,0:T(8,128)S(1)}, f...) custom-call(s32[6]{0:T(128)S(1)} %copy-done.14, bf16[128,8192]{1,0:T(8,128)(2,1)S(1)} %bitcast.18, ...), custom_call_target="tpu_custom_call" | custom-call | flops 4000000000 | bytes 1200000 | tf_op jit(solution)/shard_map/heads_backward/pallas_call | solution.py:158
  69.6 5.9 %collective-permute-done.12.weight = bf16[256,2048]{1,0:T(8,128)(2,1)S(1)} collective-permute-done((bf16[256,2048]{1,0:T(8,128)(2,1)S(1)}, bf16[256,2048]{1,0:T(8,128)(2,1)S(1)}, u32[]{:S(2)}, u32[]{:S(2)}) %collective-permute-start.12) | collective-permute-done | bytes 1048608 | tf_op jit(solution)/shard_map/ppermute | solution.py:31
  75.5 1.5 collective-permute-done.11.weight
  77.0 12.8 %heads_backward.7 = (bf16[128,8192]{1,0:T(8,128)(2,1)}, bf16[128,4096]{1,0:T(8,128)(2,1)}, bf16[128,6144]{1,0:T(8,128)(2,1)}, f32[128,2048]{1,0:T(8,128)S(1)}, f...) custom-call(s32[6]{0:T(128)S(1)} %copy-done.14, ...), custom_call_target="tpu_custom_call", output_to_operand_aliasing={{0}: (14, {}), {1}: (15, {}), {2}: (16, {})} | custom-call | flops 4000000000 | bytes 1200000 | tf_op jit(solution)/shard_map/heads_backward/pallas_call | solution.py:158
  90.4 7.2 %heads_backward.8 = (bf16[128,8192]{1,0:T(8,128)(2,1)}, bf16[128,4096]{1,0:T(8,128)(2,1)}, bf16[128,6144]{1,0:T(8,128)(2,1)}, f32[128,1024]{1,0:T(8,128)S(1)}, f...) custom-call(s32[6]{0:T(128)S(1)} %copy-done.14, ...), custom_call_target="tpu_custom_call", output_to_operand_aliasing={{0}: (14, {}), {1}: (15, {}), {2}: (16, {})} | custom-call | flops 2000000000 | bytes 600000 | tf_op jit(solution)/shard_map/heads_backward/pallas_call | solution.py:158
  98.8 1.5 collective-permute-start.19
  100.3 7.3 %heads_backward.9 = (bf16[128,8192]{1,0:T(8,128)(2,1)}, bf16[128,4096]{1,0:T(8,128)(2,1)}, bf16[128,6144]{1,0:T(8,128)(2,1)}, f32[128,1024]{1,0:T(8,128)S(1)}, f...) custom-call(s32[6]{0:T(128)S(1)} %copy-done.14, ...), custom_call_target="tpu_custom_call", output_to_operand_aliasing={{0}: (14, {}), {1}: (15, {}), {2}: (16, {})} | custom-call | flops 2000000000 | bytes 600000 | tf_op jit(solution)/shard_map/heads_backward/pallas_call | solution.py:158
  109.0 7.5 %heads_backward.10 = (bf16[128,8192]{1,0:T(8,128)(2,1)}, bf16[128,4096]{1,0:T(8,128)(2,1)}, bf16[128,6144]{1,0:T(8,128)(2,1)}, f32[128,1024]{1,0:T(8,128)S(1)}, ...) custom-call(s32[6]{0:T(128)S(1)} %copy-done.14, ...), custom_call_target="tpu_custom_call", output_to_operand_aliasing={{0}: (14, {}), {1}: (15, {}), {2}: (16, {})} | custom-call | flops 2000000000 | bytes 600000 | tf_op jit(solution)/shard_map/heads_backward/pallas_call | solution.py:158
  116.6 6.6 %collective-permute-done.20 = f32[128,1024]{1,0:T(8,128)S(1)} collective-permute-done((f32[128,1024]{1,0:T(8,128)S(1)}, f32[128,1024]{1,0:T(8,128)S(1)}, u32[]{:S(2)}, u32[]{:S(2)}) %collective-permute-start.20) | collective-permute-done | bytes 524320 | tf_op jit(solution)/shard_map/ppermute | solution.py:31
  123.3 1.5 collective-permute-start.24
  125.4 6.3 %collective-permute-done.23 = f32[128,1024]{1,0:T(8,128)S(1)} collective-permute-done((f32[128,1024]{1,0:T(8,128)S(1)}, f32[128,1024]{1,0:T(8,128)S(1)}, u32[]{:S(2)}, u32[]{:S(2)}) %collective-permute-start.23) | collective-permute-done | bytes 524320 | tf_op jit(solution)/shard_map/ppermute | solution.py:31
  131.8 3.8 %collective-permute-done.24 = f32[128,1024]{1,0:T(8,128)S(1)} collective-permute-done((f32[128,1024]{1,0:T(8,128)S(1)}, f32[128,1024]{1,0:T(8,128)S(1)}, u32[]{:S(2)}, u32[]{:S(2)}) %collective-permute-start.24) | collective-permute-done | bytes 524320 | tf_op jit(solution)/shard_map/ppermute | solution.py:31
  135.6 1.5 collective-permute-start.26
  137.1 7.3 %heads_backward.11 = (bf16[128,8192]{1,0:T(8,128)(2,1)}, bf16[128,4096]{1,0:T(8,128)(2,1)}, bf16[128,6144]{1,0:T(8,128)(2,1)}, f32[128,1024]{1,0:T(8,128)S(1)}, ...) custom-call(s32[6]{0:T(128)S(1)} %copy-done.14, ...), custom_call_target="tpu_custom_call", output_to_operand_aliasing={{0}: (14, {}), {1}: (15, {}), {2}: (16, {})} | custom-call | flops 2000000000 | bytes 600000 | tf_op jit(solution)/shard_map/heads_backward/pallas_call | solution.py:158
  144.4 2.6 %collective-permute-done.25 = f32[128,1024]{1,0:T(8,128)S(1)} collective-permute-done((f32[128,1024]{1,0:T(8,128)S(1)}, f32[128,1024]{1,0:T(8,128)S(1)}, u32[]{:S(2)}, u32[]{:S(2)}) %collective-permute-start.25) | collective-permute-done | bytes 524320 | tf_op jit(solution)/shard_map/ppermute | solution.py:31
  148.0 1.7 collective-permute-start.28
  150.6 3.4 %collective-permute-start.32 = (f32[64,1024]{1,0:T(8,128)}, f32[64,1024]{1,0:T(8,128)}, u32[]{:S(2)}, u32[]{:S(2)}) collective-permute-start(f32[64,1024]{1,0:T(8,128)} %slice.82), channel_id=1, source_target_pairs={{0,4},{1,5},{2,6},{3,7},{4,0},{5,1},{6,2},{7,3},{8,12},{9,13},{10,... | collective-permute-start | bytes 786440 | tf_op jit(solution)/shard_map/ppermute | solution.py:31
  154.1 1.7 spread.1
  156.9 8.3 %collective-permute-done.32 = f32[64,1024]{1,0:T(8,128)} collective-permute-done((f32[64,1024]{1,0:T(8,128)}, f32[64,1024]{1,0:T(8,128)}, u32[]{:S(2)}, u32[]{:S(2)}) %collective-permute-start.32) | collective-permute-done | bytes 262176 | tf_op jit(solution)/shard_map/ppermute | solution.py:31
  166.2 1.6 add_add_fusion.1
  168.7 3.4 %collective-permute-start.29 = (f32[64,1024]{1,0:T(8,128)}, f32[64,1024]{1,0:T(8,128)}, u32[]{:S(2)}, u32[]{:S(2)}) collective-permute-start(f32[64,1024]{1,0:T(8,128)} %slice.65), channel_id=1, source_target_pairs={{0,4},{1,5},{2,6},{3,7},{4,0},{5,1},{6,2},{7,3},{8,12},{9,13},{10,... | collective-permute-start | bytes 786440 | tf_op jit(solution)/shard_map/ppermute | solution.py:31
  172.2 1.3 copy.37
  174.7 1.5 collective-permute-start.35
  176.3 1.5 collective-permute-start.34
  177.8 3.8 %collective-permute-done.29 = f32[64,1024]{1,0:T(8,128)} collective-permute-done((f32[64,1024]{1,0:T(8,128)}, f32[64,1024]{1,0:T(8,128)}, u32[]{:S(2)}, u32[]{:S(2)}) %collective-permute-start.29) | collective-permute-done | bytes 262176 | tf_op jit(solution)/shard_map/ppermute | solution.py:31
  182.5 1.3 collective-permute-start.30
  183.8 1.3 collective-permute-start.31
  185.3 3.5 %collective-permute-done.35.refs_4_ = f32[32,2048]{1,0:T(8,128)S(1)} collective-permute-done((f32[32,2048]{1,0:T(8,128)S(1)}, f32[32,2048]{1,0:T(8,128)S(1)}, u32[]{:S(2)}, u32[]{:S(2)}) %collective-permute-start.35) | collective-permute-done | bytes 262176 | tf_op jit(solution)/shard_map/ppermute | solution.py:31
  189.4 1.3 collective-permute-start.40
  190.7 1.4 collective-permute-start.39
  192.9 2.4 %place_columns.1 = (bf16[128,8192]{1,0:T(8,128)(2,1)}, bf16[128,4096]{1,0:T(8,128)(2,1)}) custom-call(s32[6]{0:T(128)S(1)} %copy-done.14, bf16[128,6144]{1,0:T(8,128)(2,1)S(1)} %collective-permute-done.21.received, bf16[128,8192]{1,0:T(8,128)(2,1)} %get-tuple-element.137.q_in, ...), custom_call_target="tpu_custom_call", output_to_operand_aliasing={{0}: (2, {}), {1}: (3, {})} | custom-call | bytes 4000000 | tf_op jit(solution)/shard_map/place_columns/pallas_call | solution.py:187
  195.3 3.5 %collective-permute-done.31 = f32[128,320]{1,0:T(8,128)S(1)} collective-permute-done((f32[128,320]{1,0:T(8,128)S(1)}, f32[128,320]{1,0:T(8,128)S(1)}, u32[]{:S(2)}, u32[]{:S(2)}) %collective-permute-start.31) | collective-permute-done | bytes 163872 | tf_op jit(solution)/shard_map/ppermute | solution.py:26
  199.6 4.0 %collective-permute-done.39.refs_5_ = f32[32,2048]{1,0:T(8,128)S(1)} collective-permute-done((f32[32,2048]{1,0:T(8,128)S(1)}, f32[32,2048]{1,0:T(8,128)S(1)}, u32[]{:S(2)}, u32[]{:S(2)}) %collective-permute-start.39) | collective-permute-done | bytes 262176 | tf_op jit(solution)/shard_map/ppermute | solution.py:31
  204.1 3.4 %lay_out.1 = f32[32,16384]{1,0:T(8,128)} custom-call(s32[6]{0:T(128)S(1)} %copy-done.14, f32[32,2048]{1,0:T(8,128)S(1)} %join_cores.2.refs_0_, f32[32,2048]{1,0:T(8,128)S(1)} %join_cores.3.refs_1_, f32[32,2048]{1,0:T(8,128)S(1)} %collective-permute-done.34.refs_2_, f32[32,2048]{1,0:T(8,128)} %collective-permute-done.38.refs_3_, ...), custom_call_target="tpu_custom_call" | custom-call | bytes 4000000 | tf_op jit(solution)/shard_map/lay_out/pallas_call | solution.py:288
  (122 shorter events, 29.1 us)
Async XLA Ops:
  0.6 3.0 %collective-permute-start = (bf16[32,16384]{1,0:T(8,128)(2,1)}, bf16[32,16384]{1,0:T(8,128)(2,1)S(1)}, u32[]{:S(2)}, u32[]{:S(2)}) collective-permute-start(bf16[32,16384]{1,0:T(8,128)(2,1)} %distant.1), channel_id=1, source_target_pairs={{0,1},{1,0},{2,3},{3,2},{4,5},{5,4},{6,7},{7,6},{8,9},{9,8},{10,11... | collective-permute-start | bytes 3145736 | tf_op jit(solution)/shard_map/ppermute | solution.py:31
  4.6 10.9 %collective-permute-start.2 = (bf16[128,8192]{1,0:T(8,128)(2,1)}, bf16[128,8192]{1,0:T(8,128)(2,1)S(1)}, u32[]{:S(2)}, u32[]{:S(2)}) collective-permute-start(bf16[128,8192]{1,0:T(8,128)(2,1)} %bitcast.17), channel_id=1, source_target_pairs={{0,1},{1,0},{2,3},{3,2},{4,5},{5,4},{6,7},{7,6},{8,9},{9,8},{10,11... | collective-permute-start | bytes 6291464 | tf_op jit(solution)/shard_map/ppermute | solution.py:31
  5.0 10.6 %collective-permute-start.4 = (bf16[128,8192]{1,0:T(8,128)(2,1)}, bf16[128,8192]{1,0:T(8,128)(2,1)}, u32[]{:S(2)}, u32[]{:S(2)}) collective-permute-start(bf16[128,8192]{1,0:T(8,128)(2,1)} %bitcast.24), channel_id=1, source_target_pairs={{0,1},{1,0},{2,3},{3,2},{4,5},{5,4},{6,7},{7,6},{8,9},{9,8},{10,11... | collective-permute-start | bytes 6291464 | tf_op jit(solution)/shard_map/ppermute | solution.py:31
  5.1 38.7 %copy-start.5 = (f32[1,64,128]{2,1,0:T(8,128)S(1)}, f32[1,64,128]{2,1,0:T(8,128)}, u32[]{:S(2)}) copy-start(f32[1,64,128]{2,1,0:T(8,128)} %param.11) | copy-start | bytes 98308
  5.1 38.7 %copy-start.22 = (s32[1,8,4]{1,2,0:T(4,128)S(1)}, s32[1,8,4]{1,2,0:T(4,128)}, u32[]{:S(2)}) copy-start(s32[1,8,4]{1,2,0:T(4,128)} %param.15) | copy-start | bytes 388
  5.1 38.8 %copy-start.14 = (s32[6]{0:T(128)S(1)}, s32[6]{0:T(128)}, u32[]{:S(2)}) copy-start(s32[6]{0:T(128)} %stack.30.place) | copy-start | bytes 76
  5.1 9.4 %collective-permute-start.3 = (bf16[128,4096]{1,0:T(8,128)(2,1)}, bf16[128,4096]{1,0:T(8,128)(2,1)S(1)}, u32[]{:S(2)}, u32[]{:S(2)}) collective-permute-start(bf16[128,4096]{1,0:T(8,128)(2,1)} %bitcast.31), channel_id=1, source_target_pairs={{0,1},{1,0},{2,3},{3,2},{4,5},{5,4},{6,7},{7,6},{8,9},{9,8},{10,11... | collective-permute-start | bytes 3145736 | tf_op jit(solution)/shard_map/ppermute | solution.py:31
  8.1 16.5 %collective-permute-start.1 = (bf16[64,2048]{1,0:T(8,128)(2,1)}, bf16[64,2048]{1,0:T(8,128)(2,1)S(1)}, u32[]{:S(2)}, u32[]{:S(2)}) collective-permute-start(bf16[64,2048]{1,0:T(8,128)(2,1)} %get-tuple-element.103.refs_0_), channel_id=1, source_target_pairs={{0,4},{1,5},{2,6},{3,7},{4,0},{5,1},{6,2},{7,3},{8,12},{9,13},{10,... | collective-permute-start | bytes 786440 | tf_op jit(solution)/shard_map/ppermute | solution.py:31
  11.9 17.6 %collective-permute-start.9 = (bf16[64,2048]{1,0:T(8,128)(2,1)}, bf16[64,2048]{1,0:T(8,128)(2,1)}, u32[]{:S(2)}, u32[]{:S(2)}) collective-permute-start(bf16[64,2048]{1,0:T(8,128)(2,1)} %get-tuple-element.103.refs_0_), channel_id=1, source_target_pairs={{0,2},{1,3},{2,0},{3,1},{4,6},{5,7},{6,4},{7,5},{8,10},{9,11},{10,... | collective-permute-start | bytes 786440 | tf_op jit(solution)/shard_map/ppermute | solution.py:31
  15.6 13.7 %collective-permute-start.7 = (bf16[144,320]{1,0:T(8,128)(2,1)S(1)}, bf16[144,320]{1,0:T(8,128)(2,1)S(1)}, u32[]{:S(2)}, u32[]{:S(2)}) collective-permute-start(bf16[144,320]{1,0:T(8,128)(2,1)S(1)} %fusion.3.refs_0_), channel_id=1, source_target_pairs={{0,4},{1,5},{2,6},{3,7},{8,12},{9,13},{10,14},{11,15},{16,20},{17,... | collective-permute-start | bytes 276488 | tf_op jit(solution)/shard_map/ppermute | solution.py:26
  20.3 9.0 %collective-permute-start.6 = (bf16[144,320]{1,0:T(8,128)(2,1)S(1)}, bf16[144,320]{1,0:T(8,128)(2,1)S(1)}, u32[]{:S(2)}, u32[]{:S(2)}) collective-permute-start(bf16[144,320]{1,0:T(8,128)(2,1)S(1)} %fusion.3.refs_0_), channel_id=1, source_target_pairs={{0,2},{1,3},{2,4},{3,5},{4,6},{5,7},{8,10},{9,11},{10,12},{11,13},... | collective-permute-start | bytes 276488 | tf_op jit(solution)/shard_map/ppermute | solution.py:26
  24.6 14.8 %collective-permute-start.14 = (bf16[64,2048]{1,0:T(8,128)(2,1)}, bf16[64,2048]{1,0:T(8,128)(2,1)S(1)}, u32[]{:S(2)}, u32[]{:S(2)}) collective-permute-start(bf16[64,2048]{1,0:T(8,128)(2,1)} %get-tuple-element.110.refs_0_), channel_id=1, source_target_pairs={{0,2},{1,3},{2,0},{3,1},{4,6},{5,7},{6,4},{7,5},{8,10},{9,11},{10,... | collective-permute-start | bytes 786440 | tf_op jit(solution)/shard_map/ppermute | solution.py:31
  25.8 15.2 %collective-permute-start.13 = (bf16[64,2048]{1,0:T(8,128)(2,1)}, bf16[64,2048]{1,0:T(8,128)(2,1)}, u32[]{:S(2)}, u32[]{:S(2)}) collective-permute-start(bf16[64,2048]{1,0:T(8,128)(2,1)} %get-tuple-element.110.refs_0_), channel_id=1, source_target_pairs={{0,4},{1,5},{2,6},{3,7},{4,0},{5,1},{6,2},{7,3},{8,12},{9,13},{10,... | collective-permute-start | bytes 786440 | tf_op jit(solution)/shard_map/ppermute | solution.py:31
  29.3 24.3 %copy-start.2 = (bf16[1,128,4096]{2,1,0:T(8,128)(2,1)S(1)}, bf16[1,128,4096]{2,1,0:T(8,128)(2,1)}, u32[]{:S(2)}) copy-start(bf16[1,128,4096]{2,1,0:T(8,128)(2,1)} %param.9) | copy-start | bytes 3145732
  29.4 14.6 %collective-permute-start.8 = (bf16[432,320]{1,0:T(8,128)(2,1)S(1)}, bf16[432,320]{1,0:T(8,128)(2,1)}, u32[]{:S(2)}, u32[]{:S(2)}) collective-permute-start(bf16[432,320]{1,0:T(8,128)(2,1)S(1)} %stack.31.own), channel_id=1, source_target_pairs={{0,1},{1,0},{2,3},{3,2},{4,5},{5,4},{6,7},{7,6},{8,9},{9,8},{10,11... | collective-permute-start | bytes 829448 | tf_op jit(solution)/shard_map/ppermute | solution.py:31
  29.5 16.7 %collective-permute-start.10 = (bf16[64,2048]{1,0:T(8,128)(2,1)}, bf16[64,2048]{1,0:T(8,128)(2,1)}, u32[]{:S(2)}, u32[]{:S(2)}) collective-permute-start(bf16[64,2048]{1,0:T(8,128)(2,1)} %copy-done.10), channel_id=1, source_target_pairs={{0,2},{1,3},{2,0},{3,1},{4,6},{5,7},{6,4},{7,5},{8,10},{9,11},{10,... | collective-permute-start | bytes 786440 | tf_op jit(solution)/shard_map/ppermute | solution.py:31
  41.0 11.5 %collective-permute-start.15 = (bf16[64,2048]{1,0:T(8,128)(2,1)}, bf16[64,2048]{1,0:T(8,128)(2,1)}, u32[]{:S(2)}, u32[]{:S(2)}) collective-permute-start(bf16[64,2048]{1,0:T(8,128)(2,1)} %collective-permute-done.13.refs_1_), channel_id=1, source_target_pairs={{0,2},{1,3},{2,0},{3,1},{4,6},{5,7},{6,4},{7,5},{8,10},{9,11},{10,... | collective-permute-start | bytes 786440 | tf_op jit(solution)/shard_map/ppermute | solution.py:31
  43.8 2.2 %collective-permute-start.5 = (f32[64,128]{1,0:T(8,128)S(1)}, f32[64,128]{1,0:T(8,128)S(1)}, u32[]{:S(2)}, u32[]{:S(2)}) collective-permute-start(f32[64,128]{1,0:T(8,128)S(1)} %bitcast.38), channel_id=1, source_target_pairs={{0,1},{1,0},{2,3},{3,2},{4,5},{5,4},{6,7},{7,6},{8,9},{9,8},{10,11... | collective-permute-start | bytes 98312 | tf_op jit(solution)/shard_map/ppermute | solution.py:31
  43.9 8.6 %copy-start.13 = (bf16[64,2048]{1,0:T(8,128)(2,1)S(1)}, bf16[64,2048]{1,0:T(8,128)(2,1)}, u32[]{:S(2)}) copy-start(bf16[64,2048]{1,0:T(8,128)(2,1)} %copy-done.12) | copy-start | bytes 786436
  49.5 26.0 %collective-permute-start.12 = (bf16[256,2048]{1,0:T(8,128)(2,1)S(1)}, bf16[256,2048]{1,0:T(8,128)(2,1)S(1)}, u32[]{:S(2)}, u32[]{:S(2)}) collective-permute-start(bf16[256,2048]{1,0:T(8,128)(2,1)S(1)} %stack.32.weight), channel_id=1, source_target_pairs={{0,8},{8,0},{16,24},{24,16},{1,9},{9,1},{17,25},{25,17},{2,10},{10... | collective-permute-start | bytes 3145736 | tf_op jit(solution)/shard_map/ppermute | solution.py:31
  51.0 26.0 %collective-permute-start.11 = (bf16[256,2048]{1,0:T(8,128)(2,1)S(1)}, bf16[256,2048]{1,0:T(8,128)(2,1)S(1)}, u32[]{:S(2)}, u32[]{:S(2)}) collective-permute-start(bf16[256,2048]{1,0:T(8,128)(2,1)S(1)} %stack.32.weight), channel_id=1, source_target_pairs={{0,16},{8,24},{16,0},{24,8},{1,17},{9,25},{17,1},{25,9},{2,18},{10... | collective-permute-start | bytes 3145736 | tf_op jit(solution)/shard_map/ppermute | solution.py:31
  67.9 30.0 %collective-permute-start.16 = (f32[128,2048]{1,0:T(8,128)S(1)}, f32[128,2048]{1,0:T(8,128)S(1)}, u32[]{:S(2)}, u32[]{:S(2)}) collective-permute-start(f32[128,2048]{1,0:T(8,128)S(1)} %get-tuple-element.119), channel_id=1, source_target_pairs={{0,8},{8,0},{16,24},{24,16},{1,9},{9,1},{17,25},{25,17},{2,10},{10... | collective-permute-start | bytes 3145736 | tf_op jit(solution)/shard_map/ppermute | solution.py:31
  68.5 30.3 %collective-permute-start.17 = (f32[128,2048]{1,0:T(8,128)S(1)}, f32[128,2048]{1,0:T(8,128)S(1)}, u32[]{:S(2)}, u32[]{:S(2)}) collective-permute-start(f32[128,2048]{1,0:T(8,128)S(1)} %get-tuple-element.120), channel_id=1, source_target_pairs={{0,16},{8,24},{16,0},{24,8},{1,17},{9,25},{17,1},{25,9},{2,18},{10... | collective-permute-start | bytes 3145736 | tf_op jit(solution)/shard_map/ppermute | solution.py:31
  89.8 33.4 %collective-permute-start.18 = (f32[128,2048]{1,0:T(8,128)S(1)}, f32[128,2048]{1,0:T(8,128)S(1)}, u32[]{:S(2)}, u32[]{:S(2)}) collective-permute-start(f32[128,2048]{1,0:T(8,128)S(1)} %get-tuple-element.129), channel_id=1, source_target_pairs={{0,8},{8,0},{16,24},{24,16},{1,9},{9,1},{17,25},{25,17},{2,10},{10... | collective-permute-start | bytes 3145736 | tf_op jit(solution)/shard_map/ppermute | solution.py:31
  98.8 32.9 %collective-permute-start.19 = (f32[128,1024]{1,0:T(8,128)S(1)}, f32[128,1024]{1,0:T(8,128)S(1)}, u32[]{:S(2)}, u32[]{:S(2)}) collective-permute-start(f32[128,1024]{1,0:T(8,128)S(1)} %get-tuple-element.130), channel_id=1, source_target_pairs={{0,16},{8,24},{16,0},{24,8},{1,17},{9,25},{17,1},{25,9},{2,18},{10... | collective-permute-start | bytes 1572872 | tf_op jit(solution)/shard_map/ppermute | solution.py:31
  107.6 15.7 %collective-permute-start.20 = (f32[128,1024]{1,0:T(8,128)S(1)}, f32[128,1024]{1,0:T(8,128)S(1)}, u32[]{:S(2)}, u32[]{:S(2)}) collective-permute-start(f32[128,1024]{1,0:T(8,128)S(1)} %get-tuple-element.131), channel_id=1, source_target_pairs={{0,16},{8,24},{16,0},{24,8},{1,17},{9,25},{17,1},{25,9},{2,18},{10... | collective-permute-start | bytes 1572872 | tf_op jit(solution)/shard_map/ppermute | solution.py:31
  108.3 23.4 %collective-permute-start.23 = (f32[128,1024]{1,0:T(8,128)S(1)}, f32[128,1024]{1,0:T(8,128)S(1)}, u32[]{:S(2)}, u32[]{:S(2)}) collective-permute-start(f32[128,1024]{1,0:T(8,128)S(1)} %get-tuple-element.156), channel_id=1, source_target_pairs={{0,8},{8,0},{16,24},{24,16},{1,9},{9,1},{17,25},{25,17},{2,10},{10... | collective-permute-start | bytes 1572872 | tf_op jit(solution)/shard_map/ppermute | solution.py:31
  123.3 26.4 %copy-start.19 = (f32[128,2048]{1,0:T(8,128)}, f32[128,2048]{1,0:T(8,128)S(1)}, u32[]{:S(2)}) copy-start(f32[128,2048]{1,0:T(8,128)S(1)} %collective-permute-done.18) | copy-start | bytes 3145732
  123.3 12.3 %collective-permute-start.24 = (f32[128,1024]{1,0:T(8,128)S(1)}, f32[128,1024]{1,0:T(8,128)S(1)}, u32[]{:S(2)}, u32[]{:S(2)}) collective-permute-start(f32[128,1024]{1,0:T(8,128)S(1)} %get-tuple-element.158), channel_id=1, source_target_pairs={{0,16},{8,24},{16,0},{24,8},{1,17},{9,25},{17,1},{25,9},{2,18},{10... | collective-permute-start | bytes 1572872 | tf_op jit(solution)/shard_map/ppermute | solution.py:31
  124.8 19.6 %collective-permute-start.27 = (f32[128,1024]{1,0:T(8,128)S(1)}, f32[128,1024]{1,0:T(8,128)S(1)}, u32[]{:S(2)}, u32[]{:S(2)}) collective-permute-start(f32[128,1024]{1,0:T(8,128)S(1)} %get-tuple-element.168), channel_id=1, source_target_pairs={{0,8},{8,0},{16,24},{24,16},{1,9},{9,1},{17,25},{25,17},{2,10},{10... | collective-permute-start | bytes 1572872 | tf_op jit(solution)/shard_map/ppermute | solution.py:31
  135.6 11.4 %collective-permute-start.25 = (f32[128,1024]{1,0:T(8,128)S(1)}, f32[128,1024]{1,0:T(8,128)S(1)}, u32[]{:S(2)}, u32[]{:S(2)}) collective-permute-start(f32[128,1024]{1,0:T(8,128)S(1)} %add_add_fusion.2), channel_id=1, source_target_pairs={{0,2},{1,3},{2,0},{3,1},{4,6},{5,7},{6,4},{7,5},{8,10},{9,11},{10,... | collective-permute-start | bytes 1572872 | tf_op jit(solution)/shard_map/ppermute | solution.py:31
  135.6 11.4 %collective-permute-start.26 = (f32[128,1024]{1,0:T(8,128)S(1)}, f32[128,1024]{1,0:T(8,128)S(1)}, u32[]{:S(2)}, u32[]{:S(2)}) collective-permute-start(f32[128,1024]{1,0:T(8,128)S(1)} %get-tuple-element.163), channel_id=1, source_target_pairs={{0,16},{8,24},{16,0},{24,8},{1,17},{9,25},{17,1},{25,9},{2,18},{10... | collective-permute-start | bytes 1572872 | tf_op jit(solution)/shard_map/ppermute | solution.py:31
  144.3 23.5 %collective-permute-start.21 = (bf16[128,6144]{1,0:T(8,128)(2,1)}, bf16[128,6144]{1,0:T(8,128)(2,1)S(1)}, u32[]{:S(2)}, u32[]{:S(2)}) collective-permute-start(bf16[128,6144]{1,0:T(8,128)(2,1)} %get-tuple-element.136), channel_id=1, source_target_pairs={{0,1},{1,0},{2,3},{3,2},{4,5},{5,4},{6,7},{7,6},{8,9},{9,8},{10,11... | collective-permute-start | bytes 4718600 | tf_op jit(solution)/shard_map/ppermute | solution.py:31
  148.0 18.3 %collective-permute-start.28 = (f32[128,1024]{1,0:T(8,128)}, f32[128,1024]{1,0:T(8,128)}, u32[]{:S(2)}, u32[]{:S(2)}) collective-permute-start(f32[128,1024]{1,0:T(8,128)} %add_add_fusion), channel_id=1, source_target_pairs={{0,2},{1,3},{2,0},{3,1},{4,6},{5,7},{6,4},{7,5},{8,10},{9,11},{10,... | collective-permute-start | bytes 1572872 | tf_op jit(solution)/shard_map/ppermute | solution.py:31
  150.6 14.5 %collective-permute-start.32 = (f32[64,1024]{1,0:T(8,128)}, f32[64,1024]{1,0:T(8,128)}, u32[]{:S(2)}, u32[]{:S(2)}) collective-permute-start(f32[64,1024]{1,0:T(8,128)} %slice.82), channel_id=1, source_target_pairs={{0,4},{1,5},{2,6},{3,7},{4,0},{5,1},{6,2},{7,3},{8,12},{9,13},{10,... | collective-permute-start | bytes 786440 | tf_op jit(solution)/shard_map/ppermute | solution.py:31
  155.8 10.5 %copy-start.7 = (f32[128,1024]{1,0:T(8,128)S(1)}, f32[128,1024]{1,0:T(8,128)}, u32[]{:S(2)}) copy-start(f32[128,1024]{1,0:T(8,128)} %copy-done.6) | copy-start | bytes 1572868
  156.9 10.9 %collective-permute-start.22 = (f32[432,320]{0,1:T(8,128)}, f32[432,320]{0,1:T(8,128)S(1)}, u32[]{:S(2)}, u32[]{:S(2)}) collective-permute-start(f32[432,320]{0,1:T(8,128)} %copy.36), channel_id=1, source_target_pairs={{0,1},{1,0},{2,3},{3,2},{4,5},{5,4},{6,7},{7,6},{8,9},{9,8},{10,11... | collective-permute-start | bytes 1658888 | tf_op jit(solution)/shard_map/ppermute | solution.py:31
  168.7 12.9 %collective-permute-start.29 = (f32[64,1024]{1,0:T(8,128)}, f32[64,1024]{1,0:T(8,128)}, u32[]{:S(2)}, u32[]{:S(2)}) collective-permute-start(f32[64,1024]{1,0:T(8,128)} %slice.65), channel_id=1, source_target_pairs={{0,4},{1,5},{2,6},{3,7},{4,0},{5,1},{6,2},{7,3},{8,12},{9,13},{10,... | collective-permute-start | bytes 786440 | tf_op jit(solution)/shard_map/ppermute | solution.py:31
  172.1 1.5 collective-permute-start.33
  174.2 11.0 %collective-permute-start.36 = (f32[32,2048]{1,0:T(8,128)S(1)}, f32[32,2048]{1,0:T(8,128)S(1)}, u32[]{:S(2)}, u32[]{:S(2)}) collective-permute-start(f32[32,2048]{1,0:T(8,128)S(1)} %join_cores.2.refs_0_), channel_id=1, source_target_pairs={{0,24},{8,16},{16,8},{24,0},{1,25},{9,17},{17,9},{25,1},{2,26},{10... | collective-permute-start | bytes 786440 | tf_op jit(solution)/shard_map/ppermute | solution.py:31
  174.7 14.0 %collective-permute-start.35 = (f32[32,2048]{1,0:T(8,128)S(1)}, f32[32,2048]{1,0:T(8,128)S(1)}, u32[]{:S(2)}, u32[]{:S(2)}) collective-permute-start(f32[32,2048]{1,0:T(8,128)S(1)} %join_cores.2.refs_0_), channel_id=1, source_target_pairs={{0,16},{8,24},{16,0},{24,8},{1,17},{9,25},{17,1},{25,9},{2,18},{10... | collective-permute-start | bytes 786440 | tf_op jit(solution)/shard_map/ppermute | solution.py:31
  176.3 12.5 %collective-permute-start.34 = (f32[32,2048]{1,0:T(8,128)S(1)}, f32[32,2048]{1,0:T(8,128)S(1)}, u32[]{:S(2)}, u32[]{:S(2)}) collective-permute-start(f32[32,2048]{1,0:T(8,128)S(1)} %join_cores.2.refs_0_), channel_id=1, source_target_pairs={{0,8},{8,0},{16,24},{24,16},{1,9},{9,1},{17,25},{25,17},{2,10},{10... | collective-permute-start | bytes 786440 | tf_op jit(solution)/shard_map/ppermute | solution.py:31
  182.5 12.8 %collective-permute-start.30 = (f32[128,320]{1,0:T(8,128)S(1)}, f32[128,320]{1,0:T(8,128)S(1)}, u32[]{:S(2)}, u32[]{:S(2)}) collective-permute-start(f32[128,320]{1,0:T(8,128)S(1)} %get-tuple-element.188), channel_id=1, source_target_pairs={{2,0},{3,1},{4,2},{5,3},{6,4},{7,5},{10,8},{11,9},{12,10},{13,11},... | collective-permute-start | bytes 491528 | tf_op jit(solution)/shard_map/ppermute | solution.py:26
  183.8 14.9 %collective-permute-start.31 = (f32[128,320]{1,0:T(8,128)S(1)}, f32[128,320]{1,0:T(8,128)S(1)}, u32[]{:S(2)}, u32[]{:S(2)}) collective-permute-start(f32[128,320]{1,0:T(8,128)S(1)} %get-tuple-element.189), channel_id=1, source_target_pairs={{4,0},{5,1},{6,2},{7,3},{12,8},{13,9},{14,10},{15,11},{20,16},{21,... | collective-permute-start | bytes 491528 | tf_op jit(solution)/shard_map/ppermute | solution.py:26
  185.2 3.6 %collective-permute-start.37 = (f32[32,1024]{1,0:T(8,128)S(1)}, f32[32,1024]{1,0:T(8,128)S(1)}, u32[]{:S(2)}, u32[]{:S(2)}) collective-permute-start(f32[32,1024]{1,0:T(8,128)S(1)} %get-tuple-element.190), channel_id=1, source_target_pairs={{0,1},{1,0},{2,3},{3,2},{4,5},{5,4},{6,7},{7,6},{8,9},{9,8},{10,11... | collective-permute-start | bytes 393224 | tf_op jit(solution)/shard_map/ppermute | solution.py:31
  189.4 10.2 %collective-permute-start.40 = (f32[32,2048]{1,0:T(8,128)S(1)}, f32[32,2048]{1,0:T(8,128)S(1)}, u32[]{:S(2)}, u32[]{:S(2)}) collective-permute-start(f32[32,2048]{1,0:T(8,128)S(1)} %join_cores.3.refs_1_), channel_id=1, source_target_pairs={{0,24},{8,16},{16,8},{24,0},{1,25},{9,17},{17,9},{25,1},{2,26},{10... | collective-permute-start | bytes 786440 | tf_op jit(solution)/shard_map/ppermute | solution.py:31
  190.7 13.0 %collective-permute-start.39 = (f32[32,2048]{1,0:T(8,128)S(1)}, f32[32,2048]{1,0:T(8,128)S(1)}, u32[]{:S(2)}, u32[]{:S(2)}) collective-permute-start(f32[32,2048]{1,0:T(8,128)S(1)} %join_cores.3.refs_1_), channel_id=1, source_target_pairs={{0,16},{8,24},{16,0},{24,8},{1,17},{9,25},{17,1},{25,9},{2,18},{10... | collective-permute-start | bytes 786440 | tf_op jit(solution)/shard_map/ppermute | solution.py:31
  192.1 12.0 %collective-permute-start.38 = (f32[32,2048]{1,0:T(8,128)S(1)}, f32[32,2048]{1,0:T(8,128)}, u32[]{:S(2)}, u32[]{:S(2)}) collective-permute-start(f32[32,2048]{1,0:T(8,128)S(1)} %join_cores.3.refs_1_), channel_id=1, source_target_pairs={{0,8},{8,0},{16,24},{24,16},{1,9},{9,1},{17,25},{25,17},{2,10},{10... | collective-permute-start | bytes 786440 | tf_op jit(solution)/shard_map/ppermute | solution.py:31
  (17 other events, 71.9 us)

commit v14 on v13

--- a/solution.py
+++ b/solution.py
@@ -602,7 +602,7 @@
             for t in sorted((t for t in addends if t & bit), reverse=True):
                 leaving = [total(addends[t], half) for half in range(2)]
                 if side == 0:
-                    behind = [(first_sums[0][order[0]][0], last_sums[-1], latents[-2])] * 2
+                    behind = [(last_sums[0],), (first_sums[0][order[0]][0], last_sums[-1], latents[-2])]
                 else:
                     behind = [(weight_grads[far - 1][side][0],)] * 2
                 leaving = [after(half, *there) for half, there in zip(leaving, behind)]

time: 208 us -> 206 us (level)
  waiting for transfers between devices: 61.9 us -> 57.7 us
  starting transfers between devices: 55.9 us -> 58 us
    ppermute x37, waiting for transfers between devices: 58.4 us -> 55.8 us  [exchange(): lax.ppermute(value, axis, [(source, source ^ bits) for source in range(co...]
  transfers between devices with their start and end apart: 41 -> 41, of which waited for: 19 -> 18; matrix products, arithmetic and copies ran while one was open for 5% -> 5% of each run, Pallas kernels for 32% -> 33%
where the time goes in v14:
time: 206 us; the launch traced here: 205 us
  Pallas kernels  70.5 us (34%)
  starting transfers between devices  58 us (28%)
  waiting for transfers between devices  57.7 us (28%)
  local copies, waits for them, and re-layouts  12.8 us (6%)
  other arithmetic  5.22 us (3%)
    ppermute x37, waiting for transfers between devices, exchange(): lax.ppermute(value, axis, [(source, source ^ bits) for source in range(co...  55.8 us
    pallas_call x6, Pallas kernels, chunk_backward(): pl.pallas_call(functools.partial(heads_kernel, earlier=len(aliases)), gri...  55.1 us
    ppermute x37, starting transfers between devices, exchange(): lax.ppermute(value, axis, [(source, source ^ bits) for source in range(co...  47.1 us
    ppermute x4, starting transfers between devices, from_behind(): lax.ppermute(value, axis, [(source, source + steps) for source in range(i...  10.8 us
    unnamed x49, local copies, waits for them, and re-layouts  6.91 us
  transfers between devices with their start and end apart: 41, of which 18 were waited for; matrix products, arithmetic and copies ran while one was open for 5% of the time, Pallas kernels for 33%

profile of v14, /device:TPU:0, one launch (start us, length us, event | category | flops | bytes accessed | tf_op | source)
XLA Modules:
  0.0 205.2 jit_solution(4808086272920150900)
XLA Ops:
  1.7 1.9 collective-permute-done.near_crossed.distant_crossed
  5.6 2.6 %weight_parts.1 = (bf16[64,2048]{1,0:T(8,128)(2,1)}, bf16[64,2048]{1,0:T(8,128)(2,1)}) custom-call(s32[6]{0:T(128)} %stack.30.place, bf16[32,16384]{1,0:T(8,128)(2,1)} %distant.1, bf16[32,16384]{1,0:T(8,128)(2,1)} %distant.1, bf16[32,16384]{1,0:T(8,128)(2,1)} %copy-done.15, bf16[32,16384]{1,0:T(8,128)(2,1)} %copy-done.15), custom_call_target="tpu_custom_call" | custom-call | bytes 1000000 | tf_op jit(solution)/shard_map/weight_parts/pallas_call | solution.py:256
  8.1 3.7 %collective-permute-start.1 = (bf16[64,2048]{1,0:T(8,128)(2,1)}, bf16[64,2048]{1,0:T(8,128)(2,1)S(1)}, u32[]{:S(2)}, u32[]{:S(2)}) collective-permute-start(bf16[64,2048]{1,0:T(8,128)(2,1)} %get-tuple-element.103.refs_0_), channel_id=1, source_target_pairs={{0,4},{1,5},{2,6},{3,7},{4,0},{5,1},{6,2},{7,3},{8,12},{9,13},{10,... | collective-permute-start | bytes 786440 | tf_op jit(solution)/shard_map/ppermute | solution.py:31
  11.9 1.6 collective-permute-start.9
  15.6 4.8 %collective-permute-start.7 = (bf16[144,320]{1,0:T(8,128)(2,1)S(1)}, bf16[144,320]{1,0:T(8,128)(2,1)S(1)}, u32[]{:S(2)}, u32[]{:S(2)}) collective-permute-start(bf16[144,320]{1,0:T(8,128)(2,1)S(1)} %fusion.3.refs_0_), channel_id=1, source_target_pairs={{0,4},{1,5},{2,6},{3,7},{8,12},{9,13},{10,14},{11,15},{16,20},{17,... | collective-permute-start | bytes 276488 | tf_op jit(solution)/shard_map/ppermute | solution.py:26
  20.3 3.5 %collective-permute-start.6 = (bf16[144,320]{1,0:T(8,128)(2,1)S(1)}, bf16[144,320]{1,0:T(8,128)(2,1)S(1)}, u32[]{:S(2)}, u32[]{:S(2)}) collective-permute-start(bf16[144,320]{1,0:T(8,128)(2,1)S(1)} %fusion.3.refs_0_), channel_id=1, source_target_pairs={{0,2},{1,3},{2,4},{3,5},{4,6},{5,7},{8,10},{9,11},{10,12},{11,13},... | collective-permute-start | bytes 276488 | tf_op jit(solution)/shard_map/ppermute | solution.py:26
  25.8 3.5 %collective-permute-start.13 = (bf16[64,2048]{1,0:T(8,128)(2,1)}, bf16[64,2048]{1,0:T(8,128)(2,1)}, u32[]{:S(2)}, u32[]{:S(2)}) collective-permute-start(bf16[64,2048]{1,0:T(8,128)(2,1)} %get-tuple-element.110.refs_0_), channel_id=1, source_target_pairs={{0,4},{1,5},{2,6},{3,7},{4,0},{5,1},{6,2},{7,3},{8,12},{9,13},{10,... | collective-permute-start | bytes 786440 | tf_op jit(solution)/shard_map/ppermute | solution.py:31
  29.5 3.2 %collective-permute-start.10 = (bf16[64,2048]{1,0:T(8,128)(2,1)}, bf16[64,2048]{1,0:T(8,128)(2,1)}, u32[]{:S(2)}, u32[]{:S(2)}) collective-permute-start(bf16[64,2048]{1,0:T(8,128)(2,1)} %copy-done.10), channel_id=1, source_target_pairs={{0,2},{1,3},{2,0},{3,1},{4,6},{5,7},{6,4},{7,5},{8,10},{9,11},{10,... | collective-permute-start | bytes 786440 | tf_op jit(solution)/shard_map/ppermute | solution.py:31
  32.7 6.8 %collective-permute-done.14.refs_2_ = bf16[64,2048]{1,0:T(8,128)(2,1)S(1)} collective-permute-done((bf16[64,2048]{1,0:T(8,128)(2,1)}, bf16[64,2048]{1,0:T(8,128)(2,1)S(1)}, u32[]{:S(2)}, u32[]{:S(2)}) %collective-permute-start.14) | collective-permute-done | bytes 262176 | tf_op jit(solution)/shard_map/ppermute | solution.py:31
  41.0 2.8 %collective-permute-start.15 = (bf16[64,2048]{1,0:T(8,128)(2,1)}, bf16[64,2048]{1,0:T(8,128)(2,1)}, u32[]{:S(2)}, u32[]{:S(2)}) collective-permute-start(bf16[64,2048]{1,0:T(8,128)(2,1)} %collective-permute-done.13.refs_1_), channel_id=1, source_target_pairs={{0,2},{1,3},{2,0},{3,1},{4,6},{5,7},{6,4},{7,5},{8,10},{9,11},{10,... | collective-permute-start | bytes 786440 | tf_op jit(solution)/shard_map/ppermute | solution.py:31
  43.9 2.1 %collect.1 = (bf16[768,256]{1,0:T(8,128)(2,1)S(1)}, bf16[256,768]{1,0:T(8,128)(2,1)S(1)}, bf16[768,128]{1,0:T(8,128)(2,1)S(1)}, f32[768,128]{1,0:T(8,128)S(1)}) custom-call(s32[6]{0:T(128)S(1)} %copy-done.14, s32[8,4]{1,0:T(8,128)S(1)} %copy.34.offered, bf16[432,320]{1,0:T(8,128)(2,1)S(1)} %stack.31.own, bf16[432,320]{1,0:T(8,128)(2,1)} %collective-permute-done.8.sib), custom_call_target="tpu_custom_call" | custom-call | flops 250000000 | bytes 3000000 | tf_op jit(solution)/shard_map/collect/pallas_call | solution.py:415
  49.5 1.6 collective-permute-start.12
  51.0 1.5 collective-permute-start.11
  53.7 1.2 copy-done.4
  54.9 13.0 %heads_backward.6 = (bf16[128,8192]{1,0:T(8,128)(2,1)}, bf16[128,4096]{1,0:T(8,128)(2,1)}, bf16[128,6144]{1,0:T(8,128)(2,1)}, f32[128,2048]{1,0:T(8,128)S(1)}, f...) custom-call(s32[6]{0:T(128)S(1)} %copy-done.14, bf16[128,8192]{1,0:T(8,128)(2,1)S(1)} %bitcast.18, ...), custom_call_target="tpu_custom_call" | custom-call | flops 4000000000 | bytes 1200000 | tf_op jit(solution)/shard_map/heads_backward/pallas_call | solution.py:158
  69.6 5.9 %collective-permute-done.12.weight = bf16[256,2048]{1,0:T(8,128)(2,1)S(1)} collective-permute-done((bf16[256,2048]{1,0:T(8,128)(2,1)S(1)}, bf16[256,2048]{1,0:T(8,128)(2,1)S(1)}, u32[]{:S(2)}, u32[]{:S(2)}) %collective-permute-start.12) | collective-permute-done | bytes 1048608 | tf_op jit(solution)/shard_map/ppermute | solution.py:31
  75.5 1.5 collective-permute-done.11.weight
  77.0 12.8 %heads_backward.7 = (bf16[128,8192]{1,0:T(8,128)(2,1)}, bf16[128,4096]{1,0:T(8,128)(2,1)}, bf16[128,6144]{1,0:T(8,128)(2,1)}, f32[128,2048]{1,0:T(8,128)S(1)}, f...) custom-call(s32[6]{0:T(128)S(1)} %copy-done.14, ...), custom_call_target="tpu_custom_call", output_to_operand_aliasing={{0}: (14, {}), {1}: (15, {}), {2}: (16, {})} | custom-call | flops 4000000000 | bytes 1200000 | tf_op jit(solution)/shard_map/heads_backward/pallas_call | solution.py:158
  90.4 7.2 %heads_backward.8 = (bf16[128,8192]{1,0:T(8,128)(2,1)}, bf16[128,4096]{1,0:T(8,128)(2,1)}, bf16[128,6144]{1,0:T(8,128)(2,1)}, f32[128,1024]{1,0:T(8,128)S(1)}, f...) custom-call(s32[6]{0:T(128)S(1)} %copy-done.14, ...), custom_call_target="tpu_custom_call", output_to_operand_aliasing={{0}: (14, {}), {1}: (15, {}), {2}: (16, {})} | custom-call | flops 2000000000 | bytes 600000 | tf_op jit(solution)/shard_map/heads_backward/pallas_call | solution.py:158
  97.6 1.5 collective-permute-start.19
  99.3 1.6 collective-permute-start.23
  100.9 7.3 %heads_backward.9 = (bf16[128,8192]{1,0:T(8,128)(2,1)}, bf16[128,4096]{1,0:T(8,128)(2,1)}, bf16[128,6144]{1,0:T(8,128)(2,1)}, f32[128,1024]{1,0:T(8,128)S(1)}, f...) custom-call(s32[6]{0:T(128)S(1)} %copy-done.14, ...), custom_call_target="tpu_custom_call", output_to_operand_aliasing={{0}: (14, {}), {1}: (15, {}), {2}: (16, {})} | custom-call | flops 2000000000 | bytes 600000 | tf_op jit(solution)/shard_map/heads_backward/pallas_call | solution.py:158
  108.3 1.7 collective-permute-done.19
  110.0 1.5 collective-permute-start.24
  111.5 1.3 collective-permute-start.27
  113.4 7.5 %heads_backward.10 = (bf16[128,8192]{1,0:T(8,128)(2,1)}, bf16[128,4096]{1,0:T(8,128)(2,1)}, bf16[128,6144]{1,0:T(8,128)(2,1)}, f32[128,1024]{1,0:T(8,128)S(1)}, ...) custom-call(s32[6]{0:T(128)S(1)} %copy-done.14, ...), custom_call_target="tpu_custom_call", output_to_operand_aliasing={{0}: (14, {}), {1}: (15, {}), {2}: (16, {})} | custom-call | flops 2000000000 | bytes 600000 | tf_op jit(solution)/shard_map/heads_backward/pallas_call | solution.py:158
  120.9 10.8 %collective-permute-done.23 = f32[128,1024]{1,0:T(8,128)S(1)} collective-permute-done((f32[128,1024]{1,0:T(8,128)S(1)}, f32[128,1024]{1,0:T(8,128)S(1)}, u32[]{:S(2)}, u32[]{:S(2)}) %collective-permute-start.23) | collective-permute-done | bytes 524320 | tf_op jit(solution)/shard_map/ppermute | solution.py:31
  131.8 2.4 %collective-permute-start.25 = (f32[128,1024]{1,0:T(8,128)S(1)}, f32[128,1024]{1,0:T(8,128)S(1)}, u32[]{:S(2)}, u32[]{:S(2)}) collective-permute-start(f32[128,1024]{1,0:T(8,128)S(1)} %add_add_fusion.2), channel_id=1, source_target_pairs={{0,2},{1,3},{2,0},{3,1},{4,6},{5,7},{6,4},{7,5},{8,10},{9,11},{10,... | collective-permute-start | bytes 1572872 | tf_op jit(solution)/shard_map/ppermute | solution.py:31
  134.2 1.6 collective-permute-start.26
  135.8 7.3 %heads_backward.11 = (bf16[128,8192]{1,0:T(8,128)(2,1)}, bf16[128,4096]{1,0:T(8,128)(2,1)}, bf16[128,6144]{1,0:T(8,128)(2,1)}, f32[128,1024]{1,0:T(8,128)S(1)}, ...) custom-call(s32[6]{0:T(128)S(1)} %copy-done.14, ...), custom_call_target="tpu_custom_call", output_to_operand_aliasing={{0}: (14, {}), {1}: (15, {}), {2}: (16, {})} | custom-call | flops 2000000000 | bytes 600000 | tf_op jit(solution)/shard_map/heads_backward/pallas_call | solution.py:158
  143.0 2.0 collective-permute-done.25
  147.8 3.4 %collective-permute-start.32 = (f32[64,1024]{1,0:T(8,128)}, f32[64,1024]{1,0:T(8,128)}, u32[]{:S(2)}, u32[]{:S(2)}) collective-permute-start(f32[64,1024]{1,0:T(8,128)} %slice.82), channel_id=1, source_target_pairs={{0,4},{1,5},{2,6},{3,7},{4,0},{5,1},{6,2},{7,3},{8,12},{9,13},{10,... | collective-permute-start | bytes 786440 | tf_op jit(solution)/shard_map/ppermute | solution.py:31
  151.2 1.7 spread.1
  154.0 8.0 %collective-permute-done.32 = f32[64,1024]{1,0:T(8,128)} collective-permute-done((f32[64,1024]{1,0:T(8,128)}, f32[64,1024]{1,0:T(8,128)}, u32[]{:S(2)}, u32[]{:S(2)}) %collective-permute-start.32) | collective-permute-done | bytes 262176 | tf_op jit(solution)/shard_map/ppermute | solution.py:31
  164.2 1.6 add_add_fusion.1
  166.6 2.3 %collective-permute-start.29 = (f32[64,1024]{1,0:T(8,128)}, f32[64,1024]{1,0:T(8,128)}, u32[]{:S(2)}, u32[]{:S(2)}) collective-permute-start(f32[64,1024]{1,0:T(8,128)} %slice.65), channel_id=1, source_target_pairs={{0,4},{1,5},{2,6},{3,7},{4,0},{5,1},{6,2},{7,3},{8,12},{9,13},{10,... | collective-permute-start | bytes 786440 | tf_op jit(solution)/shard_map/ppermute | solution.py:31
  169.0 1.3 copy.37
  171.0 2.4 %collective-permute-start.36 = (f32[32,2048]{1,0:T(8,128)S(1)}, f32[32,2048]{1,0:T(8,128)S(1)}, u32[]{:S(2)}, u32[]{:S(2)}) collective-permute-start(f32[32,2048]{1,0:T(8,128)S(1)} %join_cores.2.refs_0_), channel_id=1, source_target_pairs={{0,24},{8,16},{16,8},{24,0},{1,25},{9,17},{17,9},{25,1},{2,26},{10... | collective-permute-start | bytes 786440 | tf_op jit(solution)/shard_map/ppermute | solution.py:31
  174.6 5.2 %collective-permute-done.29 = f32[64,1024]{1,0:T(8,128)} collective-permute-done((f32[64,1024]{1,0:T(8,128)}, f32[64,1024]{1,0:T(8,128)}, u32[]{:S(2)}, u32[]{:S(2)}) %collective-permute-start.29) | collective-permute-done | bytes 262176 | tf_op jit(solution)/shard_map/ppermute | solution.py:31
  180.9 1.3 collective-permute-start.30
  182.2 1.3 collective-permute-start.31
  183.6 2.8 %collective-permute-done.35.refs_4_ = f32[32,2048]{1,0:T(8,128)S(1)} collective-permute-done((f32[32,2048]{1,0:T(8,128)S(1)}, f32[32,2048]{1,0:T(8,128)S(1)}, u32[]{:S(2)}, u32[]{:S(2)}) %collective-permute-start.35) | collective-permute-done | bytes 262176 | tf_op jit(solution)/shard_map/ppermute | solution.py:31
  186.9 1.8 collective-permute-start.40
  190.5 2.4 %place_columns.1 = (bf16[128,8192]{1,0:T(8,128)(2,1)}, bf16[128,4096]{1,0:T(8,128)(2,1)}) custom-call(s32[6]{0:T(128)S(1)} %copy-done.14, bf16[128,6144]{1,0:T(8,128)(2,1)S(1)} %collective-permute-done.21.received, bf16[128,8192]{1,0:T(8,128)(2,1)} %get-tuple-element.137.q_in, ...), custom_call_target="tpu_custom_call", output_to_operand_aliasing={{0}: (2, {}), {1}: (3, {})} | custom-call | bytes 4000000 | tf_op jit(solution)/shard_map/place_columns/pallas_call | solution.py:187
  192.9 1.9 collective-permute-done.31
  195.6 1.5 collective-permute-done.40.refs_7_
  197.1 4.7 %collective-permute-done.39.refs_5_ = f32[32,2048]{1,0:T(8,128)S(1)} collective-permute-done((f32[32,2048]{1,0:T(8,128)S(1)}, f32[32,2048]{1,0:T(8,128)S(1)}, u32[]{:S(2)}, u32[]{:S(2)}) %collective-permute-start.39) | collective-permute-done | bytes 262176 | tf_op jit(solution)/shard_map/ppermute | solution.py:31
  201.9 3.4 %lay_out.1 = f32[32,16384]{1,0:T(8,128)} custom-call(s32[6]{0:T(128)S(1)} %copy-done.14, f32[32,2048]{1,0:T(8,128)S(1)} %join_cores.2.refs_0_, f32[32,2048]{1,0:T(8,128)S(1)} %join_cores.3.refs_1_, f32[32,2048]{1,0:T(8,128)S(1)} %collective-permute-done.34.refs_2_, f32[32,2048]{1,0:T(8,128)} %collective-permute-done.38.refs_3_, ...), custom_call_target="tpu_custom_call" | custom-call | bytes 4000000 | tf_op jit(solution)/shard_map/lay_out/pallas_call | solution.py:288
  (122 shorter events, 29.8 us)
Async XLA Ops:
  0.6 3.0 %collective-permute-start = (bf16[32,16384]{1,0:T(8,128)(2,1)}, bf16[32,16384]{1,0:T(8,128)(2,1)S(1)}, u32[]{:S(2)}, u32[]{:S(2)}) collective-permute-start(bf16[32,16384]{1,0:T(8,128)(2,1)} %distant.1), channel_id=1, source_target_pairs={{0,1},{1,0},{2,3},{3,2},{4,5},{5,4},{6,7},{7,6},{8,9},{9,8},{10,11... | collective-permute-start | bytes 3145736 | tf_op jit(solution)/shard_map/ppermute | solution.py:31
  4.6 10.9 %collective-permute-start.2 = (bf16[128,8192]{1,0:T(8,128)(2,1)}, bf16[128,8192]{1,0:T(8,128)(2,1)S(1)}, u32[]{:S(2)}, u32[]{:S(2)}) collective-permute-start(bf16[128,8192]{1,0:T(8,128)(2,1)} %bitcast.17), channel_id=1, source_target_pairs={{0,1},{1,0},{2,3},{3,2},{4,5},{5,4},{6,7},{7,6},{8,9},{9,8},{10,11... | collective-permute-start | bytes 6291464 | tf_op jit(solution)/shard_map/ppermute | solution.py:31
  5.0 10.6 %collective-permute-start.4 = (bf16[128,8192]{1,0:T(8,128)(2,1)}, bf16[128,8192]{1,0:T(8,128)(2,1)}, u32[]{:S(2)}, u32[]{:S(2)}) collective-permute-start(bf16[128,8192]{1,0:T(8,128)(2,1)} %bitcast.24), channel_id=1, source_target_pairs={{0,1},{1,0},{2,3},{3,2},{4,5},{5,4},{6,7},{7,6},{8,9},{9,8},{10,11... | collective-permute-start | bytes 6291464 | tf_op jit(solution)/shard_map/ppermute | solution.py:31
  5.1 38.7 %copy-start.5 = (f32[1,64,128]{2,1,0:T(8,128)S(1)}, f32[1,64,128]{2,1,0:T(8,128)}, u32[]{:S(2)}) copy-start(f32[1,64,128]{2,1,0:T(8,128)} %param.11) | copy-start | bytes 98308
  5.1 38.7 %copy-start.22 = (s32[1,8,4]{1,2,0:T(4,128)S(1)}, s32[1,8,4]{1,2,0:T(4,128)}, u32[]{:S(2)}) copy-start(s32[1,8,4]{1,2,0:T(4,128)} %param.15) | copy-start | bytes 388
  5.1 38.8 %copy-start.14 = (s32[6]{0:T(128)S(1)}, s32[6]{0:T(128)}, u32[]{:S(2)}) copy-start(s32[6]{0:T(128)} %stack.30.place) | copy-start | bytes 76
  5.1 9.4 %collective-permute-start.3 = (bf16[128,4096]{1,0:T(8,128)(2,1)}, bf16[128,4096]{1,0:T(8,128)(2,1)S(1)}, u32[]{:S(2)}, u32[]{:S(2)}) collective-permute-start(bf16[128,4096]{1,0:T(8,128)(2,1)} %bitcast.31), channel_id=1, source_target_pairs={{0,1},{1,0},{2,3},{3,2},{4,5},{5,4},{6,7},{7,6},{8,9},{9,8},{10,11... | collective-permute-start | bytes 3145736 | tf_op jit(solution)/shard_map/ppermute | solution.py:31
  8.1 16.5 %collective-permute-start.1 = (bf16[64,2048]{1,0:T(8,128)(2,1)}, bf16[64,2048]{1,0:T(8,128)(2,1)S(1)}, u32[]{:S(2)}, u32[]{:S(2)}) collective-permute-start(bf16[64,2048]{1,0:T(8,128)(2,1)} %get-tuple-element.103.refs_0_), channel_id=1, source_target_pairs={{0,4},{1,5},{2,6},{3,7},{4,0},{5,1},{6,2},{7,3},{8,12},{9,13},{10,... | collective-permute-start | bytes 786440 | tf_op jit(solution)/shard_map/ppermute | solution.py:31
  11.9 17.6 %collective-permute-start.9 = (bf16[64,2048]{1,0:T(8,128)(2,1)}, bf16[64,2048]{1,0:T(8,128)(2,1)}, u32[]{:S(2)}, u32[]{:S(2)}) collective-permute-start(bf16[64,2048]{1,0:T(8,128)(2,1)} %get-tuple-element.103.refs_0_), channel_id=1, source_target_pairs={{0,2},{1,3},{2,0},{3,1},{4,6},{5,7},{6,4},{7,5},{8,10},{9,11},{10,... | collective-permute-start | bytes 786440 | tf_op jit(solution)/shard_map/ppermute | solution.py:31
  15.6 13.7 %collective-permute-start.7 = (bf16[144,320]{1,0:T(8,128)(2,1)S(1)}, bf16[144,320]{1,0:T(8,128)(2,1)S(1)}, u32[]{:S(2)}, u32[]{:S(2)}) collective-permute-start(bf16[144,320]{1,0:T(8,128)(2,1)S(1)} %fusion.3.refs_0_), channel_id=1, source_target_pairs={{0,4},{1,5},{2,6},{3,7},{8,12},{9,13},{10,14},{11,15},{16,20},{17,... | collective-permute-start | bytes 276488 | tf_op jit(solution)/shard_map/ppermute | solution.py:26
  20.3 9.0 %collective-permute-start.6 = (bf16[144,320]{1,0:T(8,128)(2,1)S(1)}, bf16[144,320]{1,0:T(8,128)(2,1)S(1)}, u32[]{:S(2)}, u32[]{:S(2)}) collective-permute-start(bf16[144,320]{1,0:T(8,128)(2,1)S(1)} %fusion.3.refs_0_), channel_id=1, source_target_pairs={{0,2},{1,3},{2,4},{3,5},{4,6},{5,7},{8,10},{9,11},{10,12},{11,13},... | collective-permute-start | bytes 276488 | tf_op jit(solution)/shard_map/ppermute | solution.py:26
  24.6 14.8 %collective-permute-start.14 = (bf16[64,2048]{1,0:T(8,128)(2,1)}, bf16[64,2048]{1,0:T(8,128)(2,1)S(1)}, u32[]{:S(2)}, u32[]{:S(2)}) collective-permute-start(bf16[64,2048]{1,0:T(8,128)(2,1)} %get-tuple-element.110.refs_0_), channel_id=1, source_target_pairs={{0,2},{1,3},{2,0},{3,1},{4,6},{5,7},{6,4},{7,5},{8,10},{9,11},{10,... | collective-permute-start | bytes 786440 | tf_op jit(solution)/shard_map/ppermute | solution.py:31
  25.8 15.2 %collective-permute-start.13 = (bf16[64,2048]{1,0:T(8,128)(2,1)}, bf16[64,2048]{1,0:T(8,128)(2,1)}, u32[]{:S(2)}, u32[]{:S(2)}) collective-permute-start(bf16[64,2048]{1,0:T(8,128)(2,1)} %get-tuple-element.110.refs_0_), channel_id=1, source_target_pairs={{0,4},{1,5},{2,6},{3,7},{4,0},{5,1},{6,2},{7,3},{8,12},{9,13},{10,... | collective-permute-start | bytes 786440 | tf_op jit(solution)/shard_map/ppermute | solution.py:31
  29.3 24.3 %copy-start.2 = (bf16[1,128,4096]{2,1,0:T(8,128)(2,1)S(1)}, bf16[1,128,4096]{2,1,0:T(8,128)(2,1)}, u32[]{:S(2)}) copy-start(bf16[1,128,4096]{2,1,0:T(8,128)(2,1)} %param.9) | copy-start | bytes 3145732
  29.4 14.6 %collective-permute-start.8 = (bf16[432,320]{1,0:T(8,128)(2,1)S(1)}, bf16[432,320]{1,0:T(8,128)(2,1)}, u32[]{:S(2)}, u32[]{:S(2)}) collective-permute-start(bf16[432,320]{1,0:T(8,128)(2,1)S(1)} %stack.31.own), channel_id=1, source_target_pairs={{0,1},{1,0},{2,3},{3,2},{4,5},{5,4},{6,7},{7,6},{8,9},{9,8},{10,11... | collective-permute-start | bytes 829448 | tf_op jit(solution)/shard_map/ppermute | solution.py:31
  29.5 16.7 %collective-permute-start.10 = (bf16[64,2048]{1,0:T(8,128)(2,1)}, bf16[64,2048]{1,0:T(8,128)(2,1)}, u32[]{:S(2)}, u32[]{:S(2)}) collective-permute-start(bf16[64,2048]{1,0:T(8,128)(2,1)} %copy-done.10), channel_id=1, source_target_pairs={{0,2},{1,3},{2,0},{3,1},{4,6},{5,7},{6,4},{7,5},{8,10},{9,11},{10,... | collective-permute-start | bytes 786440 | tf_op jit(solution)/shard_map/ppermute | solution.py:31
  41.0 11.5 %collective-permute-start.15 = (bf16[64,2048]{1,0:T(8,128)(2,1)}, bf16[64,2048]{1,0:T(8,128)(2,1)}, u32[]{:S(2)}, u32[]{:S(2)}) collective-permute-start(bf16[64,2048]{1,0:T(8,128)(2,1)} %collective-permute-done.13.refs_1_), channel_id=1, source_target_pairs={{0,2},{1,3},{2,0},{3,1},{4,6},{5,7},{6,4},{7,5},{8,10},{9,11},{10,... | collective-permute-start | bytes 786440 | tf_op jit(solution)/shard_map/ppermute | solution.py:31
  43.8 2.2 %collective-permute-start.5 = (f32[64,128]{1,0:T(8,128)S(1)}, f32[64,128]{1,0:T(8,128)S(1)}, u32[]{:S(2)}, u32[]{:S(2)}) collective-permute-start(f32[64,128]{1,0:T(8,128)S(1)} %bitcast.38), channel_id=1, source_target_pairs={{0,1},{1,0},{2,3},{3,2},{4,5},{5,4},{6,7},{7,6},{8,9},{9,8},{10,11... | collective-permute-start | bytes 98312 | tf_op jit(solution)/shard_map/ppermute | solution.py:31
  49.5 26.0 %collective-permute-start.12 = (bf16[256,2048]{1,0:T(8,128)(2,1)S(1)}, bf16[256,2048]{1,0:T(8,128)(2,1)S(1)}, u32[]{:S(2)}, u32[]{:S(2)}) collective-permute-start(bf16[256,2048]{1,0:T(8,128)(2,1)S(1)} %stack.32.weight), channel_id=1, source_target_pairs={{0,8},{8,0},{16,24},{24,16},{1,9},{9,1},{17,25},{25,17},{2,10},{10... | collective-permute-start | bytes 3145736 | tf_op jit(solution)/shard_map/ppermute | solution.py:31
  51.0 26.0 %collective-permute-start.11 = (bf16[256,2048]{1,0:T(8,128)(2,1)S(1)}, bf16[256,2048]{1,0:T(8,128)(2,1)S(1)}, u32[]{:S(2)}, u32[]{:S(2)}) collective-permute-start(bf16[256,2048]{1,0:T(8,128)(2,1)S(1)} %stack.32.weight), channel_id=1, source_target_pairs={{0,16},{8,24},{16,0},{24,8},{1,17},{9,25},{17,1},{25,9},{2,18},{10... | collective-permute-start | bytes 3145736 | tf_op jit(solution)/shard_map/ppermute | solution.py:31
  67.9 31.2 %collective-permute-start.17 = (f32[128,2048]{1,0:T(8,128)S(1)}, f32[128,2048]{1,0:T(8,128)S(1)}, u32[]{:S(2)}, u32[]{:S(2)}) collective-permute-start(f32[128,2048]{1,0:T(8,128)S(1)} %get-tuple-element.120), channel_id=1, source_target_pairs={{0,16},{8,24},{16,0},{24,8},{1,17},{9,25},{17,1},{25,9},{2,18},{10... | collective-permute-start | bytes 3145736 | tf_op jit(solution)/shard_map/ppermute | solution.py:31
  68.4 30.9 %collective-permute-start.16 = (f32[128,2048]{1,0:T(8,128)S(1)}, f32[128,2048]{1,0:T(8,128)S(1)}, u32[]{:S(2)}, u32[]{:S(2)}) collective-permute-start(f32[128,2048]{1,0:T(8,128)S(1)} %get-tuple-element.119), channel_id=1, source_target_pairs={{0,8},{8,0},{16,24},{24,16},{1,9},{9,1},{17,25},{25,17},{2,10},{10... | collective-permute-start | bytes 3145736 | tf_op jit(solution)/shard_map/ppermute | solution.py:31
  89.8 44.3 %collective-permute-start.18 = (f32[128,2048]{1,0:T(8,128)S(1)}, f32[128,2048]{1,0:T(8,128)S(1)}, u32[]{:S(2)}, u32[]{:S(2)}) collective-permute-start(f32[128,2048]{1,0:T(8,128)S(1)} %get-tuple-element.129), channel_id=1, source_target_pairs={{0,8},{8,0},{16,24},{24,16},{1,9},{9,1},{17,25},{25,17},{2,10},{10... | collective-permute-start | bytes 3145736 | tf_op jit(solution)/shard_map/ppermute | solution.py:31
  97.6 12.4 %collective-permute-start.19 = (f32[128,1024]{1,0:T(8,128)S(1)}, f32[128,1024]{1,0:T(8,128)S(1)}, u32[]{:S(2)}, u32[]{:S(2)}) collective-permute-start(f32[128,1024]{1,0:T(8,128)S(1)} %get-tuple-element.130), channel_id=1, source_target_pairs={{0,16},{8,24},{16,0},{24,8},{1,17},{9,25},{17,1},{25,9},{2,18},{10... | collective-permute-start | bytes 1572872 | tf_op jit(solution)/shard_map/ppermute | solution.py:31
  99.3 32.3 %collective-permute-start.23 = (f32[128,1024]{1,0:T(8,128)S(1)}, f32[128,1024]{1,0:T(8,128)S(1)}, u32[]{:S(2)}, u32[]{:S(2)}) collective-permute-start(f32[128,1024]{1,0:T(8,128)S(1)} %get-tuple-element.156), channel_id=1, source_target_pairs={{0,8},{8,0},{16,24},{24,16},{1,9},{9,1},{17,25},{25,17},{2,10},{10... | collective-permute-start | bytes 1572872 | tf_op jit(solution)/shard_map/ppermute | solution.py:31
  110.0 21.7 %collective-permute-start.24 = (f32[128,1024]{1,0:T(8,128)S(1)}, f32[128,1024]{1,0:T(8,128)S(1)}, u32[]{:S(2)}, u32[]{:S(2)}) collective-permute-start(f32[128,1024]{1,0:T(8,128)S(1)} %get-tuple-element.158), channel_id=1, source_target_pairs={{0,16},{8,24},{16,0},{24,8},{1,17},{9,25},{17,1},{25,9},{2,18},{10... | collective-permute-start | bytes 1572872 | tf_op jit(solution)/shard_map/ppermute | solution.py:31
  111.5 31.5 %collective-permute-start.27 = (f32[128,1024]{1,0:T(8,128)S(1)}, f32[128,1024]{1,0:T(8,128)S(1)}, u32[]{:S(2)}, u32[]{:S(2)}) collective-permute-start(f32[128,1024]{1,0:T(8,128)S(1)} %get-tuple-element.168), channel_id=1, source_target_pairs={{0,8},{8,0},{16,24},{24,16},{1,9},{9,1},{17,25},{25,17},{2,10},{10... | collective-permute-start | bytes 1572872 | tf_op jit(solution)/shard_map/ppermute | solution.py:31
  112.9 21.3 %collective-permute-start.20 = (f32[128,1024]{1,0:T(8,128)S(1)}, f32[128,1024]{1,0:T(8,128)S(1)}, u32[]{:S(2)}, u32[]{:S(2)}) collective-permute-start(f32[128,1024]{1,0:T(8,128)S(1)} %get-tuple-element.131), channel_id=1, source_target_pairs={{0,16},{8,24},{16,0},{24,8},{1,17},{9,25},{17,1},{25,9},{2,18},{10... | collective-permute-start | bytes 1572872 | tf_op jit(solution)/shard_map/ppermute | solution.py:31
  131.8 13.2 %collective-permute-start.25 = (f32[128,1024]{1,0:T(8,128)S(1)}, f32[128,1024]{1,0:T(8,128)S(1)}, u32[]{:S(2)}, u32[]{:S(2)}) collective-permute-start(f32[128,1024]{1,0:T(8,128)S(1)} %add_add_fusion.2), channel_id=1, source_target_pairs={{0,2},{1,3},{2,0},{3,1},{4,6},{5,7},{6,4},{7,5},{8,10},{9,11},{10,... | collective-permute-start | bytes 1572872 | tf_op jit(solution)/shard_map/ppermute | solution.py:31
  134.2 12.7 %copy-start.19 = (f32[128,2048]{1,0:T(8,128)}, f32[128,2048]{1,0:T(8,128)S(1)}, u32[]{:S(2)}) copy-start(f32[128,2048]{1,0:T(8,128)S(1)} %collective-permute-done.18) | copy-start | bytes 3145732
  134.2 11.7 %collective-permute-start.26 = (f32[128,1024]{1,0:T(8,128)S(1)}, f32[128,1024]{1,0:T(8,128)S(1)}, u32[]{:S(2)}, u32[]{:S(2)}) collective-permute-start(f32[128,1024]{1,0:T(8,128)S(1)} %get-tuple-element.163), channel_id=1, source_target_pairs={{0,16},{8,24},{16,0},{24,8},{1,17},{9,25},{17,1},{25,9},{2,18},{10... | collective-permute-start | bytes 1572872 | tf_op jit(solution)/shard_map/ppermute | solution.py:31
  143.0 22.8 %collective-permute-start.21 = (bf16[128,6144]{1,0:T(8,128)(2,1)}, bf16[128,6144]{1,0:T(8,128)(2,1)S(1)}, u32[]{:S(2)}, u32[]{:S(2)}) collective-permute-start(bf16[128,6144]{1,0:T(8,128)(2,1)} %get-tuple-element.136), channel_id=1, source_target_pairs={{0,1},{1,0},{2,3},{3,2},{4,5},{5,4},{6,7},{7,6},{8,9},{9,8},{10,11... | collective-permute-start | bytes 4718600 | tf_op jit(solution)/shard_map/ppermute | solution.py:31
  145.9 18.3 %collective-permute-start.28 = (f32[128,1024]{1,0:T(8,128)}, f32[128,1024]{1,0:T(8,128)}, u32[]{:S(2)}, u32[]{:S(2)}) collective-permute-start(f32[128,1024]{1,0:T(8,128)} %add_add_fusion), channel_id=1, source_target_pairs={{0,2},{1,3},{2,0},{3,1},{4,6},{5,7},{6,4},{7,5},{8,10},{9,11},{10,... | collective-permute-start | bytes 1572872 | tf_op jit(solution)/shard_map/ppermute | solution.py:31
  147.8 14.2 %collective-permute-start.32 = (f32[64,1024]{1,0:T(8,128)}, f32[64,1024]{1,0:T(8,128)}, u32[]{:S(2)}, u32[]{:S(2)}) collective-permute-start(f32[64,1024]{1,0:T(8,128)} %slice.82), channel_id=1, source_target_pairs={{0,4},{1,5},{2,6},{3,7},{4,0},{5,1},{6,2},{7,3},{8,12},{9,13},{10,... | collective-permute-start | bytes 786440 | tf_op jit(solution)/shard_map/ppermute | solution.py:31
  152.9 11.3 %copy-start.7 = (f32[128,1024]{1,0:T(8,128)S(1)}, f32[128,1024]{1,0:T(8,128)}, u32[]{:S(2)}) copy-start(f32[128,1024]{1,0:T(8,128)} %copy-done.6) | copy-start | bytes 1572868
  154.0 11.8 %collective-permute-start.22 = (f32[432,320]{0,1:T(8,128)}, f32[432,320]{0,1:T(8,128)S(1)}, u32[]{:S(2)}, u32[]{:S(2)}) collective-permute-start(f32[432,320]{0,1:T(8,128)} %copy.36), channel_id=1, source_target_pairs={{0,1},{1,0},{2,3},{3,2},{4,5},{5,4},{6,7},{7,6},{8,9},{9,8},{10,11... | collective-permute-start | bytes 1658888 | tf_op jit(solution)/shard_map/ppermute | solution.py:31
  166.6 13.2 %collective-permute-start.29 = (f32[64,1024]{1,0:T(8,128)}, f32[64,1024]{1,0:T(8,128)}, u32[]{:S(2)}, u32[]{:S(2)}) collective-permute-start(f32[64,1024]{1,0:T(8,128)} %slice.65), channel_id=1, source_target_pairs={{0,4},{1,5},{2,6},{3,7},{4,0},{5,1},{6,2},{7,3},{8,12},{9,13},{10,... | collective-permute-start | bytes 786440 | tf_op jit(solution)/shard_map/ppermute | solution.py:31
  168.9 1.5 collective-permute-start.33
  170.4 9.5 %copy-start.17 = (f32[128,1024]{1,0:T(8,128)S(1)}, f32[128,1024]{1,0:T(8,128)}, u32[]{:S(2)}) copy-start(f32[128,1024]{1,0:T(8,128)} %copy-done.16) | copy-start | bytes 1572868
  171.0 12.4 %collective-permute-start.36 = (f32[32,2048]{1,0:T(8,128)S(1)}, f32[32,2048]{1,0:T(8,128)S(1)}, u32[]{:S(2)}, u32[]{:S(2)}) collective-permute-start(f32[32,2048]{1,0:T(8,128)S(1)} %join_cores.2.refs_0_), channel_id=1, source_target_pairs={{0,24},{8,16},{16,8},{24,0},{1,25},{9,17},{17,9},{25,1},{2,26},{10... | collective-permute-start | bytes 786440 | tf_op jit(solution)/shard_map/ppermute | solution.py:31
  173.4 12.9 %collective-permute-start.35 = (f32[32,2048]{1,0:T(8,128)S(1)}, f32[32,2048]{1,0:T(8,128)S(1)}, u32[]{:S(2)}, u32[]{:S(2)}) collective-permute-start(f32[32,2048]{1,0:T(8,128)S(1)} %join_cores.2.refs_0_), channel_id=1, source_target_pairs={{0,16},{8,24},{16,0},{24,8},{1,17},{9,25},{17,1},{25,9},{2,18},{10... | collective-permute-start | bytes 786440 | tf_op jit(solution)/shard_map/ppermute | solution.py:31
  174.1 12.3 %collective-permute-start.34 = (f32[32,2048]{1,0:T(8,128)S(1)}, f32[32,2048]{1,0:T(8,128)S(1)}, u32[]{:S(2)}, u32[]{:S(2)}) collective-permute-start(f32[32,2048]{1,0:T(8,128)S(1)} %join_cores.2.refs_0_), channel_id=1, source_target_pairs={{0,8},{8,0},{16,24},{24,16},{1,9},{9,1},{17,25},{25,17},{2,10},{10... | collective-permute-start | bytes 786440 | tf_op jit(solution)/shard_map/ppermute | solution.py:31
  180.9 12.0 %collective-permute-start.30 = (f32[128,320]{1,0:T(8,128)S(1)}, f32[128,320]{1,0:T(8,128)S(1)}, u32[]{:S(2)}, u32[]{:S(2)}) collective-permute-start(f32[128,320]{1,0:T(8,128)S(1)} %get-tuple-element.188), channel_id=1, source_target_pairs={{2,0},{3,1},{4,2},{5,3},{6,4},{7,5},{10,8},{11,9},{12,10},{13,11},... | collective-permute-start | bytes 491528 | tf_op jit(solution)/shard_map/ppermute | solution.py:26
  182.2 12.6 %collective-permute-start.31 = (f32[128,320]{1,0:T(8,128)S(1)}, f32[128,320]{1,0:T(8,128)S(1)}, u32[]{:S(2)}, u32[]{:S(2)}) collective-permute-start(f32[128,320]{1,0:T(8,128)S(1)} %get-tuple-element.189), channel_id=1, source_target_pairs={{4,0},{5,1},{6,2},{7,3},{12,8},{13,9},{14,10},{15,11},{20,16},{21,... | collective-permute-start | bytes 491528 | tf_op jit(solution)/shard_map/ppermute | solution.py:26
  183.5 2.8 %collective-permute-start.37 = (f32[32,1024]{1,0:T(8,128)S(1)}, f32[32,1024]{1,0:T(8,128)S(1)}, u32[]{:S(2)}, u32[]{:S(2)}) collective-permute-start(f32[32,1024]{1,0:T(8,128)S(1)} %get-tuple-element.190), channel_id=1, source_target_pairs={{0,1},{1,0},{2,3},{3,2},{4,5},{5,4},{6,7},{7,6},{8,9},{9,8},{10,11... | collective-permute-start | bytes 393224 | tf_op jit(solution)/shard_map/ppermute | solution.py:31
  186.9 10.2 %collective-permute-start.40 = (f32[32,2048]{1,0:T(8,128)S(1)}, f32[32,2048]{1,0:T(8,128)S(1)}, u32[]{:S(2)}, u32[]{:S(2)}) collective-permute-start(f32[32,2048]{1,0:T(8,128)S(1)} %join_cores.3.refs_1_), channel_id=1, source_target_pairs={{0,24},{8,16},{16,8},{24,0},{1,25},{9,17},{17,9},{25,1},{2,26},{10... | collective-permute-start | bytes 786440 | tf_op jit(solution)/shard_map/ppermute | solution.py:31
  188.7 13.0 %collective-permute-start.39 = (f32[32,2048]{1,0:T(8,128)S(1)}, f32[32,2048]{1,0:T(8,128)S(1)}, u32[]{:S(2)}, u32[]{:S(2)}) collective-permute-start(f32[32,2048]{1,0:T(8,128)S(1)} %join_cores.3.refs_1_), channel_id=1, source_target_pairs={{0,16},{8,24},{16,0},{24,8},{1,17},{9,25},{17,1},{25,9},{2,18},{10... | collective-permute-start | bytes 786440 | tf_op jit(solution)/shard_map/ppermute | solution.py:31
  189.9 11.9 %collective-permute-start.38 = (f32[32,2048]{1,0:T(8,128)S(1)}, f32[32,2048]{1,0:T(8,128)}, u32[]{:S(2)}, u32[]{:S(2)}) collective-permute-start(f32[32,2048]{1,0:T(8,128)S(1)} %join_cores.3.refs_1_), channel_id=1, source_target_pairs={{0,8},{8,0},{16,24},{24,16},{1,9},{9,1},{17,25},{25,17},{2,10},{10... | collective-permute-start | bytes 786440 | tf_op jit(solution)/shard_map/ppermute | solution.py:31
  (17 other events, 66.9 us)
